TPU v7x, 256 devices: a whole 4x4x8 slice. The times are simulated.
256 devices in a mesh: dp: 32 (over y, x, z_hi), ctx: 8 (over z_lo, core).
Axes of the slice: x: 4, y: 4, z: 8 (z_hi: 2, z_lo: 4; z = z_hi * 4 + z_lo), core: 2. Of those that a mesh axis runs over, the one named last changes fastest.
Arguments:
- queries: bfloat16 [32, 1024, 2048], P('dp', 'ctx'), may hold values from -9 to 9
- keys: bfloat16 [32, 1024, 256], P('dp', 'ctx'), may hold values from -9 to 9
- values: bfloat16 [32, 1024, 256], P('dp', 'ctx'), may hold values from -6 to 6
- out_grad: bfloat16 [32, 1024, 2048], P('dp', 'ctx'), may hold values from -6 to 6
- layer_input: bfloat16 [32, 1024, 8192], P('dp', 'ctx'), may hold values from -6 to 6
- segment_ids: int32 [32, 1024], P('dp'), may hold values from 0 to 7, never falling along the last dimension, each value on 1 to 512 neighbouring positions
Outputs:
- query_grad: bfloat16 [32, 1024, 2048], P('dp', 'ctx')
- kv_weight_grad: float32 [8192, 512], P(('dp', 'ctx'))
Inputs may be any that keep to these rules, and one draw needn't show every extreme that they name: `segment_ids`: never falls along a sequence; each document holds 1 to 512 positions and one holds exactly 512.
All inputs are finite; a program needn't handle non-finite values.
Results may differ from a plain program's by a relative error of at most 0.01.
The roundings to bfloat16 on the way count: a program that leaves them out, or rounds other values in their place, can miss the bound.
Values may be sent and summed in bfloat16 or wider, within the bound.
No kernel may reach another device: no remote copies, remote signals or barrier semaphores. Data moves between devices by JAX's collectives and lax.ppermute only.
A program may use at most 128 MiB of HBM per device.

v0:
```python
import jax
import jax.numpy as jnp
from jax import lax
from jax.sharding import PartitionSpec as P

H = 16
KV = 2
DH = 128


masked_score = -1e30


def block_mask(seg_row, query_doc, query_pos, block, rows):
    start = block * rows
    key_pos = start + jnp.arange(rows, dtype=jnp.int32)
    key_doc = lax.dynamic_slice_in_dim(seg_row, start, rows, 0)
    return (key_pos[None, :] <= query_pos[:, None]) & (key_doc[None, :] == query_doc[:, None])


def contract_rows(left, right):
    return lax.dot_general(
        left, right, (((0,), (0,)), ((), ())), preferred_element_type=jnp.float32
    )


def per_device(queries, keys, values, out_grad, layer_input, segment_ids):
    rows = queries.shape[1]
    width = keys.shape[2]
    per_group = H // KV
    scale = 1.0 / DH**0.5
    n_ctx = lax.axis_size("ctx")
    here = lax.axis_index("ctx")
    seg_row = segment_ids[0]
    query_pos = here * rows + jnp.arange(rows, dtype=jnp.int32)
    query_doc = lax.dynamic_slice_in_dim(seg_row, here * rows, rows, 0)
    query_heads = queries[0].reshape(rows, KV, per_group, DH)
    grad_heads = out_grad[0].reshape(rows, KV, per_group, DH)

    def scores(key_block, block):
        allowed = block_mask(seg_row, query_doc, query_pos, block, rows)
        key_heads = key_block.reshape(rows, KV, DH)
        raw = (
            jnp.einsum("qgrd,kgd->grqk", query_heads, key_heads, preferred_element_type=jnp.float32)
            * scale
        )
        return (jnp.where(allowed, raw, masked_score), allowed)

    def running_stats(state, key_block, block):
        top, row_sum = state
        masked, allowed = scores(key_block, block)
        new_top = jnp.maximum(top, jnp.max(masked, axis=3, keepdims=True))
        weights = jnp.where(allowed, jnp.exp(masked - new_top), 0.0)
        return (new_top, row_sum * jnp.exp(top - new_top) + jnp.sum(weights, axis=3, keepdims=True))

    def probabilities(key_block, block, stats):
        masked, allowed = scores(key_block, block)
        prob = jnp.where(allowed, jnp.exp(masked - stats[0]), 0.0) / stats[1]
        return (prob, prob.astype(jnp.bfloat16))

    def output_add(acc, pair, block, stats):
        prob, prob_half = probabilities(pair[0], block, stats)
        value_heads = pair[1].reshape(rows, KV, DH)
        return acc + jnp.einsum(
            "grqk,kgd->qgrd", prob_half, value_heads, preferred_element_type=jnp.float32
        )

    def gradient_terms(pair, block, stats, delta):
        prob, prob_half = probabilities(pair[0], block, stats)
        key_heads = pair[0].reshape(rows, KV, DH)
        value_heads = pair[1].reshape(rows, KV, DH)
        prob_grad = jnp.einsum(
            "qgrd,kgd->grqk", grad_heads, value_heads, preferred_element_type=jnp.float32
        )
        score_grad = (prob * (prob_grad - delta) * scale).astype(jnp.bfloat16)
        query_part = jnp.einsum(
            "grqk,kgd->qgrd", score_grad, key_heads, preferred_element_type=jnp.float32
        )
        key_part = jnp.einsum(
            "grqk,qgrd->kgd", score_grad, query_heads, preferred_element_type=jnp.float32
        )
        value_part = jnp.einsum(
            "grqk,qgrd->kgd", prob_half, grad_heads, preferred_element_type=jnp.float32
        )
        joined = jnp.concatenate(
            [key_part.reshape(rows, width), value_part.reshape(rows, width)], axis=1
        )
        return (query_part, joined)

    start_stats = (
        jnp.full((KV, per_group, rows, 1), masked_score, jnp.float32),
        jnp.zeros((KV, per_group, rows, 1), jnp.float32),
    )
    empty_out = jnp.zeros((rows, KV, per_group, DH), jnp.float32)
    key_all, value_all = (
        lax.all_gather(keys, "ctx", axis=1, tiled=True),
        lax.all_gather(values, "ctx", axis=1, tiled=True),
    )
    key_all = key_all[0]
    value_all = value_all[0]

    def fetch(block):
        return (
            lax.dynamic_slice_in_dim(key_all, block * rows, rows, 0),
            lax.dynamic_slice_in_dim(value_all, block * rows, rows, 0),
        )

    lowest = jnp.int32(0)
    needed = here + 1

    def stats_step(block, state):
        return running_stats(state, fetch(block)[0], block)

    stats = lax.fori_loop(lowest, needed, stats_step, start_stats)

    def output_step(block, acc):
        return output_add(acc, fetch(block), block, stats)

    delta = jnp.sum(
        grad_heads.astype(jnp.float32) * lax.fori_loop(lowest, needed, output_step, empty_out),
        axis=3,
    ).transpose(1, 2, 0)[..., None]

    def grad_step(block, state):
        query_acc, term_rows = state
        query_part, pair_part = gradient_terms(fetch(block), block, stats, delta)
        return (
            query_acc + query_part,
            lax.dynamic_update_slice_in_dim(term_rows, pair_part, block * rows, 0),
        )

    start_terms = jnp.zeros((rows * n_ctx, 2 * width), jnp.float32)
    query_acc, term_rows = lax.fori_loop(lowest, needed, grad_step, (empty_out, start_terms))
    pair_grad = lax.psum_scatter(term_rows, "ctx", scatter_dimension=0, tiled=True).astype(
        jnp.bfloat16
    )
    query_grad = query_acc.reshape(1, rows, H * DH).astype(jnp.bfloat16)
    columns = layer_input[0]
    weight_grad = lax.psum_scatter(
        contract_rows(columns, pair_grad), ("dp", "ctx"), scatter_dimension=0, tiled=True
    )
    return (query_grad, weight_grad)


def solution(mesh):
    return jax.shard_map(
        per_device,
        mesh=mesh,
        in_specs=(
            P("dp", "ctx", None),
            P("dp", "ctx", None),
            P("dp", "ctx", None),
            P("dp", "ctx", None),
            P("dp", "ctx", None),
            P("dp", None),
        ),
        out_specs=(P("dp", "ctx", None), P(("dp", "ctx"), None)),
        check_vma=False,
    )
```

profile of v0, /device:TPU:1, one launch (start us, length us, event | category | flops | bytes accessed | tf_op | source)
XLA Modules:
  0.0 1501.2 jit_solution(702369194861011529)
XLA Ops:
  7.2 1.1 copy.66
  8.3 1.0 copy.69
  9.3 17.7 %all_gather.7 = bf16[1,1024,256]{1,2,0:T(8,128)(2,1)} all-gather(bf16[1,128,256]{1,2,0:T(8,128)(2,1)S(1)} %copy.69), channel_id=1, replica_groups=mesh['dp'=32,'ctx'=8] {'ctx'}, dimensions={1}, use_global_device_ids=true | all-gather | bytes 589824 | tf_op jit(solution)/shard_map/all_gather | solution.py:97
  27.0 14.7 all_gather.6
  41.7 1.3 copy.67
  43.0 1.0 copy.68
  44.0 5.4 while.37
  44.2 0.9 constant_dynamic-slice_fusion.8
  45.1 1.4 fusion.80
  46.5 0.2 select_reduce_fusion.2
  47.0 0.9 constant_dynamic-slice_fusion.8
  47.8 1.4 fusion.80
  49.5 1.3 copy.70
  50.8 1.1 broadcast_in_dim.65.clone
  51.9 8.3 while.38
  52.1 0.9 constant_dynamic-slice_fusion.9
  53.0 3.1 fusion.84
  56.2 0.9 constant_dynamic-slice_fusion.9
  57.1 3.1 fusion.84
  60.2 1.3 multiply_reduce_fusion
  61.6 1.1 broadcast_in_dim.65
  62.6 1.6 broadcast_in_dim.66
  64.2 9.0 while.39
  64.4 0.9 constant_dynamic-slice_fusion.10
  65.3 0.5 fusion.95
  65.8 0.3 fusion.98
  66.1 0.3 fusion.96
  66.5 0.3 fusion.99
  66.8 0.6 copy-done.1
  67.3 0.3 fusion.97
  67.7 0.8 maximum_dynamic-update-slice_fusion.2
  68.5 0.3 copy-done.2
  68.9 0.9 constant_dynamic-slice_fusion.10
  69.8 0.5 fusion.95
  70.3 0.3 fusion.98
  70.6 0.3 fusion.96
  71.0 0.3 fusion.99
  71.3 0.6 copy-done.1
  71.8 0.3 fusion.97
  72.2 0.8 maximum_dynamic-update-slice_fusion.2
  73.0 0.3 copy-done.2
  73.3 103.6 %reduce-scatter.5.cloned.1.call-done = f32[128,512]{0,1:T(8,128)} async-done(((f32[1024,512]{0,1:T(8,128)}), f32[128,512]{0,1:T(8,128)}) %reduce-scatter.5.cloned.1.call-update) | async-done | bytes 262160 | tf_op jit(solution)/shard_map/reduce_scatter | solution.py:134
  176.9 9.0 convolution_bitcast_fusion.3
  185.9 17.5 %copy.97 = f32[8192,512]{1,0:T(8,128)} copy(f32[8192,512]{0,1:T(8,128)} %convolution_bitcast_fusion.3) | data formatting | bytes 33554432
  203.4 1.2 copy-done.3
  204.6 0.9 convert_element_type.30
  205.5 2.0 copy.88
  207.5 1286.8 %reduce-scatter.7.cloned.1.call-done = f32[32,512]{1,0:T(8,128)} async-done(((f32[8192,512]{1,0:T(8,128)}), f32[32,512]{1,0:T(8,128)}) %reduce-scatter.7.cloned.1.call-update) | async-done | bytes 65552
  (41 shorter events, 1.5 us)
Async XLA Ops:
  7.2 169.8 %copy-start = (bf16[1,128,8192]{2,1,0:T(8,128)(2,1)S(1)}, bf16[1,128,8192]{2,1,0:T(8,128)(2,1)}, u32[]{:S(2)}) copy-start(bf16[1,128,8192]{2,1,0:T(8,128)(2,1)} %param.16) | copy-start | bytes 6291460
  7.2 36.8 %copy-start.4 = (s32[1,1024]{1,0:T(1,128)S(1)}, s32[1,1024]{1,0:T(1,128)}, u32[]{:S(2)}) copy-start(s32[1,1024]{1,0:T(1,128)} %param.17) | copy-start | bytes 12292
  7.2 169.7 %reduce-scatter.5.cloned.1.call-start = ((), (), s32[]{:S(2)}) async-start(), calls=%async_computation.2 | async-start | bytes 2359296 | tf_op jit(solution)/shard_map/reduce_scatter | solution.py:134
  66.1 1.2 copy-start.1
  67.7 1.1 copy-start.2
  70.6 1.2 copy-start.1
  72.2 1.1 copy-start.2
  73.3 1421.0 %reduce-scatter.7.cloned.1.call-start = ((), (), s32[]{:S(2)}) async-start(), calls=%async_computation.3 | async-start | bytes 16842752
  203.4 1.2 copy-start.3
Sparse Core Ops, SparseCore 0:
  73.4 103.4 reduce-scatter.4
  203.5 1290.7 reduce-scatter.6
where the time goes:
time: 1510 us; the launch traced here: 1500 us
  waiting for transfers between devices  1390 us (92%)
  local copies, waits for them, and re-layouts  37.5 us (2%)
  blocking collectives  32.4 us (2%)
  matrix products  21.4 us (1%)
    unnamed x3, waiting for transfers between devices  1290 us
    reduce_scatter x1, waiting for transfers between devices, per_device(): lax.psum_scatter(term_rows, 'ctx', scatter_dimension=0, tiled=True)  104 us
  transfers between devices with their start and end apart: 2, of which 2 were waited for; matrix products, arithmetic and copies ran while one was open for 0% of the time, Pallas kernels for 0%

commit v1 on v0

v1 whole, which is shorter than its diff:
```python
import jax
import jax.numpy as jnp
from jax import lax
from jax.experimental import pallas as pl
from jax.experimental.pallas import tpu as pltpu
from jax.sharding import Mesh, PartitionSpec as P

H = 16
KV = 2
DH = 128
GROUP = H // KV
SCALE = 1.0 / DH**0.5
LOG2E = 1.4426950408889634
REACH = 2
MASKED = -1e30


def dot_nt(left, right):
    return lax.dot_general(
        left, right, (((1,), (1,)), ((), ())), preferred_element_type=jnp.float32
    )


def dot_nn(left, right):
    return jnp.dot(left, right, preferred_element_type=jnp.float32)


def attention_kernel(
    q_mine, do_mine, qdo_other, k0, k1, k2, k3, k4, k5, bias,
    dq_mine, dq_other, own_grad, near_grad, far_grad, dk_acc, dv_acc,
):
    pairs = jnp.concatenate([ref[...] for ref in (k0, k1, k2, k3, k4, k5)], axis=0)
    key, value = pairs[:, :DH], pairs[:, DH:]
    key_t = key.T
    rows = q_mine.shape[0]
    for head in range(GROUP):
        cols = slice(head * DH, (head + 1) * DH)
        grad_cols = slice((GROUP + head) * DH, (GROUP + head + 1) * DH)
        query = jnp.concatenate([q_mine[:, cols], qdo_other[:, cols]], axis=0)
        grad = jnp.concatenate([do_mine[:, cols], qdo_other[:, grad_cols]], axis=0)
        score = dot_nt(key, query) * (SCALE * LOG2E) + bias[...]
        top = jnp.max(score, axis=0, keepdims=True)
        weight = jnp.exp2(score - top)
        inverse = 1.0 / jnp.sum(weight, axis=0, keepdims=True)
        prob = weight * inverse
        prob_half = prob.astype(jnp.bfloat16)
        prob_grad = dot_nt(value, grad)
        delta = jnp.sum(prob_half.astype(jnp.float32) * prob_grad, axis=0, keepdims=True)
        score_grad = (prob * (prob_grad - delta) * SCALE).astype(jnp.bfloat16)
        dq = dot_nn(key_t, score_grad).T.astype(jnp.bfloat16)
        dq_mine[:, cols] = dq[:rows]
        dq_other[:, cols] = dq[rows:]
        dk = dot_nn(score_grad, query)
        dv = dot_nn(prob_half, grad)
        if head == 0:
            dk_acc[...] = dk
            dv_acc[...] = dv
        else:
            dk_acc[...] += dk
            dv_acc[...] += dv
    chip = 2 * rows
    own_grad[:, :DH] = dk_acc[:chip]
    own_grad[:, DH:] = dv_acc[:chip]
    near_grad[:, :DH] = dk_acc[chip : 2 * chip].astype(jnp.bfloat16)
    near_grad[:, DH:] = dv_acc[chip : 2 * chip].astype(jnp.bfloat16)
    far_grad[:, :DH] = dk_acc[2 * chip :].astype(jnp.bfloat16)
    far_grad[:, DH:] = dv_acc[2 * chip :].astype(jnp.bfloat16)


def attention(q_mine, do_mine, qdo_other, blocks, bias):
    rows = q_mine.shape[0]
    chip = 2 * rows
    keys = chip * (REACH + 1)
    half = jnp.bfloat16
    return pl.pallas_call(
        attention_kernel,
        out_shape=(
            jax.ShapeDtypeStruct((rows, GROUP * DH), half),
            jax.ShapeDtypeStruct((rows, GROUP * DH), half),
            jax.ShapeDtypeStruct((chip, 2 * DH), jnp.float32),
            jax.ShapeDtypeStruct((chip, 2 * DH), half),
            jax.ShapeDtypeStruct((chip, 2 * DH), half),
        ),
        scratch_shapes=[
            pltpu.VMEM((keys, DH), jnp.float32),
            pltpu.VMEM((keys, DH), jnp.float32),
        ],
        compiler_params=pltpu.CompilerParams(vmem_limit_bytes=32 * 1024 * 1024),
        cost_estimate=pl.CostEstimate(
            flops=10 * keys * chip * DH * GROUP,
            bytes_accessed=4 * 1024 * 1024,
            transcendentals=keys * chip * GROUP,
        ),
    )(q_mine, do_mine, qdo_other, *blocks, bias)


def per_device(queries, keys, values, out_grad, layer_input, segment_ids):
    rows = queries.shape[1]
    chip = 2 * rows
    z_lo = lax.axis_index("z_lo")
    core = lax.axis_index("core")
    n_chips = lax.axis_size("z_lo")
    n_plane = lax.axis_size("y") * lax.axis_size("x")

    def half_of(array, which):
        width = array.shape[-1] // 2
        return lax.dynamic_slice_in_dim(array[0], which * width, width, 1)

    swap = [(0, 1), (1, 0)]

    pair_mine = jnp.concatenate([half_of(keys, core), half_of(values, core)], axis=1)
    pair_other = jnp.concatenate([half_of(keys, 1 - core), half_of(values, 1 - core)], axis=1)

    def behind(distance, flip):
        return [
            (chip_at * 2 + c, (chip_at + distance) * 2 + (c ^ flip))
            for chip_at in range(n_chips - distance)
            for c in range(2)
        ]

    blocks = [pair_mine, lax.ppermute(pair_other, "core", swap)]
    for distance in range(1, REACH + 1):
        blocks.append(lax.ppermute(pair_mine, ("z_lo", "core"), behind(distance, 0)))
        blocks.append(lax.ppermute(pair_other, ("z_lo", "core"), behind(distance, 1)))
    q_mine, do_mine = half_of(queries, core), half_of(out_grad, core)
    qdo_other = lax.ppermute(
        jnp.concatenate([half_of(queries, 1 - core), half_of(out_grad, 1 - core)], axis=1),
        "core",
        swap,
    )

    n_z = lax.axis_size("z_hi") * n_chips
    depth = layer_input.shape[2] // n_plane
    columns = layer_input[0].reshape(rows, n_plane, depth).transpose(1, 0, 2)
    columns_mine = lax.all_to_all(columns, ("y", "x"), 0, 0, tiled=True)
    columns_other = lax.ppermute(columns_mine, "core", swap)
    columns_all = jnp.concatenate([columns_mine, columns_other], axis=1).reshape(
        n_plane * chip, depth
    )

    seg_row = segment_ids[0]
    lane = jnp.arange(rows, dtype=jnp.int32)

    def places(chip_at, which):
        start = chip_at * chip + which * rows
        return (start + lane, lax.dynamic_slice_in_dim(seg_row, jnp.maximum(start, 0), rows, 0))

    key_places = [
        places(z_lo - distance, which)
        for distance in range(REACH + 1)
        for which in (core, 1 - core)
    ]
    key_pos = jnp.concatenate([place[0] for place in key_places])[:, None]
    key_doc = jnp.concatenate([place[1] for place in key_places])[:, None]
    query_pos = jnp.concatenate([place[0] for place in key_places[:2]])[None, :]
    query_doc = jnp.concatenate([place[1] for place in key_places[:2]])[None, :]
    allowed = (key_pos >= 0) & (key_pos <= query_pos) & (key_doc == query_doc)
    bias = jnp.where(allowed, 0.0, MASKED).astype(jnp.float32)

    dq_mine, dq_other, pair_grad, near_grad, far_grad = attention(
        q_mine, do_mine, qdo_other, blocks, bias
    )
    dq_back = lax.ppermute(dq_other, "core", swap)
    query_grad = jnp.where(
        core == 0,
        jnp.concatenate([dq_mine, dq_back], axis=1),
        jnp.concatenate([dq_back, dq_mine], axis=1),
    )[None]

    for distance, part in ((1, near_grad), (2, far_grad)):
        back = [(b, a) for a, b in behind(distance, 0)]
        pair_grad = pair_grad + lax.ppermute(part, ("z_lo", "core"), back).astype(jnp.float32)
    pair_grad = pair_grad.astype(jnp.bfloat16)

    gathered = lax.all_to_all(
        jnp.broadcast_to(pair_grad, (n_plane, chip, 2 * DH)), ("y", "x"), 0, 0, tiled=True
    ).reshape(n_plane * chip, 2 * DH)
    term = lax.dot_general(
        columns_all, gathered, (((0,), (0,)), ((), ())), preferred_element_type=jnp.float32
    ).astype(jnp.bfloat16)
    spread = lax.all_to_all(
        term.reshape(n_z * 2, depth // (n_z * 2), 2 * DH), ("z_hi", "z_lo", "core"), 0, 0, tiled=True
    )
    by_head = jnp.sum(spread.reshape(n_z, 2, depth // (n_z * 2), 2 * DH).astype(jnp.float32), axis=0)
    weight_grad = jnp.concatenate(
        [by_head[0, :, :DH], by_head[1, :, :DH], by_head[0, :, DH:], by_head[1, :, DH:]], axis=1
    )
    return (query_grad, weight_grad)


def solution(mesh):
    axes = ("y", "x", "z_hi", "z_lo", "core")
    fine = Mesh(mesh.devices.reshape(4, 4, 2, 4, 2), axes)
    dp, ctx = axes[:3], axes[3:]
    return jax.shard_map(
        per_device,
        mesh=fine,
        in_specs=(P(dp, ctx, None),) * 5 + (P(dp, None),),
        out_specs=(P(dp, ctx, None), P(axes, None)),
        check_vma=False,
    )
```

time: 1510 us -> 124 us (0.08)
  waiting for transfers between devices: 1390 us -> 64.3 us
  starting transfers between devices: 0.08 us -> 36.9 us
  blocking collectives: 32.4 us -> 0 us
  local copies, waits for them, and re-layouts: 37.5 us -> 6.65 us
  matrix products: 21.4 us -> 4.81 us
    unnamed x3 -> x0, waiting for transfers between devices: 1290 us -> none
    reduce_scatter x1 -> x0, waiting for transfers between devices: 104 us -> none  [per_device(): lax.psum_scatter(term_rows, 'ctx', scatter_dimension=0, tiled=True)]
    all_to_all x0 -> x3, waiting for transfers between devices: none -> 63.7 us  [the longest x1 33.9 us: per_device(): lax.all_to_all(jnp.broadcast_to(pair_grad, (n_plane, chip, 2 * DH)), ('y'...]
    all_gather x2 -> x0, blocking collectives: 32.4 us -> none  [the longest x1 17.7 us: per_device(): lax.all_gather(values, 'ctx', axis=1, tiled=True)]
    unnamed x12 -> x10, local copies, waits for them, and re-layouts: 24.3 us -> 2.83 us
    ppermute x0 -> x10, starting transfers between devices: none -> 18.5 us  [the longest x2 9.27 us: per_device(): lax.ppermute(pair_mine, ('z_lo', 'core'), behind(distance, 0))]
    all_to_all x0 -> x3, starting transfers between devices: none -> 18.4 us  [the longest x1 6.99 us: per_device(): lax.all_to_all(term.reshape(n_z * 2, depth // (n_z * 2), 2 * DH), ('z_hi'...]
    dot_general x15 -> x1, matrix products: 21.4 us -> 4.81 us  [per_device(): lax.dot_general(columns_all, gathered, (((0,), (0,)), ((), ())), preferre...]
  transfers between devices with their start and end apart: 2 -> 13, of which waited for: 2 -> 4; matrix products, arithmetic and copies ran while one was open for 0% -> 10% of each run, Pallas kernels for 0% -> 6%
where the time goes in v1:
time: 124 us
  waiting for transfers between devices  64.3 us (52%)
  starting transfers between devices  36.9 us (30%)
  Pallas kernels  7.24 us (6%)
  local copies, waits for them, and re-layouts  6.65 us (5%)
  matrix products  4.81 us (4%)
  other arithmetic  2.99 us (2%)
    all_to_all x1, waiting for transfers between devices, per_device(): lax.all_to_all(jnp.broadcast_to(pair_grad, (n_plane, chip, 2 * DH)), ('y'...  33.9 us
    all_to_all x1, waiting for transfers between devices, per_device(): columns_mine = lax.all_to_all(columns, ('y', 'x'), 0, 0, tiled=True)  19.1 us
    all_to_all x1, waiting for transfers between devices, per_device(): lax.all_to_all(term.reshape(n_z * 2, depth // (n_z * 2), 2 * DH), ('z_hi'...  10.8 us
    ppermute x2, starting transfers between devices, per_device(): lax.ppermute(pair_mine, ('z_lo', 'core'), behind(distance, 0))  9.27 us
    pallas_call x1, Pallas kernels, attention(): pl.pallas_call(attention_kernel, out_shape=(jax.ShapeDtypeStruct((rows, G...  7.24 us
    all_to_all x1, starting transfers between devices, per_device(): lax.all_to_all(term.reshape(n_z * 2, depth // (n_z * 2), 2 * DH), ('z_hi'...  6.99 us
    all_to_all x1, starting transfers between devices, per_device(): columns_mine = lax.all_to_all(columns, ('y', 'x'), 0, 0, tiled=True)  6.94 us
    dot_general x1, matrix products, per_device(): lax.dot_general(columns_all, gathered, (((0,), (0,)), ((), ())), preferre...  4.81 us
  transfers between devices with their start and end apart: 13, of which 4 were waited for; matrix products, arithmetic and copies ran while one was open for 10% of the time, Pallas kernels for 6%

profile of v1, /device:TPU:1, one launch (start us, length us, event | category | flops | bytes accessed | tf_op | source)
XLA Modules:
  0.0 123.8 jit_solution(13697036364124713454)
XLA Ops:
  0.6 0.0 copy-start
  0.6 1.0 dynamic-slice_bitcast_fusion.4
  1.6 5.7 %collective-permute-start.4 = (bf16[128,256]{1,0:T(8,128)(2,1)S(1)}, bf16[128,256]{1,0:T(8,128)(2,1)S(1)}, u32[]{:S(2)}, u32[]{:S(2)}) collective-permute-start(bf16[128,256]{1,0:T(8,128)(2,1)S(1)} %pad_maximum_fusion.1.k0), channel_id=1, source_target_pairs={{0,4},{1,5},{2,6},{3,7},{8,12},{9,13},{10,14},{11,15},{16,20},{17,... | collective-permute-start | bytes 196616 | tf_op jit(solution)/shard_map/ppermute | solution.py:123
  7.4 3.5 %collective-permute-start.2 = (bf16[128,256]{1,0:T(8,128)(2,1)S(1)}, bf16[128,256]{1,0:T(8,128)(2,1)S(1)}, u32[]{:S(2)}, u32[]{:S(2)}) collective-permute-start(bf16[128,256]{1,0:T(8,128)(2,1)S(1)} %pad_maximum_fusion.1.k0), channel_id=1, source_target_pairs={{0,2},{1,3},{2,4},{3,5},{4,6},{5,7},{8,10},{9,11},{10,12},{11,13},... | collective-permute-start | bytes 196616 | tf_op jit(solution)/shard_map/ppermute | solution.py:123
  10.9 2.1 %collective-permute-start.5 = (bf16[128,256]{1,0:T(8,128)(2,1)S(1)}, bf16[128,256]{1,0:T(8,128)(2,1)S(1)}, u32[]{:S(2)}, u32[]{:S(2)}) collective-permute-start(bf16[128,256]{1,0:T(8,128)(2,1)S(1)} %pad_maximum_fusion.2), channel_id=1, source_target_pairs={{0,5},{1,4},{2,7},{3,6},{8,13},{9,12},{10,15},{11,14},{16,21},{17,... | collective-permute-start | bytes 196616 | tf_op jit(solution)/shard_map/ppermute | solution.py:124
  13.1 1.9 %collective-permute-start.3 = (bf16[128,256]{1,0:T(8,128)(2,1)S(1)}, bf16[128,256]{1,0:T(8,128)(2,1)S(1)}, u32[]{:S(2)}, u32[]{:S(2)}) collective-permute-start(bf16[128,256]{1,0:T(8,128)(2,1)S(1)} %pad_maximum_fusion.2), channel_id=1, source_target_pairs={{0,3},{1,2},{2,5},{3,4},{4,7},{5,6},{8,11},{9,10},{10,13},{11,12},... | collective-permute-start | bytes 196616 | tf_op jit(solution)/shard_map/ppermute | solution.py:124
  15.0 1.3 %dynamic-slice_bitcast_fusion = (bf16[128,1024]{1,0:T(8,128)(2,1)S(1)}, bf16[128,1024]{1,0:T(8,128)(2,1)S(1)}, bf16[128,1024]{1,0:T(8,128)(2,1)S(1)}, bf16[128,1024]{1,0:T(8,128)(2,1)S(1)}) fusion(bf16[1,128,2048]{2,1,0:T(8,128)(2,1)} %param.9, s32[]{:T(128)S(6)} %select_n.43, s32[]{:T(128)S(6)} %select_n.42, bf16[1,128,2048]{2,1,0:T(8,128)(2,1)} %param.6), kind=kLoop, calls=%fused_computation.11 | loop fusion | bytes 2097160 | tf_op jit(solution)/shard_map/dynamic_slice | solution.py:107
  16.3 0.8 pad_maximum_fusion
  17.1 0.0 collective-permute-start
  17.1 0.0 copy-done
  17.1 2.4 %copy.8 = bf16[1,128,8192]{1,2,0:T(8,128)(2,1)} copy(bf16[1,128,8192]{2,1,0:T(8,128)(2,1)S(1)} %copy-done) | data formatting | bytes 4194304 | tf_op args[4]
  19.6 0.0 copy-start.1
  19.6 6.9 %all-to-all-start = ((bf16[16,128,512]{1,2,0:T(8,128)(2,1)}), bf16[16,128,512]{1,2,0:T(8,128)(2,1)}, u32[]{:S(2)}, u32[]{:S(2)}) async-start(bf16[16,128,512]{1,2,0:T(8,128)(2,1)} %bitcast.17), calls=%async_computation | async-start | bytes 4194304 | tf_op jit(solution)/shard_map/all_to_all | solution.py:135
  26.6 0.0 copy-done.1
  26.6 0.1 constant_dynamic-update-slice_fusion.11
  26.7 0.1 constant_dynamic-update-slice_fusion.9
  26.8 0.1 constant_dynamic-update-slice_fusion.7
  26.9 0.1 constant_dynamic-update-slice_fusion.5
  27.0 0.1 constant_dynamic-update-slice_fusion.3
  27.0 0.1 constant_dynamic-update-slice_fusion
  27.2 0.0 collective-permute-done.4.k4
  27.2 0.9 collective-permute-start.1
  28.0 0.4 and_select_fusion.bias
  28.4 0.0 collective-permute-done.2.k2
  28.4 0.0 collective-permute-done.5.k5
  28.4 0.0 collective-permute-done.3.k3
  28.5 0.5 collective-permute-done.1.k1
  28.9 0.0 collective-permute-done.qdo_other
  29.0 7.2 %shard_map.77 = (bf16[128,1024]{1,0:T(8,128)(2,1)S(1)}, bf16[128,1024]{1,0:T(8,128)(2,1)S(1)}, f32[256,256]{1,0:T(8,128)S(1)}, bf16[256,256]{1,0:T(8,128)(2,1)S(1)}, bf16[256,256]{1,0:T(8,128)(2,1)S(1)}) custom-call(bf16[128,1024]{1,0:T(8,128)(2,1)S(1)} %get-tuple-element.30.q_mine, bf16[128,1024]{1,0:T(8,128)(2,1)S(1)} %get-tuple-element.19.do_mine, ...), custom_call_target="tpu_custom_call" | custom-call | flops 2013265920 | bytes 4194304 | tf_op jit(solution)/shard_map/pallas_call | solution.py:75
  36.2 1.3 %collective-permute-start.8 = (bf16[256,256]{1,0:T(8,128)(2,1)S(1)}, bf16[256,256]{1,0:T(8,128)(2,1)S(1)}, u32[]{:S(2)}, u32[]{:S(2)}) collective-permute-start(bf16[256,256]{1,0:T(8,128)(2,1)S(1)} %get-tuple-element.10), channel_id=1, source_target_pairs={{2,0},{3,1},{4,2},{5,3},{6,4},{7,5},{10,8},{11,9},{12,10},{13,11},... | collective-permute-start | bytes 393224 | tf_op jit(solution)/shard_map/ppermute | solution.py:172
  37.5 1.3 %collective-permute-start.9 = (bf16[256,256]{1,0:T(8,128)(2,1)S(1)}, bf16[256,256]{1,0:T(8,128)(2,1)S(1)}, u32[]{:S(2)}, u32[]{:S(2)}) collective-permute-start(bf16[256,256]{1,0:T(8,128)(2,1)S(1)} %get-tuple-element.11), channel_id=1, source_target_pairs={{4,0},{5,1},{6,2},{7,3},{12,8},{13,9},{14,10},{15,11},{20,16},{21,... | collective-permute-start | bytes 393224 | tf_op jit(solution)/shard_map/ppermute | solution.py:172
  38.8 19.1 %all-to-all-done = bf16[16,128,512]{1,2,0:T(8,128)(2,1)} async-done(((bf16[16,128,512]{1,2,0:T(8,128)(2,1)}), bf16[16,128,512]{1,2,0:T(8,128)(2,1)}, u32[]{:S(2)}, u32[]{:S(2)}) %all-to-all-start) | async-done | bytes 2097184 | tf_op jit(solution)/shard_map/all_to_all | solution.py:135
  57.9 1.6 %collective-permute-start.7 = (bf16[16,128,512]{1,2,0:T(8,128)(2,1)}, bf16[16,128,512]{1,2,0:T(8,128)(2,1)}, u32[]{:S(2)}, u32[]{:S(2)}) collective-permute-start(bf16[16,128,512]{1,2,0:T(8,128)(2,1)} %all-to-all-done), channel_id=1, source_target_pairs={{0,1},{1,0},{2,3},{3,2},{4,5},{5,4},{6,7},{7,6},{8,9},{9,8},{10,11... | collective-permute-start | bytes 6291464 | tf_op jit(solution)/shard_map/ppermute | solution.py:136
  59.5 0.0 collective-permute-done.8
  59.5 0.0 collective-permute-done.9
  59.6 1.6 %broadcast_in_dim.18 = bf16[16,256,256]{2,1,0:T(8,128)(2,1)} broadcast(bf16[256,256]{1,0:T(8,128)(2,1)S(1)} %add_convert_fusion), dimensions={1,2} | broadcast | bytes 2228224 | tf_op jit(solution)/shard_map/broadcast_in_dim | solution.py:176
  61.1 4.4 %all-to-all-start.1 = ((bf16[16,256,256]{2,1,0:T(8,128)(2,1)}), bf16[16,256,256]{2,1,0:T(8,128)(2,1)}, u32[]{:S(2)}, u32[]{:S(2)}) async-start(bf16[16,256,256]{2,1,0:T(8,128)(2,1)} %broadcast_in_dim.18), calls=%async_computation.1 | async-start | bytes 4194304 | tf_op jit(solution)/shard_map/all_to_all | solution.py:175
  65.6 0.1 collective-permute-start.6
  65.7 33.9 %all-to-all-done.1 = bf16[16,256,256]{2,1,0:T(8,128)(2,1)} async-done(((bf16[16,256,256]{2,1,0:T(8,128)(2,1)}), bf16[16,256,256]{2,1,0:T(8,128)(2,1)}, u32[]{:S(2)}, u32[]{:S(2)}) %all-to-all-start.1) | async-done | bytes 2097184 | tf_op jit(solution)/shard_map/all_to_all | solution.py:175
  99.6 0.0 collective-permute-done.7
  99.6 4.8 %fusion.7 = bf16[512,256]{1,0:T(8,128)(2,1)} fusion(bf16[16,256,256]{2,1,0:T(8,128)(2,1)} %all-to-all-done.1, bf16[16,128,512]{1,2,0:T(8,128)(2,1)} %collective-permute-done.7, bf16[16,128,512]{1,2,0:T(8,128)(2,1)} %all-to-all-done), kind=kOutput, calls=%fused_computation.5 | convolution fusion | flops 1082261504 | bytes 6553600 | tf_op jit(solution)/shard_map/dot_general | solution.py:178
  104.4 7.0 %all-to-all-start.2 = ((bf16[16,32,256]{2,1,0:T(8,128)(2,1)}), bf16[16,32,256]{2,1,0:T(8,128)(2,1)S(1)}, u32[]{:S(2)}, u32[]{:S(2)}) async-start(bf16[16,32,256]{2,1,0:T(8,128)(2,1)} %bitcast.19), calls=%async_computation.2 | async-start | bytes 524288 | tf_op jit(solution)/shard_map/all_to_all | solution.py:181
  111.4 0.0 collective-permute-done.6
  111.4 0.9 maximum_select_fusion
  112.3 10.8 %all-to-all-done.2 = bf16[16,32,256]{2,1,0:T(8,128)(2,1)S(1)} async-done(((bf16[16,32,256]{2,1,0:T(8,128)(2,1)}), bf16[16,32,256]{2,1,0:T(8,128)(2,1)S(1)}, u32[]{:S(2)}, u32[]{:S(2)}) %all-to-all-start.2) | async-done | bytes 262176 | tf_op jit(solution)/shard_map/all_to_all | solution.py:181
  123.1 0.6 pad_maximum_fusion.3
  (16 shorter events, 0.2 us)
Async XLA Ops:
  0.6 16.5 %copy-start = (bf16[1,128,8192]{2,1,0:T(8,128)(2,1)S(1)}, bf16[1,128,8192]{2,1,0:T(8,128)(2,1)}, u32[]{:S(2)}) copy-start(bf16[1,128,8192]{2,1,0:T(8,128)(2,1)} %param.10) | copy-start | bytes 6291460
  1.6 25.5 %collective-permute-start.4 = (bf16[128,256]{1,0:T(8,128)(2,1)S(1)}, bf16[128,256]{1,0:T(8,128)(2,1)S(1)}, u32[]{:S(2)}, u32[]{:S(2)}) collective-permute-start(bf16[128,256]{1,0:T(8,128)(2,1)S(1)} %pad_maximum_fusion.1.k0), channel_id=1, source_target_pairs={{0,4},{1,5},{2,6},{3,7},{8,12},{9,13},{10,14},{11,15},{16,20},{17,... | collective-permute-start | bytes 196616 | tf_op jit(solution)/shard_map/ppermute | solution.py:123
  7.4 21.1 %collective-permute-start.2 = (bf16[128,256]{1,0:T(8,128)(2,1)S(1)}, bf16[128,256]{1,0:T(8,128)(2,1)S(1)}, u32[]{:S(2)}, u32[]{:S(2)}) collective-permute-start(bf16[128,256]{1,0:T(8,128)(2,1)S(1)} %pad_maximum_fusion.1.k0), channel_id=1, source_target_pairs={{0,2},{1,3},{2,4},{3,5},{4,6},{5,7},{8,10},{9,11},{10,12},{11,13},... | collective-permute-start | bytes 196616 | tf_op jit(solution)/shard_map/ppermute | solution.py:123
  10.9 17.5 %collective-permute-start.5 = (bf16[128,256]{1,0:T(8,128)(2,1)S(1)}, bf16[128,256]{1,0:T(8,128)(2,1)S(1)}, u32[]{:S(2)}, u32[]{:S(2)}) collective-permute-start(bf16[128,256]{1,0:T(8,128)(2,1)S(1)} %pad_maximum_fusion.2), channel_id=1, source_target_pairs={{0,5},{1,4},{2,7},{3,6},{8,13},{9,12},{10,15},{11,14},{16,21},{17,... | collective-permute-start | bytes 196616 | tf_op jit(solution)/shard_map/ppermute | solution.py:124
  13.1 15.4 %collective-permute-start.3 = (bf16[128,256]{1,0:T(8,128)(2,1)S(1)}, bf16[128,256]{1,0:T(8,128)(2,1)S(1)}, u32[]{:S(2)}, u32[]{:S(2)}) collective-permute-start(bf16[128,256]{1,0:T(8,128)(2,1)S(1)} %pad_maximum_fusion.2), channel_id=1, source_target_pairs={{0,3},{1,2},{2,5},{3,4},{4,7},{5,6},{8,11},{9,10},{10,13},{11,12},... | collective-permute-start | bytes 196616 | tf_op jit(solution)/shard_map/ppermute | solution.py:124
  17.1 11.8 %collective-permute-start = (bf16[128,2048]{1,0:T(8,128)(2,1)}, bf16[128,2048]{1,0:T(8,128)(2,1)S(1)}, u32[]{:S(2)}, u32[]{:S(2)}) collective-permute-start(bf16[128,2048]{1,0:T(8,128)(2,1)} %pad_maximum_fusion), channel_id=1, source_target_pairs={{0,1},{1,0},{2,3},{3,2},{4,5},{5,4},{6,7},{7,6},{8,9},{9,8},{10,11... | collective-permute-start | bytes 1572872 | tf_op jit(solution)/shard_map/ppermute | solution.py:126
  19.6 7.1 %copy-start.1 = (s32[1,1024]{1,0:T(1,128)S(1)}, s32[1,1024]{1,0:T(1,128)}, u32[]{:S(2)}) copy-start(s32[1,1024]{1,0:T(1,128)} %param.11) | copy-start | bytes 12292
  19.6 38.3 %all-to-all-start = ((bf16[16,128,512]{1,2,0:T(8,128)(2,1)}), bf16[16,128,512]{1,2,0:T(8,128)(2,1)}, u32[]{:S(2)}, u32[]{:S(2)}) async-start(bf16[16,128,512]{1,2,0:T(8,128)(2,1)} %bitcast.17), calls=%async_computation | async-start | bytes 4194304 | tf_op jit(solution)/shard_map/all_to_all | solution.py:135
  27.2 1.8 %collective-permute-start.1 = (bf16[128,256]{1,0:T(8,128)(2,1)S(1)}, bf16[128,256]{1,0:T(8,128)(2,1)S(1)}, u32[]{:S(2)}, u32[]{:S(2)}) collective-permute-start(bf16[128,256]{1,0:T(8,128)(2,1)S(1)} %pad_maximum_fusion.2), channel_id=1, source_target_pairs={{0,1},{1,0},{2,3},{3,2},{4,5},{5,4},{6,7},{7,6},{8,9},{9,8},{10,11... | collective-permute-start | bytes 196616 | tf_op jit(solution)/shard_map/ppermute | solution.py:121
  36.2 23.3 %collective-permute-start.8 = (bf16[256,256]{1,0:T(8,128)(2,1)S(1)}, bf16[256,256]{1,0:T(8,128)(2,1)S(1)}, u32[]{:S(2)}, u32[]{:S(2)}) collective-permute-start(bf16[256,256]{1,0:T(8,128)(2,1)S(1)} %get-tuple-element.10), channel_id=1, source_target_pairs={{2,0},{3,1},{4,2},{5,3},{6,4},{7,5},{10,8},{11,9},{12,10},{13,11},... | collective-permute-start | bytes 393224 | tf_op jit(solution)/shard_map/ppermute | solution.py:172
  37.5 22.0 %collective-permute-start.9 = (bf16[256,256]{1,0:T(8,128)(2,1)S(1)}, bf16[256,256]{1,0:T(8,128)(2,1)S(1)}, u32[]{:S(2)}, u32[]{:S(2)}) collective-permute-start(bf16[256,256]{1,0:T(8,128)(2,1)S(1)} %get-tuple-element.11), channel_id=1, source_target_pairs={{4,0},{5,1},{6,2},{7,3},{12,8},{13,9},{14,10},{15,11},{20,16},{21,... | collective-permute-start | bytes 393224 | tf_op jit(solution)/shard_map/ppermute | solution.py:172
  57.9 41.7 %collective-permute-start.7 = (bf16[16,128,512]{1,2,0:T(8,128)(2,1)}, bf16[16,128,512]{1,2,0:T(8,128)(2,1)}, u32[]{:S(2)}, u32[]{:S(2)}) collective-permute-start(bf16[16,128,512]{1,2,0:T(8,128)(2,1)} %all-to-all-done), channel_id=1, source_target_pairs={{0,1},{1,0},{2,3},{3,2},{4,5},{5,4},{6,7},{7,6},{8,9},{9,8},{10,11... | collective-permute-start | bytes 6291464 | tf_op jit(solution)/shard_map/ppermute | solution.py:136
  61.1 38.4 %all-to-all-start.1 = ((bf16[16,256,256]{2,1,0:T(8,128)(2,1)}), bf16[16,256,256]{2,1,0:T(8,128)(2,1)}, u32[]{:S(2)}, u32[]{:S(2)}) async-start(bf16[16,256,256]{2,1,0:T(8,128)(2,1)} %broadcast_in_dim.18), calls=%async_computation.1 | async-start | bytes 4194304 | tf_op jit(solution)/shard_map/all_to_all | solution.py:175
  65.6 45.8 %collective-permute-start.6 = (bf16[128,1024]{1,0:T(8,128)(2,1)S(1)}, bf16[128,1024]{1,0:T(8,128)(2,1)S(1)}, u32[]{:S(2)}, u32[]{:S(2)}) collective-permute-start(bf16[128,1024]{1,0:T(8,128)(2,1)S(1)} %get-tuple-element.8), channel_id=1, source_target_pairs={{0,1},{1,0},{2,3},{3,2},{4,5},{5,4},{6,7},{7,6},{8,9},{9,8},{10,11... | collective-permute-start | bytes 786440 | tf_op jit(solution)/shard_map/ppermute | solution.py:163
  104.4 18.7 %all-to-all-start.2 = ((bf16[16,32,256]{2,1,0:T(8,128)(2,1)}), bf16[16,32,256]{2,1,0:T(8,128)(2,1)S(1)}, u32[]{:S(2)}, u32[]{:S(2)}) async-start(bf16[16,32,256]{2,1,0:T(8,128)(2,1)} %bitcast.19), calls=%async_computation.2 | async-start | bytes 524288 | tf_op jit(solution)/shard_map/all_to_all | solution.py:181

commit v2 on v1

--- a/solution.py
+++ b/solution.py
@@ -94,13 +94,60 @@
     )(q_mine, do_mine, qdo_other, *blocks, bias)
 
 
+def project_kernel(mine, other, grads, out):
+    total = None
+    for place in range(mine.shape[0]):
+        block = jnp.concatenate([mine[place], other[place]], axis=1)
+        part = dot_nn(block, grads[place])
+        total = part if total is None else total + part
+    out[...] = total.astype(jnp.bfloat16)
+
+
+def project(mine, other, grads, blocks):
+    places, columns, rows = mine.shape
+    width = grads.shape[2]
+    step = columns // blocks
+    return pl.pallas_call(
+        project_kernel,
+        out_shape=jax.ShapeDtypeStruct((columns, width), jnp.bfloat16),
+        grid=(blocks,),
+        in_specs=[
+            pl.BlockSpec((places, step, rows), lambda i: (0, i, 0)),
+            pl.BlockSpec((places, step, rows), lambda i: (0, i, 0)),
+            pl.BlockSpec(grads.shape, lambda i: (0, 0, 0)),
+        ],
+        out_specs=pl.BlockSpec((step, width), lambda i: (i, 0)),
+        compiler_params=pltpu.CompilerParams(vmem_limit_bytes=32 * 1024 * 1024),
+        cost_estimate=pl.CostEstimate(
+            flops=4 * places * rows * columns * width, bytes_accessed=6 * 1024 * 1024, transcendentals=0
+        ),
+    )(mine, other, grads)
+
+
+def final_kernel(parts, out):
+    n_z = parts.shape[0] // 2
+    for head in range(KV):
+        total = parts[head].astype(jnp.float32)
+        for z in range(1, n_z):
+            total = total + parts[2 * z + head].astype(jnp.float32)
+        out[:, head * DH : (head + 1) * DH] = total[:, :DH]
+        out[:, (KV + head) * DH : (KV + head + 1) * DH] = total[:, DH:]
+
+
+def final_sum(parts):
+    return pl.pallas_call(
+        final_kernel,
+        out_shape=jax.ShapeDtypeStruct((parts.shape[1], 2 * KV * DH), jnp.float32),
+        cost_estimate=pl.CostEstimate(flops=0, bytes_accessed=512 * 1024, transcendentals=0),
+    )(parts)
+
+
 def per_device(queries, keys, values, out_grad, layer_input, segment_ids):
     rows = queries.shape[1]
     chip = 2 * rows
     z_lo = lax.axis_index("z_lo")
     core = lax.axis_index("core")
     n_chips = lax.axis_size("z_lo")
-    n_plane = lax.axis_size("y") * lax.axis_size("x")
 
     def half_of(array, which):
         width = array.shape[-1] // 2
@@ -129,14 +176,14 @@
         swap,
     )
 
+    n_y, n_x = lax.axis_size("y"), lax.axis_size("x")
     n_z = lax.axis_size("z_hi") * n_chips
-    depth = layer_input.shape[2] // n_plane
-    columns = layer_input[0].reshape(rows, n_plane, depth).transpose(1, 0, 2)
-    columns_mine = lax.all_to_all(columns, ("y", "x"), 0, 0, tiled=True)
+    depth = layer_input.shape[2] // (n_y * n_x)
+    columns = (
+        layer_input[0].reshape(rows, n_y, n_x, depth).transpose(2, 1, 3, 0).reshape(n_x, n_y * depth, rows)
+    )
+    columns_mine = lax.all_to_all(columns, "x", 0, 0, tiled=True)
     columns_other = lax.ppermute(columns_mine, "core", swap)
-    columns_all = jnp.concatenate([columns_mine, columns_other], axis=1).reshape(
-        n_plane * chip, depth
-    )
 
     seg_row = segment_ids[0]
     lane = jnp.arange(rows, dtype=jnp.int32)
@@ -173,18 +220,15 @@
     pair_grad = pair_grad.astype(jnp.bfloat16)
 
     gathered = lax.all_to_all(
-        jnp.broadcast_to(pair_grad, (n_plane, chip, 2 * DH)), ("y", "x"), 0, 0, tiled=True
-    ).reshape(n_plane * chip, 2 * DH)
-    term = lax.dot_general(
-        columns_all, gathered, (((0,), (0,)), ((), ())), preferred_element_type=jnp.float32
-    ).astype(jnp.bfloat16)
+        jnp.broadcast_to(pair_grad, (n_x, chip, 2 * DH)), "x", 0, 0, tiled=True
+    )
+    term = project(columns_mine, columns_other, gathered, n_y)
+    over_y = lax.all_to_all(term.reshape(n_y, depth, 2 * DH), "y", 0, 0, tiled=True)
+    term = jnp.sum(over_y.astype(jnp.float32), axis=0).astype(jnp.bfloat16)
     spread = lax.all_to_all(
         term.reshape(n_z * 2, depth // (n_z * 2), 2 * DH), ("z_hi", "z_lo", "core"), 0, 0, tiled=True
     )
-    by_head = jnp.sum(spread.reshape(n_z, 2, depth // (n_z * 2), 2 * DH).astype(jnp.float32), axis=0)
-    weight_grad = jnp.concatenate(
-        [by_head[0, :, :DH], by_head[1, :, :DH], by_head[0, :, DH:], by_head[1, :, DH:]], axis=1
-    )
+    weight_grad = final_sum(spread)
     return (query_grad, weight_grad)
 
 

time: 124 us -> 127 us (1.024)
  waiting for transfers between devices: 64.3 us -> 44.4 us
  blocking collectives: 0 us -> 11 us
  Pallas kernels: 7.24 us -> 13.3 us
  starting transfers between devices: 36.9 us -> 42.7 us
  matrix products: 4.81 us -> 0 us
  local copies, waits for them, and re-layouts: 6.65 us -> 11.2 us
    all_to_all x2, waiting for transfers between devices: 53 us -> 21.5 us  [the longest x1 10.8 us: per_device(): lax.all_to_all(term.reshape(n_y, depth, 2 * DH), 'y', 0, 0, tiled=True)]
    ppermute x2, waiting for transfers between devices: 0.01 us -> 12.1 us  [per_device(): lax.ppermute(part, ('z_lo', 'core'), back).astype(jnp.float32)]
    all_to_all x0 -> x1, blocking collectives: none -> 11 us  [per_device(): lax.all_to_all(jnp.broadcast_to(pair_grad, (n_x, chip, 2 * DH)), 'x', 0,...]
    another operation x0 -> x2, local copies, waits for them, and re-layouts: none -> 6.45 us  [per_device(): layer_input[0].reshape(rows, n_y, n_x, depth).transpose(2, 1, 3, 0)]
    pallas_call x0 -> x2, Pallas kernels: none -> 6.09 us  [the longest x1 4.48 us: project(): pl.pallas_call(project_kernel, out_shape=jax.ShapeDtypeStruct((columns, w...]
    dot_general x1 -> x0, matrix products: 4.81 us -> none  [per_device(): lax.dot_general(columns_all, gathered, (((0,), (0,)), ((), ())), preferre...]
    all_to_all x1, starting transfers between devices: 6.99 us -> 10.5 us  [per_device(): lax.all_to_all(term.reshape(n_z * 2, depth // (n_z * 2), 2 * DH), ('z_hi'...]
    all_to_all x2, starting transfers between devices: 11.4 us -> 9.29 us  [the longest x1 4.97 us: per_device(): columns_mine = lax.all_to_all(columns, 'x', 0, 0, tiled=True)]
  transfers between devices with their start and end apart: 13 -> 13, of which waited for: 4 -> 5; matrix products, arithmetic and copies ran while one was open for 10% -> 4% of each run, Pallas kernels for 6% -> 6%
where the time goes in v2:
time: 127 us
  waiting for transfers between devices  44.4 us (35%)
  starting transfers between devices  42.7 us (34%)
  Pallas kernels  13.3 us (10%)
  local copies, waits for them, and re-layouts  11.2 us (9%)
  blocking collectives  11 us (9%)
  other arithmetic  3.23 us (3%)
    ppermute x2, waiting for transfers between devices, per_device(): lax.ppermute(part, ('z_lo', 'core'), back).astype(jnp.float32)  12.1 us
    all_to_all x1, blocking collectives, per_device(): lax.all_to_all(jnp.broadcast_to(pair_grad, (n_x, chip, 2 * DH)), 'x', 0,...  11 us
    all_to_all x1, waiting for transfers between devices, per_device(): lax.all_to_all(term.reshape(n_y, depth, 2 * DH), 'y', 0, 0, tiled=True)  10.8 us
    all_to_all x1, waiting for transfers between devices, per_device(): lax.all_to_all(term.reshape(n_z * 2, depth // (n_z * 2), 2 * DH), ('z_hi'...  10.8 us
    all_to_all x1, waiting for transfers between devices, per_device(): columns_mine = lax.all_to_all(columns, 'x', 0, 0, tiled=True)  10.7 us
    all_to_all x1, starting transfers between devices, per_device(): lax.all_to_all(term.reshape(n_z * 2, depth // (n_z * 2), 2 * DH), ('z_hi'...  10.5 us
    ppermute x2, starting transfers between devices, per_device(): lax.ppermute(pair_mine, ('z_lo', 'core'), behind(distance, 0))  8.44 us
    pallas_call x1, Pallas kernels, attention(): pl.pallas_call(attention_kernel, out_shape=(jax.ShapeDtypeStruct((rows, G...  7.24 us
  transfers between devices with their start and end apart: 13, of which 5 were waited for; matrix products, arithmetic and copies ran while one was open for 4% of the time, Pallas kernels for 6%

profile of v2, /device:TPU:1, one launch (start us, length us, event | category | flops | bytes accessed | tf_op | source)
XLA Modules:
  0.0 126.6 jit_solution(12128206887811421959)
XLA Ops:
  0.6 3.3 %reshape_squeeze.3 = bf16[128,4,4,512]{3,2,1,0:T(4,128)(2,1)S(1)} reshape(bf16[1,128,8192]{2,1,0:T(8,128)(2,1)} %param.10) | data formatting | bytes 4194304 | tf_op jit(solution)/shard_map/reshape;squeeze | solution.py:183
  4.0 3.1 %copy.8 = bf16[128,4,4,512]{0,3,1,2:T(8,128)(2,1)} copy(bf16[128,4,4,512]{3,2,1,0:T(4,128)(2,1)S(1)} %reshape_squeeze.3) | data formatting | bytes 4194304 | tf_op jit(solution)/shard_map/reshape;squeeze | solution.py:183
  7.1 5.0 %all-to-all-start = ((bf16[4,2048,128]{2,1,0:T(8,128)(2,1)}), bf16[4,2048,128]{2,1,0:T(8,128)(2,1)S(1)}, u32[]{:S(2)}, u32[]{:S(2)}) async-start(bf16[4,2048,128]{2,1,0:T(8,128)(2,1)} %bitcast.46), calls=%async_computation | async-start | bytes 4194304 | tf_op jit(solution)/shard_map/all_to_all | solution.py:185
  12.1 4.9 %collective-permute-start.4 = (bf16[128,256]{1,0:T(8,128)(2,1)S(1)}, bf16[128,256]{1,0:T(8,128)(2,1)S(1)}, u32[]{:S(2)}, u32[]{:S(2)}) collective-permute-start(bf16[128,256]{1,0:T(8,128)(2,1)S(1)} %pad_maximum_fusion.1.k0), channel_id=1, source_target_pairs={{0,4},{1,5},{2,6},{3,7},{8,12},{9,13},{10,14},{11,15},{16,20},{17,... | collective-permute-start | bytes 196616 | tf_op jit(solution)/shard_map/ppermute | solution.py:170
  17.0 3.5 %collective-permute-start.2 = (bf16[128,256]{1,0:T(8,128)(2,1)S(1)}, bf16[128,256]{1,0:T(8,128)(2,1)S(1)}, u32[]{:S(2)}, u32[]{:S(2)}) collective-permute-start(bf16[128,256]{1,0:T(8,128)(2,1)S(1)} %pad_maximum_fusion.1.k0), channel_id=1, source_target_pairs={{0,2},{1,3},{2,4},{3,5},{4,6},{5,7},{8,10},{9,11},{10,12},{11,13},... | collective-permute-start | bytes 196616 | tf_op jit(solution)/shard_map/ppermute | solution.py:170
  20.6 2.4 %collective-permute-start.5 = (bf16[128,256]{1,0:T(8,128)(2,1)S(1)}, bf16[128,256]{1,0:T(8,128)(2,1)S(1)}, u32[]{:S(2)}, u32[]{:S(2)}) collective-permute-start(bf16[128,256]{1,0:T(8,128)(2,1)S(1)} %pad_maximum_fusion.2), channel_id=1, source_target_pairs={{0,5},{1,4},{2,7},{3,6},{8,13},{9,12},{10,15},{11,14},{16,21},{17,... | collective-permute-start | bytes 196616 | tf_op jit(solution)/shard_map/ppermute | solution.py:171
  23.0 1.3 dynamic-slice_bitcast_fusion
  24.3 0.8 pad_maximum_fusion
  25.1 0.4 collective-permute-start
  25.6 0.1 constant_dynamic-update-slice_fusion.11
  25.7 0.1 constant_dynamic-update-slice_fusion.9
  25.7 10.7 %all-to-all-done.mine = bf16[4,2048,128]{2,1,0:T(8,128)(2,1)S(1)} async-done(((bf16[4,2048,128]{2,1,0:T(8,128)(2,1)}), bf16[4,2048,128]{2,1,0:T(8,128)(2,1)S(1)}, u32[]{:S(2)}, u32[]{:S(2)}) %all-to-all-start) | async-done | bytes 2097184 | tf_op jit(solution)/shard_map/all_to_all | solution.py:185
  36.4 2.9 %collective-permute-start.7 = (bf16[4,2048,128]{2,1,0:T(8,128)(2,1)S(1)}, bf16[4,2048,128]{2,1,0:T(8,128)(2,1)}, u32[]{:S(2)}, u32[]{:S(2)}) collective-permute-start(bf16[4,2048,128]{2,1,0:T(8,128)(2,1)S(1)} %all-to-all-done.mine), channel_id=1, source_target_pairs={{0,1},{1,0},{2,3},{3,2},{4,5},{5,4},{6,7},{7,6},{8,9},{9,8},{10,11... | collective-permute-start | bytes 6291464 | tf_op jit(solution)/shard_map/ppermute | solution.py:186
  39.3 0.1 constant_dynamic-update-slice_fusion.7
  39.4 0.1 constant_dynamic-update-slice_fusion.5
  39.5 0.1 constant_dynamic-update-slice_fusion.3
  39.6 0.1 constant_dynamic-update-slice_fusion
  39.7 3.4 %collective-permute-start.3 = (bf16[128,256]{1,0:T(8,128)(2,1)S(1)}, bf16[128,256]{1,0:T(8,128)(2,1)S(1)}, u32[]{:S(2)}, u32[]{:S(2)}) collective-permute-start(bf16[128,256]{1,0:T(8,128)(2,1)S(1)} %pad_maximum_fusion.2), channel_id=1, source_target_pairs={{0,3},{1,2},{2,5},{3,4},{4,7},{5,6},{8,11},{9,10},{10,13},{11,12},... | collective-permute-start | bytes 196616 | tf_op jit(solution)/shard_map/ppermute | solution.py:171
  43.2 0.0 collective-permute-done.2.k2
  43.2 0.0 copy-start.2
  43.2 0.6 collective-permute-start.1
  43.8 0.4 and_select_fusion.bias
  44.2 0.6 copy-done.4
  44.8 0.0 collective-permute-done.3.k3
  44.8 0.0 collective-permute-done.1.k1
  44.8 0.0 collective-permute-done.qdo_other
  44.8 0.0 copy-start.3
  44.8 0.8 copy-done.3
  45.6 0.8 copy-done.5
  46.5 7.2 %shard_map.77 = (bf16[128,1024]{1,0:T(8,128)(2,1)S(1)}, bf16[128,1024]{1,0:T(8,128)(2,1)S(1)}, f32[256,256]{1,0:T(8,128)S(1)}, bf16[256,256]{1,0:T(8,128)(2,1)S(1)}, bf16[256,256]{1,0:T(8,128)(2,1)S(1)}) custom-call(bf16[128,1024]{1,0:T(8,128)(2,1)S(1)} %get-tuple-element.26.q_mine, bf16[128,1024]{1,0:T(8,128)(2,1)S(1)} %get-tuple-element.19.do_mine, ...), custom_call_target="tpu_custom_call" | custom-call | flops 2013265920 | bytes 4194304 | tf_op jit(solution)/shard_map/pallas_call | solution.py:75
  53.7 0.0 copy-start
  53.7 1.3 %collective-permute-start.8 = (bf16[256,256]{1,0:T(8,128)(2,1)S(1)}, bf16[256,256]{1,0:T(8,128)(2,1)S(1)}, u32[]{:S(2)}, u32[]{:S(2)}) collective-permute-start(bf16[256,256]{1,0:T(8,128)(2,1)S(1)} %get-tuple-element.10), channel_id=1, source_target_pairs={{2,0},{3,1},{4,2},{5,3},{6,4},{7,5},{10,8},{11,9},{12,10},{13,11},... | collective-permute-start | bytes 393224 | tf_op jit(solution)/shard_map/ppermute | solution.py:219
  55.0 1.3 %collective-permute-start.9 = (bf16[256,256]{1,0:T(8,128)(2,1)S(1)}, bf16[256,256]{1,0:T(8,128)(2,1)S(1)}, u32[]{:S(2)}, u32[]{:S(2)}) collective-permute-start(bf16[256,256]{1,0:T(8,128)(2,1)S(1)} %get-tuple-element.11), channel_id=1, source_target_pairs={{4,0},{5,1},{6,2},{7,3},{12,8},{13,9},{14,10},{15,11},{20,16},{21,... | collective-permute-start | bytes 393224 | tf_op jit(solution)/shard_map/ppermute | solution.py:219
  56.3 5.1 %collective-permute-done.8 = bf16[256,256]{1,0:T(8,128)(2,1)S(1)} collective-permute-done((bf16[256,256]{1,0:T(8,128)(2,1)S(1)}, bf16[256,256]{1,0:T(8,128)(2,1)S(1)}, u32[]{:S(2)}, u32[]{:S(2)}) %collective-permute-start.8) | collective-permute-done | bytes 131104 | tf_op jit(solution)/shard_map/ppermute | solution.py:219
  61.4 7.0 %collective-permute-done.9 = bf16[256,256]{1,0:T(8,128)(2,1)S(1)} collective-permute-done((bf16[256,256]{1,0:T(8,128)(2,1)S(1)}, bf16[256,256]{1,0:T(8,128)(2,1)S(1)}, u32[]{:S(2)}, u32[]{:S(2)}) %collective-permute-start.9) | collective-permute-done | bytes 131104 | tf_op jit(solution)/shard_map/ppermute | solution.py:219
  68.5 11.0 %all_to_all.20.grads = bf16[4,256,256]{2,1,0:T(8,128)(2,1)S(1)} all-to-all(bf16[4,256,256]{2,1,0:T(8,128)(2,1)S(1)} %broadcast_in_dim.18), channel_id=1, replica_groups=mesh['y'=4,'x'=4,'z_hi'=2,'z_lo'=4,'core'=2] {'x'}, dimensions={0} | all-to-all | bytes 1048576 | tf_op jit(solution)/shard_map/all_to_all | solution.py:222
  79.5 0.0 collective-permute-done.7.other
  79.5 4.5 %shard_map.78 = bf16[2048,256]{1,0:T(8,128)(2,1)} custom-call(bf16[4,2048,128]{2,1,0:T(8,128)(2,1)S(1)} %all-to-all-done.mine, bf16[4,2048,128]{2,1,0:T(8,128)(2,1)} %collective-permute-done.7.other, bf16[4,256,256]{2,1,0:T(8,128)(2,1)S(1)} %all_to_all.20.grads), custom_call_target="tpu_custom_call" | custom-call | flops 1073741824 | bytes 6291456 | tf_op jit(solution)/shard_map/pallas_call | solution.py:110
  83.9 4.3 %all-to-all-start.2 = ((bf16[4,512,256]{2,1,0:T(8,128)(2,1)}), bf16[4,512,256]{2,1,0:T(8,128)(2,1)S(1)}, u32[]{:S(2)}, u32[]{:S(2)}) async-start(bf16[4,512,256]{2,1,0:T(8,128)(2,1)} %bitcast.18), calls=%async_computation.2 | async-start | bytes 2097152 | tf_op jit(solution)/shard_map/all_to_all | solution.py:226
  88.3 2.2 %collective-permute-start.6 = (bf16[128,1024]{1,0:T(8,128)(2,1)S(1)}, bf16[128,1024]{1,0:T(8,128)(2,1)S(1)}, u32[]{:S(2)}, u32[]{:S(2)}) collective-permute-start(bf16[128,1024]{1,0:T(8,128)(2,1)S(1)} %copy-done.1), channel_id=1, source_target_pairs={{0,1},{1,0},{2,3},{3,2},{4,5},{5,4},{6,7},{7,6},{8,9},{9,8},{10,11... | collective-permute-start | bytes 786440 | tf_op jit(solution)/shard_map/ppermute | solution.py:210
  90.4 10.8 %all-to-all-done.2 = bf16[4,512,256]{2,1,0:T(8,128)(2,1)S(1)} async-done(((bf16[4,512,256]{2,1,0:T(8,128)(2,1)}), bf16[4,512,256]{2,1,0:T(8,128)(2,1)S(1)}, u32[]{:S(2)}, u32[]{:S(2)}) %all-to-all-start.2) | async-done | bytes 1048608 | tf_op jit(solution)/shard_map/all_to_all | solution.py:226
  101.2 0.9 reduce_sum.12
  102.1 10.5 %all-to-all-start.3 = ((bf16[16,32,256]{2,1,0:T(8,128)(2,1)}), bf16[16,32,256]{2,1,0:T(8,128)(2,1)S(1)}, u32[]{:S(2)}, u32[]{:S(2)}) async-start(bf16[16,32,256]{2,1,0:T(8,128)(2,1)} %bitcast.19), calls=%async_computation.3 | async-start | bytes 524288 | tf_op jit(solution)/shard_map/all_to_all | solution.py:228
  112.6 0.0 collective-permute-done.6
  112.6 0.9 maximum_select_fusion
  113.5 10.8 %all-to-all-done.3.parts = bf16[16,32,256]{2,1,0:T(8,128)(2,1)S(1)} async-done(((bf16[16,32,256]{2,1,0:T(8,128)(2,1)}), bf16[16,32,256]{2,1,0:T(8,128)(2,1)S(1)}, u32[]{:S(2)}, u32[]{:S(2)}) %all-to-all-start.3) | async-done | bytes 262176 | tf_op jit(solution)/shard_map/all_to_all | solution.py:228
  124.3 0.7 copy-done.6
  125.0 1.6 %shard_map.79 = f32[32,512]{1,0:T(8,128)} custom-call(bf16[16,32,256]{2,1,0:T(8,128)(2,1)} %copy-done.6), custom_call_target="tpu_custom_call" | custom-call | bytes 524288 | tf_op jit(solution)/shard_map/pallas_call | solution.py:138
  (31 shorter events, 0.2 us)
Async XLA Ops:
  7.1 5.0 %copy-start.7 = (bf16[1,128,256]{2,1,0:T(8,128)(2,1)S(1)}, bf16[1,128,256]{2,1,0:T(8,128)(2,1)}, u32[]{:S(2)}) copy-start(bf16[1,128,256]{2,1,0:T(8,128)(2,1)} %param.8) | copy-start | bytes 196612
  7.1 5.0 %copy-start.8 = (bf16[1,128,256]{2,1,0:T(8,128)(2,1)S(1)}, bf16[1,128,256]{2,1,0:T(8,128)(2,1)}, u32[]{:S(2)}) copy-start(bf16[1,128,256]{2,1,0:T(8,128)(2,1)} %param.7) | copy-start | bytes 196612
  7.1 29.4 %all-to-all-start = ((bf16[4,2048,128]{2,1,0:T(8,128)(2,1)}), bf16[4,2048,128]{2,1,0:T(8,128)(2,1)S(1)}, u32[]{:S(2)}, u32[]{:S(2)}) async-start(bf16[4,2048,128]{2,1,0:T(8,128)(2,1)} %bitcast.46), calls=%async_computation | async-start | bytes 4194304 | tf_op jit(solution)/shard_map/all_to_all | solution.py:185
  12.1 13.5 %copy-start.9 = (s32[1,1024]{1,0:T(1,128)S(1)}, s32[1,1024]{1,0:T(1,128)}, u32[]{:S(2)}) copy-start(s32[1,1024]{1,0:T(1,128)} %param.11) | copy-start | bytes 12292
  12.1 27.6 %collective-permute-start.4 = (bf16[128,256]{1,0:T(8,128)(2,1)S(1)}, bf16[128,256]{1,0:T(8,128)(2,1)S(1)}, u32[]{:S(2)}, u32[]{:S(2)}) collective-permute-start(bf16[128,256]{1,0:T(8,128)(2,1)S(1)} %pad_maximum_fusion.1.k0), channel_id=1, source_target_pairs={{0,4},{1,5},{2,6},{3,7},{8,12},{9,13},{10,14},{11,15},{16,20},{17,... | collective-permute-start | bytes 196616 | tf_op jit(solution)/shard_map/ppermute | solution.py:170
  17.0 26.1 %collective-permute-start.2 = (bf16[128,256]{1,0:T(8,128)(2,1)S(1)}, bf16[128,256]{1,0:T(8,128)(2,1)S(1)}, u32[]{:S(2)}, u32[]{:S(2)}) collective-permute-start(bf16[128,256]{1,0:T(8,128)(2,1)S(1)} %pad_maximum_fusion.1.k0), channel_id=1, source_target_pairs={{0,2},{1,3},{2,4},{3,5},{4,6},{5,7},{8,10},{9,11},{10,12},{11,13},... | collective-permute-start | bytes 196616 | tf_op jit(solution)/shard_map/ppermute | solution.py:170
  20.6 23.5 %collective-permute-start.5 = (bf16[128,256]{1,0:T(8,128)(2,1)S(1)}, bf16[128,256]{1,0:T(8,128)(2,1)S(1)}, u32[]{:S(2)}, u32[]{:S(2)}) collective-permute-start(bf16[128,256]{1,0:T(8,128)(2,1)S(1)} %pad_maximum_fusion.2), channel_id=1, source_target_pairs={{0,5},{1,4},{2,7},{3,6},{8,13},{9,12},{10,15},{11,14},{16,21},{17,... | collective-permute-start | bytes 196616 | tf_op jit(solution)/shard_map/ppermute | solution.py:171
  25.1 19.7 %collective-permute-start = (bf16[128,2048]{1,0:T(8,128)(2,1)}, bf16[128,2048]{1,0:T(8,128)(2,1)S(1)}, u32[]{:S(2)}, u32[]{:S(2)}) collective-permute-start(bf16[128,2048]{1,0:T(8,128)(2,1)} %pad_maximum_fusion), channel_id=1, source_target_pairs={{0,1},{1,0},{2,3},{3,2},{4,5},{5,4},{6,7},{7,6},{8,9},{9,8},{10,11... | collective-permute-start | bytes 1572872 | tf_op jit(solution)/shard_map/ppermute | solution.py:173
  36.4 43.0 %collective-permute-start.7 = (bf16[4,2048,128]{2,1,0:T(8,128)(2,1)S(1)}, bf16[4,2048,128]{2,1,0:T(8,128)(2,1)}, u32[]{:S(2)}, u32[]{:S(2)}) collective-permute-start(bf16[4,2048,128]{2,1,0:T(8,128)(2,1)S(1)} %all-to-all-done.mine), channel_id=1, source_target_pairs={{0,1},{1,0},{2,3},{3,2},{4,5},{5,4},{6,7},{7,6},{8,9},{9,8},{10,11... | collective-permute-start | bytes 6291464 | tf_op jit(solution)/shard_map/ppermute | solution.py:186
  39.7 5.1 %collective-permute-start.3 = (bf16[128,256]{1,0:T(8,128)(2,1)S(1)}, bf16[128,256]{1,0:T(8,128)(2,1)S(1)}, u32[]{:S(2)}, u32[]{:S(2)}) collective-permute-start(bf16[128,256]{1,0:T(8,128)(2,1)S(1)} %pad_maximum_fusion.2), channel_id=1, source_target_pairs={{0,3},{1,2},{2,5},{3,4},{4,7},{5,6},{8,11},{9,10},{10,13},{11,12},... | collective-permute-start | bytes 196616 | tf_op jit(solution)/shard_map/ppermute | solution.py:171
  43.2 1.6 %copy-start.2 = (bf16[128,256]{1,0:T(8,128)(2,1)}, bf16[128,256]{1,0:T(8,128)(2,1)S(1)}, u32[]{:S(2)}) copy-start(bf16[128,256]{1,0:T(8,128)(2,1)S(1)} %collective-permute-done.2.k2) | copy-start | bytes 196612
  43.2 1.6 %collective-permute-start.1 = (bf16[128,256]{1,0:T(8,128)(2,1)S(1)}, bf16[128,256]{1,0:T(8,128)(2,1)S(1)}, u32[]{:S(2)}, u32[]{:S(2)}) collective-permute-start(bf16[128,256]{1,0:T(8,128)(2,1)S(1)} %pad_maximum_fusion.2), channel_id=1, source_target_pairs={{0,1},{1,0},{2,3},{3,2},{4,5},{5,4},{6,7},{7,6},{8,9},{9,8},{10,11... | collective-permute-start | bytes 196616 | tf_op jit(solution)/shard_map/ppermute | solution.py:168
  44.2 0.6 copy-start.4
  44.8 0.8 copy-start.3
  45.6 0.8 copy-start.5
  53.7 14.7 %copy-start = (bf16[128,1024]{1,0:T(8,128)(2,1)}, bf16[128,1024]{1,0:T(8,128)(2,1)S(1)}, u32[]{:S(2)}) copy-start(bf16[128,1024]{1,0:T(8,128)(2,1)S(1)} %get-tuple-element.8) | copy-start | bytes 786436
  53.7 7.7 %collective-permute-start.8 = (bf16[256,256]{1,0:T(8,128)(2,1)S(1)}, bf16[256,256]{1,0:T(8,128)(2,1)S(1)}, u32[]{:S(2)}, u32[]{:S(2)}) collective-permute-start(bf16[256,256]{1,0:T(8,128)(2,1)S(1)} %get-tuple-element.10), channel_id=1, source_target_pairs={{2,0},{3,1},{4,2},{5,3},{6,4},{7,5},{10,8},{11,9},{12,10},{13,11},... | collective-permute-start | bytes 393224 | tf_op jit(solution)/shard_map/ppermute | solution.py:219
  55.0 13.4 %collective-permute-start.9 = (bf16[256,256]{1,0:T(8,128)(2,1)S(1)}, bf16[256,256]{1,0:T(8,128)(2,1)S(1)}, u32[]{:S(2)}, u32[]{:S(2)}) collective-permute-start(bf16[256,256]{1,0:T(8,128)(2,1)S(1)} %get-tuple-element.11), channel_id=1, source_target_pairs={{4,0},{5,1},{6,2},{7,3},{12,8},{13,9},{14,10},{15,11},{20,16},{21,... | collective-permute-start | bytes 393224 | tf_op jit(solution)/shard_map/ppermute | solution.py:219
  83.9 4.3 %copy-start.1 = (bf16[128,1024]{1,0:T(8,128)(2,1)S(1)}, bf16[128,1024]{1,0:T(8,128)(2,1)}, u32[]{:S(2)}) copy-start(bf16[128,1024]{1,0:T(8,128)(2,1)} %copy-done) | copy-start | bytes 786436
  83.9 17.3 %all-to-all-start.2 = ((bf16[4,512,256]{2,1,0:T(8,128)(2,1)}), bf16[4,512,256]{2,1,0:T(8,128)(2,1)S(1)}, u32[]{:S(2)}, u32[]{:S(2)}) async-start(bf16[4,512,256]{2,1,0:T(8,128)(2,1)} %bitcast.18), calls=%async_computation.2 | async-start | bytes 2097152 | tf_op jit(solution)/shard_map/all_to_all | solution.py:226
  88.3 24.3 %collective-permute-start.6 = (bf16[128,1024]{1,0:T(8,128)(2,1)S(1)}, bf16[128,1024]{1,0:T(8,128)(2,1)S(1)}, u32[]{:S(2)}, u32[]{:S(2)}) collective-permute-start(bf16[128,1024]{1,0:T(8,128)(2,1)S(1)} %copy-done.1), channel_id=1, source_target_pairs={{0,1},{1,0},{2,3},{3,2},{4,5},{5,4},{6,7},{7,6},{8,9},{9,8},{10,11... | collective-permute-start | bytes 786440 | tf_op jit(solution)/shard_map/ppermute | solution.py:210
  102.1 22.2 %all-to-all-start.3 = ((bf16[16,32,256]{2,1,0:T(8,128)(2,1)}), bf16[16,32,256]{2,1,0:T(8,128)(2,1)S(1)}, u32[]{:S(2)}, u32[]{:S(2)}) async-start(bf16[16,32,256]{2,1,0:T(8,128)(2,1)} %bitcast.19), calls=%async_computation.3 | async-start | bytes 524288 | tf_op jit(solution)/shard_map/all_to_all | solution.py:228
  124.3 0.7 copy-start.6

commit v3 on v2

v3 whole, which is shorter than its diff:
```python
import jax
import jax.numpy as jnp
from jax import lax
from jax.experimental import pallas as pl
from jax.experimental.pallas import tpu as pltpu
from jax.sharding import Mesh, PartitionSpec as P

H = 16
KV = 2
DH = 128
GROUP = H // KV
SCALE = 1.0 / DH**0.5
LOG2E = 1.4426950408889634
REACH = 2
MASKED = -1e30
MIB = 1024 * 1024
SMALL = pltpu.CompilerParams(vmem_limit_bytes=4 * MIB)


def dot_nt(left, right):
    return lax.dot_general(
        left, right, (((1,), (1,)), ((), ())), preferred_element_type=jnp.float32
    )


def dot_nn(left, right):
    return jnp.dot(left, right, preferred_element_type=jnp.float32)


def whole(shape, dtype=jnp.bfloat16):
    return jax.ShapeDtypeStruct(shape, dtype)


HBM = pl.BlockSpec(memory_space=pltpu.HBM)
SCALAR = pl.BlockSpec(memory_space=pltpu.SMEM)
VMEM = pl.BlockSpec(memory_space=pltpu.VMEM)


def half(which, width):
    return pl.ds(pl.multiple_of(which * width, width), width)


def pair_kernel(core_ref, keys, values, mine, other):
    core = core_ref[0]
    for out, which in ((mine, core), (other, 1 - core)):
        out[:, :DH] = keys[:, half(which, DH)]
        out[:, DH:] = values[:, half(which, DH)]


def split_pairs(core, keys, values):
    return pl.pallas_call(
        pair_kernel,
        out_shape=(whole(keys.shape), whole(keys.shape)),
        in_specs=[SCALAR, VMEM, VMEM],
        compiler_params=SMALL,
        cost_estimate=pl.CostEstimate(flops=0, bytes_accessed=256 * 1024, transcendentals=0),
    )(core, keys, values)


def run_copies(copies, sems):
    started = [pltpu.make_async_copy(src, dst, sems.at[i]) for i, (src, dst) in enumerate(copies)]
    for copy in started:
        copy.start()
    for copy in started:
        copy.wait()


def other_kernel(core_ref, queries, out_grad, keys, values, out, sems):
    other = 1 - core_ref[0]
    wide = GROUP * DH
    run_copies(
        [
            (queries.at[:, half(other, wide)], out.at[:, :wide]),
            (out_grad.at[:, half(other, wide)], out.at[:, wide : 2 * wide]),
            (keys.at[:, half(other, DH)], out.at[:, 2 * wide : 2 * wide + DH]),
            (values.at[:, half(other, DH)], out.at[:, 2 * wide + DH :]),
        ],
        sems,
    )


def split_other(core, queries, out_grad, keys, values):
    rows = queries.shape[0]
    return pl.pallas_call(
        other_kernel,
        out_shape=whole((rows, 2 * GROUP * DH + 2 * DH)),
        in_specs=[SCALAR, HBM, HBM, HBM, HBM],
        out_specs=HBM,
        scratch_shapes=[pltpu.SemaphoreType.DMA((4,))],
        compiler_params=SMALL,
        cost_estimate=pl.CostEstimate(flops=0, bytes_accessed=1200 * 1024, transcendentals=0),
    )(core, queries, out_grad, keys, values)


def chunk_kernel(columns, out, sems):
    width = out.shape[2]
    run_copies(
        [(columns.at[:, i * width : (i + 1) * width], out.at[i]) for i in range(out.shape[0])], sems
    )


def split_columns(columns, chunks):
    rows, width = columns.shape
    return pl.pallas_call(
        chunk_kernel,
        out_shape=whole((chunks, rows, width // chunks)),
        in_specs=[HBM],
        out_specs=HBM,
        scratch_shapes=[pltpu.SemaphoreType.DMA((chunks,))],
        compiler_params=SMALL,
        cost_estimate=pl.CostEstimate(flops=0, bytes_accessed=4 * 1024 * 1024, transcendentals=0),
    )(columns)


def attention_kernel(
    core_ref, queries, out_grad, swapped, k0, k2, k3, k4, k5, bias,
    dq_mine, dq_other, own_grad, near_grad, far_grad, dk_acc, dv_acc,
):
    wide = GROUP * DH
    core = core_ref[0]
    k1 = swapped[:, 2 * wide :]
    pairs = jnp.concatenate([k0[...], k1, k2[...], k3[...], k4[...], k5[...]], axis=0)
    key, value = pairs[:, :DH], pairs[:, DH:]
    key_t = key.T
    rows = queries.shape[0]
    for head in range(GROUP):
        cols = slice(head * DH, (head + 1) * DH)
        grad_cols = slice(wide + head * DH, wide + (head + 1) * DH)
        mine = pl.ds(pl.multiple_of(core * wide + head * DH, DH), DH)
        query = jnp.concatenate([queries[:, mine], swapped[:, cols]], axis=0)
        grad = jnp.concatenate([out_grad[:, mine], swapped[:, grad_cols]], axis=0)
        score = dot_nt(key, query) * (SCALE * LOG2E) + bias[...]
        top = jnp.max(score, axis=0, keepdims=True)
        weight = jnp.exp2(score - top)
        inverse = 1.0 / jnp.sum(weight, axis=0, keepdims=True)
        prob = weight * inverse
        prob_half = prob.astype(jnp.bfloat16)
        prob_grad = dot_nt(value, grad)
        delta = jnp.sum(prob_half.astype(jnp.float32) * prob_grad, axis=0, keepdims=True)
        score_grad = (prob * (prob_grad - delta) * SCALE).astype(jnp.bfloat16)
        dq = dot_nn(key_t, score_grad).T.astype(jnp.bfloat16)
        dq_mine[:, cols] = dq[:rows]
        dq_other[:, cols] = dq[rows:]
        dk = dot_nn(score_grad, query)
        dv = dot_nn(prob_half, grad)
        if head == 0:
            dk_acc[...] = dk
            dv_acc[...] = dv
        else:
            dk_acc[...] += dk
            dv_acc[...] += dv
    chip = 2 * rows
    own_grad[:, :DH] = dk_acc[:chip]
    own_grad[:, DH:] = dv_acc[:chip]
    near_grad[:, :DH] = dk_acc[chip : 2 * chip].astype(jnp.bfloat16)
    near_grad[:, DH:] = dv_acc[chip : 2 * chip].astype(jnp.bfloat16)
    far_grad[:, :DH] = dk_acc[2 * chip :].astype(jnp.bfloat16)
    far_grad[:, DH:] = dv_acc[2 * chip :].astype(jnp.bfloat16)


def attention(core, queries, out_grad, swapped, blocks, bias):
    rows = queries.shape[0]
    chip = 2 * rows
    keys = chip * (REACH + 1)
    return pl.pallas_call(
        attention_kernel,
        out_shape=(
            whole((rows, GROUP * DH)),
            whole((rows, GROUP * DH)),
            whole((chip, 2 * DH), jnp.float32),
            whole((chip, 2 * DH)),
            whole((chip, 2 * DH)),
        ),
        in_specs=[SCALAR] + [VMEM] * (4 + len(blocks)),
        scratch_shapes=[
            pltpu.VMEM((keys, DH), jnp.float32),
            pltpu.VMEM((keys, DH), jnp.float32),
        ],
        compiler_params=pltpu.CompilerParams(vmem_limit_bytes=16 * MIB),
        cost_estimate=pl.CostEstimate(
            flops=10 * keys * chip * DH * GROUP,
            bytes_accessed=4 * 1024 * 1024,
            transcendentals=keys * chip * GROUP,
        ),
    )(core, queries, out_grad, swapped, *blocks, bias)


def combine_kernel(own, near, far, out):
    total = own[...] + near[...].astype(jnp.float32) + far[...].astype(jnp.float32)
    turned = total.T.astype(jnp.bfloat16)
    for i in range(out.shape[0]):
        out[i] = turned


def combine(own, near, far, copies):
    return pl.pallas_call(
        combine_kernel,
        out_shape=whole((copies, own.shape[1], own.shape[0])),
        compiler_params=SMALL,
        cost_estimate=pl.CostEstimate(flops=0, bytes_accessed=2 * 1024 * 1024, transcendentals=0),
    )(own, near, far)


def project_kernel(mine, other, grads, out):
    places = range(mine.shape[0])
    left = jnp.concatenate([grads[i] for i in places], axis=1)
    right = jnp.concatenate([part[i] for i in places for part in (mine, other)], axis=0)
    out[...] = dot_nn(left, right).T.astype(jnp.bfloat16)


def project(mine, other, grads, blocks):
    places, rows, columns = mine.shape
    width = grads.shape[1]
    step = columns // blocks
    return pl.pallas_call(
        project_kernel,
        out_shape=whole((columns, width)),
        grid=(blocks,),
        in_specs=[
            pl.BlockSpec((places, rows, step), lambda i: (0, 0, i)),
            pl.BlockSpec((places, rows, step), lambda i: (0, 0, i)),
            pl.BlockSpec(grads.shape, lambda i: (0, 0, 0)),
        ],
        out_specs=pl.BlockSpec((step, width), lambda i: (i, 0)),
        compiler_params=pltpu.CompilerParams(vmem_limit_bytes=8 * MIB),
        cost_estimate=pl.CostEstimate(
            flops=4 * places * rows * columns * width, bytes_accessed=6 * 1024 * 1024, transcendentals=0
        ),
    )(mine, other, grads)


def final_kernel(parts, out):
    for head in range(KV):
        total = parts[head].astype(jnp.float32)
        for i in range(1, parts.shape[0] // KV):
            total = total + parts[KV * i + head].astype(jnp.float32)
        out[:, head * DH : (head + 1) * DH] = total[:, :DH]
        out[:, (KV + head) * DH : (KV + head + 1) * DH] = total[:, DH:]


def final_sum(parts):
    return pl.pallas_call(
        final_kernel,
        out_shape=whole((parts.shape[1], 2 * KV * DH), jnp.float32),
        compiler_params=SMALL,
        cost_estimate=pl.CostEstimate(flops=0, bytes_accessed=512 * 1024, transcendentals=0),
    )(parts)


def per_device(queries, keys, values, out_grad, layer_input, segment_ids):
    rows = queries.shape[1]
    chip = 2 * rows
    z_lo = lax.axis_index("z_lo")
    core = lax.axis_index("core")
    core_ref = core.astype(jnp.int32).reshape(1)
    n_chips = lax.axis_size("z_lo")
    swap = [(0, 1), (1, 0)]

    group = ("y", "x_hi")
    n_group = lax.axis_size("y") * lax.axis_size("x_hi")
    columns = split_columns(layer_input[0], n_group)
    core_ref, columns = lax.optimization_barrier((core_ref, columns))

    pair_mine, pair_other = split_pairs(core_ref, keys[0], values[0])

    def behind(distance, flip):
        return [
            (chip_at * 2 + c, (chip_at + distance) * 2 + (c ^ flip))
            for chip_at in range(n_chips - distance)
            for c in range(2)
        ]

    blocks = [pair_mine]
    for distance in range(1, REACH + 1):
        blocks.append(lax.ppermute(pair_mine, ("z_lo", "core"), behind(distance, 0)))
        blocks.append(lax.ppermute(pair_other, ("z_lo", "core"), behind(distance, 1)))
    swapped = lax.ppermute(
        split_other(core_ref, queries[0], out_grad[0], keys[0], values[0]), "core", swap
    )

    columns_mine = lax.all_to_all(columns, group, 0, 0, tiled=True)

    seg_row = segment_ids[0]
    lane = jnp.arange(rows, dtype=jnp.int32)

    def places(chip_at, which):
        start = chip_at * chip + which * rows
        return (start + lane, lax.dynamic_slice_in_dim(seg_row, jnp.maximum(start, 0), rows, 0))

    key_places = [
        places(z_lo - distance, which)
        for distance in range(REACH + 1)
        for which in (core, 1 - core)
    ]
    key_pos = jnp.concatenate([place[0] for place in key_places])[:, None]
    key_doc = jnp.concatenate([place[1] for place in key_places])[:, None]
    query_pos = jnp.concatenate([place[0] for place in key_places[:2]])[None, :]
    query_doc = jnp.concatenate([place[1] for place in key_places[:2]])[None, :]
    allowed = (key_pos >= 0) & (key_pos <= query_pos) & (key_doc == query_doc)
    bias = jnp.where(allowed, 0.0, MASKED).astype(jnp.float32)

    dq_mine, dq_other, own_grad, near_grad, far_grad = attention(
        core_ref, queries[0], out_grad[0], swapped, blocks, bias
    )
    dq_back = lax.ppermute(dq_other, "core", swap)
    query_grad = jnp.where(
        core == 0,
        jnp.concatenate([dq_mine, dq_back], axis=1),
        jnp.concatenate([dq_back, dq_mine], axis=1),
    )[None]

    near_back, far_back = (
        lax.ppermute(part, ("z_lo", "core"), [(b, a) for a, b in behind(distance, 0)])
        for distance, part in ((1, near_grad), (2, far_grad))
    )

    copies = combine(own_grad, near_back, far_back, n_group)
    gathered = lax.all_to_all(copies, group, 0, 0, tiled=True)
    columns_mine, _ = lax.optimization_barrier((columns_mine, copies))
    columns_other = lax.ppermute(columns_mine, "core", swap)
    term = project(columns_mine, columns_other, gathered, 4)
    rest = ("x_lo", "z_hi", "z_lo", "core")
    n_rest = lax.axis_size(rest)
    spread = lax.all_to_all(
        term.reshape(n_rest, term.shape[0] // n_rest, term.shape[1]), rest, 0, 0, tiled=True
    )
    return (query_grad, final_sum(spread))


def solution(mesh):
    axes = ("y", "x_hi", "x_lo", "z_hi", "z_lo", "core")
    fine = Mesh(mesh.devices.reshape(4, 2, 2, 2, 4, 2), axes)
    dp, ctx = axes[:4], axes[4:]
    return jax.shard_map(
        per_device,
        mesh=fine,
        in_specs=(P(dp, ctx, None),) * 5 + (P(dp, None),),
        out_specs=(P(dp, ctx, None), P(axes, None)),
        check_vma=False,
    )
```

time: 127 us -> 106 us (0.83)
  waiting for transfers between devices: 44.4 us -> 24.9 us
  blocking collectives: 11 us -> 23.3 us
  starting transfers between devices: 42.7 us -> 32.7 us
  local copies, waits for them, and re-layouts: 11.2 us -> 7.78 us
  other arithmetic: 3.23 us -> 1.36 us
  Pallas kernels: 13.3 us -> 14.9 us
    all_to_all x3 -> x2, waiting for transfers between devices: 32.3 us -> 14.3 us  [the longest x1 14 us: per_device(): lax.all_to_all(term.reshape(n_rest, term.shape[0] // n_rest, term.shape[1...]
    all_to_all x1, blocking collectives: 11 us -> 23.3 us  [per_device(): gathered = lax.all_to_all(copies, group, 0, 0, tiled=True)]
    another operation x2 -> x0, local copies, waits for them, and re-layouts: 6.45 us -> none  [per_device(): layer_input[0].reshape(rows, n_y, n_x, depth).transpose(2, 1, 3, 0)]
    all_to_all x3 -> x2, starting transfers between devices: 19.8 us -> 13.8 us  [the longest x1 7.07 us: per_device(): lax.all_to_all(term.reshape(n_rest, term.shape[0] // n_rest, term.shape[1...]
    unnamed x25 -> x31, local copies, waits for them, and re-layouts: 3.4 us -> 7.7 us
    ppermute x2, starting transfers between devices: 5.85 us -> 9.54 us  [per_device(): lax.ppermute(pair_other, ('z_lo', 'core'), behind(distance, 1))]
    ppermute x2, starting transfers between devices: 8.44 us -> 4.86 us  [per_device(): lax.ppermute(pair_mine, ('z_lo', 'core'), behind(distance, 0))]
    ppermute x4 -> x3, waiting for transfers between devices: 12.1 us -> 9.29 us  [the longest x2 9.29 us: per_device(): lax.ppermute(part, ('z_lo', 'core'), [(b, a) for a, b in behind(distance,...]
  transfers between devices with their start and end apart: 13 -> 11, of which waited for: 5 -> 5; matrix products, arithmetic and copies ran while one was open for 4% -> 2% of each run, Pallas kernels for 6% -> 8%
where the time goes in v3:
time: 106 us
  starting transfers between devices  32.7 us (31%)
  waiting for transfers between devices  24.9 us (23%)
  blocking collectives  23.3 us (22%)
  Pallas kernels  14.9 us (14%)
  local copies, waits for them, and re-layouts  7.78 us (7%)
  other arithmetic  1.36 us (1%)
    all_to_all x1, blocking collectives, per_device(): gathered = lax.all_to_all(copies, group, 0, 0, tiled=True)  23.3 us
    all_to_all x1, waiting for transfers between devices, per_device(): lax.all_to_all(term.reshape(n_rest, term.shape[0] // n_rest, term.shape[1...  14 us
    ppermute x2, starting transfers between devices, per_device(): lax.ppermute(pair_other, ('z_lo', 'core'), behind(distance, 1))  9.54 us
    ppermute x2, waiting for transfers between devices, per_device(): lax.ppermute(part, ('z_lo', 'core'), [(b, a) for a, b in behind(distance,...  9.29 us
    pallas_call x1, Pallas kernels, attention(): pl.pallas_call(attention_kernel, out_shape=(whole((rows, GROUP * DH)), wh...  8.49 us
    unnamed x31, local copies, waits for them, and re-layouts  7.7 us
    all_to_all x1, starting transfers between devices, per_device(): lax.all_to_all(term.reshape(n_rest, term.shape[0] // n_rest, term.shape[1...  7.07 us
    all_to_all x1, starting transfers between devices, per_device(): columns_mine = lax.all_to_all(columns, group, 0, 0, tiled=True)  6.68 us
  transfers between devices with their start and end apart: 11, of which 5 were waited for; matrix products, arithmetic and copies ran while one was open for 2% of the time, Pallas kernels for 8%

profile of v3, /device:TPU:1, one launch (start us, length us, event | category | flops | bytes accessed | tf_op | source)
XLA Modules:
  0.0 105.8 jit_solution(11154638512974790235)
XLA Ops:
  0.6 1.6 %copy-done = bf16[1,128,8192]{2,1,0:T(8,128)(2,1)S(1)} copy-done((bf16[1,128,8192]{2,1,0:T(8,128)(2,1)S(1)}, bf16[1,128,8192]{2,1,0:T(8,128)(2,1)}, u32[]{:S(2)}) %copy-start) | copy-done | bytes 2097176
  2.2 1.4 %shard_map.77 = bf16[8,128,1024]{2,1,0:T(8,128)(2,1)} custom-call(bf16[128,8192]{1,0:T(8,128)(2,1)S(1)} %bitcast.31), custom_call_target="tpu_custom_call" | custom-call | bytes 4194304 | tf_op jit(solution)/shard_map/pallas_call | solution.py:104
  3.7 0.7 shard_map.79
  4.3 6.3 %collective-permute-start.4 = (bf16[128,256]{1,0:T(8,128)(2,1)}, bf16[128,256]{1,0:T(8,128)(2,1)S(1)}, u32[]{:S(2)}, u32[]{:S(2)}) collective-permute-start(bf16[128,256]{1,0:T(8,128)(2,1)} %get-tuple-element.14), channel_id=1, source_target_pairs={{0,5},{1,4},{2,7},{3,6},{8,13},{9,12},{10,15},{11,14},{16,21},{17,... | collective-permute-start | bytes 196616 | tf_op jit(solution)/shard_map/ppermute | solution.py:276
  10.6 3.3 %collective-permute-start.2 = (bf16[128,256]{1,0:T(8,128)(2,1)}, bf16[128,256]{1,0:T(8,128)(2,1)S(1)}, u32[]{:S(2)}, u32[]{:S(2)}) collective-permute-start(bf16[128,256]{1,0:T(8,128)(2,1)} %get-tuple-element.14), channel_id=1, source_target_pairs={{0,3},{1,2},{2,5},{3,4},{4,7},{5,6},{8,11},{9,10},{10,13},{11,12},... | collective-permute-start | bytes 196616 | tf_op jit(solution)/shard_map/ppermute | solution.py:276
  13.9 0.0 copy-start.1
  13.9 0.0 copy-start.12
  13.9 2.3 %collective-permute-start.3 = (bf16[128,256]{1,0:T(8,128)(2,1)S(1)}, bf16[128,256]{1,0:T(8,128)(2,1)}, u32[]{:S(2)}, u32[]{:S(2)}) collective-permute-start(bf16[128,256]{1,0:T(8,128)(2,1)S(1)} %get-tuple-element.13.k0), channel_id=1, source_target_pairs={{0,4},{1,5},{2,6},{3,7},{8,12},{9,13},{10,14},{11,15},{16,20},{17,... | collective-permute-start | bytes 196616 | tf_op jit(solution)/shard_map/ppermute | solution.py:275
  16.3 2.5 %collective-permute-start.1 = (bf16[128,256]{1,0:T(8,128)(2,1)S(1)}, bf16[128,256]{1,0:T(8,128)(2,1)}, u32[]{:S(2)}, u32[]{:S(2)}) collective-permute-start(bf16[128,256]{1,0:T(8,128)(2,1)S(1)} %get-tuple-element.13.k0), channel_id=1, source_target_pairs={{0,2},{1,3},{2,4},{3,5},{4,6},{5,7},{8,10},{9,11},{10,12},{11,13},... | collective-permute-start | bytes 196616 | tf_op jit(solution)/shard_map/ppermute | solution.py:275
  18.8 6.7 %all-to-all-start = ((bf16[8,128,1024]{2,1,0:T(8,128)(2,1)}), bf16[8,128,1024]{2,1,0:T(8,128)(2,1)S(1)}, u32[]{:S(2)}, u32[]{:S(2)}) async-start(bf16[8,128,1024]{2,1,0:T(8,128)(2,1)} %shard_map.77), calls=%async_computation | async-start | bytes 4194304 | tf_op jit(solution)/shard_map/all_to_all | solution.py:281
  25.5 0.0 copy-start.2
  25.5 1.0 copy-done.2
  26.5 0.1 shard_map.78
  26.6 0.4 collective-permute-start
  27.2 0.1 constant_dynamic-update-slice_fusion.11
  27.3 0.1 constant_dynamic-update-slice_fusion.9
  27.4 0.1 constant_dynamic-update-slice_fusion.7
  27.4 0.1 constant_dynamic-update-slice_fusion.5
  27.5 0.1 constant_dynamic-update-slice_fusion.3
  27.6 0.1 constant_dynamic-update-slice_fusion.1
  27.7 0.4 and_select_fusion.bias
  28.1 0.0 collective-permute-done.4.k5
  28.1 0.0 copy-start.8
  28.1 0.6 copy-done.8
  28.7 0.0 collective-permute-done.2.k3
  28.7 0.6 copy-done.10
  29.4 0.0 copy-start.3
  29.4 1.0 copy-done.3
  30.4 0.8 copy-done.9
  31.2 0.8 copy-done.11
  32.1 8.5 %shard_map.80 = (bf16[128,1024]{1,0:T(8,128)(2,1)S(1)}, bf16[128,1024]{1,0:T(8,128)(2,1)S(1)}, f32[256,256]{1,0:T(8,128)S(1)}, bf16[256,256]{1,0:T(8,128)(2,1)S(1)}, bf16[256,256]{1,0:T(8,128)(2,1)S(1)}) custom-call(s32[1]{0:T(128)} %bitcast.core_ref, bf16[128,2048]{1,0:T(8,128)(2,1)S(1)} %bitcast.33, bf16[128,2048]{1,0:T(8,128)(2,1)S(1)} %bitcast.35, ...), custom_call_target="tpu_custom_call" | custom-call | flops 2013265920 | bytes 4194304 | tf_op jit(solution)/shard_map/pallas_call | solution.py:165
  40.6 0.0 copy-start.6
  40.6 0.7 copy-done.6
  41.3 1.3 %collective-permute-start.6 = (bf16[256,256]{1,0:T(8,128)(2,1)S(1)}, bf16[256,256]{1,0:T(8,128)(2,1)S(1)}, u32[]{:S(2)}, u32[]{:S(2)}) collective-permute-start(bf16[256,256]{1,0:T(8,128)(2,1)S(1)} %get-tuple-element.19), channel_id=1, source_target_pairs={{2,0},{3,1},{4,2},{5,3},{6,4},{7,5},{10,8},{11,9},{12,10},{13,11},... | collective-permute-start | bytes 393224 | tf_op jit(solution)/shard_map/ppermute | solution.py:313
  42.6 1.3 %collective-permute-start.7 = (bf16[256,256]{1,0:T(8,128)(2,1)S(1)}, bf16[256,256]{1,0:T(8,128)(2,1)S(1)}, u32[]{:S(2)}, u32[]{:S(2)}) collective-permute-start(bf16[256,256]{1,0:T(8,128)(2,1)S(1)} %get-tuple-element.20), channel_id=1, source_target_pairs={{4,0},{5,1},{6,2},{7,3},{12,8},{13,9},{14,10},{15,11},{20,16},{21,... | collective-permute-start | bytes 393224 | tf_op jit(solution)/shard_map/ppermute | solution.py:313
  43.9 4.3 %collective-permute-done.6.near = bf16[256,256]{1,0:T(8,128)(2,1)S(1)} collective-permute-done((bf16[256,256]{1,0:T(8,128)(2,1)S(1)}, bf16[256,256]{1,0:T(8,128)(2,1)S(1)}, u32[]{:S(2)}, u32[]{:S(2)}) %collective-permute-start.6) | collective-permute-done | bytes 131104 | tf_op jit(solution)/shard_map/ppermute | solution.py:313
  48.1 5.0 %collective-permute-done.7.far = bf16[256,256]{1,0:T(8,128)(2,1)S(1)} collective-permute-done((bf16[256,256]{1,0:T(8,128)(2,1)S(1)}, bf16[256,256]{1,0:T(8,128)(2,1)S(1)}, u32[]{:S(2)}, u32[]{:S(2)}) %collective-permute-start.7) | collective-permute-done | bytes 131104 | tf_op jit(solution)/shard_map/ppermute | solution.py:313
  53.2 0.2 shard_map.81
  53.4 0.3 all-to-all-done.mine
  53.7 1.2 %collective-permute-start.8 = (bf16[8,128,1024]{2,1,0:T(8,128)(2,1)S(1)}, bf16[8,128,1024]{2,1,0:T(8,128)(2,1)S(1)}, u32[]{:S(2)}, u32[]{:S(2)}) collective-permute-start(bf16[8,128,1024]{2,1,0:T(8,128)(2,1)S(1)} %all-to-all-done.mine), channel_id=1, source_target_pairs={{0,1},{1,0},{2,3},{3,2},{4,5},{5,4},{6,7},{7,6},{8,9},{9,8},{10,11... | collective-permute-start | bytes 6291464 | tf_op jit(solution)/shard_map/ppermute | solution.py:320
  54.9 23.3 %all_to_all.15.grads = bf16[8,256,256]{2,1,0:T(8,128)(2,1)S(1)} all-to-all(bf16[8,256,256]{2,1,0:T(8,128)(2,1)S(1)} %shard_map.81), channel_id=1, replica_groups=mesh['y'=4,'x_hi'=2,'x_lo'=2,'z_hi'=2,'z_lo'=4,'core'=2] {'y','x_hi'}, dimensions={0} | all-to-all | bytes 2097152 | tf_op jit(solution)/shard_map/all_to_all | solution.py:318
  78.2 3.3 %shard_map.82 = bf16[1024,256]{1,0:T(8,128)(2,1)} custom-call(bf16[8,128,1024]{2,1,0:T(8,128)(2,1)S(1)} %all-to-all-done.mine, bf16[8,128,1024]{2,1,0:T(8,128)(2,1)S(1)} %collective-permute-done.8.other, bf16[8,256,256]{2,1,0:T(8,128)(2,1)S(1)} %all_to_all.15.grads), custom_call_target="tpu_custom_call" | custom-call | flops 1073741824 | bytes 6291456 | tf_op jit(solution)/shard_map/pallas_call | solution.py:215
  81.5 7.1 %all-to-all-start.2 = ((bf16[32,32,256]{2,1,0:T(8,128)(2,1)}), bf16[32,32,256]{2,1,0:T(8,128)(2,1)S(1)}, u32[]{:S(2)}, u32[]{:S(2)}) async-start(bf16[32,32,256]{2,1,0:T(8,128)(2,1)} %bitcast.14), calls=%async_computation.2 | async-start | bytes 1048576 | tf_op jit(solution)/shard_map/all_to_all | solution.py:324
  88.6 0.3 collective-permute-start.5
  88.9 1.3 %collective-permute-done.5 = bf16[128,1024]{1,0:T(8,128)(2,1)S(1)} collective-permute-done((bf16[128,1024]{1,0:T(8,128)(2,1)S(1)}, bf16[128,1024]{1,0:T(8,128)(2,1)S(1)}, u32[]{:S(2)}, u32[]{:S(2)}) %collective-permute-start.5) | collective-permute-done | bytes 262176 | tf_op jit(solution)/shard_map/ppermute | solution.py:305
  90.2 0.9 maximum_select_fusion
  91.1 14.0 %all-to-all-done.2.parts = bf16[32,32,256]{2,1,0:T(8,128)(2,1)S(1)} async-done(((bf16[32,32,256]{2,1,0:T(8,128)(2,1)}), bf16[32,32,256]{2,1,0:T(8,128)(2,1)S(1)}, u32[]{:S(2)}, u32[]{:S(2)}) %all-to-all-start.2) | async-done | bytes 524320 | tf_op jit(solution)/shard_map/all_to_all | solution.py:324
  105.1 0.7 shard_map.83
  (28 shorter events, 0.1 us)
Async XLA Ops:
  0.6 1.6 %copy-start = (bf16[1,128,8192]{2,1,0:T(8,128)(2,1)S(1)}, bf16[1,128,8192]{2,1,0:T(8,128)(2,1)}, u32[]{:S(2)}) copy-start(bf16[1,128,8192]{2,1,0:T(8,128)(2,1)} %param.10) | copy-start | bytes 6291460
  2.2 1.4 %copy-start.4 = (bf16[1,128,256]{2,1,0:T(8,128)(2,1)S(1)}, bf16[1,128,256]{2,1,0:T(8,128)(2,1)}, u32[]{:S(2)}) copy-start(bf16[1,128,256]{2,1,0:T(8,128)(2,1)} %param.7) | copy-start | bytes 196612
  2.2 1.4 %copy-start.5 = (bf16[1,128,256]{2,1,0:T(8,128)(2,1)S(1)}, bf16[1,128,256]{2,1,0:T(8,128)(2,1)}, u32[]{:S(2)}) copy-start(bf16[1,128,256]{2,1,0:T(8,128)(2,1)} %param.8) | copy-start | bytes 196612
  4.3 23.7 %collective-permute-start.4 = (bf16[128,256]{1,0:T(8,128)(2,1)}, bf16[128,256]{1,0:T(8,128)(2,1)S(1)}, u32[]{:S(2)}, u32[]{:S(2)}) collective-permute-start(bf16[128,256]{1,0:T(8,128)(2,1)} %get-tuple-element.14), channel_id=1, source_target_pairs={{0,5},{1,4},{2,7},{3,6},{8,13},{9,12},{10,15},{11,14},{16,21},{17,... | collective-permute-start | bytes 196616 | tf_op jit(solution)/shard_map/ppermute | solution.py:276
  10.6 18.1 %collective-permute-start.2 = (bf16[128,256]{1,0:T(8,128)(2,1)}, bf16[128,256]{1,0:T(8,128)(2,1)S(1)}, u32[]{:S(2)}, u32[]{:S(2)}) collective-permute-start(bf16[128,256]{1,0:T(8,128)(2,1)} %get-tuple-element.14), channel_id=1, source_target_pairs={{0,3},{1,2},{2,5},{3,4},{4,7},{5,6},{8,11},{9,10},{10,13},{11,12},... | collective-permute-start | bytes 196616 | tf_op jit(solution)/shard_map/ppermute | solution.py:276
  13.9 11.6 %copy-start.1 = (bf16[1,128,2048]{2,1,0:T(8,128)(2,1)S(1)}, bf16[1,128,2048]{2,1,0:T(8,128)(2,1)}, u32[]{:S(2)}) copy-start(bf16[1,128,2048]{2,1,0:T(8,128)(2,1)} %param.6) | copy-start | bytes 1572868
  13.9 13.3 %copy-start.12 = (s32[1,1024]{1,0:T(1,128)S(1)}, s32[1,1024]{1,0:T(1,128)}, u32[]{:S(2)}) copy-start(s32[1,1024]{1,0:T(1,128)} %param.11) | copy-start | bytes 12292
  13.9 15.4 %collective-permute-start.3 = (bf16[128,256]{1,0:T(8,128)(2,1)S(1)}, bf16[128,256]{1,0:T(8,128)(2,1)}, u32[]{:S(2)}, u32[]{:S(2)}) collective-permute-start(bf16[128,256]{1,0:T(8,128)(2,1)S(1)} %get-tuple-element.13.k0), channel_id=1, source_target_pairs={{0,4},{1,5},{2,6},{3,7},{8,12},{9,13},{10,14},{11,15},{16,20},{17,... | collective-permute-start | bytes 196616 | tf_op jit(solution)/shard_map/ppermute | solution.py:275
  16.3 13.1 %collective-permute-start.1 = (bf16[128,256]{1,0:T(8,128)(2,1)S(1)}, bf16[128,256]{1,0:T(8,128)(2,1)}, u32[]{:S(2)}, u32[]{:S(2)}) collective-permute-start(bf16[128,256]{1,0:T(8,128)(2,1)S(1)} %get-tuple-element.13.k0), channel_id=1, source_target_pairs={{0,2},{1,3},{2,4},{3,5},{4,6},{5,7},{8,10},{9,11},{10,12},{11,13},... | collective-permute-start | bytes 196616 | tf_op jit(solution)/shard_map/ppermute | solution.py:275
  18.8 34.9 %all-to-all-start = ((bf16[8,128,1024]{2,1,0:T(8,128)(2,1)}), bf16[8,128,1024]{2,1,0:T(8,128)(2,1)S(1)}, u32[]{:S(2)}, u32[]{:S(2)}) async-start(bf16[8,128,1024]{2,1,0:T(8,128)(2,1)} %shard_map.77), calls=%async_computation | async-start | bytes 4194304 | tf_op jit(solution)/shard_map/all_to_all | solution.py:281
  25.5 1.0 copy-start.2
  26.6 2.7 %collective-permute-start = (bf16[128,2304]{1,0:T(8,128)(2,1)S(1)}, bf16[128,2304]{1,0:T(8,128)(2,1)}, u32[]{:S(2)}, u32[]{:S(2)}) collective-permute-start(bf16[128,2304]{1,0:T(8,128)(2,1)S(1)} %shard_map.78), channel_id=1, source_target_pairs={{0,1},{1,0},{2,3},{3,2},{4,5},{5,4},{6,7},{7,6},{8,9},{9,8},{10,11... | collective-permute-start | bytes 1769480 | tf_op jit(solution)/shard_map/ppermute | solution.py:277
  28.1 0.6 copy-start.8
  28.7 0.6 copy-start.10
  29.4 1.0 copy-start.3
  30.4 0.8 copy-start.9
  31.2 0.8 copy-start.11
  40.6 0.7 copy-start.6
  41.3 6.8 %collective-permute-start.6 = (bf16[256,256]{1,0:T(8,128)(2,1)S(1)}, bf16[256,256]{1,0:T(8,128)(2,1)S(1)}, u32[]{:S(2)}, u32[]{:S(2)}) collective-permute-start(bf16[256,256]{1,0:T(8,128)(2,1)S(1)} %get-tuple-element.19), channel_id=1, source_target_pairs={{2,0},{3,1},{4,2},{5,3},{6,4},{7,5},{10,8},{11,9},{12,10},{13,11},... | collective-permute-start | bytes 393224 | tf_op jit(solution)/shard_map/ppermute | solution.py:313
  42.6 10.6 %collective-permute-start.7 = (bf16[256,256]{1,0:T(8,128)(2,1)S(1)}, bf16[256,256]{1,0:T(8,128)(2,1)S(1)}, u32[]{:S(2)}, u32[]{:S(2)}) collective-permute-start(bf16[256,256]{1,0:T(8,128)(2,1)S(1)} %get-tuple-element.20), channel_id=1, source_target_pairs={{4,0},{5,1},{6,2},{7,3},{12,8},{13,9},{14,10},{15,11},{20,16},{21,... | collective-permute-start | bytes 393224 | tf_op jit(solution)/shard_map/ppermute | solution.py:313
  53.7 24.5 %collective-permute-start.8 = (bf16[8,128,1024]{2,1,0:T(8,128)(2,1)S(1)}, bf16[8,128,1024]{2,1,0:T(8,128)(2,1)S(1)}, u32[]{:S(2)}, u32[]{:S(2)}) collective-permute-start(bf16[8,128,1024]{2,1,0:T(8,128)(2,1)S(1)} %all-to-all-done.mine), channel_id=1, source_target_pairs={{0,1},{1,0},{2,3},{3,2},{4,5},{5,4},{6,7},{7,6},{8,9},{9,8},{10,11... | collective-permute-start | bytes 6291464 | tf_op jit(solution)/shard_map/ppermute | solution.py:320
  78.2 10.4 %copy-start.7 = (bf16[128,1024]{1,0:T(8,128)(2,1)S(1)}, bf16[128,1024]{1,0:T(8,128)(2,1)}, u32[]{:S(2)}) copy-start(bf16[128,1024]{1,0:T(8,128)(2,1)} %copy-done.6) | copy-start | bytes 786436
  81.5 23.6 %all-to-all-start.2 = ((bf16[32,32,256]{2,1,0:T(8,128)(2,1)}), bf16[32,32,256]{2,1,0:T(8,128)(2,1)S(1)}, u32[]{:S(2)}, u32[]{:S(2)}) async-start(bf16[32,32,256]{2,1,0:T(8,128)(2,1)} %bitcast.14), calls=%async_computation.2 | async-start | bytes 1048576 | tf_op jit(solution)/shard_map/all_to_all | solution.py:324
  88.6 1.6 %collective-permute-start.5 = (bf16[128,1024]{1,0:T(8,128)(2,1)S(1)}, bf16[128,1024]{1,0:T(8,128)(2,1)S(1)}, u32[]{:S(2)}, u32[]{:S(2)}) collective-permute-start(bf16[128,1024]{1,0:T(8,128)(2,1)S(1)} %copy-done.7), channel_id=1, source_target_pairs={{0,1},{1,0},{2,3},{3,2},{4,5},{5,4},{6,7},{7,6},{8,9},{9,8},{10,11... | collective-permute-start | bytes 786440 | tf_op jit(solution)/shard_map/ppermute | solution.py:305

commit v4 on v3

--- a/solution.py
+++ b/solution.py
@@ -32,29 +32,6 @@
 
 
 HBM = pl.BlockSpec(memory_space=pltpu.HBM)
-SCALAR = pl.BlockSpec(memory_space=pltpu.SMEM)
-VMEM = pl.BlockSpec(memory_space=pltpu.VMEM)
-
-
-def half(which, width):
-    return pl.ds(pl.multiple_of(which * width, width), width)
-
-
-def pair_kernel(core_ref, keys, values, mine, other):
-    core = core_ref[0]
-    for out, which in ((mine, core), (other, 1 - core)):
-        out[:, :DH] = keys[:, half(which, DH)]
-        out[:, DH:] = values[:, half(which, DH)]
-
-
-def split_pairs(core, keys, values):
-    return pl.pallas_call(
-        pair_kernel,
-        out_shape=(whole(keys.shape), whole(keys.shape)),
-        in_specs=[SCALAR, VMEM, VMEM],
-        compiler_params=SMALL,
-        cost_estimate=pl.CostEstimate(flops=0, bytes_accessed=256 * 1024, transcendentals=0),
-    )(core, keys, values)
 
 
 def run_copies(copies, sems):
@@ -65,31 +42,20 @@
         copy.wait()
 
 
-def other_kernel(core_ref, queries, out_grad, keys, values, out, sems):
-    other = 1 - core_ref[0]
-    wide = GROUP * DH
-    run_copies(
-        [
-            (queries.at[:, half(other, wide)], out.at[:, :wide]),
-            (out_grad.at[:, half(other, wide)], out.at[:, wide : 2 * wide]),
-            (keys.at[:, half(other, DH)], out.at[:, 2 * wide : 2 * wide + DH]),
-            (values.at[:, half(other, DH)], out.at[:, 2 * wide + DH :]),
-        ],
-        sems,
-    )
-
-
-def split_other(core, queries, out_grad, keys, values):
-    rows = queries.shape[0]
-    return pl.pallas_call(
-        other_kernel,
-        out_shape=whole((rows, 2 * GROUP * DH + 2 * DH)),
-        in_specs=[SCALAR, HBM, HBM, HBM, HBM],
-        out_specs=HBM,
-        scratch_shapes=[pltpu.SemaphoreType.DMA((4,))],
+def pair_kernel(keys, values, swapped, out):
+    rows = keys.shape[0]
+    out[:rows, :DH] = keys[...]
+    out[:rows, DH:] = values[...]
+    out[rows:] = swapped[:, 2 * GROUP * DH :]
+
+
+def chip_pairs(keys, values, swapped):
+    return pl.pallas_call(
+        pair_kernel,
+        out_shape=whole((2 * keys.shape[0], 2 * DH)),
         compiler_params=SMALL,
-        cost_estimate=pl.CostEstimate(flops=0, bytes_accessed=1200 * 1024, transcendentals=0),
-    )(core, queries, out_grad, keys, values)
+        cost_estimate=pl.CostEstimate(flops=0, bytes_accessed=256 * 1024, transcendentals=0),
+    )(keys, values, swapped)
 
 
 def chunk_kernel(columns, out, sems):
@@ -113,22 +79,19 @@
 
 
 def attention_kernel(
-    core_ref, queries, out_grad, swapped, k0, k2, k3, k4, k5, bias,
+    queries, out_grad, swapped, chip_pair, near_pair, far_pair, bias,
     dq_mine, dq_other, own_grad, near_grad, far_grad, dk_acc, dv_acc,
 ):
     wide = GROUP * DH
-    core = core_ref[0]
-    k1 = swapped[:, 2 * wide :]
-    pairs = jnp.concatenate([k0[...], k1, k2[...], k3[...], k4[...], k5[...]], axis=0)
+    pairs = jnp.concatenate([chip_pair[...], near_pair[...], far_pair[...]], axis=0)
     key, value = pairs[:, :DH], pairs[:, DH:]
     key_t = key.T
     rows = queries.shape[0]
     for head in range(GROUP):
         cols = slice(head * DH, (head + 1) * DH)
         grad_cols = slice(wide + head * DH, wide + (head + 1) * DH)
-        mine = pl.ds(pl.multiple_of(core * wide + head * DH, DH), DH)
-        query = jnp.concatenate([queries[:, mine], swapped[:, cols]], axis=0)
-        grad = jnp.concatenate([out_grad[:, mine], swapped[:, grad_cols]], axis=0)
+        query = jnp.concatenate([queries[:, cols], swapped[:, cols]], axis=0)
+        grad = jnp.concatenate([out_grad[:, cols], swapped[:, grad_cols]], axis=0)
         score = dot_nt(key, query) * (SCALE * LOG2E) + bias[...]
         top = jnp.max(score, axis=0, keepdims=True)
         weight = jnp.exp2(score - top)
@@ -158,7 +121,7 @@
     far_grad[:, DH:] = dv_acc[2 * chip :].astype(jnp.bfloat16)
 
 
-def attention(core, queries, out_grad, swapped, blocks, bias):
+def attention(queries, out_grad, swapped, blocks, bias):
     rows = queries.shape[0]
     chip = 2 * rows
     keys = chip * (REACH + 1)
@@ -171,18 +134,17 @@
             whole((chip, 2 * DH)),
             whole((chip, 2 * DH)),
         ),
-        in_specs=[SCALAR] + [VMEM] * (4 + len(blocks)),
         scratch_shapes=[
             pltpu.VMEM((keys, DH), jnp.float32),
             pltpu.VMEM((keys, DH), jnp.float32),
         ],
         compiler_params=pltpu.CompilerParams(vmem_limit_bytes=16 * MIB),
         cost_estimate=pl.CostEstimate(
-            flops=10 * keys * chip * DH * GROUP,
+            flops=160 * keys * chip * DH * GROUP,
             bytes_accessed=4 * 1024 * 1024,
             transcendentals=keys * chip * GROUP,
         ),
-    )(core, queries, out_grad, swapped, *blocks, bias)
+    )(queries, out_grad, swapped, *blocks, bias)
 
 
 def combine_kernel(own, near, far, out):
@@ -252,31 +214,35 @@
     chip = 2 * rows
     z_lo = lax.axis_index("z_lo")
     core = lax.axis_index("core")
-    core_ref = core.astype(jnp.int32).reshape(1)
     n_chips = lax.axis_size("z_lo")
     swap = [(0, 1), (1, 0)]
+
+    def half_of(array, which):
+        width = array.shape[-1] // 2
+        return lax.dynamic_slice_in_dim(array[0], which * width, width, 1)
+
+    sources = (queries, out_grad, keys, values)
+    q_mine, do_mine, k_mine, v_mine = (half_of(array, core) for array in sources)
+    swapped = lax.ppermute(
+        jnp.concatenate([half_of(array, 1 - core) for array in sources], axis=1), "core", swap
+    )
+    chip_pair = chip_pairs(k_mine, v_mine, swapped)
+
+    def behind(distance):
+        return [
+            (chip_at * 2 + c, (chip_at + distance) * 2 + c)
+            for chip_at in range(n_chips - distance)
+            for c in range(2)
+        ]
+
+    blocks = [chip_pair] + [
+        lax.ppermute(chip_pair, ("z_lo", "core"), behind(distance)) for distance in (2, 1)
+    ][::-1]
 
     group = ("y", "x_hi")
     n_group = lax.axis_size("y") * lax.axis_size("x_hi")
     columns = split_columns(layer_input[0], n_group)
-    core_ref, columns = lax.optimization_barrier((core_ref, columns))
-
-    pair_mine, pair_other = split_pairs(core_ref, keys[0], values[0])
-
-    def behind(distance, flip):
-        return [
-            (chip_at * 2 + c, (chip_at + distance) * 2 + (c ^ flip))
-            for chip_at in range(n_chips - distance)
-            for c in range(2)
-        ]
-
-    blocks = [pair_mine]
-    for distance in range(1, REACH + 1):
-        blocks.append(lax.ppermute(pair_mine, ("z_lo", "core"), behind(distance, 0)))
-        blocks.append(lax.ppermute(pair_other, ("z_lo", "core"), behind(distance, 1)))
-    swapped = lax.ppermute(
-        split_other(core_ref, queries[0], out_grad[0], keys[0], values[0]), "core", swap
-    )
+    columns, _ = lax.optimization_barrier((columns, chip_pair))
 
     columns_mine = lax.all_to_all(columns, group, 0, 0, tiled=True)
 
@@ -300,7 +266,7 @@
     bias = jnp.where(allowed, 0.0, MASKED).astype(jnp.float32)
 
     dq_mine, dq_other, own_grad, near_grad, far_grad = attention(
-        core_ref, queries[0], out_grad[0], swapped, blocks, bias
+        q_mine, do_mine, swapped, blocks, bias
     )
     dq_back = lax.ppermute(dq_other, "core", swap)
     query_grad = jnp.where(
@@ -310,9 +276,11 @@
     )[None]
 
     near_back, far_back = (
-        lax.ppermute(part, ("z_lo", "core"), [(b, a) for a, b in behind(distance, 0)])
+        lax.ppermute(part, ("z_lo", "core"), [(b, a) for a, b in behind(distance)])
         for distance, part in ((1, near_grad), (2, far_grad))
     )
+
+    near_back, query_grad = lax.optimization_barrier((near_back, query_grad))
 
     copies = combine(own_grad, near_back, far_back, n_group)
     gathered = lax.all_to_all(copies, group, 0, 0, tiled=True)

time: 106 us -> 104 us (0.981)
  blocking collectives: 23.3 us -> 45.6 us
  waiting for transfers between devices: 24.9 us -> 8.38 us
  starting transfers between devices: 32.7 us -> 23.3 us
  other arithmetic: 1.36 us -> 2.49 us
    all_to_all x0 -> x1, blocking collectives: none -> 23.4 us  [per_device(): lax.all_to_all(term.reshape(n_rest, term.shape[0] // n_rest, term.shape[1...]
    all_to_all x1 -> x0, waiting for transfers between devices: 14 us -> none  [per_device(): lax.all_to_all(term.reshape(n_rest, term.shape[0] // n_rest, term.shape[1...]
    all_to_all x1 -> x0, starting transfers between devices: 7.07 us -> none  [per_device(): lax.all_to_all(term.reshape(n_rest, term.shape[0] // n_rest, term.shape[1...]
    ppermute x7 -> x5, starting transfers between devices: 17.4 us -> 13.9 us  [the longest x2 8 us: per_device(): lax.ppermute(chip_pair, ('z_lo', 'core'), behind(distance))]
    dynamic_slice x0 -> x2, local copies, waits for them, and re-layouts: none -> 3.03 us  [half_of(): return lax.dynamic_slice_in_dim(array[0], which * width, width, 1)]
    unnamed x31 -> x23, local copies, waits for them, and re-layouts: 7.7 us -> 5.02 us
    ppermute x7 -> x5, waiting for transfers between devices: 9.31 us -> 7.57 us  [the longest x2 7.56 us: per_device(): lax.ppermute(part, ('z_lo', 'core'), [(b, a) for a, b in behind(distance)])]
    ppermute x1, waiting for transfers between devices: 1.3 us -> 0.01 us  [per_device(): dq_back = lax.ppermute(dq_other, 'core', swap)]
  transfers between devices with their start and end apart: 11 -> 8, of which waited for: 5 -> 3; matrix products, arithmetic and copies ran while one was open for 2% -> 3% of each run, Pallas kernels for 8% -> 10%
where the time goes in v4:
time: 104 us; the launch traced here: 103 us
  blocking collectives  45.6 us (44%)
  starting transfers between devices  23.3 us (22%)
  Pallas kernels  14.5 us (14%)
  waiting for transfers between devices  8.38 us (8%)
  local copies, waits for them, and re-layouts  8.05 us (8%)
  other arithmetic  2.49 us (2%)
    all_to_all x1, blocking collectives, per_device(): lax.all_to_all(term.reshape(n_rest, term.shape[0] // n_rest, term.shape[1...  23.4 us
    all_to_all x1, blocking collectives, per_device(): gathered = lax.all_to_all(copies, group, 0, 0, tiled=True)  22.1 us
    pallas_call x1, Pallas kernels, attention(): pl.pallas_call(attention_kernel, out_shape=(whole((rows, GROUP * DH)), wh...  8.93 us
    ppermute x2, starting transfers between devices, per_device(): lax.ppermute(chip_pair, ('z_lo', 'core'), behind(distance))  8 us
    ppermute x2, waiting for transfers between devices, per_device(): lax.ppermute(part, ('z_lo', 'core'), [(b, a) for a, b in behind(distance)])  7.56 us
    all_to_all x1, starting transfers between devices, per_device(): columns_mine = lax.all_to_all(columns, group, 0, 0, tiled=True)  6.66 us
    unnamed x23, local copies, waits for them, and re-layouts  5.02 us
    ppermute x1, starting transfers between devices, per_device(): lax.ppermute(jnp.concatenate([half_of(array, 1 - core) for array in sourc...  3.33 us
  transfers between devices with their start and end apart: 8, of which 3 were waited for; matrix products, arithmetic and copies ran while one was open for 3% of the time, Pallas kernels for 10%

profile of v4, /device:TPU:1, one launch (start us, length us, event | category | flops | bytes accessed | tf_op | source)
XLA Modules:
  0.0 103.2 jit_solution(8945482933980628030)
XLA Ops:
  0.6 0.8 dynamic-slice_bitcast_fusion.4
  1.5 0.0 copy-start.8
  1.5 0.0 copy-start
  1.5 2.2 %dynamic-slice_bitcast_fusion = (bf16[128,1024]{1,0:T(8,128)(2,1)S(1)}, bf16[128,1024]{1,0:T(8,128)(2,1)}, bf16[128,1024]{1,0:T(8,128)(2,1)}, bf16[128,1024]{1,0:T(8,128)(2,1)S(1)}) fusion(bf16[1,128,2048]{2,1,0:T(8,128)(2,1)} %param.9, s32[]{:T(128)S(6)} %select_n.42, s32[]{:T(128)S(6)} %select_n.41, bf16[1,128,2048]{2,1,0:T(8,128)(2,1)} %param.6), kind=kLoop, calls=%fused_computation.3 | loop fusion | bytes 2097160 | tf_op jit(solution)/shard_map/dynamic_slice | solution.py:222
  3.7 3.3 %collective-permute-start = (bf16[128,2304]{1,0:T(8,128)(2,1)S(1)}, bf16[128,2304]{1,0:T(8,128)(2,1)S(1)}, u32[]{:S(2)}, u32[]{:S(2)}) collective-permute-start(bf16[128,2304]{1,0:T(8,128)(2,1)S(1)} %pad_maximum_fusion), channel_id=1, source_target_pairs={{0,1},{1,0},{2,3},{3,2},{4,5},{5,4},{6,7},{7,6},{8,9},{9,8},{10,11... | collective-permute-start | bytes 1769480 | tf_op jit(solution)/shard_map/ppermute | solution.py:226
  7.2 0.0 copy-done.8
  7.2 0.1 constant_dynamic-update-slice_fusion.11
  7.3 0.1 constant_dynamic-update-slice_fusion.9
  7.3 0.1 constant_dynamic-update-slice_fusion.7
  7.4 0.1 constant_dynamic-update-slice_fusion.5
  7.5 0.0 copy-done
  7.5 1.4 %shard_map.79 = bf16[8,128,1024]{2,1,0:T(8,128)(2,1)} custom-call(bf16[128,8192]{1,0:T(8,128)(2,1)S(1)} %bitcast.42), custom_call_target="tpu_custom_call" | custom-call | bytes 4194304 | tf_op jit(solution)/shard_map/pallas_call | solution.py:70
  8.9 0.1 constant_dynamic-update-slice_fusion.3
  9.0 0.1 constant_dynamic-update-slice_fusion
  9.1 0.0 collective-permute-done.swapped
  9.1 0.7 shard_map.77.chip_pair
  9.8 3.8 %collective-permute-start.2 = (bf16[256,256]{1,0:T(8,128)(2,1)}, bf16[256,256]{1,0:T(8,128)(2,1)}, u32[]{:S(2)}, u32[]{:S(2)}) collective-permute-start(bf16[256,256]{1,0:T(8,128)(2,1)} %shard_map.77.chip_pair), channel_id=1, source_target_pairs={{0,4},{1,5},{2,6},{3,7},{8,12},{9,13},{10,14},{11,15},{16,20},{17,... | collective-permute-start | bytes 393224 | tf_op jit(solution)/shard_map/ppermute | solution.py:239
  13.6 4.2 %collective-permute-start.1 = (bf16[256,256]{1,0:T(8,128)(2,1)}, bf16[256,256]{1,0:T(8,128)(2,1)}, u32[]{:S(2)}, u32[]{:S(2)}) collective-permute-start(bf16[256,256]{1,0:T(8,128)(2,1)} %shard_map.77.chip_pair), channel_id=1, source_target_pairs={{0,2},{1,3},{2,4},{3,5},{4,6},{5,7},{8,10},{9,11},{10,12},{11,13},... | collective-permute-start | bytes 393224 | tf_op jit(solution)/shard_map/ppermute | solution.py:239
  17.8 0.4 and_select_fusion.bias
  18.1 6.7 %all-to-all-start = ((bf16[8,128,1024]{2,1,0:T(8,128)(2,1)}), bf16[8,128,1024]{2,1,0:T(8,128)(2,1)S(1)}, u32[]{:S(2)}, u32[]{:S(2)}) async-start(bf16[8,128,1024]{2,1,0:T(8,128)(2,1)} %shard_map.79), calls=%async_computation | async-start | bytes 4194304 | tf_op jit(solution)/shard_map/all_to_all | solution.py:247
  24.8 0.0 collective-permute-done.2.far_pair
  24.8 0.0 collective-permute-done.1.near_pair
  24.8 0.0 copy-start.4
  24.8 0.9 copy-done.4
  25.8 0.0 copy-start.5
  25.8 0.9 copy-done.5
  26.7 8.9 %shard_map.78 = (bf16[128,1024]{1,0:T(8,128)(2,1)S(1)}, bf16[128,1024]{1,0:T(8,128)(2,1)}, f32[256,256]{1,0:T(8,128)S(1)}, bf16[256,256]{1,0:T(8,128)(2,1)S(1)}, bf16[256,256]{1,0:T(8,128)(2,1)S(1)}) custom-call(bf16[128,1024]{1,0:T(8,128)(2,1)S(1)} %copy-done.5, bf16[128,1024]{1,0:T(8,128)(2,1)S(1)} %copy-done.4, ...), custom_call_target="tpu_custom_call" | custom-call | flops 32212254720 | bytes 4194304 | tf_op jit(solution)/shard_map/pallas_call | solution.py:128
  35.7 0.0 copy-start.1
  35.7 0.7 copy-done.1
  36.4 0.7 copy-done.3
  37.1 0.7 copy-done.6
  37.7 0.6 copy-done.7
  38.4 0.9 collective-permute-start.4
  39.3 1.3 %collective-permute-start.3 = (bf16[256,256]{1,0:T(8,128)(2,1)}, bf16[256,256]{1,0:T(8,128)(2,1)S(1)}, u32[]{:S(2)}, u32[]{:S(2)}) collective-permute-start(bf16[256,256]{1,0:T(8,128)(2,1)} %copy-done.7), channel_id=1, source_target_pairs={{2,0},{3,1},{4,2},{5,3},{6,4},{7,5},{10,8},{11,9},{12,10},{13,11},... | collective-permute-start | bytes 393224 | tf_op jit(solution)/shard_map/ppermute | solution.py:279
  40.6 1.3 %collective-permute-start.5 = (bf16[256,256]{1,0:T(8,128)(2,1)}, bf16[256,256]{1,0:T(8,128)(2,1)S(1)}, u32[]{:S(2)}, u32[]{:S(2)}) collective-permute-start(bf16[256,256]{1,0:T(8,128)(2,1)} %copy-done.6), channel_id=1, source_target_pairs={{4,0},{5,1},{6,2},{7,3},{12,8},{13,9},{14,10},{15,11},{20,16},{21,... | collective-permute-start | bytes 393224 | tf_op jit(solution)/shard_map/ppermute | solution.py:279
  41.9 0.0 collective-permute-done.4
  41.9 1.9 %maximum_select_fusion = bf16[1,128,2048]{2,1,0:T(8,128)(2,1)} fusion(bf16[1,128,1024]{2,1,0:T(8,128)(2,1)S(1)} %bitcast.45, bf16[1,128,1024]{2,1,0:T(8,128)(2,1)} %bitcast.44, pred[]{:T(512)S(6)} %eq.19), kind=kLoop, calls=%fused_computation.2 | loop fusion | flops 2359296 | bytes 1048577 | tf_op jit(solution)/shard_map/jit(_where)/select_n | solution.py:272
  43.8 2.5 %collective-permute-done.3.near = bf16[256,256]{1,0:T(8,128)(2,1)S(1)} collective-permute-done((bf16[256,256]{1,0:T(8,128)(2,1)}, bf16[256,256]{1,0:T(8,128)(2,1)S(1)}, u32[]{:S(2)}, u32[]{:S(2)}) %collective-permute-start.3) | collective-permute-done | bytes 131104 | tf_op jit(solution)/shard_map/ppermute | solution.py:279
  46.4 5.0 %collective-permute-done.5.far = bf16[256,256]{1,0:T(8,128)(2,1)S(1)} collective-permute-done((bf16[256,256]{1,0:T(8,128)(2,1)}, bf16[256,256]{1,0:T(8,128)(2,1)S(1)}, u32[]{:S(2)}, u32[]{:S(2)}) %collective-permute-start.5) | collective-permute-done | bytes 131104 | tf_op jit(solution)/shard_map/ppermute | solution.py:279
  51.4 0.0 copy-done.2
  51.4 0.2 shard_map.80
  51.6 0.8 all-to-all-done.mine
  52.4 1.9 %collective-permute-start.6 = (bf16[8,128,1024]{2,1,0:T(8,128)(2,1)S(1)}, bf16[8,128,1024]{2,1,0:T(8,128)(2,1)S(1)}, u32[]{:S(2)}, u32[]{:S(2)}) collective-permute-start(bf16[8,128,1024]{2,1,0:T(8,128)(2,1)S(1)} %all-to-all-done.mine), channel_id=1, source_target_pairs={{0,1},{1,0},{2,3},{3,2},{4,5},{5,4},{6,7},{7,6},{8,9},{9,8},{10,11... | collective-permute-start | bytes 6291464 | tf_op jit(solution)/shard_map/ppermute | solution.py:288
  54.2 22.1 %all_to_all.15.grads = bf16[8,256,256]{2,1,0:T(8,128)(2,1)S(1)} all-to-all(bf16[8,256,256]{2,1,0:T(8,128)(2,1)S(1)} %shard_map.80), channel_id=1, replica_groups=mesh['y'=4,'x_hi'=2,'x_lo'=2,'z_hi'=2,'z_lo'=4,'core'=2] {'y','x_hi'}, dimensions={0} | all-to-all | bytes 2097152 | tf_op jit(solution)/shard_map/all_to_all | solution.py:286
  76.4 0.0 collective-permute-done.6.other
  76.4 2.6 %shard_map.81 = bf16[1024,256]{1,0:T(8,128)(2,1)S(1)} custom-call(bf16[8,128,1024]{2,1,0:T(8,128)(2,1)S(1)} %all-to-all-done.mine, bf16[8,128,1024]{2,1,0:T(8,128)(2,1)S(1)} %collective-permute-done.6.other, bf16[8,256,256]{2,1,0:T(8,128)(2,1)S(1)} %all_to_all.15.grads), custom_call_target="tpu_custom_call" | custom-call | flops 1073741824 | bytes 6291456 | tf_op jit(solution)/shard_map/pallas_call | solution.py:177
  79.0 23.4 %all_to_all.16.parts = bf16[32,32,256]{2,1,0:T(8,128)(2,1)S(1)} all-to-all(bf16[32,32,256]{2,1,0:T(8,128)(2,1)S(1)} %bitcast.43), channel_id=1, replica_groups=mesh['y'=4,'x_hi'=2,'x_lo'=2,'z_hi'=2,'z_lo'=4,'core'=2] {'x_lo','z_hi',..., dimensions={0} | all-to-all | bytes 1048576 | tf_op jit(solution)/shard_map/all_to_all | solution.py:292
  102.5 0.7 shard_map.82
  (16 shorter events, 0.1 us)
Async XLA Ops:
  1.5 5.7 %copy-start.8 = (s32[1,1024]{1,0:T(1,128)S(1)}, s32[1,1024]{1,0:T(1,128)}, u32[]{:S(2)}) copy-start(s32[1,1024]{1,0:T(1,128)} %param.11) | copy-start | bytes 12292
  1.5 6.0 %copy-start = (bf16[1,128,8192]{2,1,0:T(8,128)(2,1)S(1)}, bf16[1,128,8192]{2,1,0:T(8,128)(2,1)}, u32[]{:S(2)}) copy-start(bf16[1,128,8192]{2,1,0:T(8,128)(2,1)} %param.10) | copy-start | bytes 6291460
  3.7 5.4 %collective-permute-start = (bf16[128,2304]{1,0:T(8,128)(2,1)S(1)}, bf16[128,2304]{1,0:T(8,128)(2,1)S(1)}, u32[]{:S(2)}, u32[]{:S(2)}) collective-permute-start(bf16[128,2304]{1,0:T(8,128)(2,1)S(1)} %pad_maximum_fusion), channel_id=1, source_target_pairs={{0,1},{1,0},{2,3},{3,2},{4,5},{5,4},{6,7},{7,6},{8,9},{9,8},{10,11... | collective-permute-start | bytes 1769480 | tf_op jit(solution)/shard_map/ppermute | solution.py:226
  9.8 15.0 %collective-permute-start.2 = (bf16[256,256]{1,0:T(8,128)(2,1)}, bf16[256,256]{1,0:T(8,128)(2,1)}, u32[]{:S(2)}, u32[]{:S(2)}) collective-permute-start(bf16[256,256]{1,0:T(8,128)(2,1)} %shard_map.77.chip_pair), channel_id=1, source_target_pairs={{0,4},{1,5},{2,6},{3,7},{8,12},{9,13},{10,14},{11,15},{16,20},{17,... | collective-permute-start | bytes 393224 | tf_op jit(solution)/shard_map/ppermute | solution.py:239
  13.6 11.2 %collective-permute-start.1 = (bf16[256,256]{1,0:T(8,128)(2,1)}, bf16[256,256]{1,0:T(8,128)(2,1)}, u32[]{:S(2)}, u32[]{:S(2)}) collective-permute-start(bf16[256,256]{1,0:T(8,128)(2,1)} %shard_map.77.chip_pair), channel_id=1, source_target_pairs={{0,2},{1,3},{2,4},{3,5},{4,6},{5,7},{8,10},{9,11},{10,12},{11,13},... | collective-permute-start | bytes 393224 | tf_op jit(solution)/shard_map/ppermute | solution.py:239
  18.1 34.2 %all-to-all-start = ((bf16[8,128,1024]{2,1,0:T(8,128)(2,1)}), bf16[8,128,1024]{2,1,0:T(8,128)(2,1)S(1)}, u32[]{:S(2)}, u32[]{:S(2)}) async-start(bf16[8,128,1024]{2,1,0:T(8,128)(2,1)} %shard_map.79), calls=%async_computation | async-start | bytes 4194304 | tf_op jit(solution)/shard_map/all_to_all | solution.py:247
  24.8 1.0 copy-start.4
  25.8 0.9 copy-start.5
  35.7 0.7 copy-start.1
  36.4 0.7 copy-start.3
  37.1 0.7 copy-start.6
  37.7 0.6 copy-start.7
  38.4 13.0 %copy-start.2 = (f32[256,256]{1,0:T(8,128)S(1)}, f32[256,256]{1,0:T(8,128)}, u32[]{:S(2)}) copy-start(f32[256,256]{1,0:T(8,128)} %copy-done.1) | copy-start | bytes 786436
  38.4 3.5 %collective-permute-start.4 = (bf16[128,1024]{1,0:T(8,128)(2,1)}, bf16[128,1024]{1,0:T(8,128)(2,1)S(1)}, u32[]{:S(2)}, u32[]{:S(2)}) collective-permute-start(bf16[128,1024]{1,0:T(8,128)(2,1)} %get-tuple-element.13), channel_id=1, source_target_pairs={{0,1},{1,0},{2,3},{3,2},{4,5},{5,4},{6,7},{7,6},{8,9},{9,8},{10,11... | collective-permute-start | bytes 786440 | tf_op jit(solution)/shard_map/ppermute | solution.py:271
  39.3 7.1 %collective-permute-start.3 = (bf16[256,256]{1,0:T(8,128)(2,1)}, bf16[256,256]{1,0:T(8,128)(2,1)S(1)}, u32[]{:S(2)}, u32[]{:S(2)}) collective-permute-start(bf16[256,256]{1,0:T(8,128)(2,1)} %copy-done.7), channel_id=1, source_target_pairs={{2,0},{3,1},{4,2},{5,3},{6,4},{7,5},{10,8},{11,9},{12,10},{13,11},... | collective-permute-start | bytes 393224 | tf_op jit(solution)/shard_map/ppermute | solution.py:279
  40.6 10.8 %collective-permute-start.5 = (bf16[256,256]{1,0:T(8,128)(2,1)}, bf16[256,256]{1,0:T(8,128)(2,1)S(1)}, u32[]{:S(2)}, u32[]{:S(2)}) collective-permute-start(bf16[256,256]{1,0:T(8,128)(2,1)} %copy-done.6), channel_id=1, source_target_pairs={{4,0},{5,1},{6,2},{7,3},{12,8},{13,9},{14,10},{15,11},{20,16},{21,... | collective-permute-start | bytes 393224 | tf_op jit(solution)/shard_map/ppermute | solution.py:279
  52.4 24.0 %collective-permute-start.6 = (bf16[8,128,1024]{2,1,0:T(8,128)(2,1)S(1)}, bf16[8,128,1024]{2,1,0:T(8,128)(2,1)S(1)}, u32[]{:S(2)}, u32[]{:S(2)}) collective-permute-start(bf16[8,128,1024]{2,1,0:T(8,128)(2,1)S(1)} %all-to-all-done.mine), channel_id=1, source_target_pairs={{0,1},{1,0},{2,3},{3,2},{4,5},{5,4},{6,7},{7,6},{8,9},{9,8},{10,11... | collective-permute-start | bytes 6291464 | tf_op jit(solution)/shard_map/ppermute | solution.py:288

commit v5 on v4

--- a/solution.py
+++ b/solution.py
@@ -32,14 +32,7 @@
 
 
 HBM = pl.BlockSpec(memory_space=pltpu.HBM)
-
-
-def run_copies(copies, sems):
-    started = [pltpu.make_async_copy(src, dst, sems.at[i]) for i, (src, dst) in enumerate(copies)]
-    for copy in started:
-        copy.start()
-    for copy in started:
-        copy.wait()
+SCALAR = pl.BlockSpec(memory_space=pltpu.SMEM)
 
 
 def pair_kernel(keys, values, swapped, out):
@@ -58,24 +51,30 @@
     )(keys, values, swapped)
 
 
-def chunk_kernel(columns, out, sems):
-    width = out.shape[2]
-    run_copies(
-        [(columns.at[:, i * width : (i + 1) * width], out.at[i]) for i in range(out.shape[0])], sems
-    )
-
-
-def split_columns(columns, chunks):
+def chunk_kernel(place_ref, columns, *refs):
+    outs, sems = refs[:-1], refs[-1]
+    width = outs[0].shape[1]
+    copies = []
+    for k, out in enumerate(outs):
+        start = pl.multiple_of((place_ref[0] ^ k) * width, width)
+        copies.append(pltpu.make_async_copy(columns.at[:, pl.ds(start, width)], out, sems.at[k]))
+    for copy in copies:
+        copy.start()
+    for copy in copies:
+        copy.wait()
+
+
+def split_columns(place, columns, chunks):
     rows, width = columns.shape
     return pl.pallas_call(
         chunk_kernel,
-        out_shape=whole((chunks, rows, width // chunks)),
-        in_specs=[HBM],
-        out_specs=HBM,
+        out_shape=(whole((rows, width // chunks)),) * chunks,
+        in_specs=[SCALAR, HBM],
+        out_specs=(HBM,) * chunks,
         scratch_shapes=[pltpu.SemaphoreType.DMA((chunks,))],
         compiler_params=SMALL,
-        cost_estimate=pl.CostEstimate(flops=0, bytes_accessed=4 * 1024 * 1024, transcendentals=0),
-    )(columns)
+        cost_estimate=pl.CostEstimate(flops=0, bytes_accessed=4 * MIB, transcendentals=0),
+    )(place, columns)
 
 
 def attention_kernel(
@@ -140,7 +139,7 @@
         ],
         compiler_params=pltpu.CompilerParams(vmem_limit_bytes=16 * MIB),
         cost_estimate=pl.CostEstimate(
-            flops=160 * keys * chip * DH * GROUP,
+            flops=40 * keys * chip * DH * GROUP,
             bytes_accessed=4 * 1024 * 1024,
             transcendentals=keys * chip * GROUP,
         ),
@@ -163,32 +162,50 @@
     )(own, near, far)
 
 
-def project_kernel(mine, other, grads, out):
-    places = range(mine.shape[0])
-    left = jnp.concatenate([grads[i] for i in places], axis=1)
-    right = jnp.concatenate([part[i] for i in places for part in (mine, other)], axis=0)
+def assemble_kernel(core_ref, mine, other, out):
+    width = mine.shape[1]
+    core = core_ref[0]
+    out[:, pl.ds(pl.multiple_of(core * width, width), width)] = mine[...]
+    out[:, pl.ds(pl.multiple_of((1 - core) * width, width), width)] = other[...]
+
+
+def assemble(core, mine, other):
+    return pl.pallas_call(
+        assemble_kernel,
+        out_shape=whole((mine.shape[0], 2 * mine.shape[1])),
+        in_specs=[SCALAR, pl.BlockSpec(), pl.BlockSpec()],
+        compiler_params=SMALL,
+        cost_estimate=pl.CostEstimate(flops=0, bytes_accessed=MIB, transcendentals=0),
+    )(core, mine, other)
+
+
+def project_kernel(place_ref, *refs):
+    pieces, grads, out = refs[:-2], refs[-2], refs[-1]
+    places = range(len(pieces) // 2)
+    left = jnp.concatenate([grads[place_ref[0] ^ k] for k in places], axis=1)
+    right = jnp.concatenate([ref[...] for ref in pieces], axis=0)
     out[...] = dot_nn(left, right).T.astype(jnp.bfloat16)
 
 
-def project(mine, other, grads, blocks):
-    places, rows, columns = mine.shape
+def project(place, pieces, grads, blocks):
+    rows, columns = pieces[0].shape
     width = grads.shape[1]
     step = columns // blocks
     return pl.pallas_call(
         project_kernel,
         out_shape=whole((columns, width)),
         grid=(blocks,),
-        in_specs=[
-            pl.BlockSpec((places, rows, step), lambda i: (0, 0, i)),
-            pl.BlockSpec((places, rows, step), lambda i: (0, 0, i)),
-            pl.BlockSpec(grads.shape, lambda i: (0, 0, 0)),
-        ],
+        in_specs=[SCALAR]
+        + [pl.BlockSpec((rows, step), lambda i: (0, i))] * len(pieces)
+        + [pl.BlockSpec(grads.shape, lambda i: (0, 0, 0))],
         out_specs=pl.BlockSpec((step, width), lambda i: (i, 0)),
-        compiler_params=pltpu.CompilerParams(vmem_limit_bytes=8 * MIB),
+        compiler_params=pltpu.CompilerParams(vmem_limit_bytes=16 * MIB),
         cost_estimate=pl.CostEstimate(
-            flops=4 * places * rows * columns * width, bytes_accessed=6 * 1024 * 1024, transcendentals=0
+            flops=2 * len(pieces) * rows * columns * width,
+            bytes_accessed=6 * MIB,
+            transcendentals=0,
         ),
-    )(mine, other, grads)
+    )(place, *pieces, grads)
 
 
 def final_kernel(parts, out):
@@ -216,6 +233,8 @@
     core = lax.axis_index("core")
     n_chips = lax.axis_size("z_lo")
     swap = [(0, 1), (1, 0)]
+    core_ref = core.astype(jnp.int32).reshape(1)
+    place_ref = lax.axis_index("y").astype(jnp.int32).reshape(1)
 
     def half_of(array, which):
         width = array.shape[-1] // 2
@@ -239,12 +258,12 @@
         lax.ppermute(chip_pair, ("z_lo", "core"), behind(distance)) for distance in (2, 1)
     ][::-1]
 
-    group = ("y", "x_hi")
-    n_group = lax.axis_size("y") * lax.axis_size("x_hi")
-    columns = split_columns(layer_input[0], n_group)
-    columns, _ = lax.optimization_barrier((columns, chip_pair))
-
-    columns_mine = lax.all_to_all(columns, group, 0, 0, tiled=True)
+    n_y = lax.axis_size("y")
+    chunks = split_columns(place_ref, layer_input[0], n_y)
+    chunks, _ = lax.optimization_barrier((chunks, chip_pair))
+    pieces = [chunks[0]] + [
+        lax.ppermute(chunks[k], "y", [(i, i ^ k) for i in range(n_y)]) for k in range(1, n_y)
+    ]
 
     seg_row = segment_ids[0]
     lane = jnp.arange(rows, dtype=jnp.int32)
@@ -269,11 +288,7 @@
         q_mine, do_mine, swapped, blocks, bias
     )
     dq_back = lax.ppermute(dq_other, "core", swap)
-    query_grad = jnp.where(
-        core == 0,
-        jnp.concatenate([dq_mine, dq_back], axis=1),
-        jnp.concatenate([dq_back, dq_mine], axis=1),
-    )[None]
+    query_grad = assemble(core_ref, dq_mine, dq_back)[None]
 
     near_back, far_back = (
         lax.ppermute(part, ("z_lo", "core"), [(b, a) for a, b in behind(distance)])
@@ -282,12 +297,15 @@
 
     near_back, query_grad = lax.optimization_barrier((near_back, query_grad))
 
-    copies = combine(own_grad, near_back, far_back, n_group)
-    gathered = lax.all_to_all(copies, group, 0, 0, tiled=True)
-    columns_mine, _ = lax.optimization_barrier((columns_mine, copies))
-    columns_other = lax.ppermute(columns_mine, "core", swap)
-    term = project(columns_mine, columns_other, gathered, 4)
-    rest = ("x_lo", "z_hi", "z_lo", "core")
+    copies = combine(own_grad, near_back, far_back, n_y)
+    gathered = lax.all_to_all(copies, "y", 0, 0, tiled=True)
+    pieces, _ = lax.optimization_barrier((pieces, copies))
+    both = [part for piece in pieces for part in (piece, lax.ppermute(piece, "core", swap))]
+    term = project(place_ref, both, gathered, 4)
+    n_x = lax.axis_size("x")
+    over_x = lax.all_to_all(term.reshape(n_x, -1, term.shape[1]), "x", 0, 0, tiled=True)
+    term = jnp.sum(over_x.astype(jnp.float32), axis=0).astype(jnp.bfloat16)
+    rest = ("z_hi", "z_lo", "core")
     n_rest = lax.axis_size(rest)
     spread = lax.all_to_all(
         term.reshape(n_rest, term.shape[0] // n_rest, term.shape[1]), rest, 0, 0, tiled=True
@@ -296,9 +314,9 @@
 
 
 def solution(mesh):
-    axes = ("y", "x_hi", "x_lo", "z_hi", "z_lo", "core")
-    fine = Mesh(mesh.devices.reshape(4, 2, 2, 2, 4, 2), axes)
-    dp, ctx = axes[:4], axes[4:]
+    axes = ("y", "x", "z_hi", "z_lo", "core")
+    fine = Mesh(mesh.devices.reshape(4, 4, 2, 4, 2), axes)
+    dp, ctx = axes[:3], axes[3:]
     return jax.shard_map(
         per_device,
         mesh=fine,

time: 104 us -> 99.6 us (0.958)
  local copies, waits for them, and re-layouts: 8.05 us -> 2.65 us
  waiting for transfers between devices: 8.38 us -> 12.8 us
  Pallas kernels: 14.5 us -> 11.5 us
  blocking collectives: 45.6 us -> 48.6 us
  starting transfers between devices: 23.3 us -> 21.3 us
    all_to_all x1 -> x0, starting transfers between devices: 6.66 us -> none  [per_device(): columns_mine = lax.all_to_all(columns, group, 0, 0, tiled=True)]
    all_to_all x1 -> x2, blocking collectives: 22.1 us -> 28.8 us  [the longest x1 17.3 us: per_device(): lax.all_to_all(term.reshape(n_x, -1, term.shape[1]), 'x', 0, 0, tiled=True)]
    ppermute x1 -> x7, starting transfers between devices: 1.86 us -> 6.94 us  [the longest x3 4.01 us: per_device(): lax.ppermute(chunks[k], 'y', [(i, i ^ k) for i in range(n_y)])]
    unnamed x23 -> x9, local copies, waits for them, and re-layouts: 5.02 us -> 0.41 us
    all_to_all x1, blocking collectives: 23.4 us -> 19.8 us  [per_device(): lax.all_to_all(term.reshape(n_rest, term.shape[0] // n_rest, term.shape[1...]
    ppermute x2, waiting for transfers between devices: 7.56 us -> 10.7 us  [per_device(): lax.ppermute(part, ('z_lo', 'core'), [(b, a) for a, b in behind(distance)])]
    select_n x1 -> x0, other arithmetic: 1.95 us -> none  [per_device(): jnp.where(core == 0, jnp.concatenate([dq_mine, dq_back], axis=1), jnp.con...]
    pallas_call x1, Pallas kernels: 8.93 us -> 7.25 us  [attention(): pl.pallas_call(attention_kernel, out_shape=(whole((rows, GROUP * DH)), wh...]
  transfers between devices with their start and end apart: 8 -> 13, of which waited for: 3 -> 4; matrix products, arithmetic and copies ran while one was open for 3% -> 1% of each run, Pallas kernels for 10% -> 8%
where the time goes in v5:
time: 99.6 us; the launch traced here: 99.3 us
  blocking collectives  48.6 us (49%)
  starting transfers between devices  21.3 us (21%)
  waiting for transfers between devices  12.8 us (13%)
  Pallas kernels  11.5 us (12%)
  local copies, waits for them, and re-layouts  2.65 us (3%)
  other arithmetic  1.63 us (2%)
    all_to_all x1, blocking collectives, per_device(): lax.all_to_all(term.reshape(n_rest, term.shape[0] // n_rest, term.shape[1...  19.8 us
    all_to_all x1, blocking collectives, per_device(): lax.all_to_all(term.reshape(n_x, -1, term.shape[1]), 'x', 0, 0, tiled=True)  17.3 us
    all_to_all x1, blocking collectives, per_device(): gathered = lax.all_to_all(copies, 'y', 0, 0, tiled=True)  11.5 us
    ppermute x2, waiting for transfers between devices, per_device(): lax.ppermute(part, ('z_lo', 'core'), [(b, a) for a, b in behind(distance)])  10.7 us
    pallas_call x1, Pallas kernels, attention(): pl.pallas_call(attention_kernel, out_shape=(whole((rows, GROUP * DH)), wh...  7.25 us
    ppermute x2, starting transfers between devices, per_device(): lax.ppermute(chip_pair, ('z_lo', 'core'), behind(distance))  6.72 us
    ppermute x3, starting transfers between devices, per_device(): lax.ppermute(chunks[k], 'y', [(i, i ^ k) for i in range(n_y)])  4.01 us
    ppermute x1, starting transfers between devices, per_device(): lax.ppermute(jnp.concatenate([half_of(array, 1 - core) for array in sourc...  3.24 us
  transfers between devices with their start and end apart: 13, of which 4 were waited for; matrix products, arithmetic and copies ran while one was open for 1% of the time, Pallas kernels for 8%

profile of v5, /device:TPU:1, one launch (start us, length us, event | category | flops | bytes accessed | tf_op | source)
XLA Modules:
  0.0 99.3 jit_solution(7333307253807291795)
XLA Ops:
  0.6 0.8 dynamic-slice_bitcast_fusion.4
  1.5 0.0 copy-start.1
  1.5 0.0 copy-start
  1.5 1.4 %dynamic-slice_bitcast_fusion = (bf16[128,1024]{1,0:T(8,128)(2,1)S(1)}, bf16[128,1024]{1,0:T(8,128)(2,1)S(1)}, bf16[128,1024]{1,0:T(8,128)(2,1)S(1)}, bf16[128,1024]{1,0:T(8,128)(2,1)S(1)}) fusion(bf16[1,128,2048]{2,1,0:T(8,128)(2,1)} %param.9, s32[]{:T(128)S(6)} %select_n.12, s32[]{:T(128)S(6)} %select_n.11, bf16[1,128,2048]{2,1,0:T(8,128)(2,1)} %param.6), kind=kLoop, calls=%fused_computation.2 | loop fusion | bytes 2097160 | tf_op jit(solution)/shard_map/dynamic_slice | solution.py:241
  2.9 0.9 pad_maximum_fusion
  3.8 3.2 %collective-permute-start = (bf16[128,2304]{1,0:T(8,128)(2,1)}, bf16[128,2304]{1,0:T(8,128)(2,1)S(1)}, u32[]{:S(2)}, u32[]{:S(2)}) collective-permute-start(bf16[128,2304]{1,0:T(8,128)(2,1)} %pad_maximum_fusion), channel_id=1, source_target_pairs={{0,1},{1,0},{2,3},{3,2},{4,5},{5,4},{6,7},{7,6},{8,9},{9,8},{10,11... | collective-permute-start | bytes 1769480 | tf_op jit(solution)/shard_map/ppermute | solution.py:245
  7.1 0.1 constant_dynamic-update-slice_fusion.11
  7.2 0.1 constant_dynamic-update-slice_fusion.9
  7.3 0.1 constant_dynamic-update-slice_fusion.7
  7.4 0.1 constant_dynamic-update-slice_fusion.5
  7.4 0.2 shard_map.80
  7.6 0.1 constant_dynamic-update-slice_fusion.3
  7.7 0.1 constant_dynamic-update-slice_fusion
  7.8 1.0 %collective-permute-done.swapped = bf16[128,2304]{1,0:T(8,128)(2,1)S(1)} collective-permute-done((bf16[128,2304]{1,0:T(8,128)(2,1)}, bf16[128,2304]{1,0:T(8,128)(2,1)S(1)}, u32[]{:S(2)}, u32[]{:S(2)}) %collective-permute-start) | collective-permute-done | bytes 589856 | tf_op jit(solution)/shard_map/ppermute | solution.py:245
  8.9 3.2 %collective-permute-start.2 = (bf16[256,256]{1,0:T(8,128)(2,1)S(1)}, bf16[256,256]{1,0:T(8,128)(2,1)S(1)}, u32[]{:S(2)}, u32[]{:S(2)}) collective-permute-start(bf16[256,256]{1,0:T(8,128)(2,1)S(1)} %shard_map.77.chip_pair), channel_id=1, source_target_pairs={{0,4},{1,5},{2,6},{3,7},{8,12},{9,13},{10,14},{11,15},{16,20},{17,... | collective-permute-start | bytes 393224 | tf_op jit(solution)/shard_map/ppermute | solution.py:258
  12.1 3.5 %collective-permute-start.1 = (bf16[256,256]{1,0:T(8,128)(2,1)S(1)}, bf16[256,256]{1,0:T(8,128)(2,1)S(1)}, u32[]{:S(2)}, u32[]{:S(2)}) collective-permute-start(bf16[256,256]{1,0:T(8,128)(2,1)S(1)} %shard_map.77.chip_pair), channel_id=1, source_target_pairs={{0,2},{1,3},{2,4},{3,5},{4,6},{5,7},{8,10},{9,11},{10,12},{11,13},... | collective-permute-start | bytes 393224 | tf_op jit(solution)/shard_map/ppermute | solution.py:258
  15.6 0.4 and_select_fusion.bias
  16.0 1.4 %collective-permute-start.5 = (bf16[128,2048]{1,0:T(8,128)(2,1)S(1)}, bf16[128,2048]{1,0:T(8,128)(2,1)S(1)}, u32[]{:S(2)}, u32[]{:S(2)}) collective-permute-start(bf16[128,2048]{1,0:T(8,128)(2,1)S(1)} %get-tuple-element.30), channel_id=1, source_target_pairs={{0,64},{64,0},{128,192},{192,128},{1,65},{65,1},{129,193},{193,129... | collective-permute-start | bytes 1572872 | tf_op jit(solution)/shard_map/ppermute | solution.py:265
  17.4 2.6 %collective-permute-start.6 = (bf16[128,2048]{1,0:T(8,128)(2,1)S(1)}, bf16[128,2048]{1,0:T(8,128)(2,1)S(1)}, u32[]{:S(2)}, u32[]{:S(2)}) collective-permute-start(bf16[128,2048]{1,0:T(8,128)(2,1)S(1)} %get-tuple-element.31), channel_id=1, source_target_pairs={{0,128},{64,192},{128,0},{192,64},{1,129},{65,193},{129,1},{193,65... | collective-permute-start | bytes 1572872 | tf_op jit(solution)/shard_map/ppermute | solution.py:265
  20.0 0.0 collective-permute-start.7
  20.0 0.0 collective-permute-done.2.far_pair
  20.0 0.0 collective-permute-done.1.near_pair
  20.0 7.3 %shard_map.78 = (bf16[128,1024]{1,0:T(8,128)(2,1)S(1)}, bf16[128,1024]{1,0:T(8,128)(2,1)S(1)}, f32[256,256]{1,0:T(8,128)S(1)}, bf16[256,256]{1,0:T(8,128)(2,1)S(1)}, bf16[256,256]{1,0:T(8,128)(2,1)S(1)}) custom-call(bf16[128,1024]{1,0:T(8,128)(2,1)S(1)} %get-tuple-element.54.queries, bf16[128,1024]{1,0:T(8,128)(2,1)S(1)} %get-tuple-element.47.out_grad, ...), custom_call_target="tpu_custom_call" | custom-call | flops 8053063680 | bytes 4194304 | tf_op jit(solution)/shard_map/pallas_call | solution.py:127
  27.3 1.8 %collective-permute-start.4 = (bf16[128,1024]{1,0:T(8,128)(2,1)S(1)}, bf16[128,1024]{1,0:T(8,128)(2,1)S(1)}, u32[]{:S(2)}, u32[]{:S(2)}) collective-permute-start(bf16[128,1024]{1,0:T(8,128)(2,1)S(1)} %get-tuple-element.23), channel_id=1, source_target_pairs={{0,1},{1,0},{2,3},{3,2},{4,5},{5,4},{6,7},{7,6},{8,9},{9,8},{10,11... | collective-permute-start | bytes 786440 | tf_op jit(solution)/shard_map/ppermute | solution.py:290
  29.1 1.3 %collective-permute-start.3 = (bf16[256,256]{1,0:T(8,128)(2,1)S(1)}, bf16[256,256]{1,0:T(8,128)(2,1)S(1)}, u32[]{:S(2)}, u32[]{:S(2)}) collective-permute-start(bf16[256,256]{1,0:T(8,128)(2,1)S(1)} %get-tuple-element.21), channel_id=1, source_target_pairs={{2,0},{3,1},{4,2},{5,3},{6,4},{7,5},{10,8},{11,9},{12,10},{13,11},... | collective-permute-start | bytes 393224 | tf_op jit(solution)/shard_map/ppermute | solution.py:294
  30.4 0.0 collective-permute-done.4.other
  30.4 1.3 %collective-permute-start.8 = (bf16[256,256]{1,0:T(8,128)(2,1)S(1)}, bf16[256,256]{1,0:T(8,128)(2,1)S(1)}, u32[]{:S(2)}, u32[]{:S(2)}) collective-permute-start(bf16[256,256]{1,0:T(8,128)(2,1)S(1)} %get-tuple-element.35), channel_id=1, source_target_pairs={{4,0},{5,1},{6,2},{7,3},{12,8},{13,9},{14,10},{15,11},{20,16},{21,... | collective-permute-start | bytes 393224 | tf_op jit(solution)/shard_map/ppermute | solution.py:294
  31.7 0.8 shard_map.79
  32.5 3.6 %collective-permute-done.3.near = bf16[256,256]{1,0:T(8,128)(2,1)S(1)} collective-permute-done((bf16[256,256]{1,0:T(8,128)(2,1)S(1)}, bf16[256,256]{1,0:T(8,128)(2,1)S(1)}, u32[]{:S(2)}, u32[]{:S(2)}) %collective-permute-start.3) | collective-permute-done | bytes 131104 | tf_op jit(solution)/shard_map/ppermute | solution.py:294
  36.1 7.1 %collective-permute-done.8.far = bf16[256,256]{1,0:T(8,128)(2,1)S(1)} collective-permute-done((bf16[256,256]{1,0:T(8,128)(2,1)S(1)}, bf16[256,256]{1,0:T(8,128)(2,1)S(1)}, u32[]{:S(2)}, u32[]{:S(2)}) %collective-permute-start.8) | collective-permute-done | bytes 131104 | tf_op jit(solution)/shard_map/ppermute | solution.py:294
  43.2 0.1 shard_map.81
  43.3 0.0 collective-permute-done.5.refs_2_
  43.3 0.0 collective-permute-done.6.refs_4_
  43.3 1.0 %collective-permute-done.7.refs_6_ = bf16[128,2048]{1,0:T(8,128)(2,1)S(1)} collective-permute-done((bf16[128,2048]{1,0:T(8,128)(2,1)S(1)}, bf16[128,2048]{1,0:T(8,128)(2,1)S(1)}, u32[]{:S(2)}, u32[]{:S(2)}) %collective-permute-start.7) | collective-permute-done | bytes 524320 | tf_op jit(solution)/shard_map/ppermute | solution.py:265
  44.4 2.4 %collective-permute-start.9 = (bf16[128,2048]{1,0:T(8,128)(2,1)S(1)}, bf16[128,2048]{1,0:T(8,128)(2,1)S(1)}, u32[]{:S(2)}, u32[]{:S(2)}) collective-permute-start(bf16[128,2048]{1,0:T(8,128)(2,1)S(1)} %get-tuple-element.36.refs_0_), channel_id=1, source_target_pairs={{0,1},{1,0},{2,3},{3,2},{4,5},{5,4},{6,7},{7,6},{8,9},{9,8},{10,11... | collective-permute-start | bytes 1572872 | tf_op jit(solution)/shard_map/ppermute | solution.py:303
  46.8 0.0 collective-permute-start.10
  46.8 0.5 collective-permute-start.11
  47.3 0.0 collective-permute-start.12
  47.3 11.5 %all_to_all.15.refs_8_ = bf16[4,256,256]{2,1,0:T(8,128)(2,1)S(1)} all-to-all(bf16[4,256,256]{2,1,0:T(8,128)(2,1)S(1)} %shard_map.81), channel_id=1, replica_groups=mesh['y'=4,'x'=4,'z_hi'=2,'z_lo'=4,'core'=2] {'y'}, dimensions={0} | all-to-all | bytes 1048576 | tf_op jit(solution)/shard_map/all_to_all | solution.py:301
  58.8 0.0 collective-permute-done.9.refs_1_
  58.8 0.0 collective-permute-done.10.refs_3_
  58.8 0.0 collective-permute-done.11.refs_5_
  58.8 0.0 collective-permute-done.12.refs_7_
  58.8 2.4 %shard_map.82 = bf16[2048,256]{1,0:T(8,128)(2,1)S(1)} custom-call(s32[1]{0:T(128)} %bitcast.16.place_ref, bf16[128,2048]{1,0:T(8,128)(2,1)S(1)} %get-tuple-element.36.refs_0_, bf16[128,2048]{1,0:T(8,128)(2,1)S(1)} %collective-permute-done.9.refs_1_, bf16[128,2048]{1,0:T(8,128)(2,1)S(1)} %collective-permute-done.5.refs_2_, ...), custom_call_target="tpu_custom_call" | custom-call | flops 1073741824 | bytes 6291456 | tf_op jit(solution)/shard_map/pallas_call | solution.py:194
  61.2 17.3 %all_to_all.16 = bf16[4,512,256]{2,1,0:T(8,128)(2,1)S(1)} all-to-all(bf16[4,512,256]{2,1,0:T(8,128)(2,1)S(1)} %bitcast.44), channel_id=1, replica_groups=mesh['y'=4,'x'=4,'z_hi'=2,'z_lo'=4,'core'=2] {'x'}, dimensions={0} | all-to-all | bytes 2097152 | tf_op jit(solution)/shard_map/all_to_all | solution.py:306
  78.5 0.3 reduce_sum.12
  78.8 19.8 %all_to_all.17.parts = bf16[16,32,256]{2,1,0:T(8,128)(2,1)S(1)} all-to-all(bf16[16,32,256]{2,1,0:T(8,128)(2,1)S(1)} %bitcast.46), channel_id=1, replica_groups=mesh['y'=4,'x'=4,'z_hi'=2,'z_lo'=4,'core'=2] {'z_hi','z_lo','core'}, dimensions={0} | all-to-all | bytes 524288 | tf_op jit(solution)/shard_map/all_to_all | solution.py:310
  98.6 0.7 shard_map.83
  (14 shorter events, 0.1 us)
Async XLA Ops:
  1.5 5.7 %copy-start.1 = (s32[1,1024]{1,0:T(1,128)S(1)}, s32[1,1024]{1,0:T(1,128)}, u32[]{:S(2)}) copy-start(s32[1,1024]{1,0:T(1,128)} %param.11) | copy-start | bytes 12292
  1.5 6.0 %copy-start = (bf16[1,128,8192]{2,1,0:T(8,128)(2,1)S(1)}, bf16[1,128,8192]{2,1,0:T(8,128)(2,1)}, u32[]{:S(2)}) copy-start(bf16[1,128,8192]{2,1,0:T(8,128)(2,1)} %param.10) | copy-start | bytes 6291460
  3.8 5.1 %collective-permute-start = (bf16[128,2304]{1,0:T(8,128)(2,1)}, bf16[128,2304]{1,0:T(8,128)(2,1)S(1)}, u32[]{:S(2)}, u32[]{:S(2)}) collective-permute-start(bf16[128,2304]{1,0:T(8,128)(2,1)} %pad_maximum_fusion), channel_id=1, source_target_pairs={{0,1},{1,0},{2,3},{3,2},{4,5},{5,4},{6,7},{7,6},{8,9},{9,8},{10,11... | collective-permute-start | bytes 1769480 | tf_op jit(solution)/shard_map/ppermute | solution.py:245
  8.9 11.1 %collective-permute-start.2 = (bf16[256,256]{1,0:T(8,128)(2,1)S(1)}, bf16[256,256]{1,0:T(8,128)(2,1)S(1)}, u32[]{:S(2)}, u32[]{:S(2)}) collective-permute-start(bf16[256,256]{1,0:T(8,128)(2,1)S(1)} %shard_map.77.chip_pair), channel_id=1, source_target_pairs={{0,4},{1,5},{2,6},{3,7},{8,12},{9,13},{10,14},{11,15},{16,20},{17,... | collective-permute-start | bytes 393224 | tf_op jit(solution)/shard_map/ppermute | solution.py:258
  12.1 7.9 %collective-permute-start.1 = (bf16[256,256]{1,0:T(8,128)(2,1)S(1)}, bf16[256,256]{1,0:T(8,128)(2,1)S(1)}, u32[]{:S(2)}, u32[]{:S(2)}) collective-permute-start(bf16[256,256]{1,0:T(8,128)(2,1)S(1)} %shard_map.77.chip_pair), channel_id=1, source_target_pairs={{0,2},{1,3},{2,4},{3,5},{4,6},{5,7},{8,10},{9,11},{10,12},{11,13},... | collective-permute-start | bytes 393224 | tf_op jit(solution)/shard_map/ppermute | solution.py:258
  16.0 27.3 %collective-permute-start.5 = (bf16[128,2048]{1,0:T(8,128)(2,1)S(1)}, bf16[128,2048]{1,0:T(8,128)(2,1)S(1)}, u32[]{:S(2)}, u32[]{:S(2)}) collective-permute-start(bf16[128,2048]{1,0:T(8,128)(2,1)S(1)} %get-tuple-element.30), channel_id=1, source_target_pairs={{0,64},{64,0},{128,192},{192,128},{1,65},{65,1},{129,193},{193,129... | collective-permute-start | bytes 1572872 | tf_op jit(solution)/shard_map/ppermute | solution.py:265
  17.4 25.9 %collective-permute-start.6 = (bf16[128,2048]{1,0:T(8,128)(2,1)S(1)}, bf16[128,2048]{1,0:T(8,128)(2,1)S(1)}, u32[]{:S(2)}, u32[]{:S(2)}) collective-permute-start(bf16[128,2048]{1,0:T(8,128)(2,1)S(1)} %get-tuple-element.31), channel_id=1, source_target_pairs={{0,128},{64,192},{128,0},{192,64},{1,129},{65,193},{129,1},{193,65... | collective-permute-start | bytes 1572872 | tf_op jit(solution)/shard_map/ppermute | solution.py:265
  20.0 24.4 %collective-permute-start.7 = (bf16[128,2048]{1,0:T(8,128)(2,1)S(1)}, bf16[128,2048]{1,0:T(8,128)(2,1)S(1)}, u32[]{:S(2)}, u32[]{:S(2)}) collective-permute-start(bf16[128,2048]{1,0:T(8,128)(2,1)S(1)} %get-tuple-element.32), channel_id=1, source_target_pairs={{0,192},{64,128},{128,64},{192,0},{1,193},{65,129},{129,65},{193,1... | collective-permute-start | bytes 1572872 | tf_op jit(solution)/shard_map/ppermute | solution.py:265
  27.3 3.1 %collective-permute-start.4 = (bf16[128,1024]{1,0:T(8,128)(2,1)S(1)}, bf16[128,1024]{1,0:T(8,128)(2,1)S(1)}, u32[]{:S(2)}, u32[]{:S(2)}) collective-permute-start(bf16[128,1024]{1,0:T(8,128)(2,1)S(1)} %get-tuple-element.23), channel_id=1, source_target_pairs={{0,1},{1,0},{2,3},{3,2},{4,5},{5,4},{6,7},{7,6},{8,9},{9,8},{10,11... | collective-permute-start | bytes 786440 | tf_op jit(solution)/shard_map/ppermute | solution.py:290
  29.1 7.0 %collective-permute-start.3 = (bf16[256,256]{1,0:T(8,128)(2,1)S(1)}, bf16[256,256]{1,0:T(8,128)(2,1)S(1)}, u32[]{:S(2)}, u32[]{:S(2)}) collective-permute-start(bf16[256,256]{1,0:T(8,128)(2,1)S(1)} %get-tuple-element.21), channel_id=1, source_target_pairs={{2,0},{3,1},{4,2},{5,3},{6,4},{7,5},{10,8},{11,9},{12,10},{13,11},... | collective-permute-start | bytes 393224 | tf_op jit(solution)/shard_map/ppermute | solution.py:294
  30.4 12.8 %collective-permute-start.8 = (bf16[256,256]{1,0:T(8,128)(2,1)S(1)}, bf16[256,256]{1,0:T(8,128)(2,1)S(1)}, u32[]{:S(2)}, u32[]{:S(2)}) collective-permute-start(bf16[256,256]{1,0:T(8,128)(2,1)S(1)} %get-tuple-element.35), channel_id=1, source_target_pairs={{4,0},{5,1},{6,2},{7,3},{12,8},{13,9},{14,10},{15,11},{20,16},{21,... | collective-permute-start | bytes 393224 | tf_op jit(solution)/shard_map/ppermute | solution.py:294
  44.4 14.4 %collective-permute-start.9 = (bf16[128,2048]{1,0:T(8,128)(2,1)S(1)}, bf16[128,2048]{1,0:T(8,128)(2,1)S(1)}, u32[]{:S(2)}, u32[]{:S(2)}) collective-permute-start(bf16[128,2048]{1,0:T(8,128)(2,1)S(1)} %get-tuple-element.36.refs_0_), channel_id=1, source_target_pairs={{0,1},{1,0},{2,3},{3,2},{4,5},{5,4},{6,7},{7,6},{8,9},{9,8},{10,11... | collective-permute-start | bytes 1572872 | tf_op jit(solution)/shard_map/ppermute | solution.py:303
  46.8 12.0 %collective-permute-start.10 = (bf16[128,2048]{1,0:T(8,128)(2,1)S(1)}, bf16[128,2048]{1,0:T(8,128)(2,1)S(1)}, u32[]{:S(2)}, u32[]{:S(2)}) collective-permute-start(bf16[128,2048]{1,0:T(8,128)(2,1)S(1)} %collective-permute-done.5.refs_2_), channel_id=1, source_target_pairs={{0,1},{1,0},{2,3},{3,2},{4,5},{5,4},{6,7},{7,6},{8,9},{9,8},{10,11... | collective-permute-start | bytes 1572872 | tf_op jit(solution)/shard_map/ppermute | solution.py:303
  46.8 12.0 %collective-permute-start.11 = (bf16[128,2048]{1,0:T(8,128)(2,1)S(1)}, bf16[128,2048]{1,0:T(8,128)(2,1)S(1)}, u32[]{:S(2)}, u32[]{:S(2)}) collective-permute-start(bf16[128,2048]{1,0:T(8,128)(2,1)S(1)} %collective-permute-done.6.refs_4_), channel_id=1, source_target_pairs={{0,1},{1,0},{2,3},{3,2},{4,5},{5,4},{6,7},{7,6},{8,9},{9,8},{10,11... | collective-permute-start | bytes 1572872 | tf_op jit(solution)/shard_map/ppermute | solution.py:303
  47.3 11.5 %collective-permute-start.12 = (bf16[128,2048]{1,0:T(8,128)(2,1)S(1)}, bf16[128,2048]{1,0:T(8,128)(2,1)S(1)}, u32[]{:S(2)}, u32[]{:S(2)}) collective-permute-start(bf16[128,2048]{1,0:T(8,128)(2,1)S(1)} %collective-permute-done.7.refs_6_), channel_id=1, source_target_pairs={{0,1},{1,0},{2,3},{3,2},{4,5},{5,4},{6,7},{7,6},{8,9},{9,8},{10,11... | collective-permute-start | bytes 1572872 | tf_op jit(solution)/shard_map/ppermute | solution.py:303

commit v6 on v5

--- a/solution.py
+++ b/solution.py
@@ -1,3 +1,5 @@
+import functools
+
 import jax
 import jax.numpy as jnp
 from jax import lax
@@ -39,7 +41,7 @@
     rows = keys.shape[0]
     out[:rows, :DH] = keys[...]
     out[:rows, DH:] = values[...]
-    out[rows:] = swapped[:, 2 * GROUP * DH :]
+    out[rows:] = swapped[...]
 
 
 def chip_pairs(keys, values, swapped):
@@ -78,19 +80,17 @@
 
 
 def attention_kernel(
-    queries, out_grad, swapped, chip_pair, near_pair, far_pair, bias,
+    queries, out_grad, q_other, do_other, chip_pair, near_pair, far_pair, bias,
     dq_mine, dq_other, own_grad, near_grad, far_grad, dk_acc, dv_acc,
 ):
-    wide = GROUP * DH
     pairs = jnp.concatenate([chip_pair[...], near_pair[...], far_pair[...]], axis=0)
     key, value = pairs[:, :DH], pairs[:, DH:]
     key_t = key.T
     rows = queries.shape[0]
     for head in range(GROUP):
         cols = slice(head * DH, (head + 1) * DH)
-        grad_cols = slice(wide + head * DH, wide + (head + 1) * DH)
-        query = jnp.concatenate([queries[:, cols], swapped[:, cols]], axis=0)
-        grad = jnp.concatenate([out_grad[:, cols], swapped[:, grad_cols]], axis=0)
+        query = jnp.concatenate([queries[:, cols], q_other[:, cols]], axis=0)
+        grad = jnp.concatenate([out_grad[:, cols], do_other[:, cols]], axis=0)
         score = dot_nt(key, query) * (SCALE * LOG2E) + bias[...]
         top = jnp.max(score, axis=0, keepdims=True)
         weight = jnp.exp2(score - top)
@@ -120,7 +120,7 @@
     far_grad[:, DH:] = dv_acc[2 * chip :].astype(jnp.bfloat16)
 
 
-def attention(queries, out_grad, swapped, blocks, bias):
+def attention(queries, out_grad, q_other, do_other, blocks, bias):
     rows = queries.shape[0]
     chip = 2 * rows
     keys = chip * (REACH + 1)
@@ -143,7 +143,7 @@
             bytes_accessed=4 * 1024 * 1024,
             transcendentals=keys * chip * GROUP,
         ),
-    )(queries, out_grad, swapped, *blocks, bias)
+    )(queries, out_grad, q_other, do_other, *blocks, bias)
 
 
 def combine_kernel(own, near, far, out):
@@ -179,33 +179,46 @@
     )(core, mine, other)
 
 
-def project_kernel(place_ref, *refs):
+def project_kernel(places_ref, *refs, offset):
     pieces, grads, out = refs[:-2], refs[-2], refs[-1]
-    places = range(len(pieces) // 2)
-    left = jnp.concatenate([grads[place_ref[0] ^ k] for k in places], axis=1)
-    right = jnp.concatenate([ref[...] for ref in pieces], axis=0)
-    out[...] = dot_nn(left, right).T.astype(jnp.bfloat16)
-
-
-def project(place, pieces, grads, blocks):
+    step = out.shape[0]
+    columns = pl.ds(pl.multiple_of((places_ref[1] ^ offset) * step, step), step)
+    left = jnp.concatenate([grads[places_ref[0] ^ k] for k in range(len(pieces) // 2)], axis=1)
+    right = jnp.concatenate([ref[:, columns] for ref in pieces], axis=0)
+    out[...] = dot_nn(left, right).T.astype(out.dtype)
+
+
+def project(places, pieces, grads, blocks, offset, dtype):
     rows, columns = pieces[0].shape
     width = grads.shape[1]
     step = columns // blocks
     return pl.pallas_call(
-        project_kernel,
-        out_shape=whole((columns, width)),
-        grid=(blocks,),
-        in_specs=[SCALAR]
-        + [pl.BlockSpec((rows, step), lambda i: (0, i))] * len(pieces)
-        + [pl.BlockSpec(grads.shape, lambda i: (0, 0, 0))],
-        out_specs=pl.BlockSpec((step, width), lambda i: (i, 0)),
+        functools.partial(project_kernel, offset=offset),
+        out_shape=whole((step, width), dtype),
+        in_specs=[SCALAR] + [pl.BlockSpec()] * (len(pieces) + 1),
         compiler_params=pltpu.CompilerParams(vmem_limit_bytes=16 * MIB),
         cost_estimate=pl.CostEstimate(
-            flops=2 * len(pieces) * rows * columns * width,
-            bytes_accessed=6 * MIB,
+            flops=2 * len(pieces) * rows * step * width,
+            bytes_accessed=2 * MIB,
             transcendentals=0,
         ),
-    )(place, *pieces, grads)
+    )(places, *pieces, grads)
+
+
+def add_kernel(*refs):
+    total = refs[0][...]
+    for ref in refs[1:-1]:
+        total = total + ref[...].astype(jnp.float32)
+    refs[-1][...] = total.astype(jnp.bfloat16)
+
+
+def add_parts(own, parts):
+    return pl.pallas_call(
+        add_kernel,
+        out_shape=whole(own.shape),
+        compiler_params=SMALL,
+        cost_estimate=pl.CostEstimate(flops=0, bytes_accessed=2 * MIB, transcendentals=0),
+    )(own, *parts)
 
 
 def final_kernel(parts, out):
@@ -234,18 +247,24 @@
     n_chips = lax.axis_size("z_lo")
     swap = [(0, 1), (1, 0)]
     core_ref = core.astype(jnp.int32).reshape(1)
-    place_ref = lax.axis_index("y").astype(jnp.int32).reshape(1)
+    places_ref = jnp.stack([lax.axis_index("y"), lax.axis_index("x")]).astype(jnp.int32)
 
     def half_of(array, which):
         width = array.shape[-1] // 2
         return lax.dynamic_slice_in_dim(array[0], which * width, width, 1)
 
-    sources = (queries, out_grad, keys, values)
-    q_mine, do_mine, k_mine, v_mine = (half_of(array, core) for array in sources)
-    swapped = lax.ppermute(
-        jnp.concatenate([half_of(array, 1 - core) for array in sources], axis=1), "core", swap
-    )
-    chip_pair = chip_pairs(k_mine, v_mine, swapped)
+    k_mine, v_mine = half_of(keys, core), half_of(values, core)
+    chip_pair = chip_pairs(
+        k_mine,
+        v_mine,
+        lax.ppermute(
+            jnp.concatenate([half_of(keys, 1 - core), half_of(values, 1 - core)], axis=1), "core", swap
+        ),
+    )
+    q_mine, do_mine = half_of(queries, core), half_of(out_grad, core)
+    q_out, do_out = half_of(queries, 1 - core), half_of(out_grad, 1 - core)
+    q_out, do_out, _ = lax.optimization_barrier((q_out, do_out, chip_pair))
+    q_other, do_other = (lax.ppermute(part, "core", swap) for part in (q_out, do_out))
 
     def behind(distance):
         return [
@@ -259,8 +278,8 @@
     ][::-1]
 
     n_y = lax.axis_size("y")
-    chunks = split_columns(place_ref, layer_input[0], n_y)
-    chunks, _ = lax.optimization_barrier((chunks, chip_pair))
+    chunks = split_columns(places_ref, layer_input[0], n_y)
+    chunks, _ = lax.optimization_barrier((chunks, (q_other, do_other)))
     pieces = [chunks[0]] + [
         lax.ppermute(chunks[k], "y", [(i, i ^ k) for i in range(n_y)]) for k in range(1, n_y)
     ]
@@ -285,14 +304,14 @@
     bias = jnp.where(allowed, 0.0, MASKED).astype(jnp.float32)
 
     dq_mine, dq_other, own_grad, near_grad, far_grad = attention(
-        q_mine, do_mine, swapped, blocks, bias
+        q_mine, do_mine, q_other, do_other, blocks, bias
     )
     dq_back = lax.ppermute(dq_other, "core", swap)
     query_grad = assemble(core_ref, dq_mine, dq_back)[None]
 
-    near_back, far_back = (
+    far_back, near_back = (
         lax.ppermute(part, ("z_lo", "core"), [(b, a) for a, b in behind(distance)])
-        for distance, part in ((1, near_grad), (2, far_grad))
+        for distance, part in ((2, far_grad), (1, near_grad))
     )
 
     near_back, query_grad = lax.optimization_barrier((near_back, query_grad))
@@ -301,10 +320,12 @@
     gathered = lax.all_to_all(copies, "y", 0, 0, tiled=True)
     pieces, _ = lax.optimization_barrier((pieces, copies))
     both = [part for piece in pieces for part in (piece, lax.ppermute(piece, "core", swap))]
-    term = project(place_ref, both, gathered, 4)
     n_x = lax.axis_size("x")
-    over_x = lax.all_to_all(term.reshape(n_x, -1, term.shape[1]), "x", 0, 0, tiled=True)
-    term = jnp.sum(over_x.astype(jnp.float32), axis=0).astype(jnp.bfloat16)
+    parts = []
+    for k in (2, 1, 3):
+        term = project(places_ref, both, gathered, n_x, k, jnp.bfloat16)
+        parts.append(lax.ppermute(term, "x", [(i, i ^ k) for i in range(n_x)]))
+    term = add_parts(project(places_ref, both, gathered, n_x, 0, jnp.float32), parts)
     rest = ("z_hi", "z_lo", "core")
     n_rest = lax.axis_size(rest)
     spread = lax.all_to_all(

time: 99.6 us -> 98.4 us (0.988)
  blocking collectives: 48.6 us -> 30.4 us
  waiting for transfers between devices: 12.8 us -> 20 us
  starting transfers between devices: 21.3 us -> 25.4 us
  local copies, waits for them, and re-layouts: 2.65 us -> 6.01 us
  Pallas kernels: 11.5 us -> 14 us
    all_to_all x1 -> x0, blocking collectives: 17.3 us -> none  [per_device(): lax.all_to_all(term.reshape(n_x, -1, term.shape[1]), 'x', 0, 0, tiled=True)]
    ppermute x1 -> x6, waiting for transfers between devices: 1.04 us -> 7.82 us  [the longest x3 7.81 us: per_device(): parts.append(lax.ppermute(term, 'x', [(i, i ^ k) for i in range(n_x)]))]
    ppermute x1 -> x6, starting transfers between devices: 3.24 us -> 7.8 us  [the longest x3 3.87 us: per_device(): parts.append(lax.ppermute(term, 'x', [(i, i ^ k) for i in range(n_x)]))]
    unnamed x9 -> x7, local copies, waits for them, and re-layouts: 0.41 us -> 3.79 us
    pallas_call x1 -> x5, Pallas kernels: 2.44 us -> 4.41 us  [the longest x4 4.3 us: project(): pl.pallas_call(functools.partial(project_kernel, offset=offset), out_shap...]
  transfers between devices with their start and end apart: 13 -> 18, of which waited for: 4 -> 6; matrix products, arithmetic and copies ran while one was open for 1% -> 6% of each run, Pallas kernels for 8% -> 12%
where the time goes in v6:
time: 98.4 us; the launch traced here: 98 us
  blocking collectives  30.4 us (31%)
  starting transfers between devices  25.4 us (26%)
  waiting for transfers between devices  20 us (20%)
  Pallas kernels  14 us (14%)
  local copies, waits for them, and re-layouts  6.01 us (6%)
  other arithmetic  1.27 us (1%)
    all_to_all x1, blocking collectives, per_device(): lax.all_to_all(term.reshape(n_rest, term.shape[0] // n_rest, term.shape[1...  18.9 us
    all_to_all x1, blocking collectives, per_device(): gathered = lax.all_to_all(copies, 'y', 0, 0, tiled=True)  11.5 us
    ppermute x2, waiting for transfers between devices, per_device(): lax.ppermute(part, ('z_lo', 'core'), [(b, a) for a, b in behind(distance)])  10.8 us
    ppermute x3, waiting for transfers between devices, per_device(): parts.append(lax.ppermute(term, 'x', [(i, i ^ k) for i in range(n_x)]))  7.81 us
    pallas_call x1, Pallas kernels, attention(): pl.pallas_call(attention_kernel, out_shape=(whole((rows, GROUP * DH)), wh...  7.25 us
    ppermute x2, starting transfers between devices, per_device(): lax.ppermute(chip_pair, ('z_lo', 'core'), behind(distance))  6.71 us
    pallas_call x4, Pallas kernels, project(): pl.pallas_call(functools.partial(project_kernel, offset=offset), out_shap...  4.3 us
    ppermute x3, starting transfers between devices, per_device(): lax.ppermute(chunks[k], 'y', [(i, i ^ k) for i in range(n_y)])  4.01 us
  transfers between devices with their start and end apart: 18, of which 6 were waited for; matrix products, arithmetic and copies ran while one was open for 6% of the time, Pallas kernels for 12%

profile of v6, /device:TPU:1, one launch (start us, length us, event | category | flops | bytes accessed | tf_op | source)
XLA Modules:
  0.0 98.0 jit_solution(11618983751069538958)
XLA Ops:
  0.6 1.0 dynamic-slice_bitcast_fusion.4
  1.6 3.3 %collective-permute-start = (bf16[128,256]{1,0:T(8,128)(2,1)S(1)}, bf16[128,256]{1,0:T(8,128)(2,1)S(1)}, u32[]{:S(2)}, u32[]{:S(2)}) collective-permute-start(bf16[128,256]{1,0:T(8,128)(2,1)S(1)} %pad_maximum_fusion), channel_id=1, source_target_pairs={{0,1},{1,0},{2,3},{3,2},{4,5},{5,4},{6,7},{7,6},{8,9},{9,8},{10,11... | collective-permute-start | bytes 196616 | tf_op jit(solution)/shard_map/ppermute | solution.py:260
  5.1 0.8 constant_dynamic-update-slice_fusion.11
  5.8 0.8 constant_dynamic-update-slice_fusion.9
  6.6 0.8 constant_dynamic-update-slice_fusion.7
  7.3 0.8 constant_dynamic-update-slice_fusion.5
  8.1 0.8 constant_dynamic-update-slice_fusion.3
  8.9 0.8 constant_dynamic-update-slice_fusion
  9.6 1.3 %dynamic-slice_bitcast_fusion = (bf16[128,1024]{1,0:T(8,128)(2,1)S(1)}, bf16[128,1024]{1,0:T(8,128)(2,1)S(1)}, bf16[128,1024]{1,0:T(8,128)(2,1)S(1)}, bf16[128,1024]{1,0:T(8,128)(2,1)S(1)}) fusion(bf16[1,128,2048]{2,1,0:T(8,128)(2,1)} %param.9, s32[]{:T(128)S(6)} %select_n.12, s32[]{:T(128)S(6)} %select_n.11, bf16[1,128,2048]{2,1,0:T(8,128)(2,1)} %param.6), kind=kLoop, calls=%fused_computation.1 | loop fusion | bytes 2097160 | tf_op jit(solution)/shard_map/dynamic_slice | solution.py:254
  10.9 0.0 collective-permute-done.swapped
  10.9 0.2 collective-permute-start.1
  11.1 0.4 collective-permute-start.2
  11.5 0.1 pad_add_fusion.2.place_ref.places_ref
  11.6 0.7 shard_map.80
  12.4 3.2 %collective-permute-start.4 = (bf16[256,256]{1,0:T(8,128)(2,1)S(1)}, bf16[256,256]{1,0:T(8,128)(2,1)S(1)}, u32[]{:S(2)}, u32[]{:S(2)}) collective-permute-start(bf16[256,256]{1,0:T(8,128)(2,1)S(1)} %shard_map.77.chip_pair), channel_id=1, source_target_pairs={{0,4},{1,5},{2,6},{3,7},{8,12},{9,13},{10,14},{11,15},{16,20},{17,... | collective-permute-start | bytes 393224 | tf_op jit(solution)/shard_map/ppermute | solution.py:277
  15.5 3.5 %collective-permute-start.3 = (bf16[256,256]{1,0:T(8,128)(2,1)S(1)}, bf16[256,256]{1,0:T(8,128)(2,1)S(1)}, u32[]{:S(2)}, u32[]{:S(2)}) collective-permute-start(bf16[256,256]{1,0:T(8,128)(2,1)S(1)} %shard_map.77.chip_pair), channel_id=1, source_target_pairs={{0,2},{1,3},{2,4},{3,5},{4,6},{5,7},{8,10},{9,11},{10,12},{11,13},... | collective-permute-start | bytes 393224 | tf_op jit(solution)/shard_map/ppermute | solution.py:277
  19.1 0.4 and_select_fusion.bias
  19.5 0.0 collective-permute-done.1.q_other
  19.5 1.4 %collective-permute-start.7 = (bf16[128,2048]{1,0:T(8,128)(2,1)S(1)}, bf16[128,2048]{1,0:T(8,128)(2,1)S(1)}, u32[]{:S(2)}, u32[]{:S(2)}) collective-permute-start(bf16[128,2048]{1,0:T(8,128)(2,1)S(1)} %get-tuple-element.34), channel_id=1, source_target_pairs={{0,64},{64,0},{128,192},{192,128},{1,65},{65,1},{129,193},{193,129... | collective-permute-start | bytes 1572872 | tf_op jit(solution)/shard_map/ppermute | solution.py:284
  20.9 2.6 %collective-permute-start.8 = (bf16[128,2048]{1,0:T(8,128)(2,1)S(1)}, bf16[128,2048]{1,0:T(8,128)(2,1)S(1)}, u32[]{:S(2)}, u32[]{:S(2)}) collective-permute-start(bf16[128,2048]{1,0:T(8,128)(2,1)S(1)} %get-tuple-element.35), channel_id=1, source_target_pairs={{0,128},{64,192},{128,0},{192,64},{1,129},{65,193},{129,1},{193,65... | collective-permute-start | bytes 1572872 | tf_op jit(solution)/shard_map/ppermute | solution.py:284
  23.5 7.2 %shard_map.78 = (bf16[128,1024]{1,0:T(8,128)(2,1)S(1)}, bf16[128,1024]{1,0:T(8,128)(2,1)S(1)}, f32[256,256]{1,0:T(8,128)S(1)}, bf16[256,256]{1,0:T(8,128)(2,1)S(1)}, bf16[256,256]{1,0:T(8,128)(2,1)S(1)}) custom-call(bf16[128,1024]{1,0:T(8,128)(2,1)S(1)} %get-tuple-element.58.queries, bf16[128,1024]{1,0:T(8,128)(2,1)S(1)} %get-tuple-element.49.out_grad, ...), custom_call_target="tpu_custom_call" | custom-call | flops 8053063680 | bytes 4194304 | tf_op jit(solution)/shard_map/pallas_call | solution.py:127
  30.7 1.5 %collective-permute-start.6 = (bf16[128,1024]{1,0:T(8,128)(2,1)S(1)}, bf16[128,1024]{1,0:T(8,128)(2,1)S(1)}, u32[]{:S(2)}, u32[]{:S(2)}) collective-permute-start(bf16[128,1024]{1,0:T(8,128)(2,1)S(1)} %get-tuple-element.27), channel_id=1, source_target_pairs={{0,1},{1,0},{2,3},{3,2},{4,5},{5,4},{6,7},{7,6},{8,9},{9,8},{10,11... | collective-permute-start | bytes 786440 | tf_op jit(solution)/shard_map/ppermute | solution.py:309
  32.2 1.3 %collective-permute-start.5 = (bf16[256,256]{1,0:T(8,128)(2,1)S(1)}, bf16[256,256]{1,0:T(8,128)(2,1)S(1)}, u32[]{:S(2)}, u32[]{:S(2)}) collective-permute-start(bf16[256,256]{1,0:T(8,128)(2,1)S(1)} %get-tuple-element.25), channel_id=1, source_target_pairs={{2,0},{3,1},{4,2},{5,3},{6,4},{7,5},{10,8},{11,9},{12,10},{13,11},... | collective-permute-start | bytes 393224 | tf_op jit(solution)/shard_map/ppermute | solution.py:313
  33.5 0.0 collective-permute-done.6.other
  33.5 1.5 %collective-permute-start.10 = (bf16[256,256]{1,0:T(8,128)(2,1)S(1)}, bf16[256,256]{1,0:T(8,128)(2,1)S(1)}, u32[]{:S(2)}, u32[]{:S(2)}) collective-permute-start(bf16[256,256]{1,0:T(8,128)(2,1)S(1)} %get-tuple-element.39), channel_id=1, source_target_pairs={{4,0},{5,1},{6,2},{7,3},{12,8},{13,9},{14,10},{15,11},{20,16},{21,... | collective-permute-start | bytes 393224 | tf_op jit(solution)/shard_map/ppermute | solution.py:313
  35.0 0.8 shard_map.79
  35.9 3.4 %collective-permute-done.5.near = bf16[256,256]{1,0:T(8,128)(2,1)S(1)} collective-permute-done((bf16[256,256]{1,0:T(8,128)(2,1)S(1)}, bf16[256,256]{1,0:T(8,128)(2,1)S(1)}, u32[]{:S(2)}, u32[]{:S(2)}) %collective-permute-start.5) | collective-permute-done | bytes 131104 | tf_op jit(solution)/shard_map/ppermute | solution.py:313
  39.2 7.4 %collective-permute-done.10.far = bf16[256,256]{1,0:T(8,128)(2,1)S(1)} collective-permute-done((bf16[256,256]{1,0:T(8,128)(2,1)S(1)}, bf16[256,256]{1,0:T(8,128)(2,1)S(1)}, u32[]{:S(2)}, u32[]{:S(2)}) %collective-permute-start.10) | collective-permute-done | bytes 131104 | tf_op jit(solution)/shard_map/ppermute | solution.py:313
  46.6 0.1 shard_map.81
  46.8 1.4 %collective-permute-done.9.refs_6_ = bf16[128,2048]{1,0:T(8,128)(2,1)S(1)} collective-permute-done((bf16[128,2048]{1,0:T(8,128)(2,1)S(1)}, bf16[128,2048]{1,0:T(8,128)(2,1)S(1)}, u32[]{:S(2)}, u32[]{:S(2)}) %collective-permute-start.9) | collective-permute-done | bytes 524320 | tf_op jit(solution)/shard_map/ppermute | solution.py:284
  48.1 2.1 %collective-permute-start.11 = (bf16[128,2048]{1,0:T(8,128)(2,1)S(1)}, bf16[128,2048]{1,0:T(8,128)(2,1)S(1)}, u32[]{:S(2)}, u32[]{:S(2)}) collective-permute-start(bf16[128,2048]{1,0:T(8,128)(2,1)S(1)} %get-tuple-element.40.refs_0_), channel_id=1, source_target_pairs={{0,1},{1,0},{2,3},{3,2},{4,5},{5,4},{6,7},{7,6},{8,9},{9,8},{10,11... | collective-permute-start | bytes 1572872 | tf_op jit(solution)/shard_map/ppermute | solution.py:322
  50.3 0.0 collective-permute-start.12
  50.3 0.5 collective-permute-start.13
  50.8 0.0 collective-permute-start.14
  50.8 11.5 %all_to_all.10.refs_8_ = bf16[4,256,256]{2,1,0:T(8,128)(2,1)S(1)} all-to-all(bf16[4,256,256]{2,1,0:T(8,128)(2,1)S(1)} %shard_map.81), channel_id=1, replica_groups=mesh['y'=4,'x'=4,'z_hi'=2,'z_lo'=4,'core'=2] {'y'}, dimensions={0} | all-to-all | bytes 1048576 | tf_op jit(solution)/shard_map/all_to_all | solution.py:320
  62.3 1.1 %shard_map.83 = bf16[512,256]{1,0:T(8,128)(2,1)S(1)} custom-call(s32[2]{0:T(128)S(1)} %pad_add_fusion.2.place_ref.places_ref, bf16[128,2048]{1,0:T(8,128)(2,1)S(1)} %get-tuple-element.40.refs_0_, bf16[128,2048]{1,0:T(8,128)(2,1)S(1)} %collective-permute-done.11.refs_1_, bf16[128,2048]{1,0:T(8,128)(2,1)S(1)} %collective-permute-done.7.refs_2_, ...), custom_call_target="tpu_custom_call" | custom-call | flops 268435456 | bytes 2097152 | tf_op jit(solution)/shard_map/pallas_call | solution.py:195
  63.3 2.8 %collective-permute-start.15 = (bf16[512,256]{1,0:T(8,128)(2,1)S(1)}, bf16[512,256]{1,0:T(8,128)(2,1)S(1)}, u32[]{:S(2)}, u32[]{:S(2)}) collective-permute-start(bf16[512,256]{1,0:T(8,128)(2,1)S(1)} %shard_map.83), channel_id=1, source_target_pairs={{0,32},{16,48},{32,0},{48,16},{1,33},{17,49},{33,1},{49,17},{2,34}... | collective-permute-start | bytes 786440 | tf_op jit(solution)/shard_map/ppermute | solution.py:327
  66.2 1.1 %shard_map.84 = bf16[512,256]{1,0:T(8,128)(2,1)S(1)} custom-call(s32[2]{0:T(128)S(1)} %pad_add_fusion.2.place_ref.places_ref, bf16[128,2048]{1,0:T(8,128)(2,1)S(1)} %get-tuple-element.40.refs_0_, bf16[128,2048]{1,0:T(8,128)(2,1)S(1)} %collective-permute-done.11.refs_1_, bf16[128,2048]{1,0:T(8,128)(2,1)S(1)} %collective-permute-done.7.refs_2_, ...), custom_call_target="tpu_custom_call" | custom-call | flops 268435456 | bytes 2097152 | tf_op jit(solution)/shard_map/pallas_call | solution.py:195
  67.2 0.4 collective-permute-start.16
  67.6 1.1 %shard_map.85 = bf16[512,256]{1,0:T(8,128)(2,1)S(1)} custom-call(s32[2]{0:T(128)S(1)} %pad_add_fusion.2.place_ref.places_ref, bf16[128,2048]{1,0:T(8,128)(2,1)S(1)} %get-tuple-element.40.refs_0_, bf16[128,2048]{1,0:T(8,128)(2,1)S(1)} %collective-permute-done.11.refs_1_, bf16[128,2048]{1,0:T(8,128)(2,1)S(1)} %collective-permute-done.7.refs_2_, ...), custom_call_target="tpu_custom_call" | custom-call | flops 268435456 | bytes 2097152 | tf_op jit(solution)/shard_map/pallas_call | solution.py:195
  68.7 0.7 collective-permute-start.17
  69.3 1.1 %shard_map.82.refs_0_ = f32[512,256]{1,0:T(8,128)S(1)} custom-call(s32[2]{0:T(128)S(1)} %pad_add_fusion.2.place_ref.places_ref, bf16[128,2048]{1,0:T(8,128)(2,1)S(1)} %get-tuple-element.40.refs_0_, bf16[128,2048]{1,0:T(8,128)(2,1)S(1)} %collective-permute-done.11.refs_1_, bf16[128,2048]{1,0:T(8,128)(2,1)S(1)} %collective-permute-done.7.refs_2_, ...), custom_call_target="tpu_custom_call" | custom-call | flops 268435456 | bytes 2097152 | tf_op jit(solution)/shard_map/pallas_call | solution.py:195
  70.5 0.9 collective-permute-done.15.refs_1_
  71.4 5.7 %collective-permute-done.16.refs_2_ = bf16[512,256]{1,0:T(8,128)(2,1)S(1)} collective-permute-done((bf16[512,256]{1,0:T(8,128)(2,1)S(1)}, bf16[512,256]{1,0:T(8,128)(2,1)S(1)}, u32[]{:S(2)}, u32[]{:S(2)}) %collective-permute-start.16) | collective-permute-done | bytes 262176 | tf_op jit(solution)/shard_map/ppermute | solution.py:327
  77.1 1.2 %collective-permute-done.17.refs_3_ = bf16[512,256]{1,0:T(8,128)(2,1)S(1)} collective-permute-done((bf16[512,256]{1,0:T(8,128)(2,1)S(1)}, bf16[512,256]{1,0:T(8,128)(2,1)S(1)}, u32[]{:S(2)}, u32[]{:S(2)}) %collective-permute-start.17) | collective-permute-done | bytes 262176 | tf_op jit(solution)/shard_map/ppermute | solution.py:327
  78.3 0.1 shard_map.86
  78.4 18.9 %all_to_all.11.parts = bf16[16,32,256]{2,1,0:T(8,128)(2,1)S(1)} all-to-all(bf16[16,32,256]{2,1,0:T(8,128)(2,1)S(1)} %bitcast.45), channel_id=1, replica_groups=mesh['y'=4,'x'=4,'z_hi'=2,'z_lo'=4,'core'=2] {'z_hi','z_lo','core'}, dimensions={0} | all-to-all | bytes 524288 | tf_op jit(solution)/shard_map/all_to_all | solution.py:331
  97.3 0.7 shard_map.87
  (25 shorter events, 0.1 us)
Async XLA Ops:
  0.6 11.0 %copy-start = (bf16[1,128,8192]{2,1,0:T(8,128)(2,1)S(1)}, bf16[1,128,8192]{2,1,0:T(8,128)(2,1)}, u32[]{:S(2)}) copy-start(bf16[1,128,8192]{2,1,0:T(8,128)(2,1)} %param.10) | copy-start | bytes 6291460
  1.6 9.3 %collective-permute-start = (bf16[128,256]{1,0:T(8,128)(2,1)S(1)}, bf16[128,256]{1,0:T(8,128)(2,1)S(1)}, u32[]{:S(2)}, u32[]{:S(2)}) collective-permute-start(bf16[128,256]{1,0:T(8,128)(2,1)S(1)} %pad_maximum_fusion), channel_id=1, source_target_pairs={{0,1},{1,0},{2,3},{3,2},{4,5},{5,4},{6,7},{7,6},{8,9},{9,8},{10,11... | collective-permute-start | bytes 196616 | tf_op jit(solution)/shard_map/ppermute | solution.py:260
  10.9 8.5 %collective-permute-start.1 = (bf16[128,1024]{1,0:T(8,128)(2,1)S(1)}, bf16[128,1024]{1,0:T(8,128)(2,1)S(1)}, u32[]{:S(2)}, u32[]{:S(2)}) collective-permute-start(bf16[128,1024]{1,0:T(8,128)(2,1)S(1)} %get-tuple-element.23), channel_id=1, source_target_pairs={{0,1},{1,0},{2,3},{3,2},{4,5},{5,4},{6,7},{7,6},{8,9},{9,8},{10,11... | collective-permute-start | bytes 786440 | tf_op jit(solution)/shard_map/ppermute | solution.py:267
  11.1 8.4 %collective-permute-start.2 = (bf16[128,1024]{1,0:T(8,128)(2,1)S(1)}, bf16[128,1024]{1,0:T(8,128)(2,1)S(1)}, u32[]{:S(2)}, u32[]{:S(2)}) collective-permute-start(bf16[128,1024]{1,0:T(8,128)(2,1)S(1)} %get-tuple-element.24), channel_id=1, source_target_pairs={{0,1},{1,0},{2,3},{3,2},{4,5},{5,4},{6,7},{7,6},{8,9},{9,8},{10,11... | collective-permute-start | bytes 786440 | tf_op jit(solution)/shard_map/ppermute | solution.py:267
  12.4 11.1 %collective-permute-start.4 = (bf16[256,256]{1,0:T(8,128)(2,1)S(1)}, bf16[256,256]{1,0:T(8,128)(2,1)S(1)}, u32[]{:S(2)}, u32[]{:S(2)}) collective-permute-start(bf16[256,256]{1,0:T(8,128)(2,1)S(1)} %shard_map.77.chip_pair), channel_id=1, source_target_pairs={{0,4},{1,5},{2,6},{3,7},{8,12},{9,13},{10,14},{11,15},{16,20},{17,... | collective-permute-start | bytes 393224 | tf_op jit(solution)/shard_map/ppermute | solution.py:277
  15.5 7.9 %collective-permute-start.3 = (bf16[256,256]{1,0:T(8,128)(2,1)S(1)}, bf16[256,256]{1,0:T(8,128)(2,1)S(1)}, u32[]{:S(2)}, u32[]{:S(2)}) collective-permute-start(bf16[256,256]{1,0:T(8,128)(2,1)S(1)} %shard_map.77.chip_pair), channel_id=1, source_target_pairs={{0,2},{1,3},{2,4},{3,5},{4,6},{5,7},{8,10},{9,11},{10,12},{11,13},... | collective-permute-start | bytes 393224 | tf_op jit(solution)/shard_map/ppermute | solution.py:277
  19.5 27.3 %collective-permute-start.7 = (bf16[128,2048]{1,0:T(8,128)(2,1)S(1)}, bf16[128,2048]{1,0:T(8,128)(2,1)S(1)}, u32[]{:S(2)}, u32[]{:S(2)}) collective-permute-start(bf16[128,2048]{1,0:T(8,128)(2,1)S(1)} %get-tuple-element.34), channel_id=1, source_target_pairs={{0,64},{64,0},{128,192},{192,128},{1,65},{65,1},{129,193},{193,129... | collective-permute-start | bytes 1572872 | tf_op jit(solution)/shard_map/ppermute | solution.py:284
  20.9 25.9 %collective-permute-start.8 = (bf16[128,2048]{1,0:T(8,128)(2,1)S(1)}, bf16[128,2048]{1,0:T(8,128)(2,1)S(1)}, u32[]{:S(2)}, u32[]{:S(2)}) collective-permute-start(bf16[128,2048]{1,0:T(8,128)(2,1)S(1)} %get-tuple-element.35), channel_id=1, source_target_pairs={{0,128},{64,192},{128,0},{192,64},{1,129},{65,193},{129,1},{193,65... | collective-permute-start | bytes 1572872 | tf_op jit(solution)/shard_map/ppermute | solution.py:284
  23.5 24.7 %collective-permute-start.9 = (bf16[128,2048]{1,0:T(8,128)(2,1)S(1)}, bf16[128,2048]{1,0:T(8,128)(2,1)S(1)}, u32[]{:S(2)}, u32[]{:S(2)}) collective-permute-start(bf16[128,2048]{1,0:T(8,128)(2,1)S(1)} %get-tuple-element.36), channel_id=1, source_target_pairs={{0,192},{64,128},{128,64},{192,0},{1,193},{65,129},{129,65},{193,1... | collective-permute-start | bytes 1572872 | tf_op jit(solution)/shard_map/ppermute | solution.py:284
  30.7 2.8 %collective-permute-start.6 = (bf16[128,1024]{1,0:T(8,128)(2,1)S(1)}, bf16[128,1024]{1,0:T(8,128)(2,1)S(1)}, u32[]{:S(2)}, u32[]{:S(2)}) collective-permute-start(bf16[128,1024]{1,0:T(8,128)(2,1)S(1)} %get-tuple-element.27), channel_id=1, source_target_pairs={{0,1},{1,0},{2,3},{3,2},{4,5},{5,4},{6,7},{7,6},{8,9},{9,8},{10,11... | collective-permute-start | bytes 786440 | tf_op jit(solution)/shard_map/ppermute | solution.py:309
  32.2 7.0 %collective-permute-start.5 = (bf16[256,256]{1,0:T(8,128)(2,1)S(1)}, bf16[256,256]{1,0:T(8,128)(2,1)S(1)}, u32[]{:S(2)}, u32[]{:S(2)}) collective-permute-start(bf16[256,256]{1,0:T(8,128)(2,1)S(1)} %get-tuple-element.25), channel_id=1, source_target_pairs={{2,0},{3,1},{4,2},{5,3},{6,4},{7,5},{10,8},{11,9},{12,10},{13,11},... | collective-permute-start | bytes 393224 | tf_op jit(solution)/shard_map/ppermute | solution.py:313
  33.5 13.1 %collective-permute-start.10 = (bf16[256,256]{1,0:T(8,128)(2,1)S(1)}, bf16[256,256]{1,0:T(8,128)(2,1)S(1)}, u32[]{:S(2)}, u32[]{:S(2)}) collective-permute-start(bf16[256,256]{1,0:T(8,128)(2,1)S(1)} %get-tuple-element.39), channel_id=1, source_target_pairs={{4,0},{5,1},{6,2},{7,3},{12,8},{13,9},{14,10},{15,11},{20,16},{21,... | collective-permute-start | bytes 393224 | tf_op jit(solution)/shard_map/ppermute | solution.py:313
  48.1 14.1 %collective-permute-start.11 = (bf16[128,2048]{1,0:T(8,128)(2,1)S(1)}, bf16[128,2048]{1,0:T(8,128)(2,1)S(1)}, u32[]{:S(2)}, u32[]{:S(2)}) collective-permute-start(bf16[128,2048]{1,0:T(8,128)(2,1)S(1)} %get-tuple-element.40.refs_0_), channel_id=1, source_target_pairs={{0,1},{1,0},{2,3},{3,2},{4,5},{5,4},{6,7},{7,6},{8,9},{9,8},{10,11... | collective-permute-start | bytes 1572872 | tf_op jit(solution)/shard_map/ppermute | solution.py:322
  50.3 12.0 %collective-permute-start.12 = (bf16[128,2048]{1,0:T(8,128)(2,1)S(1)}, bf16[128,2048]{1,0:T(8,128)(2,1)S(1)}, u32[]{:S(2)}, u32[]{:S(2)}) collective-permute-start(bf16[128,2048]{1,0:T(8,128)(2,1)S(1)} %collective-permute-done.7.refs_2_), channel_id=1, source_target_pairs={{0,1},{1,0},{2,3},{3,2},{4,5},{5,4},{6,7},{7,6},{8,9},{9,8},{10,11... | collective-permute-start | bytes 1572872 | tf_op jit(solution)/shard_map/ppermute | solution.py:322
  50.3 12.0 %collective-permute-start.13 = (bf16[128,2048]{1,0:T(8,128)(2,1)S(1)}, bf16[128,2048]{1,0:T(8,128)(2,1)S(1)}, u32[]{:S(2)}, u32[]{:S(2)}) collective-permute-start(bf16[128,2048]{1,0:T(8,128)(2,1)S(1)} %collective-permute-done.8.refs_4_), channel_id=1, source_target_pairs={{0,1},{1,0},{2,3},{3,2},{4,5},{5,4},{6,7},{7,6},{8,9},{9,8},{10,11... | collective-permute-start | bytes 1572872 | tf_op jit(solution)/shard_map/ppermute | solution.py:322
  50.8 11.5 %collective-permute-start.14 = (bf16[128,2048]{1,0:T(8,128)(2,1)S(1)}, bf16[128,2048]{1,0:T(8,128)(2,1)S(1)}, u32[]{:S(2)}, u32[]{:S(2)}) collective-permute-start(bf16[128,2048]{1,0:T(8,128)(2,1)S(1)} %collective-permute-done.9.refs_6_), channel_id=1, source_target_pairs={{0,1},{1,0},{2,3},{3,2},{4,5},{5,4},{6,7},{7,6},{8,9},{9,8},{10,11... | collective-permute-start | bytes 1572872 | tf_op jit(solution)/shard_map/ppermute | solution.py:322
  63.3 8.0 %collective-permute-start.15 = (bf16[512,256]{1,0:T(8,128)(2,1)S(1)}, bf16[512,256]{1,0:T(8,128)(2,1)S(1)}, u32[]{:S(2)}, u32[]{:S(2)}) collective-permute-start(bf16[512,256]{1,0:T(8,128)(2,1)S(1)} %shard_map.83), channel_id=1, source_target_pairs={{0,32},{16,48},{32,0},{48,16},{1,33},{17,49},{33,1},{49,17},{2,34}... | collective-permute-start | bytes 786440 | tf_op jit(solution)/shard_map/ppermute | solution.py:327
  67.2 9.8 %collective-permute-start.16 = (bf16[512,256]{1,0:T(8,128)(2,1)S(1)}, bf16[512,256]{1,0:T(8,128)(2,1)S(1)}, u32[]{:S(2)}, u32[]{:S(2)}) collective-permute-start(bf16[512,256]{1,0:T(8,128)(2,1)S(1)} %shard_map.84), channel_id=1, source_target_pairs={{0,16},{16,0},{32,48},{48,32},{1,17},{17,1},{33,49},{49,33},{2,18}... | collective-permute-start | bytes 786440 | tf_op jit(solution)/shard_map/ppermute | solution.py:327
  68.7 9.6 %collective-permute-start.17 = (bf16[512,256]{1,0:T(8,128)(2,1)S(1)}, bf16[512,256]{1,0:T(8,128)(2,1)S(1)}, u32[]{:S(2)}, u32[]{:S(2)}) collective-permute-start(bf16[512,256]{1,0:T(8,128)(2,1)S(1)} %shard_map.85), channel_id=1, source_target_pairs={{0,48},{16,32},{32,16},{48,0},{1,49},{17,33},{33,17},{49,1},{2,50}... | collective-permute-start | bytes 786440 | tf_op jit(solution)/shard_map/ppermute | solution.py:327

commit v7 on v6

--- a/solution.py
+++ b/solution.py
@@ -79,71 +79,151 @@
     )(place, columns)
 
 
+def bias_kernel(here_ref, docs, out):
+    z_lo, core = here_ref[0], here_ref[1]
+    rows = out.shape[1] // 2
+    chip = 2 * rows
+    shape = (rows, rows)
+    down = lax.broadcasted_iota(jnp.int32, shape, 0)
+    along = lax.broadcasted_iota(jnp.int32, shape, 1)
+
+    def place(distance, which):
+        start = (z_lo - distance) * chip + (core ^ which) * rows
+        held = pl.ds(pl.multiple_of(jnp.maximum(start, 0), rows), rows)
+        return start, jnp.broadcast_to(docs[:, held].astype(jnp.float32), shape)
+
+    queries = [place(0, which) for which in range(2)]
+    for block in range(2 * (REACH + 1)):
+        key_start, key_row = place(block // 2, block % 2)
+        key_doc, key_pos = key_row.T, key_start + down
+        for which, (query_start, query_doc) in enumerate(queries):
+            allowed = (key_pos >= 0) & (key_pos <= query_start + along) & (key_doc == query_doc)
+            out[block * rows : (block + 1) * rows, which * rows : (which + 1) * rows] = jnp.where(
+                allowed, 0.0, MASKED
+            )
+
+
+def make_bias(here, docs, rows):
+    return pl.pallas_call(
+        bias_kernel,
+        out_shape=whole((2 * rows * (REACH + 1), 2 * rows), jnp.float32),
+        in_specs=[SCALAR, pl.BlockSpec()],
+        compiler_params=SMALL,
+        cost_estimate=pl.CostEstimate(flops=0, bytes_accessed=MIB, transcendentals=0),
+    )(here, docs)
+
+
 def attention_kernel(
-    queries, out_grad, q_other, do_other, chip_pair, near_pair, far_pair, bias,
-    dq_mine, dq_other, own_grad, near_grad, far_grad, dk_acc, dv_acc,
+    q_mine, do_mine, q_other, do_other, chip_pair, near_pair, far_pair, bias,
+    near_grad, far_grad, score_grads, probs, dk_acc, dv_acc,
 ):
     pairs = jnp.concatenate([chip_pair[...], near_pair[...], far_pair[...]], axis=0)
     key, value = pairs[:, :DH], pairs[:, DH:]
-    key_t = key.T
-    rows = queries.shape[0]
+    chip = chip_pair.shape[0]
+
+    def load(head):
+        cols = slice(head * DH, (head + 1) * DH)
+        return (
+            jnp.concatenate([q_mine[:, cols], q_other[:, cols]], axis=0),
+            jnp.concatenate([do_mine[:, cols], do_other[:, cols]], axis=0),
+        )
+
+    def products(head):
+        query, grad = load(head)
+        return dot_nt(key, query), dot_nt(value, grad)
+
+    ahead = products(0)
     for head in range(GROUP):
-        cols = slice(head * DH, (head + 1) * DH)
-        query = jnp.concatenate([queries[:, cols], q_other[:, cols]], axis=0)
-        grad = jnp.concatenate([out_grad[:, cols], do_other[:, cols]], axis=0)
-        score = dot_nt(key, query) * (SCALE * LOG2E) + bias[...]
+        raw, prob_grad = ahead
+        if head + 1 < GROUP:
+            ahead = products(head + 1)
+        score = raw * (SCALE * LOG2E) + bias[...]
         top = jnp.max(score, axis=0, keepdims=True)
         weight = jnp.exp2(score - top)
         inverse = 1.0 / jnp.sum(weight, axis=0, keepdims=True)
         prob = weight * inverse
         prob_half = prob.astype(jnp.bfloat16)
-        prob_grad = dot_nt(value, grad)
         delta = jnp.sum(prob_half.astype(jnp.float32) * prob_grad, axis=0, keepdims=True)
         score_grad = (prob * (prob_grad - delta) * SCALE).astype(jnp.bfloat16)
-        dq = dot_nn(key_t, score_grad).T.astype(jnp.bfloat16)
-        dq_mine[:, cols] = dq[:rows]
-        dq_other[:, cols] = dq[rows:]
-        dk = dot_nn(score_grad, query)
-        dv = dot_nn(prob_half, grad)
+        score_grads[head] = score_grad
+        probs[head] = prob_half[:chip]
+        query, grad = load(head)
+        dk = dot_nn(score_grad[chip:], query)
+        dv = dot_nn(prob_half[chip:], grad)
         if head == 0:
             dk_acc[...] = dk
             dv_acc[...] = dv
         else:
             dk_acc[...] += dk
             dv_acc[...] += dv
-    chip = 2 * rows
-    own_grad[:, :DH] = dk_acc[:chip]
-    own_grad[:, DH:] = dv_acc[:chip]
-    near_grad[:, :DH] = dk_acc[chip : 2 * chip].astype(jnp.bfloat16)
-    near_grad[:, DH:] = dv_acc[chip : 2 * chip].astype(jnp.bfloat16)
-    far_grad[:, :DH] = dk_acc[2 * chip :].astype(jnp.bfloat16)
-    far_grad[:, DH:] = dv_acc[2 * chip :].astype(jnp.bfloat16)
-
-
-def attention(queries, out_grad, q_other, do_other, blocks, bias):
-    rows = queries.shape[0]
+    for out, start in ((near_grad, 0), (far_grad, chip)):
+        out[:, :DH] = dk_acc[start : start + chip].astype(jnp.bfloat16)
+        out[:, DH:] = dv_acc[start : start + chip].astype(jnp.bfloat16)
+
+
+def attention(operands, bias):
+    rows = operands[0].shape[0]
     chip = 2 * rows
     keys = chip * (REACH + 1)
     return pl.pallas_call(
         attention_kernel,
+        out_shape=(
+            whole((chip, 2 * DH)),
+            whole((chip, 2 * DH)),
+            whole((GROUP, keys, chip)),
+            whole((GROUP, chip, chip)),
+        ),
+        scratch_shapes=[
+            pltpu.VMEM((keys - chip, DH), jnp.float32),
+            pltpu.VMEM((keys - chip, DH), jnp.float32),
+        ],
+        compiler_params=pltpu.CompilerParams(vmem_limit_bytes=24 * MIB),
+        cost_estimate=pl.CostEstimate(
+            flops=40 * keys * chip * DH * GROUP,
+            bytes_accessed=4 * MIB,
+            transcendentals=keys * chip * GROUP,
+        ),
+    )(*operands, bias)
+
+
+def own_kernel(
+    q_mine, do_mine, q_other, do_other, chip_pair, near_pair, far_pair, score_grads, probs,
+    dq_mine, dq_other, own_grad,
+):
+    key_t = jnp.concatenate([ref[:, :DH] for ref in (chip_pair, near_pair, far_pair)], axis=0).T
+    rows, chip = q_mine.shape[0], chip_pair.shape[0]
+    for head in range(GROUP):
+        cols = slice(head * DH, (head + 1) * DH)
+        query = jnp.concatenate([q_mine[:, cols], q_other[:, cols]], axis=0)
+        grad = jnp.concatenate([do_mine[:, cols], do_other[:, cols]], axis=0)
+        dq = dot_nn(key_t, score_grads[head]).T.astype(jnp.bfloat16)
+        dq_mine[:, cols] = dq[:rows]
+        dq_other[:, cols] = dq[rows:]
+        dk = dot_nn(score_grads[head, :chip], query)
+        dv = dot_nn(probs[head], grad)
+        if head == 0:
+            own_grad[:, :DH] = dk
+            own_grad[:, DH:] = dv
+        else:
+            own_grad[:, :DH] += dk
+            own_grad[:, DH:] += dv
+
+
+def own_gradients(operands, score_grads, probs):
+    rows = operands[0].shape[0]
+    chip = 2 * rows
+    return pl.pallas_call(
+        own_kernel,
         out_shape=(
             whole((rows, GROUP * DH)),
             whole((rows, GROUP * DH)),
             whole((chip, 2 * DH), jnp.float32),
-            whole((chip, 2 * DH)),
-            whole((chip, 2 * DH)),
-        ),
-        scratch_shapes=[
-            pltpu.VMEM((keys, DH), jnp.float32),
-            pltpu.VMEM((keys, DH), jnp.float32),
-        ],
-        compiler_params=pltpu.CompilerParams(vmem_limit_bytes=16 * MIB),
+        ),
+        compiler_params=pltpu.CompilerParams(vmem_limit_bytes=24 * MIB),
         cost_estimate=pl.CostEstimate(
-            flops=40 * keys * chip * DH * GROUP,
-            bytes_accessed=4 * 1024 * 1024,
-            transcendentals=keys * chip * GROUP,
-        ),
-    )(queries, out_grad, q_other, do_other, *blocks, bias)
+            flops=6 * score_grads.size * DH, bytes_accessed=6 * MIB, transcendentals=0
+        ),
+    )(*operands, score_grads, probs)
 
 
 def combine_kernel(own, near, far, out):
@@ -162,21 +242,21 @@
     )(own, near, far)
 
 
-def assemble_kernel(core_ref, mine, other, out):
+def assemble_kernel(here_ref, mine, other, out):
     width = mine.shape[1]
-    core = core_ref[0]
+    core = here_ref[1]
     out[:, pl.ds(pl.multiple_of(core * width, width), width)] = mine[...]
     out[:, pl.ds(pl.multiple_of((1 - core) * width, width), width)] = other[...]
 
 
-def assemble(core, mine, other):
+def assemble(here, mine, other):
     return pl.pallas_call(
         assemble_kernel,
         out_shape=whole((mine.shape[0], 2 * mine.shape[1])),
         in_specs=[SCALAR, pl.BlockSpec(), pl.BlockSpec()],
         compiler_params=SMALL,
         cost_estimate=pl.CostEstimate(flops=0, bytes_accessed=MIB, transcendentals=0),
-    )(core, mine, other)
+    )(here, mine, other)
 
 
 def project_kernel(places_ref, *refs, offset):
@@ -246,7 +326,7 @@
     core = lax.axis_index("core")
     n_chips = lax.axis_size("z_lo")
     swap = [(0, 1), (1, 0)]
-    core_ref = core.astype(jnp.int32).reshape(1)
+    here_ref = jnp.stack([z_lo, core]).astype(jnp.int32)
     places_ref = jnp.stack([lax.axis_index("y"), lax.axis_index("x")]).astype(jnp.int32)
 
     def half_of(array, which):
@@ -284,48 +364,31 @@
         lax.ppermute(chunks[k], "y", [(i, i ^ k) for i in range(n_y)]) for k in range(1, n_y)
     ]
 
-    seg_row = segment_ids[0]
-    lane = jnp.arange(rows, dtype=jnp.int32)
-
-    def places(chip_at, which):
-        start = chip_at * chip + which * rows
-        return (start + lane, lax.dynamic_slice_in_dim(seg_row, jnp.maximum(start, 0), rows, 0))
-
-    key_places = [
-        places(z_lo - distance, which)
-        for distance in range(REACH + 1)
-        for which in (core, 1 - core)
-    ]
-    key_pos = jnp.concatenate([place[0] for place in key_places])[:, None]
-    key_doc = jnp.concatenate([place[1] for place in key_places])[:, None]
-    query_pos = jnp.concatenate([place[0] for place in key_places[:2]])[None, :]
-    query_doc = jnp.concatenate([place[1] for place in key_places[:2]])[None, :]
-    allowed = (key_pos >= 0) & (key_pos <= query_pos) & (key_doc == query_doc)
-    bias = jnp.where(allowed, 0.0, MASKED).astype(jnp.float32)
-
-    dq_mine, dq_other, own_grad, near_grad, far_grad = attention(
-        q_mine, do_mine, q_other, do_other, blocks, bias
-    )
-    dq_back = lax.ppermute(dq_other, "core", swap)
-    query_grad = assemble(core_ref, dq_mine, dq_back)[None]
-
+    operands = (q_mine, do_mine, q_other, do_other, *blocks)
+    near_grad, far_grad, score_grads, probs = attention(
+        operands, make_bias(here_ref, segment_ids, rows)
+    )
+    dq_mine, dq_other, own_grad = own_gradients(operands, score_grads, probs)
     far_back, near_back = (
         lax.ppermute(part, ("z_lo", "core"), [(b, a) for a, b in behind(distance)])
         for distance, part in ((2, far_grad), (1, near_grad))
     )
-
-    near_back, query_grad = lax.optimization_barrier((near_back, query_grad))
 
     copies = combine(own_grad, near_back, far_back, n_y)
     gathered = lax.all_to_all(copies, "y", 0, 0, tiled=True)
     pieces, _ = lax.optimization_barrier((pieces, copies))
     both = [part for piece in pieces for part in (piece, lax.ppermute(piece, "core", swap))]
     n_x = lax.axis_size("x")
+    dq_other, gathered = lax.optimization_barrier((dq_other, gathered))
+    dq_back = lax.ppermute(dq_other, "core", swap)
+    query_grad = assemble(here_ref, dq_mine, dq_back)[None]
     parts = []
-    for k in (2, 1, 3):
+    for k in (3, 1, 2):
         term = project(places_ref, both, gathered, n_x, k, jnp.bfloat16)
         parts.append(lax.ppermute(term, "x", [(i, i ^ k) for i in range(n_x)]))
-    term = add_parts(project(places_ref, both, gathered, n_x, 0, jnp.float32), parts)
+    own_term = project(places_ref, both, gathered, n_x, 0, jnp.float32)
+    parts, query_grad = lax.optimization_barrier((parts, query_grad))
+    term = add_parts(own_term, parts)
     rest = ("z_hi", "z_lo", "core")
     n_rest = lax.axis_size(rest)
     spread = lax.all_to_all(

time: 98.4 us -> 96.4 us (0.980)
  local copies, waits for them, and re-layouts: 6.01 us -> 3.74 us
  waiting for transfers between devices: 20 us -> 22.2 us
  other arithmetic: 1.27 us -> 0.16 us
    ppermute x3, waiting for transfers between devices: 1.38 us -> 10.9 us  [per_device(): lax.ppermute(chunks[k], 'y', [(i, i ^ k) for i in range(n_y)])]
    ppermute x2, waiting for transfers between devices: 10.8 us -> 4.51 us  [per_device(): lax.ppermute(part, ('z_lo', 'core'), [(b, a) for a, b in behind(distance)])]
    unnamed x7 -> x4, local copies, waits for them, and re-layouts: 3.79 us -> 0.69 us
    ppermute x3, waiting for transfers between devices: 7.81 us -> 6.78 us  [per_device(): parts.append(lax.ppermute(term, 'x', [(i, i ^ k) for i in range(n_x)]))]
    pallas_call x1 -> x3, Pallas kernels: 7.25 us -> 7.21 us  [the longest x1 5.35 us: attention(): pl.pallas_call(attention_kernel, out_shape=(whole((chip, 2 * DH)), whole(...]
  transfers between devices with their start and end apart: 18 -> 18, of which waited for: 6 -> 6; matrix products, arithmetic and copies ran while one was open for 6% -> 2% of each run, Pallas kernels for 12% -> 14%
where the time goes in v7:
time: 96.4 us; the launch traced here: 96.1 us
  blocking collectives  29.5 us (31%)
  starting transfers between devices  25.1 us (26%)
  waiting for transfers between devices  22.2 us (23%)
  Pallas kernels  14.5 us (15%)
  local copies, waits for them, and re-layouts  3.74 us (4%)
    all_to_all x1, blocking collectives, per_device(): lax.all_to_all(term.reshape(n_rest, term.shape[0] // n_rest, term.shape[1...  18.1 us
    all_to_all x1, blocking collectives, per_device(): gathered = lax.all_to_all(copies, 'y', 0, 0, tiled=True)  11.5 us
    ppermute x3, waiting for transfers between devices, per_device(): lax.ppermute(chunks[k], 'y', [(i, i ^ k) for i in range(n_y)])  10.9 us
    ppermute x3, waiting for transfers between devices, per_device(): parts.append(lax.ppermute(term, 'x', [(i, i ^ k) for i in range(n_x)]))  6.78 us
    ppermute x2, starting transfers between devices, per_device(): lax.ppermute(chip_pair, ('z_lo', 'core'), behind(distance))  6.72 us
    pallas_call x1, Pallas kernels, attention(): pl.pallas_call(attention_kernel, out_shape=(whole((chip, 2 * DH)), whole(...  5.35 us
    ppermute x2, waiting for transfers between devices, per_device(): lax.ppermute(part, ('z_lo', 'core'), [(b, a) for a, b in behind(distance)])  4.51 us
    pallas_call x4, Pallas kernels, project(): pl.pallas_call(functools.partial(project_kernel, offset=offset), out_shap...  4.3 us
  transfers between devices with their start and end apart: 18, of which 6 were waited for; matrix products, arithmetic and copies ran while one was open for 2% of the time, Pallas kernels for 14%

profile of v7, /device:TPU:1, one launch (start us, length us, event | category | flops | bytes accessed | tf_op | source)
XLA Modules:
  0.0 96.1 jit_solution(1774537084697786754)
XLA Ops:
  0.6 1.0 %dynamic-slice_bitcast_fusion.4 = (bf16[128,128]{1,0:T(8,128)(2,1)S(1)}, bf16[128,128]{1,0:T(8,128)(2,1)S(1)}, bf16[128,128]{1,0:T(8,128)(2,1)S(1)}, bf16[128,128]{1,0:T(8,128)(2,1)S(1)}) fusion(bf16[1,128,256]{2,1,0:T(8,128)(2,1)} %param.8, s32[]{:T(128)S(6)} %select_n.18, s32[]{:T(128)S(6)} %select_n.17, bf16[1,128,256]{2,1,0:T(8,128)(2,1)} %param.7), kind=kLoop, calls=%fused_computation.5 | loop fusion | bytes 262152 | tf_op jit(solution)/shard_map/dynamic_slice | solution.py:334
  1.6 3.3 %collective-permute-start = (bf16[128,256]{1,0:T(8,128)(2,1)S(1)}, bf16[128,256]{1,0:T(8,128)(2,1)S(1)}, u32[]{:S(2)}, u32[]{:S(2)}) collective-permute-start(bf16[128,256]{1,0:T(8,128)(2,1)S(1)} %pad_maximum_fusion), channel_id=1, source_target_pairs={{0,1},{1,0},{2,3},{3,2},{4,5},{5,4},{6,7},{7,6},{8,9},{9,8},{10,11... | collective-permute-start | bytes 196616 | tf_op jit(solution)/shard_map/ppermute | solution.py:340
  5.0 2.1 %dynamic-slice_bitcast_fusion = (bf16[128,1024]{1,0:T(8,128)(2,1)S(1)}, bf16[128,1024]{1,0:T(8,128)(2,1)}, bf16[128,1024]{1,0:T(8,128)(2,1)}, bf16[128,1024]{1,0:T(8,128)(2,1)S(1)}) fusion(bf16[1,128,2048]{2,1,0:T(8,128)(2,1)} %param.9, s32[]{:T(128)S(6)} %select_n.19, s32[]{:T(128)S(6)} %select_n.16, bf16[1,128,2048]{2,1,0:T(8,128)(2,1)} %param.6), kind=kLoop, calls=%fused_computation | loop fusion | bytes 2097160 | tf_op jit(solution)/shard_map/dynamic_slice | solution.py:334
  7.0 0.0 collective-permute-done.swapped
  7.1 0.1 collective-permute-start.1
  7.2 0.5 collective-permute-start.2
  7.7 1.8 %collective-permute-start.6 = (bf16[256,256]{1,0:T(8,128)(2,1)S(1)}, bf16[256,256]{1,0:T(8,128)(2,1)S(1)}, u32[]{:S(2)}, u32[]{:S(2)}) collective-permute-start(bf16[256,256]{1,0:T(8,128)(2,1)S(1)} %shard_map.78.chip_pair), channel_id=1, source_target_pairs={{0,2},{1,3},{2,4},{3,5},{4,6},{5,7},{8,10},{9,11},{10,12},{11,13},... | collective-permute-start | bytes 393224 | tf_op jit(solution)/shard_map/ppermute | solution.py:357
  9.5 4.9 %collective-permute-start.7 = (bf16[256,256]{1,0:T(8,128)(2,1)S(1)}, bf16[256,256]{1,0:T(8,128)(2,1)S(1)}, u32[]{:S(2)}, u32[]{:S(2)}) collective-permute-start(bf16[256,256]{1,0:T(8,128)(2,1)S(1)} %shard_map.78.chip_pair), channel_id=1, source_target_pairs={{0,4},{1,5},{2,6},{3,7},{8,12},{9,13},{10,14},{11,15},{16,20},{17,... | collective-permute-start | bytes 393224 | tf_op jit(solution)/shard_map/ppermute | solution.py:357
  14.4 0.1 pad_add_fusion.1.here_ref
  14.5 0.7 copy-done.1
  15.2 0.7 shard_map.79.bias
  15.9 0.1 pad_add_fusion.place_ref.places_ref
  16.0 0.7 shard_map.77
  16.7 0.0 collective-permute-done.1.q_other
  16.7 0.0 collective-permute-done.2.do_other
  16.7 1.4 %collective-permute-start.3 = (bf16[128,2048]{1,0:T(8,128)(2,1)S(1)}, bf16[128,2048]{1,0:T(8,128)(2,1)S(1)}, u32[]{:S(2)}, u32[]{:S(2)}) collective-permute-start(bf16[128,2048]{1,0:T(8,128)(2,1)S(1)} %get-tuple-element.36), channel_id=1, source_target_pairs={{0,64},{64,0},{128,192},{192,128},{1,65},{65,1},{129,193},{193,129... | collective-permute-start | bytes 1572872 | tf_op jit(solution)/shard_map/ppermute | solution.py:364
  18.1 2.6 %collective-permute-start.4 = (bf16[128,2048]{1,0:T(8,128)(2,1)S(1)}, bf16[128,2048]{1,0:T(8,128)(2,1)S(1)}, u32[]{:S(2)}, u32[]{:S(2)}) collective-permute-start(bf16[128,2048]{1,0:T(8,128)(2,1)S(1)} %get-tuple-element.37), channel_id=1, source_target_pairs={{0,128},{64,192},{128,0},{192,64},{1,129},{65,193},{129,1},{193,65... | collective-permute-start | bytes 1572872 | tf_op jit(solution)/shard_map/ppermute | solution.py:364
  20.7 0.0 collective-permute-start.5
  20.7 0.0 collective-permute-done.6.near_pair
  20.7 0.0 collective-permute-done.7.far_pair
  20.8 5.3 %shard_map.80 = (bf16[256,256]{1,0:T(8,128)(2,1)S(1)}, bf16[256,256]{1,0:T(8,128)(2,1)S(1)}, bf16[8,768,256]{2,1,0:T(8,128)(2,1)S(1)}, bf16[8,256,256]{2,1,0:T(8,128)(2,1)S(1)}) custom-call(bf16[128,1024]{1,0:T(8,128)(2,1)S(1)} %get-tuple-element.65.q_mine, bf16[128,1024]{1,0:T(8,128)(2,1)S(1)} %get-tuple-element.56.do_mine, ...), custom_call_target="tpu_custom_call" | custom-call | flops 8053063680 | bytes 4194304 | tf_op jit(solution)/shard_map/pallas_call | solution.py:168
  26.1 1.3 %collective-permute-start.8 = (bf16[256,256]{1,0:T(8,128)(2,1)S(1)}, bf16[256,256]{1,0:T(8,128)(2,1)S(1)}, u32[]{:S(2)}, u32[]{:S(2)}) collective-permute-start(bf16[256,256]{1,0:T(8,128)(2,1)S(1)} %get-tuple-element.42), channel_id=1, source_target_pairs={{2,0},{3,1},{4,2},{5,3},{6,4},{7,5},{10,8},{11,9},{12,10},{13,11},... | collective-permute-start | bytes 393224 | tf_op jit(solution)/shard_map/ppermute | solution.py:373
  27.4 1.3 %collective-permute-start.9 = (bf16[256,256]{1,0:T(8,128)(2,1)S(1)}, bf16[256,256]{1,0:T(8,128)(2,1)S(1)}, u32[]{:S(2)}, u32[]{:S(2)}) collective-permute-start(bf16[256,256]{1,0:T(8,128)(2,1)S(1)} %get-tuple-element.43), channel_id=1, source_target_pairs={{4,0},{5,1},{6,2},{7,3},{12,8},{13,9},{14,10},{15,11},{20,16},{21,... | collective-permute-start | bytes 393224 | tf_op jit(solution)/shard_map/ppermute | solution.py:373
  28.7 1.1 %shard_map.81 = (bf16[128,1024]{1,0:T(8,128)(2,1)S(1)}, bf16[128,1024]{1,0:T(8,128)(2,1)S(1)}, f32[256,256]{1,0:T(8,128)S(1)}) custom-call(bf16[128,1024]{1,0:T(8,128)(2,1)S(1)} %get-tuple-element.65.q_mine, bf16[128,1024]{1,0:T(8,128)(2,1)S(1)} %get-tuple-element.56.do_mine, bf16[128,1024]{1,0:T(8,128)(2,1)S(1)} %collective-permute-done.1.q_other, ...), custom_call_target="tpu_custom_call" | custom-call | flops 1207959552 | bytes 6291456 | tf_op jit(solution)/shard_map/pallas_call | solution.py:215
  29.9 2.3 %collective-permute-done.8.near = bf16[256,256]{1,0:T(8,128)(2,1)S(1)} collective-permute-done((bf16[256,256]{1,0:T(8,128)(2,1)S(1)}, bf16[256,256]{1,0:T(8,128)(2,1)S(1)}, u32[]{:S(2)}, u32[]{:S(2)}) %collective-permute-start.8) | collective-permute-done | bytes 131104 | tf_op jit(solution)/shard_map/ppermute | solution.py:373
  32.1 2.2 %collective-permute-done.9.far = bf16[256,256]{1,0:T(8,128)(2,1)S(1)} collective-permute-done((bf16[256,256]{1,0:T(8,128)(2,1)S(1)}, bf16[256,256]{1,0:T(8,128)(2,1)S(1)}, u32[]{:S(2)}, u32[]{:S(2)}) %collective-permute-start.9) | collective-permute-done | bytes 131104 | tf_op jit(solution)/shard_map/ppermute | solution.py:373
  34.4 0.1 shard_map.82
  34.5 8.9 %collective-permute-done.4.refs_4_ = bf16[128,2048]{1,0:T(8,128)(2,1)S(1)} collective-permute-done((bf16[128,2048]{1,0:T(8,128)(2,1)S(1)}, bf16[128,2048]{1,0:T(8,128)(2,1)S(1)}, u32[]{:S(2)}, u32[]{:S(2)}) %collective-permute-start.4) | collective-permute-done | bytes 524320 | tf_op jit(solution)/shard_map/ppermute | solution.py:364
  43.4 2.0 %collective-permute-done.5.refs_6_ = bf16[128,2048]{1,0:T(8,128)(2,1)S(1)} collective-permute-done((bf16[128,2048]{1,0:T(8,128)(2,1)S(1)}, bf16[128,2048]{1,0:T(8,128)(2,1)S(1)}, u32[]{:S(2)}, u32[]{:S(2)}) %collective-permute-start.5) | collective-permute-done | bytes 524320 | tf_op jit(solution)/shard_map/ppermute | solution.py:364
  45.4 2.1 %collective-permute-start.10 = (bf16[128,2048]{1,0:T(8,128)(2,1)S(1)}, bf16[128,2048]{1,0:T(8,128)(2,1)S(1)}, u32[]{:S(2)}, u32[]{:S(2)}) collective-permute-start(bf16[128,2048]{1,0:T(8,128)(2,1)S(1)} %get-tuple-element.44.refs_0_), channel_id=1, source_target_pairs={{0,1},{1,0},{2,3},{3,2},{4,5},{5,4},{6,7},{7,6},{8,9},{9,8},{10,11... | collective-permute-start | bytes 1572872 | tf_op jit(solution)/shard_map/ppermute | solution.py:380
  47.5 0.0 collective-permute-start.11
  47.5 0.5 collective-permute-start.12
  48.0 0.0 collective-permute-start.13
  48.0 11.5 %all_to_all.10.refs_8_ = bf16[4,256,256]{2,1,0:T(8,128)(2,1)S(1)} all-to-all(bf16[4,256,256]{2,1,0:T(8,128)(2,1)S(1)} %shard_map.82), channel_id=1, replica_groups=mesh['y'=4,'x'=4,'z_hi'=2,'z_lo'=4,'core'=2] {'y'}, dimensions={0} | all-to-all | bytes 1048576 | tf_op jit(solution)/shard_map/all_to_all | solution.py:378
  59.5 1.4 %collective-permute-start.17 = (bf16[128,1024]{1,0:T(8,128)(2,1)S(1)}, bf16[128,1024]{1,0:T(8,128)(2,1)S(1)}, u32[]{:S(2)}, u32[]{:S(2)}) collective-permute-start(bf16[128,1024]{1,0:T(8,128)(2,1)S(1)} %get-tuple-element.51), channel_id=1, source_target_pairs={{0,1},{1,0},{2,3},{3,2},{4,5},{5,4},{6,7},{7,6},{8,9},{9,8},{10,11... | collective-permute-start | bytes 786440 | tf_op jit(solution)/shard_map/ppermute | solution.py:383
  60.9 1.1 %shard_map.85 = bf16[512,256]{1,0:T(8,128)(2,1)S(1)} custom-call(s32[2]{0:T(128)S(1)} %pad_add_fusion.place_ref.places_ref, bf16[128,2048]{1,0:T(8,128)(2,1)S(1)} %get-tuple-element.44.refs_0_, bf16[128,2048]{1,0:T(8,128)(2,1)S(1)} %collective-permute-done.10.refs_1_, bf16[128,2048]{1,0:T(8,128)(2,1)S(1)} %collective-permute-done.3.refs_2_, ...), custom_call_target="tpu_custom_call" | custom-call | flops 268435456 | bytes 2097152 | tf_op jit(solution)/shard_map/pallas_call | solution.py:275
  62.0 2.8 %collective-permute-start.16 = (bf16[512,256]{1,0:T(8,128)(2,1)S(1)}, bf16[512,256]{1,0:T(8,128)(2,1)S(1)}, u32[]{:S(2)}, u32[]{:S(2)}) collective-permute-start(bf16[512,256]{1,0:T(8,128)(2,1)S(1)} %shard_map.85), channel_id=1, source_target_pairs={{0,32},{16,48},{32,0},{48,16},{1,33},{17,49},{33,1},{49,17},{2,34}... | collective-permute-start | bytes 786440 | tf_op jit(solution)/shard_map/ppermute | solution.py:388
  64.8 1.1 %shard_map.84 = bf16[512,256]{1,0:T(8,128)(2,1)S(1)} custom-call(s32[2]{0:T(128)S(1)} %pad_add_fusion.place_ref.places_ref, bf16[128,2048]{1,0:T(8,128)(2,1)S(1)} %get-tuple-element.44.refs_0_, bf16[128,2048]{1,0:T(8,128)(2,1)S(1)} %collective-permute-done.10.refs_1_, bf16[128,2048]{1,0:T(8,128)(2,1)S(1)} %collective-permute-done.3.refs_2_, ...), custom_call_target="tpu_custom_call" | custom-call | flops 268435456 | bytes 2097152 | tf_op jit(solution)/shard_map/pallas_call | solution.py:275
  65.9 0.4 collective-permute-start.15
  66.3 1.1 %shard_map.83 = bf16[512,256]{1,0:T(8,128)(2,1)S(1)} custom-call(s32[2]{0:T(128)S(1)} %pad_add_fusion.place_ref.places_ref, bf16[128,2048]{1,0:T(8,128)(2,1)S(1)} %get-tuple-element.44.refs_0_, bf16[128,2048]{1,0:T(8,128)(2,1)S(1)} %collective-permute-done.10.refs_1_, bf16[128,2048]{1,0:T(8,128)(2,1)S(1)} %collective-permute-done.3.refs_2_, ...), custom_call_target="tpu_custom_call" | custom-call | flops 268435456 | bytes 2097152 | tf_op jit(solution)/shard_map/pallas_call | solution.py:275
  67.3 0.6 collective-permute-start.14
  68.0 1.4 %shard_map.86 = bf16[128,2048]{1,0:T(8,128)(2,1)} custom-call(s32[2]{0:T(128)S(1)} %pad_add_fusion.1.here_ref, bf16[128,1024]{1,0:T(8,128)(2,1)S(1)} %get-tuple-element.50.mine, bf16[128,1024]{1,0:T(8,128)(2,1)S(1)} %collective-permute-done.17.other), custom_call_target="tpu_custom_call" | custom-call | bytes 1048576 | tf_op jit(solution)/shard_map/pallas_call | solution.py:253
  69.3 1.1 %shard_map.87.refs_0_ = f32[512,256]{1,0:T(8,128)S(1)} custom-call(s32[2]{0:T(128)S(1)} %pad_add_fusion.place_ref.places_ref, bf16[128,2048]{1,0:T(8,128)(2,1)S(1)} %get-tuple-element.44.refs_0_, bf16[128,2048]{1,0:T(8,128)(2,1)S(1)} %collective-permute-done.10.refs_1_, bf16[128,2048]{1,0:T(8,128)(2,1)S(1)} %collective-permute-done.3.refs_2_, ...), custom_call_target="tpu_custom_call" | custom-call | flops 268435456 | bytes 2097152 | tf_op jit(solution)/shard_map/pallas_call | solution.py:275
  70.5 1.0 %collective-permute-done.16.refs_3_ = bf16[512,256]{1,0:T(8,128)(2,1)S(1)} collective-permute-done((bf16[512,256]{1,0:T(8,128)(2,1)S(1)}, bf16[512,256]{1,0:T(8,128)(2,1)S(1)}, u32[]{:S(2)}, u32[]{:S(2)}) %collective-permute-start.16) | collective-permute-done | bytes 262176 | tf_op jit(solution)/shard_map/ppermute | solution.py:388
  71.5 5.8 %collective-permute-done.15.refs_2_ = bf16[512,256]{1,0:T(8,128)(2,1)S(1)} collective-permute-done((bf16[512,256]{1,0:T(8,128)(2,1)S(1)}, bf16[512,256]{1,0:T(8,128)(2,1)S(1)}, u32[]{:S(2)}, u32[]{:S(2)}) %collective-permute-start.15) | collective-permute-done | bytes 262176 | tf_op jit(solution)/shard_map/ppermute | solution.py:388
  77.3 0.1 shard_map.88
  77.4 18.1 %all_to_all.11.parts = bf16[16,32,256]{2,1,0:T(8,128)(2,1)S(1)} all-to-all(bf16[16,32,256]{2,1,0:T(8,128)(2,1)S(1)} %bitcast.24), channel_id=1, replica_groups=mesh['y'=4,'x'=4,'z_hi'=2,'z_lo'=4,'core'=2] {'z_hi','z_lo','core'}, dimensions={0} | all-to-all | bytes 524288 | tf_op jit(solution)/shard_map/all_to_all | solution.py:394
  95.4 0.7 shard_map.89
  (12 shorter events, 0.1 us)
Async XLA Ops:
  0.6 15.3 %copy-start = (bf16[1,128,8192]{2,1,0:T(8,128)(2,1)S(1)}, bf16[1,128,8192]{2,1,0:T(8,128)(2,1)}, u32[]{:S(2)}) copy-start(bf16[1,128,8192]{2,1,0:T(8,128)(2,1)} %param.10) | copy-start | bytes 6291460
  1.6 5.4 %collective-permute-start = (bf16[128,256]{1,0:T(8,128)(2,1)S(1)}, bf16[128,256]{1,0:T(8,128)(2,1)S(1)}, u32[]{:S(2)}, u32[]{:S(2)}) collective-permute-start(bf16[128,256]{1,0:T(8,128)(2,1)S(1)} %pad_maximum_fusion), channel_id=1, source_target_pairs={{0,1},{1,0},{2,3},{3,2},{4,5},{5,4},{6,7},{7,6},{8,9},{9,8},{10,11... | collective-permute-start | bytes 196616 | tf_op jit(solution)/shard_map/ppermute | solution.py:340
  7.1 9.6 %collective-permute-start.1 = (bf16[128,1024]{1,0:T(8,128)(2,1)}, bf16[128,1024]{1,0:T(8,128)(2,1)S(1)}, u32[]{:S(2)}, u32[]{:S(2)}) collective-permute-start(bf16[128,1024]{1,0:T(8,128)(2,1)} %get-tuple-element.33), channel_id=1, source_target_pairs={{0,1},{1,0},{2,3},{3,2},{4,5},{5,4},{6,7},{7,6},{8,9},{9,8},{10,11... | collective-permute-start | bytes 786440 | tf_op jit(solution)/shard_map/ppermute | solution.py:347
  7.2 9.5 %collective-permute-start.2 = (bf16[128,1024]{1,0:T(8,128)(2,1)}, bf16[128,1024]{1,0:T(8,128)(2,1)S(1)}, u32[]{:S(2)}, u32[]{:S(2)}) collective-permute-start(bf16[128,1024]{1,0:T(8,128)(2,1)} %get-tuple-element.34), channel_id=1, source_target_pairs={{0,1},{1,0},{2,3},{3,2},{4,5},{5,4},{6,7},{7,6},{8,9},{9,8},{10,11... | collective-permute-start | bytes 786440 | tf_op jit(solution)/shard_map/ppermute | solution.py:347
  7.7 13.1 %collective-permute-start.6 = (bf16[256,256]{1,0:T(8,128)(2,1)S(1)}, bf16[256,256]{1,0:T(8,128)(2,1)S(1)}, u32[]{:S(2)}, u32[]{:S(2)}) collective-permute-start(bf16[256,256]{1,0:T(8,128)(2,1)S(1)} %shard_map.78.chip_pair), channel_id=1, source_target_pairs={{0,2},{1,3},{2,4},{3,5},{4,6},{5,7},{8,10},{9,11},{10,12},{11,13},... | collective-permute-start | bytes 393224 | tf_op jit(solution)/shard_map/ppermute | solution.py:357
  9.5 11.3 %collective-permute-start.7 = (bf16[256,256]{1,0:T(8,128)(2,1)S(1)}, bf16[256,256]{1,0:T(8,128)(2,1)S(1)}, u32[]{:S(2)}, u32[]{:S(2)}) collective-permute-start(bf16[256,256]{1,0:T(8,128)(2,1)S(1)} %shard_map.78.chip_pair), channel_id=1, source_target_pairs={{0,4},{1,5},{2,6},{3,7},{8,12},{9,13},{10,14},{11,15},{16,20},{17,... | collective-permute-start | bytes 393224 | tf_op jit(solution)/shard_map/ppermute | solution.py:357
  14.5 0.7 copy-start.1
  16.7 17.7 %collective-permute-start.3 = (bf16[128,2048]{1,0:T(8,128)(2,1)S(1)}, bf16[128,2048]{1,0:T(8,128)(2,1)S(1)}, u32[]{:S(2)}, u32[]{:S(2)}) collective-permute-start(bf16[128,2048]{1,0:T(8,128)(2,1)S(1)} %get-tuple-element.36), channel_id=1, source_target_pairs={{0,64},{64,0},{128,192},{192,128},{1,65},{65,1},{129,193},{193,129... | collective-permute-start | bytes 1572872 | tf_op jit(solution)/shard_map/ppermute | solution.py:364
  18.1 25.3 %collective-permute-start.4 = (bf16[128,2048]{1,0:T(8,128)(2,1)S(1)}, bf16[128,2048]{1,0:T(8,128)(2,1)S(1)}, u32[]{:S(2)}, u32[]{:S(2)}) collective-permute-start(bf16[128,2048]{1,0:T(8,128)(2,1)S(1)} %get-tuple-element.37), channel_id=1, source_target_pairs={{0,128},{64,192},{128,0},{192,64},{1,129},{65,193},{129,1},{193,65... | collective-permute-start | bytes 1572872 | tf_op jit(solution)/shard_map/ppermute | solution.py:364
  20.7 24.7 %collective-permute-start.5 = (bf16[128,2048]{1,0:T(8,128)(2,1)S(1)}, bf16[128,2048]{1,0:T(8,128)(2,1)S(1)}, u32[]{:S(2)}, u32[]{:S(2)}) collective-permute-start(bf16[128,2048]{1,0:T(8,128)(2,1)S(1)} %get-tuple-element.38), channel_id=1, source_target_pairs={{0,192},{64,128},{128,64},{192,0},{1,193},{65,129},{129,65},{193,1... | collective-permute-start | bytes 1572872 | tf_op jit(solution)/shard_map/ppermute | solution.py:364
  26.1 6.0 %collective-permute-start.8 = (bf16[256,256]{1,0:T(8,128)(2,1)S(1)}, bf16[256,256]{1,0:T(8,128)(2,1)S(1)}, u32[]{:S(2)}, u32[]{:S(2)}) collective-permute-start(bf16[256,256]{1,0:T(8,128)(2,1)S(1)} %get-tuple-element.42), channel_id=1, source_target_pairs={{2,0},{3,1},{4,2},{5,3},{6,4},{7,5},{10,8},{11,9},{12,10},{13,11},... | collective-permute-start | bytes 393224 | tf_op jit(solution)/shard_map/ppermute | solution.py:373
  27.4 7.0 %collective-permute-start.9 = (bf16[256,256]{1,0:T(8,128)(2,1)S(1)}, bf16[256,256]{1,0:T(8,128)(2,1)S(1)}, u32[]{:S(2)}, u32[]{:S(2)}) collective-permute-start(bf16[256,256]{1,0:T(8,128)(2,1)S(1)} %get-tuple-element.43), channel_id=1, source_target_pairs={{4,0},{5,1},{6,2},{7,3},{12,8},{13,9},{14,10},{15,11},{20,16},{21,... | collective-permute-start | bytes 393224 | tf_op jit(solution)/shard_map/ppermute | solution.py:373
  45.4 15.5 %collective-permute-start.10 = (bf16[128,2048]{1,0:T(8,128)(2,1)S(1)}, bf16[128,2048]{1,0:T(8,128)(2,1)S(1)}, u32[]{:S(2)}, u32[]{:S(2)}) collective-permute-start(bf16[128,2048]{1,0:T(8,128)(2,1)S(1)} %get-tuple-element.44.refs_0_), channel_id=1, source_target_pairs={{0,1},{1,0},{2,3},{3,2},{4,5},{5,4},{6,7},{7,6},{8,9},{9,8},{10,11... | collective-permute-start | bytes 1572872 | tf_op jit(solution)/shard_map/ppermute | solution.py:380
  47.5 13.3 %collective-permute-start.11 = (bf16[128,2048]{1,0:T(8,128)(2,1)S(1)}, bf16[128,2048]{1,0:T(8,128)(2,1)S(1)}, u32[]{:S(2)}, u32[]{:S(2)}) collective-permute-start(bf16[128,2048]{1,0:T(8,128)(2,1)S(1)} %collective-permute-done.3.refs_2_), channel_id=1, source_target_pairs={{0,1},{1,0},{2,3},{3,2},{4,5},{5,4},{6,7},{7,6},{8,9},{9,8},{10,11... | collective-permute-start | bytes 1572872 | tf_op jit(solution)/shard_map/ppermute | solution.py:380
  47.5 13.3 %collective-permute-start.12 = (bf16[128,2048]{1,0:T(8,128)(2,1)S(1)}, bf16[128,2048]{1,0:T(8,128)(2,1)S(1)}, u32[]{:S(2)}, u32[]{:S(2)}) collective-permute-start(bf16[128,2048]{1,0:T(8,128)(2,1)S(1)} %collective-permute-done.4.refs_4_), channel_id=1, source_target_pairs={{0,1},{1,0},{2,3},{3,2},{4,5},{5,4},{6,7},{7,6},{8,9},{9,8},{10,11... | collective-permute-start | bytes 1572872 | tf_op jit(solution)/shard_map/ppermute | solution.py:380
  48.0 12.8 %collective-permute-start.13 = (bf16[128,2048]{1,0:T(8,128)(2,1)S(1)}, bf16[128,2048]{1,0:T(8,128)(2,1)S(1)}, u32[]{:S(2)}, u32[]{:S(2)}) collective-permute-start(bf16[128,2048]{1,0:T(8,128)(2,1)S(1)} %collective-permute-done.5.refs_6_), channel_id=1, source_target_pairs={{0,1},{1,0},{2,3},{3,2},{4,5},{5,4},{6,7},{7,6},{8,9},{9,8},{10,11... | collective-permute-start | bytes 1572872 | tf_op jit(solution)/shard_map/ppermute | solution.py:380
  59.5 8.5 %collective-permute-start.17 = (bf16[128,1024]{1,0:T(8,128)(2,1)S(1)}, bf16[128,1024]{1,0:T(8,128)(2,1)S(1)}, u32[]{:S(2)}, u32[]{:S(2)}) collective-permute-start(bf16[128,1024]{1,0:T(8,128)(2,1)S(1)} %get-tuple-element.51), channel_id=1, source_target_pairs={{0,1},{1,0},{2,3},{3,2},{4,5},{5,4},{6,7},{7,6},{8,9},{9,8},{10,11... | collective-permute-start | bytes 786440 | tf_op jit(solution)/shard_map/ppermute | solution.py:383
  62.0 9.5 %collective-permute-start.16 = (bf16[512,256]{1,0:T(8,128)(2,1)S(1)}, bf16[512,256]{1,0:T(8,128)(2,1)S(1)}, u32[]{:S(2)}, u32[]{:S(2)}) collective-permute-start(bf16[512,256]{1,0:T(8,128)(2,1)S(1)} %shard_map.85), channel_id=1, source_target_pairs={{0,32},{16,48},{32,0},{48,16},{1,33},{17,49},{33,1},{49,17},{2,34}... | collective-permute-start | bytes 786440 | tf_op jit(solution)/shard_map/ppermute | solution.py:388
  65.9 11.4 %collective-permute-start.15 = (bf16[512,256]{1,0:T(8,128)(2,1)S(1)}, bf16[512,256]{1,0:T(8,128)(2,1)S(1)}, u32[]{:S(2)}, u32[]{:S(2)}) collective-permute-start(bf16[512,256]{1,0:T(8,128)(2,1)S(1)} %shard_map.84), channel_id=1, source_target_pairs={{0,16},{16,0},{32,48},{48,32},{1,17},{17,1},{33,49},{49,33},{2,18}... | collective-permute-start | bytes 786440 | tf_op jit(solution)/shard_map/ppermute | solution.py:388
  67.3 9.9 %collective-permute-start.14 = (bf16[512,256]{1,0:T(8,128)(2,1)S(1)}, bf16[512,256]{1,0:T(8,128)(2,1)S(1)}, u32[]{:S(2)}, u32[]{:S(2)}) collective-permute-start(bf16[512,256]{1,0:T(8,128)(2,1)S(1)} %shard_map.83), channel_id=1, source_target_pairs={{0,48},{16,32},{32,16},{48,0},{1,49},{17,33},{33,17},{49,1},{2,50}... | collective-permute-start | bytes 786440 | tf_op jit(solution)/shard_map/ppermute | solution.py:388

commit v8 on v7

--- a/solution.py
+++ b/solution.py
@@ -228,18 +228,30 @@
 
 def combine_kernel(own, near, far, out):
     total = own[...] + near[...].astype(jnp.float32) + far[...].astype(jnp.float32)
-    turned = total.T.astype(jnp.bfloat16)
-    for i in range(out.shape[0]):
-        out[i] = turned
-
-
-def combine(own, near, far, copies):
+    out[...] = total.T.astype(jnp.bfloat16)
+
+
+def combine(own, near, far):
     return pl.pallas_call(
         combine_kernel,
-        out_shape=whole((copies, own.shape[1], own.shape[0])),
-        compiler_params=SMALL,
-        cost_estimate=pl.CostEstimate(flops=0, bytes_accessed=2 * 1024 * 1024, transcendentals=0),
+        out_shape=whole((own.shape[1], own.shape[0])),
+        compiler_params=SMALL,
+        cost_estimate=pl.CostEstimate(flops=0, bytes_accessed=MIB, transcendentals=0),
     )(own, near, far)
+
+
+def stack_kernel(*refs):
+    for i, ref in enumerate(refs[:-1]):
+        refs[-1][i] = ref[...]
+
+
+def stack(pieces):
+    return pl.pallas_call(
+        stack_kernel,
+        out_shape=whole((len(pieces),) + pieces[0].shape),
+        compiler_params=pltpu.CompilerParams(vmem_limit_bytes=16 * MIB),
+        cost_estimate=pl.CostEstimate(flops=0, bytes_accessed=4 * MIB, transcendentals=0),
+    )(*pieces)
 
 
 def assemble_kernel(here_ref, mine, other, out):
@@ -259,30 +271,32 @@
     )(here, mine, other)
 
 
-def project_kernel(places_ref, *refs, offset):
-    pieces, grads, out = refs[:-2], refs[-2], refs[-1]
+def project_kernel(places_ref, mine, other, *refs, offset):
+    grads, out = refs[:-1], refs[-1]
     step = out.shape[0]
     columns = pl.ds(pl.multiple_of((places_ref[1] ^ offset) * step, step), step)
-    left = jnp.concatenate([grads[places_ref[0] ^ k] for k in range(len(pieces) // 2)], axis=1)
-    right = jnp.concatenate([ref[:, columns] for ref in pieces], axis=0)
+    left = jnp.concatenate([ref[...] for ref in grads], axis=1)
+    right = jnp.concatenate(
+        [ref[k, :, columns] for k in range(len(grads)) for ref in (mine, other)], axis=0
+    )
     out[...] = dot_nn(left, right).T.astype(out.dtype)
 
 
-def project(places, pieces, grads, blocks, offset, dtype):
-    rows, columns = pieces[0].shape
-    width = grads.shape[1]
+def project(places, mine, other, grads, blocks, offset, dtype):
+    rows, columns = mine.shape[1:]
+    width = grads[0].shape[0]
     step = columns // blocks
     return pl.pallas_call(
         functools.partial(project_kernel, offset=offset),
         out_shape=whole((step, width), dtype),
-        in_specs=[SCALAR] + [pl.BlockSpec()] * (len(pieces) + 1),
+        in_specs=[SCALAR] + [pl.BlockSpec()] * (len(grads) + 2),
         compiler_params=pltpu.CompilerParams(vmem_limit_bytes=16 * MIB),
         cost_estimate=pl.CostEstimate(
-            flops=2 * len(pieces) * rows * step * width,
+            flops=4 * len(grads) * rows * step * width,
             bytes_accessed=2 * MIB,
             transcendentals=0,
         ),
-    )(places, *pieces, grads)
+    )(places, mine, other, *grads)
 
 
 def add_kernel(*refs):
@@ -363,10 +377,11 @@
     pieces = [chunks[0]] + [
         lax.ppermute(chunks[k], "y", [(i, i ^ k) for i in range(n_y)]) for k in range(1, n_y)
     ]
+    docs, _ = lax.optimization_barrier((segment_ids, chunks[0]))
 
     operands = (q_mine, do_mine, q_other, do_other, *blocks)
     near_grad, far_grad, score_grads, probs = attention(
-        operands, make_bias(here_ref, segment_ids, rows)
+        operands, make_bias(here_ref, docs, rows)
     )
     dq_mine, dq_other, own_grad = own_gradients(operands, score_grads, probs)
     far_back, near_back = (
@@ -374,19 +389,23 @@
         for distance, part in ((2, far_grad), (1, near_grad))
     )
 
-    copies = combine(own_grad, near_back, far_back, n_y)
-    gathered = lax.all_to_all(copies, "y", 0, 0, tiled=True)
-    pieces, _ = lax.optimization_barrier((pieces, copies))
-    both = [part for piece in pieces for part in (piece, lax.ppermute(piece, "core", swap))]
+    def along_y(part, k):
+        return lax.ppermute(part, "y", [(i, i ^ k) for i in range(n_y)])
+
+    grad = combine(own_grad, near_back, far_back)
+    grads = [grad] + [along_y(grad, k) for k in range(1, n_y)]
+    pieces, grads[1:3] = lax.optimization_barrier((pieces, grads[1:3]))
+    mine = stack(pieces)
+    other = lax.ppermute(mine, "core", swap)
     n_x = lax.axis_size("x")
-    dq_other, gathered = lax.optimization_barrier((dq_other, gathered))
+    dq_other, grads = lax.optimization_barrier((dq_other, grads))
     dq_back = lax.ppermute(dq_other, "core", swap)
     query_grad = assemble(here_ref, dq_mine, dq_back)[None]
     parts = []
     for k in (3, 1, 2):
-        term = project(places_ref, both, gathered, n_x, k, jnp.bfloat16)
+        term = project(places_ref, mine, other, grads, n_x, k, jnp.bfloat16)
         parts.append(lax.ppermute(term, "x", [(i, i ^ k) for i in range(n_x)]))
-    own_term = project(places_ref, both, gathered, n_x, 0, jnp.float32)
+    own_term = project(places_ref, mine, other, grads, n_x, 0, jnp.float32)
     parts, query_grad = lax.optimization_barrier((parts, query_grad))
     term = add_parts(own_term, parts)
     rest = ("z_hi", "z_lo", "core")

time: 96.4 us -> 94.4 us (0.979)
  blocking collectives: 29.5 us -> 17.9 us
  waiting for transfers between devices: 22.2 us -> 28.8 us
  starting transfers between devices: 25.1 us -> 28.7 us
    all_to_all x1 -> x0, blocking collectives: 11.5 us -> none  [per_device(): gathered = lax.all_to_all(copies, 'y', 0, 0, tiled=True)]
    ppermute x3, waiting for transfers between devices: 10.9 us -> 0.01 us  [per_device(): lax.ppermute(chunks[k], 'y', [(i, i ^ k) for i in range(n_y)])]
    ppermute x4, waiting for transfers between devices: 0.01 us -> 10.6 us  [the longest x3 10.6 us: along_y(): return lax.ppermute(part, 'y', [(i, i ^ k) for i in range(n_y)])]
    ppermute x2, waiting for transfers between devices: 4.51 us -> 10.1 us  [per_device(): lax.ppermute(part, ('z_lo', 'core'), [(b, a) for a, b in behind(distance)])]
    ppermute x4, starting transfers between devices: 2.64 us -> 6.57 us  [the longest x3 4.42 us: along_y(): return lax.ppermute(part, 'y', [(i, i ^ k) for i in range(n_y)])]
    ppermute x3, waiting for transfers between devices: 6.78 us -> 8.11 us  [per_device(): parts.append(lax.ppermute(term, 'x', [(i, i ^ k) for i in range(n_x)]))]
  transfers between devices with their start and end apart: 18 -> 18, of which waited for: 6 -> 8; matrix products, arithmetic and copies ran while one was open for 2% -> 2% of each run, Pallas kernels for 14% -> 15%
where the time goes in v8:
time: 94.4 us; the launch traced here: 94.2 us
  waiting for transfers between devices  28.8 us (31%)
  starting transfers between devices  28.7 us (30%)
  blocking collectives  17.9 us (19%)
  Pallas kernels  14.6 us (15%)
  local copies, waits for them, and re-layouts  3.07 us (3%)
    all_to_all x1, blocking collectives, per_device(): lax.all_to_all(term.reshape(n_rest, term.shape[0] // n_rest, term.shape[1...  17.9 us
    ppermute x3, waiting for transfers between devices, along_y(): return lax.ppermute(part, 'y', [(i, i ^ k) for i in range(n_y)])  10.6 us
    ppermute x2, waiting for transfers between devices, per_device(): lax.ppermute(part, ('z_lo', 'core'), [(b, a) for a, b in behind(distance)])  10.1 us
    ppermute x3, waiting for transfers between devices, per_device(): parts.append(lax.ppermute(term, 'x', [(i, i ^ k) for i in range(n_x)]))  8.11 us
    ppermute x2, starting transfers between devices, per_device(): lax.ppermute(chip_pair, ('z_lo', 'core'), behind(distance))  6.72 us
    pallas_call x1, Pallas kernels, attention(): pl.pallas_call(attention_kernel, out_shape=(whole((chip, 2 * DH)), whole(...  5.34 us
    ppermute x3, starting transfers between devices, along_y(): return lax.ppermute(part, 'y', [(i, i ^ k) for i in range(n_y)])  4.42 us
    pallas_call x4, Pallas kernels, project(): pl.pallas_call(functools.partial(project_kernel, offset=offset), out_shap...  4.29 us
  transfers between devices with their start and end apart: 18, of which 8 were waited for; matrix products, arithmetic and copies ran while one was open for 2% of the time, Pallas kernels for 15%

profile of v8, /device:TPU:1, one launch (start us, length us, event | category | flops | bytes accessed | tf_op | source)
XLA Modules:
  0.0 94.2 jit_solution(18047067448466837487)
XLA Ops:
  0.6 1.0 %dynamic-slice_bitcast_fusion.4 = (bf16[128,128]{1,0:T(8,128)(2,1)S(1)}, bf16[128,128]{1,0:T(8,128)(2,1)S(1)}, bf16[128,128]{1,0:T(8,128)(2,1)S(1)}, bf16[128,128]{1,0:T(8,128)(2,1)S(1)}) fusion(bf16[1,128,256]{2,1,0:T(8,128)(2,1)} %param.8, s32[]{:T(128)S(6)} %select_n.18, s32[]{:T(128)S(6)} %select_n.17, bf16[1,128,256]{2,1,0:T(8,128)(2,1)} %param.7), kind=kLoop, calls=%fused_computation.5 | loop fusion | bytes 262152 | tf_op jit(solution)/shard_map/dynamic_slice | solution.py:348
  1.6 3.3 %collective-permute-start = (bf16[128,256]{1,0:T(8,128)(2,1)S(1)}, bf16[128,256]{1,0:T(8,128)(2,1)S(1)}, u32[]{:S(2)}, u32[]{:S(2)}) collective-permute-start(bf16[128,256]{1,0:T(8,128)(2,1)S(1)} %pad_maximum_fusion), channel_id=1, source_target_pairs={{0,1},{1,0},{2,3},{3,2},{4,5},{5,4},{6,7},{7,6},{8,9},{9,8},{10,11... | collective-permute-start | bytes 196616 | tf_op jit(solution)/shard_map/ppermute | solution.py:354
  5.0 2.1 %dynamic-slice_bitcast_fusion = (bf16[128,1024]{1,0:T(8,128)(2,1)S(1)}, bf16[128,1024]{1,0:T(8,128)(2,1)}, bf16[128,1024]{1,0:T(8,128)(2,1)}, bf16[128,1024]{1,0:T(8,128)(2,1)S(1)}) fusion(bf16[1,128,2048]{2,1,0:T(8,128)(2,1)} %param.9, s32[]{:T(128)S(6)} %select_n.19, s32[]{:T(128)S(6)} %select_n.16, bf16[1,128,2048]{2,1,0:T(8,128)(2,1)} %param.6), kind=kLoop, calls=%fused_computation | loop fusion | bytes 2097160 | tf_op jit(solution)/shard_map/dynamic_slice | solution.py:348
  7.1 0.0 collective-permute-done.swapped
  7.1 0.1 collective-permute-start.1
  7.2 0.5 collective-permute-start.2
  7.7 3.2 %collective-permute-start.7 = (bf16[256,256]{1,0:T(8,128)(2,1)S(1)}, bf16[256,256]{1,0:T(8,128)(2,1)S(1)}, u32[]{:S(2)}, u32[]{:S(2)}) collective-permute-start(bf16[256,256]{1,0:T(8,128)(2,1)S(1)} %shard_map.78.chip_pair), channel_id=1, source_target_pairs={{0,4},{1,5},{2,6},{3,7},{8,12},{9,13},{10,14},{11,15},{16,20},{17,... | collective-permute-start | bytes 393224 | tf_op jit(solution)/shard_map/ppermute | solution.py:371
  10.9 3.5 %collective-permute-start.6 = (bf16[256,256]{1,0:T(8,128)(2,1)S(1)}, bf16[256,256]{1,0:T(8,128)(2,1)S(1)}, u32[]{:S(2)}, u32[]{:S(2)}) collective-permute-start(bf16[256,256]{1,0:T(8,128)(2,1)S(1)} %shard_map.78.chip_pair), channel_id=1, source_target_pairs={{0,2},{1,3},{2,4},{3,5},{4,6},{5,7},{8,10},{9,11},{10,12},{11,13},... | collective-permute-start | bytes 393224 | tf_op jit(solution)/shard_map/ppermute | solution.py:371
  14.4 0.1 pad_add_fusion.place_ref.places_ref
  14.5 0.7 shard_map.77
  15.2 0.1 pad_add_fusion.1.here_ref
  15.3 1.3 %collective-permute-start.3 = (bf16[128,2048]{1,0:T(8,128)(2,1)S(1)}, bf16[128,2048]{1,0:T(8,128)(2,1)S(1)}, u32[]{:S(2)}, u32[]{:S(2)}) collective-permute-start(bf16[128,2048]{1,0:T(8,128)(2,1)S(1)} %get-tuple-element.42), channel_id=1, source_target_pairs={{0,64},{64,0},{128,192},{192,128},{1,65},{65,1},{129,193},{193,129... | collective-permute-start | bytes 1572872 | tf_op jit(solution)/shard_map/ppermute | solution.py:378
  16.7 2.6 %collective-permute-start.4 = (bf16[128,2048]{1,0:T(8,128)(2,1)S(1)}, bf16[128,2048]{1,0:T(8,128)(2,1)S(1)}, u32[]{:S(2)}, u32[]{:S(2)}) collective-permute-start(bf16[128,2048]{1,0:T(8,128)(2,1)S(1)} %get-tuple-element.43), channel_id=1, source_target_pairs={{0,128},{64,192},{128,0},{192,64},{1,129},{65,193},{129,1},{193,65... | collective-permute-start | bytes 1572872 | tf_op jit(solution)/shard_map/ppermute | solution.py:378
  19.3 0.7 shard_map.79.bias
  20.0 0.0 collective-permute-done.6.near_pair
  20.0 5.3 %shard_map.80 = (bf16[256,256]{1,0:T(8,128)(2,1)S(1)}, bf16[256,256]{1,0:T(8,128)(2,1)S(1)}, bf16[8,768,256]{2,1,0:T(8,128)(2,1)S(1)}, bf16[8,256,256]{2,1,0:T(8,128)(2,1)S(1)}) custom-call(bf16[128,1024]{1,0:T(8,128)(2,1)S(1)} %get-tuple-element.77.q_mine, bf16[128,1024]{1,0:T(8,128)(2,1)S(1)} %get-tuple-element.68.do_mine, ...), custom_call_target="tpu_custom_call" | custom-call | flops 8053063680 | bytes 4194304 | tf_op jit(solution)/shard_map/pallas_call | solution.py:168
  25.4 1.3 %collective-permute-start.8 = (bf16[256,256]{1,0:T(8,128)(2,1)S(1)}, bf16[256,256]{1,0:T(8,128)(2,1)S(1)}, u32[]{:S(2)}, u32[]{:S(2)}) collective-permute-start(bf16[256,256]{1,0:T(8,128)(2,1)S(1)} %get-tuple-element.49), channel_id=1, source_target_pairs={{2,0},{3,1},{4,2},{5,3},{6,4},{7,5},{10,8},{11,9},{12,10},{13,11},... | collective-permute-start | bytes 393224 | tf_op jit(solution)/shard_map/ppermute | solution.py:388
  26.7 1.3 %collective-permute-start.9 = (bf16[256,256]{1,0:T(8,128)(2,1)S(1)}, bf16[256,256]{1,0:T(8,128)(2,1)S(1)}, u32[]{:S(2)}, u32[]{:S(2)}) collective-permute-start(bf16[256,256]{1,0:T(8,128)(2,1)S(1)} %get-tuple-element.50), channel_id=1, source_target_pairs={{4,0},{5,1},{6,2},{7,3},{12,8},{13,9},{14,10},{15,11},{20,16},{21,... | collective-permute-start | bytes 393224 | tf_op jit(solution)/shard_map/ppermute | solution.py:388
  28.0 1.1 %shard_map.81 = (bf16[128,1024]{1,0:T(8,128)(2,1)S(1)}, bf16[128,1024]{1,0:T(8,128)(2,1)S(1)}, f32[256,256]{1,0:T(8,128)S(1)}) custom-call(bf16[128,1024]{1,0:T(8,128)(2,1)S(1)} %get-tuple-element.77.q_mine, bf16[128,1024]{1,0:T(8,128)(2,1)S(1)} %get-tuple-element.68.do_mine, bf16[128,1024]{1,0:T(8,128)(2,1)S(1)} %collective-permute-done.1.q_other, ...), custom_call_target="tpu_custom_call" | custom-call | flops 1207959552 | bytes 6291456 | tf_op jit(solution)/shard_map/pallas_call | solution.py:215
  29.1 2.3 %collective-permute-done.8.near = bf16[256,256]{1,0:T(8,128)(2,1)S(1)} collective-permute-done((bf16[256,256]{1,0:T(8,128)(2,1)S(1)}, bf16[256,256]{1,0:T(8,128)(2,1)S(1)}, u32[]{:S(2)}, u32[]{:S(2)}) %collective-permute-start.8) | collective-permute-done | bytes 131104 | tf_op jit(solution)/shard_map/ppermute | solution.py:388
  31.4 7.8 %collective-permute-done.9.far = bf16[256,256]{1,0:T(8,128)(2,1)S(1)} collective-permute-done((bf16[256,256]{1,0:T(8,128)(2,1)S(1)}, bf16[256,256]{1,0:T(8,128)(2,1)S(1)}, u32[]{:S(2)}, u32[]{:S(2)}) %collective-permute-start.9) | collective-permute-done | bytes 131104 | tf_op jit(solution)/shard_map/ppermute | solution.py:388
  39.2 0.1 shard_map.82.refs_0_
  39.3 3.0 %collective-permute-start.11 = (bf16[256,256]{1,0:T(8,128)(2,1)S(1)}, bf16[256,256]{1,0:T(8,128)(2,1)S(1)}, u32[]{:S(2)}, u32[]{:S(2)}) collective-permute-start(bf16[256,256]{1,0:T(8,128)(2,1)S(1)} %shard_map.82.refs_0_), channel_id=1, source_target_pairs={{0,128},{64,192},{128,0},{192,64},{1,129},{65,193},{129,1},{193,65... | collective-permute-start | bytes 393224 | tf_op jit(solution)/shard_map/ppermute | solution.py:393
  42.3 0.4 collective-permute-start.10
  42.7 2.1 %collective-permute-done.11.refs_2_ = bf16[256,256]{1,0:T(8,128)(2,1)S(1)} collective-permute-done((bf16[256,256]{1,0:T(8,128)(2,1)S(1)}, bf16[256,256]{1,0:T(8,128)(2,1)S(1)}, u32[]{:S(2)}, u32[]{:S(2)}) %collective-permute-start.11) | collective-permute-done | bytes 131104 | tf_op jit(solution)/shard_map/ppermute | solution.py:393
  44.8 3.3 %collective-permute-done.10.refs_1_ = bf16[256,256]{1,0:T(8,128)(2,1)S(1)} collective-permute-done((bf16[256,256]{1,0:T(8,128)(2,1)S(1)}, bf16[256,256]{1,0:T(8,128)(2,1)S(1)}, u32[]{:S(2)}, u32[]{:S(2)}) %collective-permute-start.10) | collective-permute-done | bytes 131104 | tf_op jit(solution)/shard_map/ppermute | solution.py:393
  48.1 0.0 collective-permute-done.3.refs_1_
  48.1 0.0 collective-permute-done.4.refs_2_
  48.1 0.0 collective-permute-done.5.refs_3_
  48.1 0.1 shard_map.83.mine
  48.2 2.2 %collective-permute-start.12 = (bf16[4,128,2048]{2,1,0:T(8,128)(2,1)S(1)}, bf16[4,128,2048]{2,1,0:T(8,128)(2,1)S(1)}, u32[]{:S(2)}, u32[]{:S(2)}) collective-permute-start(bf16[4,128,2048]{2,1,0:T(8,128)(2,1)S(1)} %shard_map.83.mine), channel_id=1, source_target_pairs={{0,1},{1,0},{2,3},{3,2},{4,5},{5,4},{6,7},{7,6},{8,9},{9,8},{10,11... | collective-permute-start | bytes 6291464 | tf_op jit(solution)/shard_map/ppermute | solution.py:399
  50.4 1.0 %collective-permute-start.13 = (bf16[256,256]{1,0:T(8,128)(2,1)S(1)}, bf16[256,256]{1,0:T(8,128)(2,1)S(1)}, u32[]{:S(2)}, u32[]{:S(2)}) collective-permute-start(bf16[256,256]{1,0:T(8,128)(2,1)S(1)} %shard_map.82.refs_0_), channel_id=1, source_target_pairs={{0,192},{64,128},{128,64},{192,0},{1,193},{65,129},{129,65},{193,1... | collective-permute-start | bytes 393224 | tf_op jit(solution)/shard_map/ppermute | solution.py:393
  51.4 5.3 %collective-permute-done.13.refs_3_ = bf16[256,256]{1,0:T(8,128)(2,1)S(1)} collective-permute-done((bf16[256,256]{1,0:T(8,128)(2,1)S(1)}, bf16[256,256]{1,0:T(8,128)(2,1)S(1)}, u32[]{:S(2)}, u32[]{:S(2)}) %collective-permute-start.13) | collective-permute-done | bytes 131104 | tf_op jit(solution)/shard_map/ppermute | solution.py:393
  56.7 0.9 collective-permute-start.17
  57.5 1.1 %shard_map.84 = bf16[512,256]{1,0:T(8,128)(2,1)S(1)} custom-call(s32[2]{0:T(128)S(1)} %pad_add_fusion.place_ref.places_ref, bf16[4,128,2048]{2,1,0:T(8,128)(2,1)S(1)} %shard_map.83.mine, bf16[4,128,2048]{2,1,0:T(8,128)(2,1)S(1)} %collective-permute-done.12.other, bf16[256,256]{1,0:T(8,128)(2,1)S(1)} %shard_map.82.refs_0_, ...), custom_call_target="tpu_custom_call" | custom-call | flops 268435456 | bytes 2097152 | tf_op jit(solution)/shard_map/pallas_call | solution.py:289
  58.6 2.6 %collective-permute-start.14 = (bf16[512,256]{1,0:T(8,128)(2,1)S(1)}, bf16[512,256]{1,0:T(8,128)(2,1)S(1)}, u32[]{:S(2)}, u32[]{:S(2)}) collective-permute-start(bf16[512,256]{1,0:T(8,128)(2,1)S(1)} %shard_map.84), channel_id=1, source_target_pairs={{0,48},{16,32},{32,16},{48,0},{1,49},{17,33},{33,17},{49,1},{2,50}... | collective-permute-start | bytes 786440 | tf_op jit(solution)/shard_map/ppermute | solution.py:407
  61.2 1.1 %shard_map.85 = bf16[512,256]{1,0:T(8,128)(2,1)S(1)} custom-call(s32[2]{0:T(128)S(1)} %pad_add_fusion.place_ref.places_ref, bf16[4,128,2048]{2,1,0:T(8,128)(2,1)S(1)} %shard_map.83.mine, bf16[4,128,2048]{2,1,0:T(8,128)(2,1)S(1)} %collective-permute-done.12.other, bf16[256,256]{1,0:T(8,128)(2,1)S(1)} %shard_map.82.refs_0_, ...), custom_call_target="tpu_custom_call" | custom-call | flops 268435456 | bytes 2097152 | tf_op jit(solution)/shard_map/pallas_call | solution.py:289
  62.2 0.1 collective-permute-start.15
  62.3 1.1 %shard_map.86 = bf16[512,256]{1,0:T(8,128)(2,1)S(1)} custom-call(s32[2]{0:T(128)S(1)} %pad_add_fusion.place_ref.places_ref, bf16[4,128,2048]{2,1,0:T(8,128)(2,1)S(1)} %shard_map.83.mine, bf16[4,128,2048]{2,1,0:T(8,128)(2,1)S(1)} %collective-permute-done.12.other, bf16[256,256]{1,0:T(8,128)(2,1)S(1)} %shard_map.82.refs_0_, ...), custom_call_target="tpu_custom_call" | custom-call | flops 268435456 | bytes 2097152 | tf_op jit(solution)/shard_map/pallas_call | solution.py:289
  63.4 1.4 %collective-permute-start.16 = (bf16[512,256]{1,0:T(8,128)(2,1)S(1)}, bf16[512,256]{1,0:T(8,128)(2,1)S(1)}, u32[]{:S(2)}, u32[]{:S(2)}) collective-permute-start(bf16[512,256]{1,0:T(8,128)(2,1)S(1)} %shard_map.86), channel_id=1, source_target_pairs={{0,32},{16,48},{32,0},{48,16},{1,33},{17,49},{33,1},{49,17},{2,34}... | collective-permute-start | bytes 786440 | tf_op jit(solution)/shard_map/ppermute | solution.py:407
  64.9 1.4 %shard_map.87 = bf16[128,2048]{1,0:T(8,128)(2,1)} custom-call(s32[2]{0:T(128)S(1)} %pad_add_fusion.1.here_ref, bf16[128,1024]{1,0:T(8,128)(2,1)S(1)} %get-tuple-element.62.mine, bf16[128,1024]{1,0:T(8,128)(2,1)S(1)} %collective-permute-done.17.other), custom_call_target="tpu_custom_call" | custom-call | bytes 1048576 | tf_op jit(solution)/shard_map/pallas_call | solution.py:265
  66.2 1.1 %shard_map.88.refs_0_ = f32[512,256]{1,0:T(8,128)S(1)} custom-call(s32[2]{0:T(128)S(1)} %pad_add_fusion.place_ref.places_ref, bf16[4,128,2048]{2,1,0:T(8,128)(2,1)S(1)} %shard_map.83.mine, bf16[4,128,2048]{2,1,0:T(8,128)(2,1)S(1)} %collective-permute-done.12.other, bf16[256,256]{1,0:T(8,128)(2,1)S(1)} %shard_map.82.refs_0_, ...), custom_call_target="tpu_custom_call" | custom-call | flops 268435456 | bytes 2097152 | tf_op jit(solution)/shard_map/pallas_call | solution.py:289
  67.3 0.5 collective-permute-done.14.refs_1_
  67.8 2.1 %collective-permute-done.15.refs_2_ = bf16[512,256]{1,0:T(8,128)(2,1)S(1)} collective-permute-done((bf16[512,256]{1,0:T(8,128)(2,1)S(1)}, bf16[512,256]{1,0:T(8,128)(2,1)S(1)}, u32[]{:S(2)}, u32[]{:S(2)}) %collective-permute-start.15) | collective-permute-done | bytes 262176 | tf_op jit(solution)/shard_map/ppermute | solution.py:407
  69.9 5.5 %collective-permute-done.16.refs_3_ = bf16[512,256]{1,0:T(8,128)(2,1)S(1)} collective-permute-done((bf16[512,256]{1,0:T(8,128)(2,1)S(1)}, bf16[512,256]{1,0:T(8,128)(2,1)S(1)}, u32[]{:S(2)}, u32[]{:S(2)}) %collective-permute-start.16) | collective-permute-done | bytes 262176 | tf_op jit(solution)/shard_map/ppermute | solution.py:407
  75.5 0.1 shard_map.89
  75.6 17.9 %all_to_all.5.parts = bf16[16,32,256]{2,1,0:T(8,128)(2,1)S(1)} all-to-all(bf16[16,32,256]{2,1,0:T(8,128)(2,1)S(1)} %bitcast.24), channel_id=1, replica_groups=mesh['y'=4,'x'=4,'z_hi'=2,'z_lo'=4,'core'=2] {'z_hi','z_lo','core'}, dimensions={0} | all-to-all | bytes 524288 | tf_op jit(solution)/shard_map/all_to_all | solution.py:413
  93.5 0.7 shard_map.90
  (12 shorter events, 0.1 us)
Async XLA Ops:
  0.6 13.9 %copy-start = (bf16[1,128,8192]{2,1,0:T(8,128)(2,1)S(1)}, bf16[1,128,8192]{2,1,0:T(8,128)(2,1)}, u32[]{:S(2)}) copy-start(bf16[1,128,8192]{2,1,0:T(8,128)(2,1)} %param.10) | copy-start | bytes 6291460
  1.6 5.4 %collective-permute-start = (bf16[128,256]{1,0:T(8,128)(2,1)S(1)}, bf16[128,256]{1,0:T(8,128)(2,1)S(1)}, u32[]{:S(2)}, u32[]{:S(2)}) collective-permute-start(bf16[128,256]{1,0:T(8,128)(2,1)S(1)} %pad_maximum_fusion), channel_id=1, source_target_pairs={{0,1},{1,0},{2,3},{3,2},{4,5},{5,4},{6,7},{7,6},{8,9},{9,8},{10,11... | collective-permute-start | bytes 196616 | tf_op jit(solution)/shard_map/ppermute | solution.py:354
  5.0 14.3 %copy-start.1 = (s32[1,1024]{1,0:T(1,128)S(1)}, s32[1,1024]{1,0:T(1,128)}, u32[]{:S(2)}) copy-start(s32[1,1024]{1,0:T(1,128)} %docs) | copy-start | bytes 12292
  7.1 8.2 %collective-permute-start.1 = (bf16[128,1024]{1,0:T(8,128)(2,1)}, bf16[128,1024]{1,0:T(8,128)(2,1)S(1)}, u32[]{:S(2)}, u32[]{:S(2)}) collective-permute-start(bf16[128,1024]{1,0:T(8,128)(2,1)} %get-tuple-element.39), channel_id=1, source_target_pairs={{0,1},{1,0},{2,3},{3,2},{4,5},{5,4},{6,7},{7,6},{8,9},{9,8},{10,11... | collective-permute-start | bytes 786440 | tf_op jit(solution)/shard_map/ppermute | solution.py:361
  7.2 8.1 %collective-permute-start.2 = (bf16[128,1024]{1,0:T(8,128)(2,1)}, bf16[128,1024]{1,0:T(8,128)(2,1)S(1)}, u32[]{:S(2)}, u32[]{:S(2)}) collective-permute-start(bf16[128,1024]{1,0:T(8,128)(2,1)} %get-tuple-element.40), channel_id=1, source_target_pairs={{0,1},{1,0},{2,3},{3,2},{4,5},{5,4},{6,7},{7,6},{8,9},{9,8},{10,11... | collective-permute-start | bytes 786440 | tf_op jit(solution)/shard_map/ppermute | solution.py:361
  7.7 12.3 %collective-permute-start.7 = (bf16[256,256]{1,0:T(8,128)(2,1)S(1)}, bf16[256,256]{1,0:T(8,128)(2,1)S(1)}, u32[]{:S(2)}, u32[]{:S(2)}) collective-permute-start(bf16[256,256]{1,0:T(8,128)(2,1)S(1)} %shard_map.78.chip_pair), channel_id=1, source_target_pairs={{0,4},{1,5},{2,6},{3,7},{8,12},{9,13},{10,14},{11,15},{16,20},{17,... | collective-permute-start | bytes 393224 | tf_op jit(solution)/shard_map/ppermute | solution.py:371
  10.9 9.2 %collective-permute-start.6 = (bf16[256,256]{1,0:T(8,128)(2,1)S(1)}, bf16[256,256]{1,0:T(8,128)(2,1)S(1)}, u32[]{:S(2)}, u32[]{:S(2)}) collective-permute-start(bf16[256,256]{1,0:T(8,128)(2,1)S(1)} %shard_map.78.chip_pair), channel_id=1, source_target_pairs={{0,2},{1,3},{2,4},{3,5},{4,6},{5,7},{8,10},{9,11},{10,12},{11,13},... | collective-permute-start | bytes 393224 | tf_op jit(solution)/shard_map/ppermute | solution.py:371
  15.3 32.8 %collective-permute-start.3 = (bf16[128,2048]{1,0:T(8,128)(2,1)S(1)}, bf16[128,2048]{1,0:T(8,128)(2,1)S(1)}, u32[]{:S(2)}, u32[]{:S(2)}) collective-permute-start(bf16[128,2048]{1,0:T(8,128)(2,1)S(1)} %get-tuple-element.42), channel_id=1, source_target_pairs={{0,64},{64,0},{128,192},{192,128},{1,65},{65,1},{129,193},{193,129... | collective-permute-start | bytes 1572872 | tf_op jit(solution)/shard_map/ppermute | solution.py:378
  16.7 31.4 %collective-permute-start.4 = (bf16[128,2048]{1,0:T(8,128)(2,1)S(1)}, bf16[128,2048]{1,0:T(8,128)(2,1)S(1)}, u32[]{:S(2)}, u32[]{:S(2)}) collective-permute-start(bf16[128,2048]{1,0:T(8,128)(2,1)S(1)} %get-tuple-element.43), channel_id=1, source_target_pairs={{0,128},{64,192},{128,0},{192,64},{1,129},{65,193},{129,1},{193,65... | collective-permute-start | bytes 1572872 | tf_op jit(solution)/shard_map/ppermute | solution.py:378
  19.3 28.8 %collective-permute-start.5 = (bf16[128,2048]{1,0:T(8,128)(2,1)S(1)}, bf16[128,2048]{1,0:T(8,128)(2,1)S(1)}, u32[]{:S(2)}, u32[]{:S(2)}) collective-permute-start(bf16[128,2048]{1,0:T(8,128)(2,1)S(1)} %get-tuple-element.44), channel_id=1, source_target_pairs={{0,192},{64,128},{128,64},{192,0},{1,193},{65,129},{129,65},{193,1... | collective-permute-start | bytes 1572872 | tf_op jit(solution)/shard_map/ppermute | solution.py:378
  25.4 6.0 %collective-permute-start.8 = (bf16[256,256]{1,0:T(8,128)(2,1)S(1)}, bf16[256,256]{1,0:T(8,128)(2,1)S(1)}, u32[]{:S(2)}, u32[]{:S(2)}) collective-permute-start(bf16[256,256]{1,0:T(8,128)(2,1)S(1)} %get-tuple-element.49), channel_id=1, source_target_pairs={{2,0},{3,1},{4,2},{5,3},{6,4},{7,5},{10,8},{11,9},{12,10},{13,11},... | collective-permute-start | bytes 393224 | tf_op jit(solution)/shard_map/ppermute | solution.py:388
  26.7 12.5 %collective-permute-start.9 = (bf16[256,256]{1,0:T(8,128)(2,1)S(1)}, bf16[256,256]{1,0:T(8,128)(2,1)S(1)}, u32[]{:S(2)}, u32[]{:S(2)}) collective-permute-start(bf16[256,256]{1,0:T(8,128)(2,1)S(1)} %get-tuple-element.50), channel_id=1, source_target_pairs={{4,0},{5,1},{6,2},{7,3},{12,8},{13,9},{14,10},{15,11},{20,16},{21,... | collective-permute-start | bytes 393224 | tf_op jit(solution)/shard_map/ppermute | solution.py:388
  39.3 5.5 %collective-permute-start.11 = (bf16[256,256]{1,0:T(8,128)(2,1)S(1)}, bf16[256,256]{1,0:T(8,128)(2,1)S(1)}, u32[]{:S(2)}, u32[]{:S(2)}) collective-permute-start(bf16[256,256]{1,0:T(8,128)(2,1)S(1)} %shard_map.82.refs_0_), channel_id=1, source_target_pairs={{0,128},{64,192},{128,0},{192,64},{1,129},{65,193},{129,1},{193,65... | collective-permute-start | bytes 393224 | tf_op jit(solution)/shard_map/ppermute | solution.py:393
  42.3 5.8 %collective-permute-start.10 = (bf16[256,256]{1,0:T(8,128)(2,1)S(1)}, bf16[256,256]{1,0:T(8,128)(2,1)S(1)}, u32[]{:S(2)}, u32[]{:S(2)}) collective-permute-start(bf16[256,256]{1,0:T(8,128)(2,1)S(1)} %shard_map.82.refs_0_), channel_id=1, source_target_pairs={{0,64},{64,0},{128,192},{192,128},{1,65},{65,1},{129,193},{193,129... | collective-permute-start | bytes 393224 | tf_op jit(solution)/shard_map/ppermute | solution.py:393
  48.2 9.3 %collective-permute-start.12 = (bf16[4,128,2048]{2,1,0:T(8,128)(2,1)S(1)}, bf16[4,128,2048]{2,1,0:T(8,128)(2,1)S(1)}, u32[]{:S(2)}, u32[]{:S(2)}) collective-permute-start(bf16[4,128,2048]{2,1,0:T(8,128)(2,1)S(1)} %shard_map.83.mine), channel_id=1, source_target_pairs={{0,1},{1,0},{2,3},{3,2},{4,5},{5,4},{6,7},{7,6},{8,9},{9,8},{10,11... | collective-permute-start | bytes 6291464 | tf_op jit(solution)/shard_map/ppermute | solution.py:399
  50.4 6.3 %collective-permute-start.13 = (bf16[256,256]{1,0:T(8,128)(2,1)S(1)}, bf16[256,256]{1,0:T(8,128)(2,1)S(1)}, u32[]{:S(2)}, u32[]{:S(2)}) collective-permute-start(bf16[256,256]{1,0:T(8,128)(2,1)S(1)} %shard_map.82.refs_0_), channel_id=1, source_target_pairs={{0,192},{64,128},{128,64},{192,0},{1,193},{65,129},{129,65},{193,1... | collective-permute-start | bytes 393224 | tf_op jit(solution)/shard_map/ppermute | solution.py:393
  56.7 8.2 %collective-permute-start.17 = (bf16[128,1024]{1,0:T(8,128)(2,1)S(1)}, bf16[128,1024]{1,0:T(8,128)(2,1)S(1)}, u32[]{:S(2)}, u32[]{:S(2)}) collective-permute-start(bf16[128,1024]{1,0:T(8,128)(2,1)S(1)} %get-tuple-element.63), channel_id=1, source_target_pairs={{0,1},{1,0},{2,3},{3,2},{4,5},{5,4},{6,7},{7,6},{8,9},{9,8},{10,11... | collective-permute-start | bytes 786440 | tf_op jit(solution)/shard_map/ppermute | solution.py:402
  58.6 9.2 %collective-permute-start.14 = (bf16[512,256]{1,0:T(8,128)(2,1)S(1)}, bf16[512,256]{1,0:T(8,128)(2,1)S(1)}, u32[]{:S(2)}, u32[]{:S(2)}) collective-permute-start(bf16[512,256]{1,0:T(8,128)(2,1)S(1)} %shard_map.84), channel_id=1, source_target_pairs={{0,48},{16,32},{32,16},{48,0},{1,49},{17,33},{33,17},{49,1},{2,50}... | collective-permute-start | bytes 786440 | tf_op jit(solution)/shard_map/ppermute | solution.py:407
  62.2 7.7 %collective-permute-start.15 = (bf16[512,256]{1,0:T(8,128)(2,1)S(1)}, bf16[512,256]{1,0:T(8,128)(2,1)S(1)}, u32[]{:S(2)}, u32[]{:S(2)}) collective-permute-start(bf16[512,256]{1,0:T(8,128)(2,1)S(1)} %shard_map.85), channel_id=1, source_target_pairs={{0,16},{16,0},{32,48},{48,32},{1,17},{17,1},{33,49},{49,33},{2,18}... | collective-permute-start | bytes 786440 | tf_op jit(solution)/shard_map/ppermute | solution.py:407
  63.4 12.1 %collective-permute-start.16 = (bf16[512,256]{1,0:T(8,128)(2,1)S(1)}, bf16[512,256]{1,0:T(8,128)(2,1)S(1)}, u32[]{:S(2)}, u32[]{:S(2)}) collective-permute-start(bf16[512,256]{1,0:T(8,128)(2,1)S(1)} %shard_map.86), channel_id=1, source_target_pairs={{0,32},{16,48},{32,0},{48,16},{1,33},{17,49},{33,1},{49,17},{2,34}... | collective-permute-start | bytes 786440 | tf_op jit(solution)/shard_map/ppermute | solution.py:407

commit v9 on v8

--- a/solution.py
+++ b/solution.py
@@ -394,7 +394,7 @@
 
     grad = combine(own_grad, near_back, far_back)
     grads = [grad] + [along_y(grad, k) for k in range(1, n_y)]
-    pieces, grads[1:3] = lax.optimization_barrier((pieces, grads[1:3]))
+    pieces, grads[1] = lax.optimization_barrier((pieces, grads[1]))
     mine = stack(pieces)
     other = lax.ppermute(mine, "core", swap)
     n_x = lax.axis_size("x")
@@ -402,7 +402,7 @@
     dq_back = lax.ppermute(dq_other, "core", swap)
     query_grad = assemble(here_ref, dq_mine, dq_back)[None]
     parts = []
-    for k in (3, 1, 2):
+    for k in (2, 1, 3):
         term = project(places_ref, mine, other, grads, n_x, k, jnp.bfloat16)
         parts.append(lax.ppermute(term, "x", [(i, i ^ k) for i in range(n_x)]))
     own_term = project(places_ref, mine, other, grads, n_x, 0, jnp.float32)

time: 94.4 us -> 91.7 us (0.971)
  waiting for transfers between devices: 28.8 us -> 25.8 us
    ppermute x3, waiting for transfers between devices: 10.6 us -> 8.55 us  [along_y(): return lax.ppermute(part, 'y', [(i, i ^ k) for i in range(n_y)])]
    ppermute x3, waiting for transfers between devices: 8.11 us -> 6.76 us  [per_device(): parts.append(lax.ppermute(term, 'x', [(i, i ^ k) for i in range(n_x)]))]
    ppermute x1, starting transfers between devices: 0.87 us -> 1.82 us  [per_device(): dq_back = lax.ppermute(dq_other, 'core', swap)]
where the time goes in v9:
time: 91.7 us; the launch traced here: 91.5 us
  starting transfers between devices  28.9 us (32%)
  waiting for transfers between devices  25.8 us (28%)
  blocking collectives  18.1 us (20%)
  Pallas kernels  14.7 us (16%)
  local copies, waits for them, and re-layouts  3.07 us (3%)
    all_to_all x1, blocking collectives, per_device(): lax.all_to_all(term.reshape(n_rest, term.shape[0] // n_rest, term.shape[1...  18.1 us
    ppermute x2, waiting for transfers between devices, per_device(): lax.ppermute(part, ('z_lo', 'core'), [(b, a) for a, b in behind(distance)])  10.1 us
    ppermute x3, waiting for transfers between devices, along_y(): return lax.ppermute(part, 'y', [(i, i ^ k) for i in range(n_y)])  8.55 us
    ppermute x3, waiting for transfers between devices, per_device(): parts.append(lax.ppermute(term, 'x', [(i, i ^ k) for i in range(n_x)]))  6.76 us
    ppermute x2, starting transfers between devices, per_device(): lax.ppermute(chip_pair, ('z_lo', 'core'), behind(distance))  6.72 us
    pallas_call x1, Pallas kernels, attention(): pl.pallas_call(attention_kernel, out_shape=(whole((chip, 2 * DH)), whole(...  5.34 us
    pallas_call x4, Pallas kernels, project(): pl.pallas_call(functools.partial(project_kernel, offset=offset), out_shap...  4.3 us
    ppermute x3, starting transfers between devices, per_device(): lax.ppermute(chunks[k], 'y', [(i, i ^ k) for i in range(n_y)])  3.97 us
  transfers between devices with their start and end apart: 18, of which 8 were waited for; matrix products, arithmetic and copies ran while one was open for 2% of the time, Pallas kernels for 15%

profile of v9, /device:TPU:1, one launch (start us, length us, event | category | flops | bytes accessed | tf_op | source)
XLA Modules:
  0.0 91.5 jit_solution(1279326630066569259)
XLA Ops:
  0.6 1.0 %dynamic-slice_bitcast_fusion.4 = (bf16[128,128]{1,0:T(8,128)(2,1)S(1)}, bf16[128,128]{1,0:T(8,128)(2,1)S(1)}, bf16[128,128]{1,0:T(8,128)(2,1)S(1)}, bf16[128,128]{1,0:T(8,128)(2,1)S(1)}) fusion(bf16[1,128,256]{2,1,0:T(8,128)(2,1)} %param.8, s32[]{:T(128)S(6)} %select_n.18, s32[]{:T(128)S(6)} %select_n.17, bf16[1,128,256]{2,1,0:T(8,128)(2,1)} %param.7), kind=kLoop, calls=%fused_computation.5 | loop fusion | bytes 262152 | tf_op jit(solution)/shard_map/dynamic_slice | solution.py:348
  1.6 3.3 %collective-permute-start = (bf16[128,256]{1,0:T(8,128)(2,1)S(1)}, bf16[128,256]{1,0:T(8,128)(2,1)S(1)}, u32[]{:S(2)}, u32[]{:S(2)}) collective-permute-start(bf16[128,256]{1,0:T(8,128)(2,1)S(1)} %pad_maximum_fusion), channel_id=1, source_target_pairs={{0,1},{1,0},{2,3},{3,2},{4,5},{5,4},{6,7},{7,6},{8,9},{9,8},{10,11... | collective-permute-start | bytes 196616 | tf_op jit(solution)/shard_map/ppermute | solution.py:354
  5.0 2.1 %dynamic-slice_bitcast_fusion = (bf16[128,1024]{1,0:T(8,128)(2,1)S(1)}, bf16[128,1024]{1,0:T(8,128)(2,1)}, bf16[128,1024]{1,0:T(8,128)(2,1)}, bf16[128,1024]{1,0:T(8,128)(2,1)S(1)}) fusion(bf16[1,128,2048]{2,1,0:T(8,128)(2,1)} %param.9, s32[]{:T(128)S(6)} %select_n.19, s32[]{:T(128)S(6)} %select_n.16, bf16[1,128,2048]{2,1,0:T(8,128)(2,1)} %param.6), kind=kLoop, calls=%fused_computation | loop fusion | bytes 2097160 | tf_op jit(solution)/shard_map/dynamic_slice | solution.py:348
  7.1 0.1 collective-permute-start.1
  7.2 0.5 collective-permute-start.2
  7.7 3.2 %collective-permute-start.7 = (bf16[256,256]{1,0:T(8,128)(2,1)S(1)}, bf16[256,256]{1,0:T(8,128)(2,1)S(1)}, u32[]{:S(2)}, u32[]{:S(2)}) collective-permute-start(bf16[256,256]{1,0:T(8,128)(2,1)S(1)} %shard_map.78.chip_pair), channel_id=1, source_target_pairs={{0,4},{1,5},{2,6},{3,7},{8,12},{9,13},{10,14},{11,15},{16,20},{17,... | collective-permute-start | bytes 393224 | tf_op jit(solution)/shard_map/ppermute | solution.py:371
  10.9 3.5 %collective-permute-start.6 = (bf16[256,256]{1,0:T(8,128)(2,1)S(1)}, bf16[256,256]{1,0:T(8,128)(2,1)S(1)}, u32[]{:S(2)}, u32[]{:S(2)}) collective-permute-start(bf16[256,256]{1,0:T(8,128)(2,1)S(1)} %shard_map.78.chip_pair), channel_id=1, source_target_pairs={{0,2},{1,3},{2,4},{3,5},{4,6},{5,7},{8,10},{9,11},{10,12},{11,13},... | collective-permute-start | bytes 393224 | tf_op jit(solution)/shard_map/ppermute | solution.py:371
  14.4 0.1 pad_add_fusion.place_ref.places_ref
  14.5 0.7 shard_map.77
  15.2 0.1 pad_add_fusion.1.here_ref
  15.3 0.0 collective-permute-done.1.q_other
  15.3 0.0 collective-permute-done.2.do_other
  15.3 1.3 %collective-permute-start.3 = (bf16[128,2048]{1,0:T(8,128)(2,1)S(1)}, bf16[128,2048]{1,0:T(8,128)(2,1)S(1)}, u32[]{:S(2)}, u32[]{:S(2)}) collective-permute-start(bf16[128,2048]{1,0:T(8,128)(2,1)S(1)} %get-tuple-element.41), channel_id=1, source_target_pairs={{0,64},{64,0},{128,192},{192,128},{1,65},{65,1},{129,193},{193,129... | collective-permute-start | bytes 1572872 | tf_op jit(solution)/shard_map/ppermute | solution.py:378
  16.7 2.6 %collective-permute-start.4 = (bf16[128,2048]{1,0:T(8,128)(2,1)S(1)}, bf16[128,2048]{1,0:T(8,128)(2,1)S(1)}, u32[]{:S(2)}, u32[]{:S(2)}) collective-permute-start(bf16[128,2048]{1,0:T(8,128)(2,1)S(1)} %get-tuple-element.42), channel_id=1, source_target_pairs={{0,128},{64,192},{128,0},{192,64},{1,129},{65,193},{129,1},{193,65... | collective-permute-start | bytes 1572872 | tf_op jit(solution)/shard_map/ppermute | solution.py:378
  19.3 0.0 collective-permute-start.5
  19.3 0.7 shard_map.79.bias
  20.0 0.0 collective-permute-done.6.near_pair
  20.0 5.3 %shard_map.80 = (bf16[256,256]{1,0:T(8,128)(2,1)S(1)}, bf16[256,256]{1,0:T(8,128)(2,1)S(1)}, bf16[8,768,256]{2,1,0:T(8,128)(2,1)S(1)}, bf16[8,256,256]{2,1,0:T(8,128)(2,1)S(1)}) custom-call(bf16[128,1024]{1,0:T(8,128)(2,1)S(1)} %get-tuple-element.75.q_mine, bf16[128,1024]{1,0:T(8,128)(2,1)S(1)} %get-tuple-element.66.do_mine, ...), custom_call_target="tpu_custom_call" | custom-call | flops 8053063680 | bytes 4194304 | tf_op jit(solution)/shard_map/pallas_call | solution.py:168
  25.4 1.3 %collective-permute-start.8 = (bf16[256,256]{1,0:T(8,128)(2,1)S(1)}, bf16[256,256]{1,0:T(8,128)(2,1)S(1)}, u32[]{:S(2)}, u32[]{:S(2)}) collective-permute-start(bf16[256,256]{1,0:T(8,128)(2,1)S(1)} %get-tuple-element.48), channel_id=1, source_target_pairs={{2,0},{3,1},{4,2},{5,3},{6,4},{7,5},{10,8},{11,9},{12,10},{13,11},... | collective-permute-start | bytes 393224 | tf_op jit(solution)/shard_map/ppermute | solution.py:388
  26.7 1.3 %collective-permute-start.9 = (bf16[256,256]{1,0:T(8,128)(2,1)S(1)}, bf16[256,256]{1,0:T(8,128)(2,1)S(1)}, u32[]{:S(2)}, u32[]{:S(2)}) collective-permute-start(bf16[256,256]{1,0:T(8,128)(2,1)S(1)} %get-tuple-element.49), channel_id=1, source_target_pairs={{4,0},{5,1},{6,2},{7,3},{12,8},{13,9},{14,10},{15,11},{20,16},{21,... | collective-permute-start | bytes 393224 | tf_op jit(solution)/shard_map/ppermute | solution.py:388
  28.0 1.1 %shard_map.81 = (bf16[128,1024]{1,0:T(8,128)(2,1)S(1)}, bf16[128,1024]{1,0:T(8,128)(2,1)S(1)}, f32[256,256]{1,0:T(8,128)S(1)}) custom-call(bf16[128,1024]{1,0:T(8,128)(2,1)S(1)} %get-tuple-element.75.q_mine, bf16[128,1024]{1,0:T(8,128)(2,1)S(1)} %get-tuple-element.66.do_mine, bf16[128,1024]{1,0:T(8,128)(2,1)S(1)} %collective-permute-done.1.q_other, ...), custom_call_target="tpu_custom_call" | custom-call | flops 1207959552 | bytes 6291456 | tf_op jit(solution)/shard_map/pallas_call | solution.py:215
  29.1 2.3 %collective-permute-done.8.near = bf16[256,256]{1,0:T(8,128)(2,1)S(1)} collective-permute-done((bf16[256,256]{1,0:T(8,128)(2,1)S(1)}, bf16[256,256]{1,0:T(8,128)(2,1)S(1)}, u32[]{:S(2)}, u32[]{:S(2)}) %collective-permute-start.8) | collective-permute-done | bytes 131104 | tf_op jit(solution)/shard_map/ppermute | solution.py:388
  31.4 7.8 %collective-permute-done.9.far = bf16[256,256]{1,0:T(8,128)(2,1)S(1)} collective-permute-done((bf16[256,256]{1,0:T(8,128)(2,1)S(1)}, bf16[256,256]{1,0:T(8,128)(2,1)S(1)}, u32[]{:S(2)}, u32[]{:S(2)}) %collective-permute-start.9) | collective-permute-done | bytes 131104 | tf_op jit(solution)/shard_map/ppermute | solution.py:388
  39.2 0.1 shard_map.82.refs_0_
  39.3 1.4 %collective-permute-start.10 = (bf16[256,256]{1,0:T(8,128)(2,1)S(1)}, bf16[256,256]{1,0:T(8,128)(2,1)S(1)}, u32[]{:S(2)}, u32[]{:S(2)}) collective-permute-start(bf16[256,256]{1,0:T(8,128)(2,1)S(1)} %shard_map.82.refs_0_), channel_id=1, source_target_pairs={{0,64},{64,0},{128,192},{192,128},{1,65},{65,1},{129,193},{193,129... | collective-permute-start | bytes 393224 | tf_op jit(solution)/shard_map/ppermute | solution.py:393
  40.7 2.8 %collective-permute-done.10.refs_1_ = bf16[256,256]{1,0:T(8,128)(2,1)S(1)} collective-permute-done((bf16[256,256]{1,0:T(8,128)(2,1)S(1)}, bf16[256,256]{1,0:T(8,128)(2,1)S(1)}, u32[]{:S(2)}, u32[]{:S(2)}) %collective-permute-start.10) | collective-permute-done | bytes 131104 | tf_op jit(solution)/shard_map/ppermute | solution.py:393
  43.5 0.0 collective-permute-done.3.refs_1_
  43.5 0.4 collective-permute-done.5.refs_3_
  44.0 0.1 shard_map.83.mine
  44.1 2.2 %collective-permute-start.11 = (bf16[4,128,2048]{2,1,0:T(8,128)(2,1)S(1)}, bf16[4,128,2048]{2,1,0:T(8,128)(2,1)S(1)}, u32[]{:S(2)}, u32[]{:S(2)}) collective-permute-start(bf16[4,128,2048]{2,1,0:T(8,128)(2,1)S(1)} %shard_map.83.mine), channel_id=1, source_target_pairs={{0,1},{1,0},{2,3},{3,2},{4,5},{5,4},{6,7},{7,6},{8,9},{9,8},{10,11... | collective-permute-start | bytes 6291464 | tf_op jit(solution)/shard_map/ppermute | solution.py:399
  46.3 2.0 %collective-permute-start.13 = (bf16[256,256]{1,0:T(8,128)(2,1)S(1)}, bf16[256,256]{1,0:T(8,128)(2,1)S(1)}, u32[]{:S(2)}, u32[]{:S(2)}) collective-permute-start(bf16[256,256]{1,0:T(8,128)(2,1)S(1)} %shard_map.82.refs_0_), channel_id=1, source_target_pairs={{0,192},{64,128},{128,64},{192,0},{1,193},{65,129},{129,65},{193,1... | collective-permute-start | bytes 393224 | tf_op jit(solution)/shard_map/ppermute | solution.py:393
  48.3 0.4 collective-permute-start.12
  48.7 4.9 %collective-permute-done.13.refs_3_ = bf16[256,256]{1,0:T(8,128)(2,1)S(1)} collective-permute-done((bf16[256,256]{1,0:T(8,128)(2,1)S(1)}, bf16[256,256]{1,0:T(8,128)(2,1)S(1)}, u32[]{:S(2)}, u32[]{:S(2)}) %collective-permute-start.13) | collective-permute-done | bytes 131104 | tf_op jit(solution)/shard_map/ppermute | solution.py:393
  53.6 0.8 collective-permute-done.12.refs_2_
  54.4 1.8 %collective-permute-start.17 = (bf16[128,1024]{1,0:T(8,128)(2,1)S(1)}, bf16[128,1024]{1,0:T(8,128)(2,1)S(1)}, u32[]{:S(2)}, u32[]{:S(2)}) collective-permute-start(bf16[128,1024]{1,0:T(8,128)(2,1)S(1)} %get-tuple-element.61), channel_id=1, source_target_pairs={{0,1},{1,0},{2,3},{3,2},{4,5},{5,4},{6,7},{7,6},{8,9},{9,8},{10,11... | collective-permute-start | bytes 786440 | tf_op jit(solution)/shard_map/ppermute | solution.py:402
  56.2 1.1 %shard_map.84 = bf16[512,256]{1,0:T(8,128)(2,1)S(1)} custom-call(s32[2]{0:T(128)S(1)} %pad_add_fusion.place_ref.places_ref, bf16[4,128,2048]{2,1,0:T(8,128)(2,1)S(1)} %shard_map.83.mine, bf16[4,128,2048]{2,1,0:T(8,128)(2,1)S(1)} %collective-permute-done.11.other, bf16[256,256]{1,0:T(8,128)(2,1)S(1)} %shard_map.82.refs_0_, ...), custom_call_target="tpu_custom_call" | custom-call | flops 268435456 | bytes 2097152 | tf_op jit(solution)/shard_map/pallas_call | solution.py:289
  57.3 2.8 %collective-permute-start.14 = (bf16[512,256]{1,0:T(8,128)(2,1)S(1)}, bf16[512,256]{1,0:T(8,128)(2,1)S(1)}, u32[]{:S(2)}, u32[]{:S(2)}) collective-permute-start(bf16[512,256]{1,0:T(8,128)(2,1)S(1)} %shard_map.84), channel_id=1, source_target_pairs={{0,32},{16,48},{32,0},{48,16},{1,33},{17,49},{33,1},{49,17},{2,34}... | collective-permute-start | bytes 786440 | tf_op jit(solution)/shard_map/ppermute | solution.py:407
  60.1 1.1 %shard_map.85 = bf16[512,256]{1,0:T(8,128)(2,1)S(1)} custom-call(s32[2]{0:T(128)S(1)} %pad_add_fusion.place_ref.places_ref, bf16[4,128,2048]{2,1,0:T(8,128)(2,1)S(1)} %shard_map.83.mine, bf16[4,128,2048]{2,1,0:T(8,128)(2,1)S(1)} %collective-permute-done.11.other, bf16[256,256]{1,0:T(8,128)(2,1)S(1)} %shard_map.82.refs_0_, ...), custom_call_target="tpu_custom_call" | custom-call | flops 268435456 | bytes 2097152 | tf_op jit(solution)/shard_map/pallas_call | solution.py:289
  61.2 0.4 collective-permute-start.15
  61.6 1.1 %shard_map.86 = bf16[512,256]{1,0:T(8,128)(2,1)S(1)} custom-call(s32[2]{0:T(128)S(1)} %pad_add_fusion.place_ref.places_ref, bf16[4,128,2048]{2,1,0:T(8,128)(2,1)S(1)} %shard_map.83.mine, bf16[4,128,2048]{2,1,0:T(8,128)(2,1)S(1)} %collective-permute-done.11.other, bf16[256,256]{1,0:T(8,128)(2,1)S(1)} %shard_map.82.refs_0_, ...), custom_call_target="tpu_custom_call" | custom-call | flops 268435456 | bytes 2097152 | tf_op jit(solution)/shard_map/pallas_call | solution.py:289
  62.7 0.7 collective-permute-start.16
  63.3 1.4 %shard_map.87 = bf16[128,2048]{1,0:T(8,128)(2,1)} custom-call(s32[2]{0:T(128)S(1)} %pad_add_fusion.1.here_ref, bf16[128,1024]{1,0:T(8,128)(2,1)S(1)} %get-tuple-element.60.mine, bf16[128,1024]{1,0:T(8,128)(2,1)S(1)} %collective-permute-done.17.other), custom_call_target="tpu_custom_call" | custom-call | bytes 1048576 | tf_op jit(solution)/shard_map/pallas_call | solution.py:265
  64.7 1.1 %shard_map.88.refs_0_ = f32[512,256]{1,0:T(8,128)S(1)} custom-call(s32[2]{0:T(128)S(1)} %pad_add_fusion.place_ref.places_ref, bf16[4,128,2048]{2,1,0:T(8,128)(2,1)S(1)} %shard_map.83.mine, bf16[4,128,2048]{2,1,0:T(8,128)(2,1)S(1)} %collective-permute-done.11.other, bf16[256,256]{1,0:T(8,128)(2,1)S(1)} %shard_map.82.refs_0_, ...), custom_call_target="tpu_custom_call" | custom-call | flops 268435456 | bytes 2097152 | tf_op jit(solution)/shard_map/pallas_call | solution.py:289
  65.8 1.0 %collective-permute-done.14.refs_1_ = bf16[512,256]{1,0:T(8,128)(2,1)S(1)} collective-permute-done((bf16[512,256]{1,0:T(8,128)(2,1)S(1)}, bf16[512,256]{1,0:T(8,128)(2,1)S(1)}, u32[]{:S(2)}, u32[]{:S(2)}) %collective-permute-start.14) | collective-permute-done | bytes 262176 | tf_op jit(solution)/shard_map/ppermute | solution.py:407
  66.8 5.8 %collective-permute-done.15.refs_2_ = bf16[512,256]{1,0:T(8,128)(2,1)S(1)} collective-permute-done((bf16[512,256]{1,0:T(8,128)(2,1)S(1)}, bf16[512,256]{1,0:T(8,128)(2,1)S(1)}, u32[]{:S(2)}, u32[]{:S(2)}) %collective-permute-start.15) | collective-permute-done | bytes 262176 | tf_op jit(solution)/shard_map/ppermute | solution.py:407
  72.6 0.1 shard_map.89
  72.7 18.1 %all_to_all.5.parts = bf16[16,32,256]{2,1,0:T(8,128)(2,1)S(1)} all-to-all(bf16[16,32,256]{2,1,0:T(8,128)(2,1)S(1)} %bitcast.24), channel_id=1, replica_groups=mesh['y'=4,'x'=4,'z_hi'=2,'z_lo'=4,'core'=2] {'z_hi','z_lo','core'}, dimensions={0} | all-to-all | bytes 524288 | tf_op jit(solution)/shard_map/all_to_all | solution.py:413
  90.8 0.7 shard_map.90
  (12 shorter events, 0.1 us)
Async XLA Ops:
  0.6 13.9 %copy-start = (bf16[1,128,8192]{2,1,0:T(8,128)(2,1)S(1)}, bf16[1,128,8192]{2,1,0:T(8,128)(2,1)}, u32[]{:S(2)}) copy-start(bf16[1,128,8192]{2,1,0:T(8,128)(2,1)} %param.10) | copy-start | bytes 6291460
  1.6 5.4 %collective-permute-start = (bf16[128,256]{1,0:T(8,128)(2,1)S(1)}, bf16[128,256]{1,0:T(8,128)(2,1)S(1)}, u32[]{:S(2)}, u32[]{:S(2)}) collective-permute-start(bf16[128,256]{1,0:T(8,128)(2,1)S(1)} %pad_maximum_fusion), channel_id=1, source_target_pairs={{0,1},{1,0},{2,3},{3,2},{4,5},{5,4},{6,7},{7,6},{8,9},{9,8},{10,11... | collective-permute-start | bytes 196616 | tf_op jit(solution)/shard_map/ppermute | solution.py:354
  5.0 14.3 %copy-start.1 = (s32[1,1024]{1,0:T(1,128)S(1)}, s32[1,1024]{1,0:T(1,128)}, u32[]{:S(2)}) copy-start(s32[1,1024]{1,0:T(1,128)} %docs) | copy-start | bytes 12292
  7.1 8.2 %collective-permute-start.1 = (bf16[128,1024]{1,0:T(8,128)(2,1)}, bf16[128,1024]{1,0:T(8,128)(2,1)S(1)}, u32[]{:S(2)}, u32[]{:S(2)}) collective-permute-start(bf16[128,1024]{1,0:T(8,128)(2,1)} %get-tuple-element.38), channel_id=1, source_target_pairs={{0,1},{1,0},{2,3},{3,2},{4,5},{5,4},{6,7},{7,6},{8,9},{9,8},{10,11... | collective-permute-start | bytes 786440 | tf_op jit(solution)/shard_map/ppermute | solution.py:361
  7.2 8.1 %collective-permute-start.2 = (bf16[128,1024]{1,0:T(8,128)(2,1)}, bf16[128,1024]{1,0:T(8,128)(2,1)S(1)}, u32[]{:S(2)}, u32[]{:S(2)}) collective-permute-start(bf16[128,1024]{1,0:T(8,128)(2,1)} %get-tuple-element.39), channel_id=1, source_target_pairs={{0,1},{1,0},{2,3},{3,2},{4,5},{5,4},{6,7},{7,6},{8,9},{9,8},{10,11... | collective-permute-start | bytes 786440 | tf_op jit(solution)/shard_map/ppermute | solution.py:361
  7.7 12.3 %collective-permute-start.7 = (bf16[256,256]{1,0:T(8,128)(2,1)S(1)}, bf16[256,256]{1,0:T(8,128)(2,1)S(1)}, u32[]{:S(2)}, u32[]{:S(2)}) collective-permute-start(bf16[256,256]{1,0:T(8,128)(2,1)S(1)} %shard_map.78.chip_pair), channel_id=1, source_target_pairs={{0,4},{1,5},{2,6},{3,7},{8,12},{9,13},{10,14},{11,15},{16,20},{17,... | collective-permute-start | bytes 393224 | tf_op jit(solution)/shard_map/ppermute | solution.py:371
  10.9 9.2 %collective-permute-start.6 = (bf16[256,256]{1,0:T(8,128)(2,1)S(1)}, bf16[256,256]{1,0:T(8,128)(2,1)S(1)}, u32[]{:S(2)}, u32[]{:S(2)}) collective-permute-start(bf16[256,256]{1,0:T(8,128)(2,1)S(1)} %shard_map.78.chip_pair), channel_id=1, source_target_pairs={{0,2},{1,3},{2,4},{3,5},{4,6},{5,7},{8,10},{9,11},{10,12},{11,13},... | collective-permute-start | bytes 393224 | tf_op jit(solution)/shard_map/ppermute | solution.py:371
  15.3 28.2 %collective-permute-start.3 = (bf16[128,2048]{1,0:T(8,128)(2,1)S(1)}, bf16[128,2048]{1,0:T(8,128)(2,1)S(1)}, u32[]{:S(2)}, u32[]{:S(2)}) collective-permute-start(bf16[128,2048]{1,0:T(8,128)(2,1)S(1)} %get-tuple-element.41), channel_id=1, source_target_pairs={{0,64},{64,0},{128,192},{192,128},{1,65},{65,1},{129,193},{193,129... | collective-permute-start | bytes 1572872 | tf_op jit(solution)/shard_map/ppermute | solution.py:378
  16.7 26.9 %collective-permute-start.4 = (bf16[128,2048]{1,0:T(8,128)(2,1)S(1)}, bf16[128,2048]{1,0:T(8,128)(2,1)S(1)}, u32[]{:S(2)}, u32[]{:S(2)}) collective-permute-start(bf16[128,2048]{1,0:T(8,128)(2,1)S(1)} %get-tuple-element.42), channel_id=1, source_target_pairs={{0,128},{64,192},{128,0},{192,64},{1,129},{65,193},{129,1},{193,65... | collective-permute-start | bytes 1572872 | tf_op jit(solution)/shard_map/ppermute | solution.py:378
  19.3 24.7 %collective-permute-start.5 = (bf16[128,2048]{1,0:T(8,128)(2,1)S(1)}, bf16[128,2048]{1,0:T(8,128)(2,1)S(1)}, u32[]{:S(2)}, u32[]{:S(2)}) collective-permute-start(bf16[128,2048]{1,0:T(8,128)(2,1)S(1)} %get-tuple-element.43), channel_id=1, source_target_pairs={{0,192},{64,128},{128,64},{192,0},{1,193},{65,129},{129,65},{193,1... | collective-permute-start | bytes 1572872 | tf_op jit(solution)/shard_map/ppermute | solution.py:378
  25.4 6.0 %collective-permute-start.8 = (bf16[256,256]{1,0:T(8,128)(2,1)S(1)}, bf16[256,256]{1,0:T(8,128)(2,1)S(1)}, u32[]{:S(2)}, u32[]{:S(2)}) collective-permute-start(bf16[256,256]{1,0:T(8,128)(2,1)S(1)} %get-tuple-element.48), channel_id=1, source_target_pairs={{2,0},{3,1},{4,2},{5,3},{6,4},{7,5},{10,8},{11,9},{12,10},{13,11},... | collective-permute-start | bytes 393224 | tf_op jit(solution)/shard_map/ppermute | solution.py:388
  26.7 12.5 %collective-permute-start.9 = (bf16[256,256]{1,0:T(8,128)(2,1)S(1)}, bf16[256,256]{1,0:T(8,128)(2,1)S(1)}, u32[]{:S(2)}, u32[]{:S(2)}) collective-permute-start(bf16[256,256]{1,0:T(8,128)(2,1)S(1)} %get-tuple-element.49), channel_id=1, source_target_pairs={{4,0},{5,1},{6,2},{7,3},{12,8},{13,9},{14,10},{15,11},{20,16},{21,... | collective-permute-start | bytes 393224 | tf_op jit(solution)/shard_map/ppermute | solution.py:388
  39.3 4.2 %collective-permute-start.10 = (bf16[256,256]{1,0:T(8,128)(2,1)S(1)}, bf16[256,256]{1,0:T(8,128)(2,1)S(1)}, u32[]{:S(2)}, u32[]{:S(2)}) collective-permute-start(bf16[256,256]{1,0:T(8,128)(2,1)S(1)} %shard_map.82.refs_0_), channel_id=1, source_target_pairs={{0,64},{64,0},{128,192},{192,128},{1,65},{65,1},{129,193},{193,129... | collective-permute-start | bytes 393224 | tf_op jit(solution)/shard_map/ppermute | solution.py:393
  44.1 12.2 %collective-permute-start.11 = (bf16[4,128,2048]{2,1,0:T(8,128)(2,1)S(1)}, bf16[4,128,2048]{2,1,0:T(8,128)(2,1)S(1)}, u32[]{:S(2)}, u32[]{:S(2)}) collective-permute-start(bf16[4,128,2048]{2,1,0:T(8,128)(2,1)S(1)} %shard_map.83.mine), channel_id=1, source_target_pairs={{0,1},{1,0},{2,3},{3,2},{4,5},{5,4},{6,7},{7,6},{8,9},{9,8},{10,11... | collective-permute-start | bytes 6291464 | tf_op jit(solution)/shard_map/ppermute | solution.py:399
  46.3 7.3 %collective-permute-start.13 = (bf16[256,256]{1,0:T(8,128)(2,1)S(1)}, bf16[256,256]{1,0:T(8,128)(2,1)S(1)}, u32[]{:S(2)}, u32[]{:S(2)}) collective-permute-start(bf16[256,256]{1,0:T(8,128)(2,1)S(1)} %shard_map.82.refs_0_), channel_id=1, source_target_pairs={{0,192},{64,128},{128,64},{192,0},{1,193},{65,129},{129,65},{193,1... | collective-permute-start | bytes 393224 | tf_op jit(solution)/shard_map/ppermute | solution.py:393
  48.3 6.1 %collective-permute-start.12 = (bf16[256,256]{1,0:T(8,128)(2,1)S(1)}, bf16[256,256]{1,0:T(8,128)(2,1)S(1)}, u32[]{:S(2)}, u32[]{:S(2)}) collective-permute-start(bf16[256,256]{1,0:T(8,128)(2,1)S(1)} %shard_map.82.refs_0_), channel_id=1, source_target_pairs={{0,128},{64,192},{128,0},{192,64},{1,129},{65,193},{129,1},{193,65... | collective-permute-start | bytes 393224 | tf_op jit(solution)/shard_map/ppermute | solution.py:393
  54.4 8.9 %collective-permute-start.17 = (bf16[128,1024]{1,0:T(8,128)(2,1)S(1)}, bf16[128,1024]{1,0:T(8,128)(2,1)S(1)}, u32[]{:S(2)}, u32[]{:S(2)}) collective-permute-start(bf16[128,1024]{1,0:T(8,128)(2,1)S(1)} %get-tuple-element.61), channel_id=1, source_target_pairs={{0,1},{1,0},{2,3},{3,2},{4,5},{5,4},{6,7},{7,6},{8,9},{9,8},{10,11... | collective-permute-start | bytes 786440 | tf_op jit(solution)/shard_map/ppermute | solution.py:402
  57.3 9.5 %collective-permute-start.14 = (bf16[512,256]{1,0:T(8,128)(2,1)S(1)}, bf16[512,256]{1,0:T(8,128)(2,1)S(1)}, u32[]{:S(2)}, u32[]{:S(2)}) collective-permute-start(bf16[512,256]{1,0:T(8,128)(2,1)S(1)} %shard_map.84), channel_id=1, source_target_pairs={{0,32},{16,48},{32,0},{48,16},{1,33},{17,49},{33,1},{49,17},{2,34}... | collective-permute-start | bytes 786440 | tf_op jit(solution)/shard_map/ppermute | solution.py:407
  61.2 11.4 %collective-permute-start.15 = (bf16[512,256]{1,0:T(8,128)(2,1)S(1)}, bf16[512,256]{1,0:T(8,128)(2,1)S(1)}, u32[]{:S(2)}, u32[]{:S(2)}) collective-permute-start(bf16[512,256]{1,0:T(8,128)(2,1)S(1)} %shard_map.85), channel_id=1, source_target_pairs={{0,16},{16,0},{32,48},{48,32},{1,17},{17,1},{33,49},{49,33},{2,18}... | collective-permute-start | bytes 786440 | tf_op jit(solution)/shard_map/ppermute | solution.py:407
  62.7 9.9 %collective-permute-start.16 = (bf16[512,256]{1,0:T(8,128)(2,1)S(1)}, bf16[512,256]{1,0:T(8,128)(2,1)S(1)}, u32[]{:S(2)}, u32[]{:S(2)}) collective-permute-start(bf16[512,256]{1,0:T(8,128)(2,1)S(1)} %shard_map.86), channel_id=1, source_target_pairs={{0,48},{16,32},{32,16},{48,0},{1,49},{17,33},{33,17},{49,1},{2,50}... | collective-permute-start | bytes 786440 | tf_op jit(solution)/shard_map/ppermute | solution.py:407

commit v10 on v7

--- a/solution.py
+++ b/solution.py
@@ -53,30 +53,41 @@
     )(keys, values, swapped)
 
 
-def chunk_kernel(place_ref, columns, *refs):
+def chunk_kernel(places_ref, mine, other, *refs):
     outs, sems = refs[:-1], refs[-1]
-    width = outs[0].shape[1]
+    n = len(outs)
+    rows, step = mine.shape[0], outs[0].shape[1] // n
+    y, x, core = places_ref[0], places_ref[1], places_ref[2]
     copies = []
     for k, out in enumerate(outs):
-        start = pl.multiple_of((place_ref[0] ^ k) * width, width)
-        copies.append(pltpu.make_async_copy(columns.at[:, pl.ds(start, width)], out, sems.at[k]))
+        for i in range(n):
+            block = jnp.where(core == 0, (y ^ k) * n + i, i * n + (x ^ k))
+            held = pl.ds(pl.multiple_of(block * step, step), step)
+            for half, part in enumerate((mine, other)):
+                copies.append(
+                    pltpu.make_async_copy(
+                        part.at[:, held],
+                        out.at[half * rows : (half + 1) * rows, i * step : (i + 1) * step],
+                        sems.at[len(copies)],
+                    )
+                )
     for copy in copies:
         copy.start()
     for copy in copies:
         copy.wait()
 
 
-def split_columns(place, columns, chunks):
-    rows, width = columns.shape
+def split_columns(places, mine, other, chunks):
+    rows, width = mine.shape
     return pl.pallas_call(
         chunk_kernel,
-        out_shape=(whole((rows, width // chunks)),) * chunks,
-        in_specs=[SCALAR, HBM],
+        out_shape=(whole((2 * rows, width // chunks)),) * chunks,
+        in_specs=[SCALAR, HBM, HBM],
         out_specs=(HBM,) * chunks,
-        scratch_shapes=[pltpu.SemaphoreType.DMA((chunks,))],
-        compiler_params=SMALL,
-        cost_estimate=pl.CostEstimate(flops=0, bytes_accessed=4 * MIB, transcendentals=0),
-    )(place, columns)
+        scratch_shapes=[pltpu.SemaphoreType.DMA((2 * chunks * chunks,))],
+        compiler_params=SMALL,
+        cost_estimate=pl.CostEstimate(flops=0, bytes_accessed=8 * MIB, transcendentals=0),
+    )(places, mine, other)
 
 
 def bias_kernel(here_ref, docs, out):
@@ -228,17 +239,15 @@
 
 def combine_kernel(own, near, far, out):
     total = own[...] + near[...].astype(jnp.float32) + far[...].astype(jnp.float32)
-    turned = total.T.astype(jnp.bfloat16)
-    for i in range(out.shape[0]):
-        out[i] = turned
-
-
-def combine(own, near, far, copies):
+    out[...] = total.T.astype(jnp.bfloat16)
+
+
+def combine(own, near, far):
     return pl.pallas_call(
         combine_kernel,
-        out_shape=whole((copies, own.shape[1], own.shape[0])),
-        compiler_params=SMALL,
-        cost_estimate=pl.CostEstimate(flops=0, bytes_accessed=2 * 1024 * 1024, transcendentals=0),
+        out_shape=whole((own.shape[1], own.shape[0])),
+        compiler_params=SMALL,
+        cost_estimate=pl.CostEstimate(flops=0, bytes_accessed=MIB, transcendentals=0),
     )(own, near, far)
 
 
@@ -260,29 +269,31 @@
 
 
 def project_kernel(places_ref, *refs, offset):
-    pieces, grads, out = refs[:-2], refs[-2], refs[-1]
+    n = len(refs) // 2
+    pieces, grads, out = refs[:n], refs[n:-1], refs[-1]
     step = out.shape[0]
-    columns = pl.ds(pl.multiple_of((places_ref[1] ^ offset) * step, step), step)
-    left = jnp.concatenate([grads[places_ref[0] ^ k] for k in range(len(pieces) // 2)], axis=1)
+    place = jnp.where(places_ref[2] == 0, places_ref[1], places_ref[0]) ^ offset
+    columns = pl.ds(pl.multiple_of(place * step, step), step)
+    left = jnp.concatenate([ref[...] for ref in grads], axis=1)
     right = jnp.concatenate([ref[:, columns] for ref in pieces], axis=0)
     out[...] = dot_nn(left, right).T.astype(out.dtype)
 
 
-def project(places, pieces, grads, blocks, offset, dtype):
+def project(places, pieces, grads, offset, dtype):
     rows, columns = pieces[0].shape
-    width = grads.shape[1]
-    step = columns // blocks
+    width = grads[0].shape[0]
+    step = columns // len(pieces)
     return pl.pallas_call(
         functools.partial(project_kernel, offset=offset),
         out_shape=whole((step, width), dtype),
-        in_specs=[SCALAR] + [pl.BlockSpec()] * (len(pieces) + 1),
+        in_specs=[SCALAR] + [pl.BlockSpec()] * (2 * len(pieces)),
         compiler_params=pltpu.CompilerParams(vmem_limit_bytes=16 * MIB),
         cost_estimate=pl.CostEstimate(
             flops=2 * len(pieces) * rows * step * width,
             bytes_accessed=2 * MIB,
             transcendentals=0,
         ),
-    )(places, *pieces, grads)
+    )(places, *pieces, *grads)
 
 
 def add_kernel(*refs):
@@ -327,7 +338,18 @@
     n_chips = lax.axis_size("z_lo")
     swap = [(0, 1), (1, 0)]
     here_ref = jnp.stack([z_lo, core]).astype(jnp.int32)
-    places_ref = jnp.stack([lax.axis_index("y"), lax.axis_index("x")]).astype(jnp.int32)
+    places_ref = jnp.stack([lax.axis_index("y"), lax.axis_index("x"), core]).astype(jnp.int32)
+    n_side = lax.axis_size("y")
+
+    def cross(part, k, first):
+        def pair(y, x, c):
+            along_y = (c == 0) == first
+            there = (y ^ k, x) if along_y else (y, x ^ k)
+            return ((y * n_side + x) * 2 + c, (there[0] * n_side + there[1]) * 2 + c)
+
+        pairs = [pair(y, x, c) for y in range(n_side) for x in range(n_side) for c in range(2)]
+        return lax.ppermute(part, ("y", "x", "core"), pairs)
+
 
     def half_of(array, which):
         width = array.shape[-1] // 2
@@ -357,16 +379,16 @@
         lax.ppermute(chip_pair, ("z_lo", "core"), behind(distance)) for distance in (2, 1)
     ][::-1]
 
-    n_y = lax.axis_size("y")
-    chunks = split_columns(places_ref, layer_input[0], n_y)
+    chunks = split_columns(
+        places_ref, layer_input[0], lax.ppermute(layer_input[0], "core", swap), n_side
+    )
     chunks, _ = lax.optimization_barrier((chunks, (q_other, do_other)))
-    pieces = [chunks[0]] + [
-        lax.ppermute(chunks[k], "y", [(i, i ^ k) for i in range(n_y)]) for k in range(1, n_y)
-    ]
+    pieces = [chunks[0]] + [cross(chunks[k], k, True) for k in range(1, n_side)]
+    docs, _ = lax.optimization_barrier((segment_ids, chunks[0]))
 
     operands = (q_mine, do_mine, q_other, do_other, *blocks)
     near_grad, far_grad, score_grads, probs = attention(
-        operands, make_bias(here_ref, segment_ids, rows)
+        operands, make_bias(here_ref, docs, rows)
     )
     dq_mine, dq_other, own_grad = own_gradients(operands, score_grads, probs)
     far_back, near_back = (
@@ -374,19 +396,15 @@
         for distance, part in ((2, far_grad), (1, near_grad))
     )
 
-    copies = combine(own_grad, near_back, far_back, n_y)
-    gathered = lax.all_to_all(copies, "y", 0, 0, tiled=True)
-    pieces, _ = lax.optimization_barrier((pieces, copies))
-    both = [part for piece in pieces for part in (piece, lax.ppermute(piece, "core", swap))]
-    n_x = lax.axis_size("x")
-    dq_other, gathered = lax.optimization_barrier((dq_other, gathered))
+    grad = combine(own_grad, near_back, far_back)
+    grads = [grad] + [cross(grad, k, True) for k in range(1, n_side)]
+    pieces, grads, dq_other = lax.optimization_barrier((pieces, grads, dq_other))
+    parts = []
+    for k in (2, 1, 3):
+        parts.append(cross(project(places_ref, pieces, grads, k, jnp.bfloat16), k, False))
+    own_term = project(places_ref, pieces, grads, 0, jnp.float32)
     dq_back = lax.ppermute(dq_other, "core", swap)
     query_grad = assemble(here_ref, dq_mine, dq_back)[None]
-    parts = []
-    for k in (3, 1, 2):
-        term = project(places_ref, both, gathered, n_x, k, jnp.bfloat16)
-        parts.append(lax.ppermute(term, "x", [(i, i ^ k) for i in range(n_x)]))
-    own_term = project(places_ref, both, gathered, n_x, 0, jnp.float32)
     parts, query_grad = lax.optimization_barrier((parts, query_grad))
     term = add_parts(own_term, parts)
     rest = ("z_hi", "z_lo", "core")

time: 96.4 us -> 91.4 us (0.948)
  blocking collectives: 29.5 us -> 18.7 us
  waiting for transfers between devices: 22.2 us -> 25.1 us
  starting transfers between devices: 25.1 us -> 27.1 us
  Pallas kernels: 14.5 us -> 16.4 us
    all_to_all x1 -> x0, blocking collectives: 11.5 us -> none  [per_device(): gathered = lax.all_to_all(copies, 'y', 0, 0, tiled=True)]
    ppermute x1, starting transfers between devices: 3.33 us -> 0.24 us  [per_device(): lax.ppermute(jnp.concatenate([half_of(keys, 1 - core), half_of(values, 1...]
    ppermute x10, starting transfers between devices: 10.5 us -> 13.2 us  [the longest x9 9.85 us: cross(): return lax.ppermute(part, ('y', 'x', 'core'), pairs)]
    ppermute x2, waiting for transfers between devices: 4.51 us -> 7.06 us  [per_device(): lax.ppermute(part, ('z_lo', 'core'), [(b, a) for a, b in behind(distance)])]
    ppermute x1, starting transfers between devices: 1.36 us -> 3.84 us  [per_device(): dq_back = lax.ppermute(dq_other, 'core', swap)]
    pallas_call x2, Pallas kernels: 0.85 us -> 2.66 us  [the longest x1 2.55 us: split_columns(): pl.pallas_call(chunk_kernel, out_shape=(whole((2 * rows, width // chunks)...]
  transfers between devices with their start and end apart: 18 -> 18, of which waited for: 6 -> 8; matrix products, arithmetic and copies ran while one was open for 2% -> 3% of each run, Pallas kernels for 14% -> 15%
where the time goes in v10:
time: 91.4 us; the launch traced here: 91.1 us
  starting transfers between devices  27.1 us (30%)
  waiting for transfers between devices  25.1 us (27%)
  blocking collectives  18.7 us (20%)
  Pallas kernels  16.4 us (18%)
  local copies, waits for them, and re-layouts  2.89 us (3%)
    all_to_all x1, blocking collectives, per_device(): lax.all_to_all(term.reshape(n_rest, term.shape[0] // n_rest, term.shape[1...  18.7 us
    ppermute x9, waiting for transfers between devices, cross(): return lax.ppermute(part, ('y', 'x', 'core'), pairs)  17.3 us
    ppermute x9, starting transfers between devices, cross(): return lax.ppermute(part, ('y', 'x', 'core'), pairs)  9.85 us
    ppermute x2, waiting for transfers between devices, per_device(): lax.ppermute(part, ('z_lo', 'core'), [(b, a) for a, b in behind(distance)])  7.06 us
    ppermute x2, starting transfers between devices, per_device(): lax.ppermute(chip_pair, ('z_lo', 'core'), behind(distance))  6.7 us
    pallas_call x1, Pallas kernels, attention(): pl.pallas_call(attention_kernel, out_shape=(whole((chip, 2 * DH)), whole(...  5.34 us
    pallas_call x4, Pallas kernels, project(): pl.pallas_call(functools.partial(project_kernel, offset=offset), out_shap...  4.33 us
    ppermute x1, starting transfers between devices, per_device(): dq_back = lax.ppermute(dq_other, 'core', swap)  3.84 us
  transfers between devices with their start and end apart: 18, of which 8 were waited for; matrix products, arithmetic and copies ran while one was open for 3% of the time, Pallas kernels for 15%

profile of v10, /device:TPU:1, one launch (start us, length us, event | category | flops | bytes accessed | tf_op | source)
XLA Modules:
  0.0 91.1 jit_solution(7120591295955253638)
XLA Ops:
  0.6 3.3 %collective-permute-start = (bf16[128,8192]{1,0:T(8,128)(2,1)}, bf16[128,8192]{1,0:T(8,128)(2,1)}, u32[]{:S(2)}, u32[]{:S(2)}) collective-permute-start(bf16[128,8192]{1,0:T(8,128)(2,1)} %bitcast.23), channel_id=1, source_target_pairs={{0,1},{1,0},{2,3},{3,2},{4,5},{5,4},{6,7},{7,6},{8,9},{9,8},{10,11... | collective-permute-start | bytes 6291464 | tf_op jit(solution)/shard_map/ppermute | solution.py:383
  4.0 0.8 dynamic-slice_bitcast_fusion.4
  4.8 0.2 collective-permute-start.1
  5.0 2.1 %dynamic-slice_bitcast_fusion = (bf16[128,1024]{1,0:T(8,128)(2,1)S(1)}, bf16[128,1024]{1,0:T(8,128)(2,1)}, bf16[128,1024]{1,0:T(8,128)(2,1)}, bf16[128,1024]{1,0:T(8,128)(2,1)S(1)}) fusion(bf16[1,128,2048]{2,1,0:T(8,128)(2,1)} %param.9, s32[]{:T(128)S(6)} %select_n.19, s32[]{:T(128)S(6)} %select_n.16, bf16[1,128,2048]{2,1,0:T(8,128)(2,1)} %param.6), kind=kLoop, calls=%fused_computation | loop fusion | bytes 2097160 | tf_op jit(solution)/shard_map/dynamic_slice | solution.py:356
  7.1 0.7 collective-permute-done.1.swapped
  7.9 0.5 collective-permute-start.2
  8.3 0.1 collective-permute-start.3
  8.5 3.2 %collective-permute-start.8 = (bf16[256,256]{1,0:T(8,128)(2,1)S(1)}, bf16[256,256]{1,0:T(8,128)(2,1)S(1)}, u32[]{:S(2)}, u32[]{:S(2)}) collective-permute-start(bf16[256,256]{1,0:T(8,128)(2,1)S(1)} %shard_map.78.chip_pair), channel_id=1, source_target_pairs={{0,4},{1,5},{2,6},{3,7},{8,12},{9,13},{10,14},{11,15},{16,20},{17,... | collective-permute-start | bytes 393224 | tf_op jit(solution)/shard_map/ppermute | solution.py:379
  11.6 3.5 %collective-permute-start.7 = (bf16[256,256]{1,0:T(8,128)(2,1)S(1)}, bf16[256,256]{1,0:T(8,128)(2,1)S(1)}, u32[]{:S(2)}, u32[]{:S(2)}) collective-permute-start(bf16[256,256]{1,0:T(8,128)(2,1)S(1)} %shard_map.78.chip_pair), channel_id=1, source_target_pairs={{0,2},{1,3},{2,4},{3,5},{4,6},{5,7},{8,10},{9,11},{10,12},{11,13},... | collective-permute-start | bytes 393224 | tf_op jit(solution)/shard_map/ppermute | solution.py:379
  15.2 0.1 pad_add_fusion.1.here_ref
  15.3 0.1 pad_add_fusion.places_ref
  15.3 0.0 collective-permute-done.other
  15.3 2.5 %shard_map.77 = (bf16[256,2048]{1,0:T(8,128)(2,1)S(1)}, bf16[256,2048]{1,0:T(8,128)(2,1)S(1)}, bf16[256,2048]{1,0:T(8,128)(2,1)S(1)}, bf16[256,2048]{1,0:T(8,128)(2,1)S(1)}) custom-call(s32[3]{0:T(128)S(1)} %pad_add_fusion.places_ref, bf16[128,8192]{1,0:T(8,128)(2,1)S(1)} %bitcast.24, bf16[128,8192]{1,0:T(8,128)(2,1)} %collective-permute-done.other), custom_call_target="tpu_custom_call" | custom-call | bytes 8388608 | tf_op jit(solution)/shard_map/pallas_call | solution.py:82
  17.9 0.0 collective-permute-done.2.q_other
  17.9 0.0 collective-permute-done.3.do_other
  17.9 1.3 %collective-permute-start.4 = (bf16[256,2048]{1,0:T(8,128)(2,1)S(1)}, bf16[256,2048]{1,0:T(8,128)(2,1)S(1)}, u32[]{:S(2)}, u32[]{:S(2)}) collective-permute-start(bf16[256,2048]{1,0:T(8,128)(2,1)S(1)} %get-tuple-element.40), channel_id=1, source_target_pairs={{0,64},{1,17},{16,80},{17,1},{32,96},{33,49},{48,112},{49,33},{64,... | collective-permute-start | bytes 3145736 | tf_op jit(solution)/shard_map/ppermute | solution.py:351
  19.2 2.5 %collective-permute-start.5 = (bf16[256,2048]{1,0:T(8,128)(2,1)S(1)}, bf16[256,2048]{1,0:T(8,128)(2,1)S(1)}, u32[]{:S(2)}, u32[]{:S(2)}) collective-permute-start(bf16[256,2048]{1,0:T(8,128)(2,1)S(1)} %get-tuple-element.41), channel_id=1, source_target_pairs={{0,128},{1,33},{16,144},{17,49},{32,160},{33,1},{48,176},{49,17},{... | collective-permute-start | bytes 3145736 | tf_op jit(solution)/shard_map/ppermute | solution.py:351
  21.7 0.2 collective-permute-start.6
  21.9 0.7 shard_map.79.bias
  22.6 5.3 %shard_map.80 = (bf16[256,256]{1,0:T(8,128)(2,1)S(1)}, bf16[256,256]{1,0:T(8,128)(2,1)S(1)}, bf16[8,768,256]{2,1,0:T(8,128)(2,1)S(1)}, bf16[8,256,256]{2,1,0:T(8,128)(2,1)S(1)}) custom-call(bf16[128,1024]{1,0:T(8,128)(2,1)S(1)} %get-tuple-element.73.q_mine, bf16[128,1024]{1,0:T(8,128)(2,1)S(1)} %get-tuple-element.64.do_mine, ...), custom_call_target="tpu_custom_call" | custom-call | flops 8053063680 | bytes 4194304 | tf_op jit(solution)/shard_map/pallas_call | solution.py:179
  28.0 1.3 %collective-permute-start.9 = (bf16[256,256]{1,0:T(8,128)(2,1)S(1)}, bf16[256,256]{1,0:T(8,128)(2,1)S(1)}, u32[]{:S(2)}, u32[]{:S(2)}) collective-permute-start(bf16[256,256]{1,0:T(8,128)(2,1)S(1)} %get-tuple-element.47), channel_id=1, source_target_pairs={{2,0},{3,1},{4,2},{5,3},{6,4},{7,5},{10,8},{11,9},{12,10},{13,11},... | collective-permute-start | bytes 393224 | tf_op jit(solution)/shard_map/ppermute | solution.py:395
  29.3 1.3 %collective-permute-start.10 = (bf16[256,256]{1,0:T(8,128)(2,1)S(1)}, bf16[256,256]{1,0:T(8,128)(2,1)S(1)}, u32[]{:S(2)}, u32[]{:S(2)}) collective-permute-start(bf16[256,256]{1,0:T(8,128)(2,1)S(1)} %get-tuple-element.48), channel_id=1, source_target_pairs={{4,0},{5,1},{6,2},{7,3},{12,8},{13,9},{14,10},{15,11},{20,16},{21,... | collective-permute-start | bytes 393224 | tf_op jit(solution)/shard_map/ppermute | solution.py:395
  30.6 1.1 %shard_map.81 = (bf16[128,1024]{1,0:T(8,128)(2,1)S(1)}, bf16[128,1024]{1,0:T(8,128)(2,1)S(1)}, f32[256,256]{1,0:T(8,128)S(1)}) custom-call(bf16[128,1024]{1,0:T(8,128)(2,1)S(1)} %get-tuple-element.73.q_mine, bf16[128,1024]{1,0:T(8,128)(2,1)S(1)} %get-tuple-element.64.do_mine, bf16[128,1024]{1,0:T(8,128)(2,1)S(1)} %collective-permute-done.2.q_other, ...), custom_call_target="tpu_custom_call" | custom-call | flops 1207959552 | bytes 6291456 | tf_op jit(solution)/shard_map/pallas_call | solution.py:226
  31.7 2.3 %collective-permute-done.9.near = bf16[256,256]{1,0:T(8,128)(2,1)S(1)} collective-permute-done((bf16[256,256]{1,0:T(8,128)(2,1)S(1)}, bf16[256,256]{1,0:T(8,128)(2,1)S(1)}, u32[]{:S(2)}, u32[]{:S(2)}) %collective-permute-start.9) | collective-permute-done | bytes 131104 | tf_op jit(solution)/shard_map/ppermute | solution.py:395
  34.0 4.8 %collective-permute-done.10.far = bf16[256,256]{1,0:T(8,128)(2,1)S(1)} collective-permute-done((bf16[256,256]{1,0:T(8,128)(2,1)S(1)}, bf16[256,256]{1,0:T(8,128)(2,1)S(1)}, u32[]{:S(2)}, u32[]{:S(2)}) %collective-permute-start.10) | collective-permute-done | bytes 131104 | tf_op jit(solution)/shard_map/ppermute | solution.py:395
  38.8 0.1 shard_map.82.refs_4_
  38.9 2.6 %collective-permute-start.13 = (bf16[256,256]{1,0:T(8,128)(2,1)S(1)}, bf16[256,256]{1,0:T(8,128)(2,1)S(1)}, u32[]{:S(2)}, u32[]{:S(2)}) collective-permute-start(bf16[256,256]{1,0:T(8,128)(2,1)S(1)} %shard_map.82.refs_4_), channel_id=1, source_target_pairs={{0,192},{1,49},{16,208},{17,33},{32,224},{33,17},{48,240},{49,1},{... | collective-permute-start | bytes 393224 | tf_op jit(solution)/shard_map/ppermute | solution.py:351
  41.5 0.0 collective-permute-start.12
  41.5 9.4 %collective-permute-done.13.refs_7_ = bf16[256,256]{1,0:T(8,128)(2,1)S(1)} collective-permute-done((bf16[256,256]{1,0:T(8,128)(2,1)S(1)}, bf16[256,256]{1,0:T(8,128)(2,1)S(1)}, u32[]{:S(2)}, u32[]{:S(2)}) %collective-permute-start.13) | collective-permute-done | bytes 131104 | tf_op jit(solution)/shard_map/ppermute | solution.py:351
  50.9 0.0 collective-permute-start.11
  50.9 0.0 collective-permute-done.12.refs_6_
  50.9 3.8 %collective-permute-done.11.refs_5_ = bf16[256,256]{1,0:T(8,128)(2,1)S(1)} collective-permute-done((bf16[256,256]{1,0:T(8,128)(2,1)S(1)}, bf16[256,256]{1,0:T(8,128)(2,1)S(1)}, u32[]{:S(2)}, u32[]{:S(2)}) %collective-permute-start.11) | collective-permute-done | bytes 131104 | tf_op jit(solution)/shard_map/ppermute | solution.py:351
  54.7 1.1 %shard_map.85 = bf16[512,256]{1,0:T(8,128)(2,1)S(1)} custom-call(s32[3]{0:T(128)S(1)} %pad_add_fusion.places_ref, bf16[256,2048]{1,0:T(8,128)(2,1)S(1)} %get-tuple-element.50.refs_0_, bf16[256,2048]{1,0:T(8,128)(2,1)S(1)} %collective-permute-done.4.refs_1_, bf16[256,2048]{1,0:T(8,128)(2,1)S(1)} %collective-permute-done.5.refs_2_, ...), custom_call_target="tpu_custom_call" | custom-call | flops 268435456 | bytes 2097152 | tf_op jit(solution)/shard_map/pallas_call | solution.py:286
  55.8 1.1 %shard_map.84 = bf16[512,256]{1,0:T(8,128)(2,1)S(1)} custom-call(s32[3]{0:T(128)S(1)} %pad_add_fusion.places_ref, bf16[256,2048]{1,0:T(8,128)(2,1)S(1)} %get-tuple-element.50.refs_0_, bf16[256,2048]{1,0:T(8,128)(2,1)S(1)} %collective-permute-done.4.refs_1_, bf16[256,2048]{1,0:T(8,128)(2,1)S(1)} %collective-permute-done.5.refs_2_, ...), custom_call_target="tpu_custom_call" | custom-call | flops 268435456 | bytes 2097152 | tf_op jit(solution)/shard_map/pallas_call | solution.py:286
  56.9 3.8 %collective-permute-start.17 = (bf16[128,1024]{1,0:T(8,128)(2,1)S(1)}, bf16[128,1024]{1,0:T(8,128)(2,1)S(1)}, u32[]{:S(2)}, u32[]{:S(2)}) collective-permute-start(bf16[128,1024]{1,0:T(8,128)(2,1)S(1)} %get-tuple-element.59), channel_id=1, source_target_pairs={{0,1},{1,0},{2,3},{3,2},{4,5},{5,4},{6,7},{7,6},{8,9},{9,8},{10,11... | collective-permute-start | bytes 786440 | tf_op jit(solution)/shard_map/ppermute | solution.py:406
  60.7 1.1 %shard_map.83 = bf16[512,256]{1,0:T(8,128)(2,1)S(1)} custom-call(s32[3]{0:T(128)S(1)} %pad_add_fusion.places_ref, bf16[256,2048]{1,0:T(8,128)(2,1)S(1)} %get-tuple-element.50.refs_0_, bf16[256,2048]{1,0:T(8,128)(2,1)S(1)} %collective-permute-done.4.refs_1_, bf16[256,2048]{1,0:T(8,128)(2,1)S(1)} %collective-permute-done.5.refs_2_, ...), custom_call_target="tpu_custom_call" | custom-call | flops 268435456 | bytes 2097152 | tf_op jit(solution)/shard_map/pallas_call | solution.py:286
  61.8 0.1 collective-permute-start.14
  61.9 0.5 collective-permute-start.15
  62.4 2.7 %collective-permute-start.16 = (bf16[512,256]{1,0:T(8,128)(2,1)S(1)}, bf16[512,256]{1,0:T(8,128)(2,1)S(1)}, u32[]{:S(2)}, u32[]{:S(2)}) collective-permute-start(bf16[512,256]{1,0:T(8,128)(2,1)S(1)} %shard_map.85), channel_id=1, source_target_pairs={{0,48},{1,193},{16,32},{17,209},{32,16},{33,225},{48,0},{49,241},{... | collective-permute-start | bytes 786440 | tf_op jit(solution)/shard_map/ppermute | solution.py:351
  65.1 1.1 %shard_map.87.refs_0_ = f32[512,256]{1,0:T(8,128)S(1)} custom-call(s32[3]{0:T(128)S(1)} %pad_add_fusion.places_ref, bf16[256,2048]{1,0:T(8,128)(2,1)S(1)} %get-tuple-element.50.refs_0_, bf16[256,2048]{1,0:T(8,128)(2,1)S(1)} %collective-permute-done.4.refs_1_, bf16[256,2048]{1,0:T(8,128)(2,1)S(1)} %collective-permute-done.5.refs_2_, ...), custom_call_target="tpu_custom_call" | custom-call | flops 268435456 | bytes 2097152 | tf_op jit(solution)/shard_map/pallas_call | solution.py:286
  66.2 0.0 collective-permute-done.17.other
  66.3 1.4 %shard_map.86 = bf16[128,2048]{1,0:T(8,128)(2,1)} custom-call(s32[2]{0:T(128)S(1)} %pad_add_fusion.1.here_ref, bf16[128,1024]{1,0:T(8,128)(2,1)S(1)} %get-tuple-element.58.mine, bf16[128,1024]{1,0:T(8,128)(2,1)S(1)} %collective-permute-done.17.other), custom_call_target="tpu_custom_call" | custom-call | bytes 1048576 | tf_op jit(solution)/shard_map/pallas_call | solution.py:262
  67.6 1.3 %collective-permute-done.14.refs_1_ = bf16[512,256]{1,0:T(8,128)(2,1)S(1)} collective-permute-done((bf16[512,256]{1,0:T(8,128)(2,1)S(1)}, bf16[512,256]{1,0:T(8,128)(2,1)S(1)}, u32[]{:S(2)}, u32[]{:S(2)}) %collective-permute-start.14) | collective-permute-done | bytes 262176 | tf_op jit(solution)/shard_map/ppermute | solution.py:351
  68.9 0.3 collective-permute-done.15.refs_2_
  69.2 2.4 %collective-permute-done.16.refs_3_ = bf16[512,256]{1,0:T(8,128)(2,1)S(1)} collective-permute-done((bf16[512,256]{1,0:T(8,128)(2,1)S(1)}, bf16[512,256]{1,0:T(8,128)(2,1)S(1)}, u32[]{:S(2)}, u32[]{:S(2)}) %collective-permute-start.16) | collective-permute-done | bytes 262176 | tf_op jit(solution)/shard_map/ppermute | solution.py:351
  71.7 0.1 shard_map.88
  71.8 18.7 %all_to_all.5.parts = bf16[16,32,256]{2,1,0:T(8,128)(2,1)S(1)} all-to-all(bf16[16,32,256]{2,1,0:T(8,128)(2,1)S(1)} %bitcast.25), channel_id=1, replica_groups=mesh['y'=4,'x'=4,'z_hi'=2,'z_lo'=4,'core'=2] {'z_hi','z_lo','core'}, dimensions={0} | all-to-all | bytes 524288 | tf_op jit(solution)/shard_map/all_to_all | solution.py:412
  90.5 0.7 shard_map.89
  (11 shorter events, 0.0 us)
Async XLA Ops:
  0.6 14.7 %copy-start = (bf16[1,128,8192]{2,1,0:T(8,128)(2,1)S(1)}, bf16[1,128,8192]{2,1,0:T(8,128)(2,1)}, u32[]{:S(2)}) copy-start(bf16[1,128,8192]{2,1,0:T(8,128)(2,1)} %param.10) | copy-start | bytes 6291460
  0.6 14.7 %collective-permute-start = (bf16[128,8192]{1,0:T(8,128)(2,1)}, bf16[128,8192]{1,0:T(8,128)(2,1)}, u32[]{:S(2)}, u32[]{:S(2)}) collective-permute-start(bf16[128,8192]{1,0:T(8,128)(2,1)} %bitcast.23), channel_id=1, source_target_pairs={{0,1},{1,0},{2,3},{3,2},{4,5},{5,4},{6,7},{7,6},{8,9},{9,8},{10,11... | collective-permute-start | bytes 6291464 | tf_op jit(solution)/shard_map/ppermute | solution.py:383
  4.8 3.0 %collective-permute-start.1 = (bf16[128,256]{1,0:T(8,128)(2,1)S(1)}, bf16[128,256]{1,0:T(8,128)(2,1)S(1)}, u32[]{:S(2)}, u32[]{:S(2)}) collective-permute-start(bf16[128,256]{1,0:T(8,128)(2,1)S(1)} %pad_maximum_fusion), channel_id=1, source_target_pairs={{0,1},{1,0},{2,3},{3,2},{4,5},{5,4},{6,7},{7,6},{8,9},{9,8},{10,11... | collective-permute-start | bytes 196616 | tf_op jit(solution)/shard_map/ppermute | solution.py:362
  7.9 10.0 %collective-permute-start.2 = (bf16[128,1024]{1,0:T(8,128)(2,1)}, bf16[128,1024]{1,0:T(8,128)(2,1)S(1)}, u32[]{:S(2)}, u32[]{:S(2)}) collective-permute-start(bf16[128,1024]{1,0:T(8,128)(2,1)} %get-tuple-element.37), channel_id=1, source_target_pairs={{0,1},{1,0},{2,3},{3,2},{4,5},{5,4},{6,7},{7,6},{8,9},{9,8},{10,11... | collective-permute-start | bytes 786440 | tf_op jit(solution)/shard_map/ppermute | solution.py:369
  8.3 9.6 %collective-permute-start.3 = (bf16[128,1024]{1,0:T(8,128)(2,1)}, bf16[128,1024]{1,0:T(8,128)(2,1)S(1)}, u32[]{:S(2)}, u32[]{:S(2)}) collective-permute-start(bf16[128,1024]{1,0:T(8,128)(2,1)} %get-tuple-element.38), channel_id=1, source_target_pairs={{0,1},{1,0},{2,3},{3,2},{4,5},{5,4},{6,7},{7,6},{8,9},{9,8},{10,11... | collective-permute-start | bytes 786440 | tf_op jit(solution)/shard_map/ppermute | solution.py:369
  8.5 14.1 %collective-permute-start.8 = (bf16[256,256]{1,0:T(8,128)(2,1)S(1)}, bf16[256,256]{1,0:T(8,128)(2,1)S(1)}, u32[]{:S(2)}, u32[]{:S(2)}) collective-permute-start(bf16[256,256]{1,0:T(8,128)(2,1)S(1)} %shard_map.78.chip_pair), channel_id=1, source_target_pairs={{0,4},{1,5},{2,6},{3,7},{8,12},{9,13},{10,14},{11,15},{16,20},{17,... | collective-permute-start | bytes 393224 | tf_op jit(solution)/shard_map/ppermute | solution.py:379
  11.6 11.0 %collective-permute-start.7 = (bf16[256,256]{1,0:T(8,128)(2,1)S(1)}, bf16[256,256]{1,0:T(8,128)(2,1)S(1)}, u32[]{:S(2)}, u32[]{:S(2)}) collective-permute-start(bf16[256,256]{1,0:T(8,128)(2,1)S(1)} %shard_map.78.chip_pair), channel_id=1, source_target_pairs={{0,2},{1,3},{2,4},{3,5},{4,6},{5,7},{8,10},{9,11},{10,12},{11,13},... | collective-permute-start | bytes 393224 | tf_op jit(solution)/shard_map/ppermute | solution.py:379
  15.3 6.5 %copy-start.1 = (s32[1,1024]{1,0:T(1,128)S(1)}, s32[1,1024]{1,0:T(1,128)}, u32[]{:S(2)}) copy-start(s32[1,1024]{1,0:T(1,128)} %docs) | copy-start | bytes 12292
  17.9 36.8 %collective-permute-start.4 = (bf16[256,2048]{1,0:T(8,128)(2,1)S(1)}, bf16[256,2048]{1,0:T(8,128)(2,1)S(1)}, u32[]{:S(2)}, u32[]{:S(2)}) collective-permute-start(bf16[256,2048]{1,0:T(8,128)(2,1)S(1)} %get-tuple-element.40), channel_id=1, source_target_pairs={{0,64},{1,17},{16,80},{17,1},{32,96},{33,49},{48,112},{49,33},{64,... | collective-permute-start | bytes 3145736 | tf_op jit(solution)/shard_map/ppermute | solution.py:351
  19.2 35.5 %collective-permute-start.5 = (bf16[256,2048]{1,0:T(8,128)(2,1)S(1)}, bf16[256,2048]{1,0:T(8,128)(2,1)S(1)}, u32[]{:S(2)}, u32[]{:S(2)}) collective-permute-start(bf16[256,2048]{1,0:T(8,128)(2,1)S(1)} %get-tuple-element.41), channel_id=1, source_target_pairs={{0,128},{1,33},{16,144},{17,49},{32,160},{33,1},{48,176},{49,17},{... | collective-permute-start | bytes 3145736 | tf_op jit(solution)/shard_map/ppermute | solution.py:351
  21.7 33.0 %collective-permute-start.6 = (bf16[256,2048]{1,0:T(8,128)(2,1)S(1)}, bf16[256,2048]{1,0:T(8,128)(2,1)S(1)}, u32[]{:S(2)}, u32[]{:S(2)}) collective-permute-start(bf16[256,2048]{1,0:T(8,128)(2,1)S(1)} %get-tuple-element.42), channel_id=1, source_target_pairs={{0,192},{1,49},{16,208},{17,33},{32,224},{33,17},{48,240},{49,1},{... | collective-permute-start | bytes 3145736 | tf_op jit(solution)/shard_map/ppermute | solution.py:351
  28.0 6.0 %collective-permute-start.9 = (bf16[256,256]{1,0:T(8,128)(2,1)S(1)}, bf16[256,256]{1,0:T(8,128)(2,1)S(1)}, u32[]{:S(2)}, u32[]{:S(2)}) collective-permute-start(bf16[256,256]{1,0:T(8,128)(2,1)S(1)} %get-tuple-element.47), channel_id=1, source_target_pairs={{2,0},{3,1},{4,2},{5,3},{6,4},{7,5},{10,8},{11,9},{12,10},{13,11},... | collective-permute-start | bytes 393224 | tf_op jit(solution)/shard_map/ppermute | solution.py:395
  29.3 9.5 %collective-permute-start.10 = (bf16[256,256]{1,0:T(8,128)(2,1)S(1)}, bf16[256,256]{1,0:T(8,128)(2,1)S(1)}, u32[]{:S(2)}, u32[]{:S(2)}) collective-permute-start(bf16[256,256]{1,0:T(8,128)(2,1)S(1)} %get-tuple-element.48), channel_id=1, source_target_pairs={{4,0},{5,1},{6,2},{7,3},{12,8},{13,9},{14,10},{15,11},{20,16},{21,... | collective-permute-start | bytes 393224 | tf_op jit(solution)/shard_map/ppermute | solution.py:395
  38.9 12.0 %collective-permute-start.13 = (bf16[256,256]{1,0:T(8,128)(2,1)S(1)}, bf16[256,256]{1,0:T(8,128)(2,1)S(1)}, u32[]{:S(2)}, u32[]{:S(2)}) collective-permute-start(bf16[256,256]{1,0:T(8,128)(2,1)S(1)} %shard_map.82.refs_4_), channel_id=1, source_target_pairs={{0,192},{1,49},{16,208},{17,33},{32,224},{33,17},{48,240},{49,1},{... | collective-permute-start | bytes 393224 | tf_op jit(solution)/shard_map/ppermute | solution.py:351
  41.5 9.4 %collective-permute-start.12 = (bf16[256,256]{1,0:T(8,128)(2,1)S(1)}, bf16[256,256]{1,0:T(8,128)(2,1)S(1)}, u32[]{:S(2)}, u32[]{:S(2)}) collective-permute-start(bf16[256,256]{1,0:T(8,128)(2,1)S(1)} %shard_map.82.refs_4_), channel_id=1, source_target_pairs={{0,128},{1,33},{16,144},{17,49},{32,160},{33,1},{48,176},{49,17},{... | collective-permute-start | bytes 393224 | tf_op jit(solution)/shard_map/ppermute | solution.py:351
  50.9 3.8 %collective-permute-start.11 = (bf16[256,256]{1,0:T(8,128)(2,1)S(1)}, bf16[256,256]{1,0:T(8,128)(2,1)S(1)}, u32[]{:S(2)}, u32[]{:S(2)}) collective-permute-start(bf16[256,256]{1,0:T(8,128)(2,1)S(1)} %shard_map.82.refs_4_), channel_id=1, source_target_pairs={{0,64},{1,17},{16,80},{17,1},{32,96},{33,49},{48,112},{49,33},{64,... | collective-permute-start | bytes 393224 | tf_op jit(solution)/shard_map/ppermute | solution.py:351
  56.9 9.4 %collective-permute-start.17 = (bf16[128,1024]{1,0:T(8,128)(2,1)S(1)}, bf16[128,1024]{1,0:T(8,128)(2,1)S(1)}, u32[]{:S(2)}, u32[]{:S(2)}) collective-permute-start(bf16[128,1024]{1,0:T(8,128)(2,1)S(1)} %get-tuple-element.59), channel_id=1, source_target_pairs={{0,1},{1,0},{2,3},{3,2},{4,5},{5,4},{6,7},{7,6},{8,9},{9,8},{10,11... | collective-permute-start | bytes 786440 | tf_op jit(solution)/shard_map/ppermute | solution.py:406
  61.8 7.2 %collective-permute-start.14 = (bf16[512,256]{1,0:T(8,128)(2,1)S(1)}, bf16[512,256]{1,0:T(8,128)(2,1)S(1)}, u32[]{:S(2)}, u32[]{:S(2)}) collective-permute-start(bf16[512,256]{1,0:T(8,128)(2,1)S(1)} %shard_map.83), channel_id=1, source_target_pairs={{0,32},{1,129},{16,48},{17,145},{32,0},{33,161},{48,16},{49,177},{... | collective-permute-start | bytes 786440 | tf_op jit(solution)/shard_map/ppermute | solution.py:351
  61.9 7.4 %collective-permute-start.15 = (bf16[512,256]{1,0:T(8,128)(2,1)S(1)}, bf16[512,256]{1,0:T(8,128)(2,1)S(1)}, u32[]{:S(2)}, u32[]{:S(2)}) collective-permute-start(bf16[512,256]{1,0:T(8,128)(2,1)S(1)} %shard_map.84), channel_id=1, source_target_pairs={{0,16},{1,65},{16,0},{17,81},{32,48},{33,97},{48,32},{49,113},{64,... | collective-permute-start | bytes 786440 | tf_op jit(solution)/shard_map/ppermute | solution.py:351
  62.4 9.3 %collective-permute-start.16 = (bf16[512,256]{1,0:T(8,128)(2,1)S(1)}, bf16[512,256]{1,0:T(8,128)(2,1)S(1)}, u32[]{:S(2)}, u32[]{:S(2)}) collective-permute-start(bf16[512,256]{1,0:T(8,128)(2,1)S(1)} %shard_map.85), channel_id=1, source_target_pairs={{0,48},{1,193},{16,32},{17,209},{32,16},{33,225},{48,0},{49,241},{... | collective-permute-start | bytes 786440 | tf_op jit(solution)/shard_map/ppermute | solution.py:351

commit v11 on v10

--- a/solution.py
+++ b/solution.py
@@ -33,7 +33,6 @@
     return jax.ShapeDtypeStruct(shape, dtype)
 
 
-HBM = pl.BlockSpec(memory_space=pltpu.HBM)
 SCALAR = pl.BlockSpec(memory_space=pltpu.SMEM)
 
 
@@ -53,40 +52,29 @@
     )(keys, values, swapped)
 
 
-def chunk_kernel(places_ref, mine, other, *refs):
-    outs, sems = refs[:-1], refs[-1]
-    n = len(outs)
+def block_of(places_ref, k, i, n):
+    y, x, core = places_ref[0], places_ref[1], places_ref[2]
+    return jnp.where(core == 0, (y ^ k) * n + i, i * n + (x ^ k))
+
+
+def chunk_kernel(places_ref, mine, other, *outs):
+    n = len(outs) + 1
     rows, step = mine.shape[0], outs[0].shape[1] // n
-    y, x, core = places_ref[0], places_ref[1], places_ref[2]
-    copies = []
-    for k, out in enumerate(outs):
+    for k, out in enumerate(outs, 1):
         for i in range(n):
-            block = jnp.where(core == 0, (y ^ k) * n + i, i * n + (x ^ k))
-            held = pl.ds(pl.multiple_of(block * step, step), step)
-            for half, part in enumerate((mine, other)):
-                copies.append(
-                    pltpu.make_async_copy(
-                        part.at[:, held],
-                        out.at[half * rows : (half + 1) * rows, i * step : (i + 1) * step],
-                        sems.at[len(copies)],
-                    )
-                )
-    for copy in copies:
-        copy.start()
-    for copy in copies:
-        copy.wait()
+            held = pl.ds(pl.multiple_of(block_of(places_ref, k, i, n) * step, step), step)
+            out[:rows, i * step : (i + 1) * step] = mine[:, held]
+            out[rows:, i * step : (i + 1) * step] = other[:, held]
 
 
 def split_columns(places, mine, other, chunks):
     rows, width = mine.shape
     return pl.pallas_call(
         chunk_kernel,
-        out_shape=(whole((2 * rows, width // chunks)),) * chunks,
-        in_specs=[SCALAR, HBM, HBM],
-        out_specs=(HBM,) * chunks,
-        scratch_shapes=[pltpu.SemaphoreType.DMA((2 * chunks * chunks,))],
-        compiler_params=SMALL,
-        cost_estimate=pl.CostEstimate(flops=0, bytes_accessed=8 * MIB, transcendentals=0),
+        out_shape=(whole((2 * rows, width // chunks)),) * (chunks - 1),
+        in_specs=[SCALAR, pl.BlockSpec(), pl.BlockSpec()],
+        compiler_params=pltpu.CompilerParams(vmem_limit_bytes=16 * MIB),
+        cost_estimate=pl.CostEstimate(flops=0, bytes_accessed=6 * MIB, transcendentals=0),
     )(places, mine, other)
 
 
@@ -268,32 +256,35 @@
     )(here, mine, other)
 
 
-def project_kernel(places_ref, *refs, offset):
+def project_kernel(places_ref, mine, other, *refs, offset):
     n = len(refs) // 2
-    pieces, grads, out = refs[:n], refs[n:-1], refs[-1]
+    pieces, grads, out = refs[: n - 1], refs[n - 1 : -1], refs[-1]
     step = out.shape[0]
     place = jnp.where(places_ref[2] == 0, places_ref[1], places_ref[0]) ^ offset
     columns = pl.ds(pl.multiple_of(place * step, step), step)
+    held = pl.ds(pl.multiple_of(block_of(places_ref, 0, place, n) * step, step), step)
     left = jnp.concatenate([ref[...] for ref in grads], axis=1)
-    right = jnp.concatenate([ref[:, columns] for ref in pieces], axis=0)
+    right = jnp.concatenate(
+        [mine[:, held], other[:, held]] + [ref[:, columns] for ref in pieces], axis=0
+    )
     out[...] = dot_nn(left, right).T.astype(out.dtype)
 
 
-def project(places, pieces, grads, offset, dtype):
+def project(places, own, pieces, grads, offset, dtype):
     rows, columns = pieces[0].shape
     width = grads[0].shape[0]
-    step = columns // len(pieces)
+    step = columns // len(grads)
     return pl.pallas_call(
         functools.partial(project_kernel, offset=offset),
         out_shape=whole((step, width), dtype),
-        in_specs=[SCALAR] + [pl.BlockSpec()] * (2 * len(pieces)),
+        in_specs=[SCALAR] + [pl.BlockSpec()] * (1 + 2 * len(grads)),
         compiler_params=pltpu.CompilerParams(vmem_limit_bytes=16 * MIB),
         cost_estimate=pl.CostEstimate(
-            flops=2 * len(pieces) * rows * step * width,
+            flops=2 * len(grads) * rows * step * width,
             bytes_accessed=2 * MIB,
             transcendentals=0,
         ),
-    )(places, *pieces, *grads)
+    )(places, *own, *pieces, *grads)
 
 
 def add_kernel(*refs):
@@ -379,11 +370,10 @@
         lax.ppermute(chip_pair, ("z_lo", "core"), behind(distance)) for distance in (2, 1)
     ][::-1]
 
-    chunks = split_columns(
-        places_ref, layer_input[0], lax.ppermute(layer_input[0], "core", swap), n_side
-    )
+    own = (layer_input[0], lax.ppermute(layer_input[0], "core", swap))
+    chunks = split_columns(places_ref, *own, n_side)
     chunks, _ = lax.optimization_barrier((chunks, (q_other, do_other)))
-    pieces = [chunks[0]] + [cross(chunks[k], k, True) for k in range(1, n_side)]
+    pieces = [cross(chunk, k, True) for k, chunk in enumerate(chunks, 1)]
     docs, _ = lax.optimization_barrier((segment_ids, chunks[0]))
 
     operands = (q_mine, do_mine, q_other, do_other, *blocks)
@@ -398,14 +388,13 @@
 
     grad = combine(own_grad, near_back, far_back)
     grads = [grad] + [cross(grad, k, True) for k in range(1, n_side)]
-    pieces, grads, dq_other = lax.optimization_barrier((pieces, grads, dq_other))
-    parts = []
-    for k in (2, 1, 3):
-        parts.append(cross(project(places_ref, pieces, grads, k, jnp.bfloat16), k, False))
-    own_term = project(places_ref, pieces, grads, 0, jnp.float32)
+    dq_other, grads[2:] = lax.optimization_barrier((dq_other, grads[2:]))
     dq_back = lax.ppermute(dq_other, "core", swap)
     query_grad = assemble(here_ref, dq_mine, dq_back)[None]
-    parts, query_grad = lax.optimization_barrier((parts, query_grad))
+    pieces, grads, query_grad = lax.optimization_barrier((pieces, grads, query_grad))
+    terms = [project(places_ref, own, pieces, grads, k, jnp.bfloat16) for k in (2, 1, 3)]
+    parts = [cross(term, k, False) for term, k in zip(terms, (2, 1, 3))]
+    own_term = project(places_ref, own, pieces, grads, 0, jnp.float32)
     term = add_parts(own_term, parts)
     rest = ("z_hi", "z_lo", "core")
     n_rest = lax.axis_size(rest)

time: 91.4 us -> 94.2 us (1.031)
  waiting for transfers between devices: 25.1 us -> 20.3 us
  blocking collectives: 18.7 us -> 22.4 us
  Pallas kernels: 16.4 us -> 19.9 us
    ppermute x9, waiting for transfers between devices: 17.3 us -> 12.6 us  [cross(): return lax.ppermute(part, ('y', 'x', 'core'), pairs)]
    pallas_call x4, Pallas kernels: 4.33 us -> 8.56 us  [project(): pl.pallas_call(functools.partial(project_kernel, offset=offset), out_shap...]
    all_to_all x1, blocking collectives: 18.7 us -> 22.4 us  [per_device(): lax.all_to_all(term.reshape(n_rest, term.shape[0] // n_rest, term.shape[1...]
    ppermute x9, starting transfers between devices: 9.85 us -> 11.2 us  [cross(): return lax.ppermute(part, ('y', 'x', 'core'), pairs)]
    ppermute x1, starting transfers between devices: 3.84 us -> 2.64 us  [per_device(): dq_back = lax.ppermute(dq_other, 'core', swap)]
  transfers between devices with their start and end apart: 18 -> 18, of which waited for: 8 -> 6; matrix products, arithmetic and copies ran while one was open for 3% -> 3% of each run, Pallas kernels for 15% -> 18%
where the time goes in v11:
time: 94.2 us; the launch traced here: 93.7 us
  starting transfers between devices  27.3 us (29%)
  blocking collectives  22.4 us (24%)
  waiting for transfers between devices  20.3 us (22%)
  Pallas kernels  19.9 us (21%)
  local copies, waits for them, and re-layouts  2.89 us (3%)
    all_to_all x1, blocking collectives, per_device(): lax.all_to_all(term.reshape(n_rest, term.shape[0] // n_rest, term.shape[1...  22.4 us
    ppermute x9, waiting for transfers between devices, cross(): return lax.ppermute(part, ('y', 'x', 'core'), pairs)  12.6 us
    ppermute x9, starting transfers between devices, cross(): return lax.ppermute(part, ('y', 'x', 'core'), pairs)  11.2 us
    pallas_call x4, Pallas kernels, project(): pl.pallas_call(functools.partial(project_kernel, offset=offset), out_shap...  8.56 us
    ppermute x2, waiting for transfers between devices, per_device(): lax.ppermute(part, ('z_lo', 'core'), [(b, a) for a, b in behind(distance)])  6.94 us
    ppermute x2, starting transfers between devices, per_device(): lax.ppermute(chip_pair, ('z_lo', 'core'), behind(distance))  6.7 us
    pallas_call x1, Pallas kernels, attention(): pl.pallas_call(attention_kernel, out_shape=(whole((chip, 2 * DH)), whole(...  5.34 us
    ppermute x1, starting transfers between devices, per_device(): own = (layer_input[0], lax.ppermute(layer_input[0], 'core', swap))  3.33 us
  transfers between devices with their start and end apart: 18, of which 6 were waited for; matrix products, arithmetic and copies ran while one was open for 3% of the time, Pallas kernels for 18%

profile of v11, /device:TPU:1, one launch (start us, length us, event | category | flops | bytes accessed | tf_op | source)
XLA Modules:
  0.0 93.7 jit_solution(325729869093942406)
XLA Ops:
  0.6 3.3 %collective-permute-start = (bf16[128,8192]{1,0:T(8,128)(2,1)}, bf16[128,8192]{1,0:T(8,128)(2,1)}, u32[]{:S(2)}, u32[]{:S(2)}) collective-permute-start(bf16[128,8192]{1,0:T(8,128)(2,1)} %bitcast.23), channel_id=1, source_target_pairs={{0,1},{1,0},{2,3},{3,2},{4,5},{5,4},{6,7},{7,6},{8,9},{9,8},{10,11... | collective-permute-start | bytes 6291464 | tf_op jit(solution)/shard_map/ppermute | solution.py:373
  4.0 0.8 dynamic-slice_bitcast_fusion.4
  4.8 0.2 collective-permute-start.1
  5.0 2.1 %dynamic-slice_bitcast_fusion = (bf16[128,1024]{1,0:T(8,128)(2,1)S(1)}, bf16[128,1024]{1,0:T(8,128)(2,1)}, bf16[128,1024]{1,0:T(8,128)(2,1)}, bf16[128,1024]{1,0:T(8,128)(2,1)S(1)}) fusion(bf16[1,128,2048]{2,1,0:T(8,128)(2,1)} %param.9, s32[]{:T(128)S(6)} %select_n.19, s32[]{:T(128)S(6)} %select_n.16, bf16[1,128,2048]{2,1,0:T(8,128)(2,1)} %param.6), kind=kLoop, calls=%fused_computation | loop fusion | bytes 2097160 | tf_op jit(solution)/shard_map/dynamic_slice | solution.py:347
  7.1 0.7 collective-permute-done.1.swapped
  7.9 0.5 collective-permute-start.2
  8.3 0.1 collective-permute-start.3
  8.5 3.2 %collective-permute-start.8 = (bf16[256,256]{1,0:T(8,128)(2,1)S(1)}, bf16[256,256]{1,0:T(8,128)(2,1)S(1)}, u32[]{:S(2)}, u32[]{:S(2)}) collective-permute-start(bf16[256,256]{1,0:T(8,128)(2,1)S(1)} %shard_map.78.chip_pair), channel_id=1, source_target_pairs={{0,4},{1,5},{2,6},{3,7},{8,12},{9,13},{10,14},{11,15},{16,20},{17,... | collective-permute-start | bytes 393224 | tf_op jit(solution)/shard_map/ppermute | solution.py:370
  11.6 3.5 %collective-permute-start.7 = (bf16[256,256]{1,0:T(8,128)(2,1)S(1)}, bf16[256,256]{1,0:T(8,128)(2,1)S(1)}, u32[]{:S(2)}, u32[]{:S(2)}) collective-permute-start(bf16[256,256]{1,0:T(8,128)(2,1)S(1)} %shard_map.78.chip_pair), channel_id=1, source_target_pairs={{0,2},{1,3},{2,4},{3,5},{4,6},{5,7},{8,10},{9,11},{10,12},{11,13},... | collective-permute-start | bytes 393224 | tf_op jit(solution)/shard_map/ppermute | solution.py:370
  15.2 0.1 pad_add_fusion.1.here_ref
  15.3 0.1 pad_add_fusion.places_ref
  15.3 0.0 collective-permute-done.other
  15.3 1.8 %shard_map.77 = (bf16[256,2048]{1,0:T(8,128)(2,1)S(1)}, bf16[256,2048]{1,0:T(8,128)(2,1)S(1)}, bf16[256,2048]{1,0:T(8,128)(2,1)S(1)}) custom-call(s32[3]{0:T(128)S(1)} %pad_add_fusion.places_ref, bf16[128,8192]{1,0:T(8,128)(2,1)S(1)} %bitcast.24, bf16[128,8192]{1,0:T(8,128)(2,1)} %collective-permute-done.other), custom_call_target="tpu_custom_call" | custom-call | bytes 6291456 | tf_op jit(solution)/shard_map/pallas_call | solution.py:72
  17.2 0.0 collective-permute-done.2.q_other
  17.2 0.0 collective-permute-done.3.do_other
  17.2 1.3 %collective-permute-start.4 = (bf16[256,2048]{1,0:T(8,128)(2,1)S(1)}, bf16[256,2048]{1,0:T(8,128)(2,1)S(1)}, u32[]{:S(2)}, u32[]{:S(2)}) collective-permute-start(bf16[256,2048]{1,0:T(8,128)(2,1)S(1)} %get-tuple-element.34), channel_id=1, source_target_pairs={{0,64},{1,17},{16,80},{17,1},{32,96},{33,49},{48,112},{49,33},{64,... | collective-permute-start | bytes 3145736 | tf_op jit(solution)/shard_map/ppermute | solution.py:342
  18.5 2.4 %collective-permute-start.5 = (bf16[256,2048]{1,0:T(8,128)(2,1)S(1)}, bf16[256,2048]{1,0:T(8,128)(2,1)S(1)}, u32[]{:S(2)}, u32[]{:S(2)}) collective-permute-start(bf16[256,2048]{1,0:T(8,128)(2,1)S(1)} %get-tuple-element.35), channel_id=1, source_target_pairs={{0,128},{1,33},{16,144},{17,49},{32,160},{33,1},{48,176},{49,17},{... | collective-permute-start | bytes 3145736 | tf_op jit(solution)/shard_map/ppermute | solution.py:342
  21.0 0.2 collective-permute-start.6
  21.2 0.7 shard_map.79.bias
  21.9 0.0 collective-permute-done.8.far_pair
  21.9 5.3 %shard_map.80 = (bf16[256,256]{1,0:T(8,128)(2,1)S(1)}, bf16[256,256]{1,0:T(8,128)(2,1)S(1)}, bf16[8,768,256]{2,1,0:T(8,128)(2,1)S(1)}, bf16[8,256,256]{2,1,0:T(8,128)(2,1)S(1)}) custom-call(bf16[128,1024]{1,0:T(8,128)(2,1)S(1)} %get-tuple-element.65.q_mine, bf16[128,1024]{1,0:T(8,128)(2,1)S(1)} %get-tuple-element.56.do_mine, ...), custom_call_target="tpu_custom_call" | custom-call | flops 8053063680 | bytes 4194304 | tf_op jit(solution)/shard_map/pallas_call | solution.py:167
  27.3 1.3 %collective-permute-start.9 = (bf16[256,256]{1,0:T(8,128)(2,1)S(1)}, bf16[256,256]{1,0:T(8,128)(2,1)S(1)}, u32[]{:S(2)}, u32[]{:S(2)}) collective-permute-start(bf16[256,256]{1,0:T(8,128)(2,1)S(1)} %get-tuple-element.41), channel_id=1, source_target_pairs={{2,0},{3,1},{4,2},{5,3},{6,4},{7,5},{10,8},{11,9},{12,10},{13,11},... | collective-permute-start | bytes 393224 | tf_op jit(solution)/shard_map/ppermute | solution.py:385
  28.6 1.3 %collective-permute-start.10 = (bf16[256,256]{1,0:T(8,128)(2,1)S(1)}, bf16[256,256]{1,0:T(8,128)(2,1)S(1)}, u32[]{:S(2)}, u32[]{:S(2)}) collective-permute-start(bf16[256,256]{1,0:T(8,128)(2,1)S(1)} %get-tuple-element.42), channel_id=1, source_target_pairs={{4,0},{5,1},{6,2},{7,3},{12,8},{13,9},{14,10},{15,11},{20,16},{21,... | collective-permute-start | bytes 393224 | tf_op jit(solution)/shard_map/ppermute | solution.py:385
  29.9 1.1 %shard_map.81 = (bf16[128,1024]{1,0:T(8,128)(2,1)S(1)}, bf16[128,1024]{1,0:T(8,128)(2,1)S(1)}, f32[256,256]{1,0:T(8,128)S(1)}) custom-call(bf16[128,1024]{1,0:T(8,128)(2,1)S(1)} %get-tuple-element.65.q_mine, bf16[128,1024]{1,0:T(8,128)(2,1)S(1)} %get-tuple-element.56.do_mine, bf16[128,1024]{1,0:T(8,128)(2,1)S(1)} %collective-permute-done.2.q_other, ...), custom_call_target="tpu_custom_call" | custom-call | flops 1207959552 | bytes 6291456 | tf_op jit(solution)/shard_map/pallas_call | solution.py:214
  31.0 2.3 %collective-permute-done.9.near = bf16[256,256]{1,0:T(8,128)(2,1)S(1)} collective-permute-done((bf16[256,256]{1,0:T(8,128)(2,1)S(1)}, bf16[256,256]{1,0:T(8,128)(2,1)S(1)}, u32[]{:S(2)}, u32[]{:S(2)}) %collective-permute-start.9) | collective-permute-done | bytes 131104 | tf_op jit(solution)/shard_map/ppermute | solution.py:385
  33.3 4.7 %collective-permute-done.10.far = bf16[256,256]{1,0:T(8,128)(2,1)S(1)} collective-permute-done((bf16[256,256]{1,0:T(8,128)(2,1)S(1)}, bf16[256,256]{1,0:T(8,128)(2,1)S(1)}, u32[]{:S(2)}, u32[]{:S(2)}) %collective-permute-start.10) | collective-permute-done | bytes 131104 | tf_op jit(solution)/shard_map/ppermute | solution.py:385
  37.9 0.1 shard_map.82.refs_3_
  38.1 2.6 %collective-permute-start.13 = (bf16[256,256]{1,0:T(8,128)(2,1)S(1)}, bf16[256,256]{1,0:T(8,128)(2,1)S(1)}, u32[]{:S(2)}, u32[]{:S(2)}) collective-permute-start(bf16[256,256]{1,0:T(8,128)(2,1)S(1)} %shard_map.82.refs_3_), channel_id=1, source_target_pairs={{0,192},{1,49},{16,208},{17,33},{32,224},{33,17},{48,240},{49,1},{... | collective-permute-start | bytes 393224 | tf_op jit(solution)/shard_map/ppermute | solution.py:342
  40.6 0.0 collective-permute-start.12
  40.6 9.5 %collective-permute-done.13.refs_6_ = bf16[256,256]{1,0:T(8,128)(2,1)S(1)} collective-permute-done((bf16[256,256]{1,0:T(8,128)(2,1)S(1)}, bf16[256,256]{1,0:T(8,128)(2,1)S(1)}, u32[]{:S(2)}, u32[]{:S(2)}) %collective-permute-start.13) | collective-permute-done | bytes 131104 | tf_op jit(solution)/shard_map/ppermute | solution.py:342
  50.2 2.6 %collective-permute-start.14 = (bf16[128,1024]{1,0:T(8,128)(2,1)S(1)}, bf16[128,1024]{1,0:T(8,128)(2,1)S(1)}, u32[]{:S(2)}, u32[]{:S(2)}) collective-permute-start(bf16[128,1024]{1,0:T(8,128)(2,1)S(1)} %get-tuple-element.47), channel_id=1, source_target_pairs={{0,1},{1,0},{2,3},{3,2},{4,5},{5,4},{6,7},{7,6},{8,9},{9,8},{10,11... | collective-permute-start | bytes 786440 | tf_op jit(solution)/shard_map/ppermute | solution.py:392
  52.8 1.2 %collective-permute-start.11 = (bf16[256,256]{1,0:T(8,128)(2,1)S(1)}, bf16[256,256]{1,0:T(8,128)(2,1)S(1)}, u32[]{:S(2)}, u32[]{:S(2)}) collective-permute-start(bf16[256,256]{1,0:T(8,128)(2,1)S(1)} %shard_map.82.refs_3_), channel_id=1, source_target_pairs={{0,64},{1,17},{16,80},{17,1},{32,96},{33,49},{48,112},{49,33},{64,... | collective-permute-start | bytes 393224 | tf_op jit(solution)/shard_map/ppermute | solution.py:342
  54.0 0.0 collective-permute-done.14.other
  54.0 1.4 %shard_map.83 = bf16[128,2048]{1,0:T(8,128)(2,1)} custom-call(s32[2]{0:T(128)S(1)} %pad_add_fusion.1.here_ref, bf16[128,1024]{1,0:T(8,128)(2,1)S(1)} %get-tuple-element.46.mine, bf16[128,1024]{1,0:T(8,128)(2,1)S(1)} %collective-permute-done.14.other), custom_call_target="tpu_custom_call" | custom-call | bytes 1048576 | tf_op jit(solution)/shard_map/pallas_call | solution.py:250
  55.4 1.5 %collective-permute-done.11.refs_4_ = bf16[256,256]{1,0:T(8,128)(2,1)S(1)} collective-permute-done((bf16[256,256]{1,0:T(8,128)(2,1)S(1)}, bf16[256,256]{1,0:T(8,128)(2,1)S(1)}, u32[]{:S(2)}, u32[]{:S(2)}) %collective-permute-start.11) | collective-permute-done | bytes 131104 | tf_op jit(solution)/shard_map/ppermute | solution.py:342
  56.9 2.1 %shard_map.85 = bf16[512,256]{1,0:T(8,128)(2,1)S(1)} custom-call(s32[3]{0:T(128)S(1)} %pad_add_fusion.places_ref, bf16[128,8192]{1,0:T(8,128)(2,1)S(1)} %bitcast.25, bf16[128,8192]{1,0:T(8,128)(2,1)} %collective-permute-done.other, bf16[256,2048]{1,0:T(8,128)(2,1)S(1)} %collective-permute-done.4.refs_0_, ...), custom_call_target="tpu_custom_call" | custom-call | flops 268435456 | bytes 2097152 | tf_op jit(solution)/shard_map/pallas_call | solution.py:277
  59.1 0.1 collective-permute-start.15
  59.2 2.1 %shard_map.86 = bf16[512,256]{1,0:T(8,128)(2,1)S(1)} custom-call(s32[3]{0:T(128)S(1)} %pad_add_fusion.places_ref, bf16[128,8192]{1,0:T(8,128)(2,1)S(1)} %bitcast.26, bf16[128,8192]{1,0:T(8,128)(2,1)} %collective-permute-done.other, bf16[256,2048]{1,0:T(8,128)(2,1)S(1)} %collective-permute-done.4.refs_0_, ...), custom_call_target="tpu_custom_call" | custom-call | flops 268435456 | bytes 2097152 | tf_op jit(solution)/shard_map/pallas_call | solution.py:277
  61.3 0.6 collective-permute-start.16
  61.9 2.1 %shard_map.87 = bf16[512,256]{1,0:T(8,128)(2,1)S(1)} custom-call(s32[3]{0:T(128)S(1)} %pad_add_fusion.places_ref, bf16[128,8192]{1,0:T(8,128)(2,1)S(1)} %bitcast.27, bf16[128,8192]{1,0:T(8,128)(2,1)} %collective-permute-done.other, bf16[256,2048]{1,0:T(8,128)(2,1)S(1)} %collective-permute-done.4.refs_0_, ...), custom_call_target="tpu_custom_call" | custom-call | flops 268435456 | bytes 2097152 | tf_op jit(solution)/shard_map/pallas_call | solution.py:277
  64.0 2.8 %collective-permute-start.17 = (bf16[512,256]{1,0:T(8,128)(2,1)S(1)}, bf16[512,256]{1,0:T(8,128)(2,1)S(1)}, u32[]{:S(2)}, u32[]{:S(2)}) collective-permute-start(bf16[512,256]{1,0:T(8,128)(2,1)S(1)} %shard_map.87), channel_id=1, source_target_pairs={{0,48},{1,193},{16,32},{17,209},{32,16},{33,225},{48,0},{49,241},{... | collective-permute-start | bytes 786440 | tf_op jit(solution)/shard_map/ppermute | solution.py:342
  66.8 2.2 %shard_map.84.refs_0_ = f32[512,256]{1,0:T(8,128)S(1)} custom-call(s32[3]{0:T(128)S(1)} %pad_add_fusion.places_ref, bf16[128,8192]{1,0:T(8,128)(2,1)S(1)} %bitcast.28, bf16[128,8192]{1,0:T(8,128)(2,1)} %collective-permute-done.other, bf16[256,2048]{1,0:T(8,128)(2,1)S(1)} %collective-permute-done.4.refs_0_, ...), custom_call_target="tpu_custom_call" | custom-call | flops 268435456 | bytes 2097152 | tf_op jit(solution)/shard_map/pallas_call | solution.py:277
  69.0 0.0 collective-permute-done.15.refs_1_
  69.0 0.0 collective-permute-done.16.refs_2_
  69.0 1.6 %collective-permute-done.17.refs_3_ = bf16[512,256]{1,0:T(8,128)(2,1)S(1)} collective-permute-done((bf16[512,256]{1,0:T(8,128)(2,1)S(1)}, bf16[512,256]{1,0:T(8,128)(2,1)S(1)}, u32[]{:S(2)}, u32[]{:S(2)}) %collective-permute-start.17) | collective-permute-done | bytes 262176 | tf_op jit(solution)/shard_map/ppermute | solution.py:342
  70.6 0.1 shard_map.88
  70.7 22.4 %all_to_all.5.parts = bf16[16,32,256]{2,1,0:T(8,128)(2,1)S(1)} all-to-all(bf16[16,32,256]{2,1,0:T(8,128)(2,1)S(1)} %bitcast.29), channel_id=1, replica_groups=mesh['y'=4,'x'=4,'z_hi'=2,'z_lo'=4,'core'=2] {'z_hi','z_lo','core'}, dimensions={0} | all-to-all | bytes 524288 | tf_op jit(solution)/shard_map/all_to_all | solution.py:401
  93.1 0.7 shard_map.89
  (11 shorter events, 0.0 us)
Async XLA Ops:
  0.6 14.7 %copy-start = (bf16[1,128,8192]{2,1,0:T(8,128)(2,1)S(1)}, bf16[1,128,8192]{2,1,0:T(8,128)(2,1)}, u32[]{:S(2)}) copy-start(bf16[1,128,8192]{2,1,0:T(8,128)(2,1)} %param.10) | copy-start | bytes 6291460
  0.6 14.7 %collective-permute-start = (bf16[128,8192]{1,0:T(8,128)(2,1)}, bf16[128,8192]{1,0:T(8,128)(2,1)}, u32[]{:S(2)}, u32[]{:S(2)}) collective-permute-start(bf16[128,8192]{1,0:T(8,128)(2,1)} %bitcast.23), channel_id=1, source_target_pairs={{0,1},{1,0},{2,3},{3,2},{4,5},{5,4},{6,7},{7,6},{8,9},{9,8},{10,11... | collective-permute-start | bytes 6291464 | tf_op jit(solution)/shard_map/ppermute | solution.py:373
  4.8 3.0 %collective-permute-start.1 = (bf16[128,256]{1,0:T(8,128)(2,1)S(1)}, bf16[128,256]{1,0:T(8,128)(2,1)S(1)}, u32[]{:S(2)}, u32[]{:S(2)}) collective-permute-start(bf16[128,256]{1,0:T(8,128)(2,1)S(1)} %pad_maximum_fusion), channel_id=1, source_target_pairs={{0,1},{1,0},{2,3},{3,2},{4,5},{5,4},{6,7},{7,6},{8,9},{9,8},{10,11... | collective-permute-start | bytes 196616 | tf_op jit(solution)/shard_map/ppermute | solution.py:353
  7.9 9.3 %collective-permute-start.2 = (bf16[128,1024]{1,0:T(8,128)(2,1)}, bf16[128,1024]{1,0:T(8,128)(2,1)S(1)}, u32[]{:S(2)}, u32[]{:S(2)}) collective-permute-start(bf16[128,1024]{1,0:T(8,128)(2,1)} %get-tuple-element.32), channel_id=1, source_target_pairs={{0,1},{1,0},{2,3},{3,2},{4,5},{5,4},{6,7},{7,6},{8,9},{9,8},{10,11... | collective-permute-start | bytes 786440 | tf_op jit(solution)/shard_map/ppermute | solution.py:360
  8.3 8.9 %collective-permute-start.3 = (bf16[128,1024]{1,0:T(8,128)(2,1)}, bf16[128,1024]{1,0:T(8,128)(2,1)S(1)}, u32[]{:S(2)}, u32[]{:S(2)}) collective-permute-start(bf16[128,1024]{1,0:T(8,128)(2,1)} %get-tuple-element.33), channel_id=1, source_target_pairs={{0,1},{1,0},{2,3},{3,2},{4,5},{5,4},{6,7},{7,6},{8,9},{9,8},{10,11... | collective-permute-start | bytes 786440 | tf_op jit(solution)/shard_map/ppermute | solution.py:360
  8.5 13.4 %collective-permute-start.8 = (bf16[256,256]{1,0:T(8,128)(2,1)S(1)}, bf16[256,256]{1,0:T(8,128)(2,1)S(1)}, u32[]{:S(2)}, u32[]{:S(2)}) collective-permute-start(bf16[256,256]{1,0:T(8,128)(2,1)S(1)} %shard_map.78.chip_pair), channel_id=1, source_target_pairs={{0,4},{1,5},{2,6},{3,7},{8,12},{9,13},{10,14},{11,15},{16,20},{17,... | collective-permute-start | bytes 393224 | tf_op jit(solution)/shard_map/ppermute | solution.py:370
  11.6 10.3 %collective-permute-start.7 = (bf16[256,256]{1,0:T(8,128)(2,1)S(1)}, bf16[256,256]{1,0:T(8,128)(2,1)S(1)}, u32[]{:S(2)}, u32[]{:S(2)}) collective-permute-start(bf16[256,256]{1,0:T(8,128)(2,1)S(1)} %shard_map.78.chip_pair), channel_id=1, source_target_pairs={{0,2},{1,3},{2,4},{3,5},{4,6},{5,7},{8,10},{9,11},{10,12},{11,13},... | collective-permute-start | bytes 393224 | tf_op jit(solution)/shard_map/ppermute | solution.py:370
  15.3 5.8 %copy-start.1 = (s32[1,1024]{1,0:T(1,128)S(1)}, s32[1,1024]{1,0:T(1,128)}, u32[]{:S(2)}) copy-start(s32[1,1024]{1,0:T(1,128)} %docs) | copy-start | bytes 12292
  17.2 39.7 %collective-permute-start.4 = (bf16[256,2048]{1,0:T(8,128)(2,1)S(1)}, bf16[256,2048]{1,0:T(8,128)(2,1)S(1)}, u32[]{:S(2)}, u32[]{:S(2)}) collective-permute-start(bf16[256,2048]{1,0:T(8,128)(2,1)S(1)} %get-tuple-element.34), channel_id=1, source_target_pairs={{0,64},{1,17},{16,80},{17,1},{32,96},{33,49},{48,112},{49,33},{64,... | collective-permute-start | bytes 3145736 | tf_op jit(solution)/shard_map/ppermute | solution.py:342
  18.5 38.4 %collective-permute-start.5 = (bf16[256,2048]{1,0:T(8,128)(2,1)S(1)}, bf16[256,2048]{1,0:T(8,128)(2,1)S(1)}, u32[]{:S(2)}, u32[]{:S(2)}) collective-permute-start(bf16[256,2048]{1,0:T(8,128)(2,1)S(1)} %get-tuple-element.35), channel_id=1, source_target_pairs={{0,128},{1,33},{16,144},{17,49},{32,160},{33,1},{48,176},{49,17},{... | collective-permute-start | bytes 3145736 | tf_op jit(solution)/shard_map/ppermute | solution.py:342
  21.0 36.0 %collective-permute-start.6 = (bf16[256,2048]{1,0:T(8,128)(2,1)S(1)}, bf16[256,2048]{1,0:T(8,128)(2,1)S(1)}, u32[]{:S(2)}, u32[]{:S(2)}) collective-permute-start(bf16[256,2048]{1,0:T(8,128)(2,1)S(1)} %get-tuple-element.36), channel_id=1, source_target_pairs={{0,192},{1,49},{16,208},{17,33},{32,224},{33,17},{48,240},{49,1},{... | collective-permute-start | bytes 3145736 | tf_op jit(solution)/shard_map/ppermute | solution.py:342
  27.3 6.0 %collective-permute-start.9 = (bf16[256,256]{1,0:T(8,128)(2,1)S(1)}, bf16[256,256]{1,0:T(8,128)(2,1)S(1)}, u32[]{:S(2)}, u32[]{:S(2)}) collective-permute-start(bf16[256,256]{1,0:T(8,128)(2,1)S(1)} %get-tuple-element.41), channel_id=1, source_target_pairs={{2,0},{3,1},{4,2},{5,3},{6,4},{7,5},{10,8},{11,9},{12,10},{13,11},... | collective-permute-start | bytes 393224 | tf_op jit(solution)/shard_map/ppermute | solution.py:385
  28.6 9.4 %collective-permute-start.10 = (bf16[256,256]{1,0:T(8,128)(2,1)S(1)}, bf16[256,256]{1,0:T(8,128)(2,1)S(1)}, u32[]{:S(2)}, u32[]{:S(2)}) collective-permute-start(bf16[256,256]{1,0:T(8,128)(2,1)S(1)} %get-tuple-element.42), channel_id=1, source_target_pairs={{4,0},{5,1},{6,2},{7,3},{12,8},{13,9},{14,10},{15,11},{20,16},{21,... | collective-permute-start | bytes 393224 | tf_op jit(solution)/shard_map/ppermute | solution.py:385
  38.1 12.1 %collective-permute-start.13 = (bf16[256,256]{1,0:T(8,128)(2,1)S(1)}, bf16[256,256]{1,0:T(8,128)(2,1)S(1)}, u32[]{:S(2)}, u32[]{:S(2)}) collective-permute-start(bf16[256,256]{1,0:T(8,128)(2,1)S(1)} %shard_map.82.refs_3_), channel_id=1, source_target_pairs={{0,192},{1,49},{16,208},{17,33},{32,224},{33,17},{48,240},{49,1},{... | collective-permute-start | bytes 393224 | tf_op jit(solution)/shard_map/ppermute | solution.py:342
  40.6 9.5 %collective-permute-start.12 = (bf16[256,256]{1,0:T(8,128)(2,1)S(1)}, bf16[256,256]{1,0:T(8,128)(2,1)S(1)}, u32[]{:S(2)}, u32[]{:S(2)}) collective-permute-start(bf16[256,256]{1,0:T(8,128)(2,1)S(1)} %shard_map.82.refs_3_), channel_id=1, source_target_pairs={{0,128},{1,33},{16,144},{17,49},{32,160},{33,1},{48,176},{49,17},{... | collective-permute-start | bytes 393224 | tf_op jit(solution)/shard_map/ppermute | solution.py:342
  50.2 3.9 %collective-permute-start.14 = (bf16[128,1024]{1,0:T(8,128)(2,1)S(1)}, bf16[128,1024]{1,0:T(8,128)(2,1)S(1)}, u32[]{:S(2)}, u32[]{:S(2)}) collective-permute-start(bf16[128,1024]{1,0:T(8,128)(2,1)S(1)} %get-tuple-element.47), channel_id=1, source_target_pairs={{0,1},{1,0},{2,3},{3,2},{4,5},{5,4},{6,7},{7,6},{8,9},{9,8},{10,11... | collective-permute-start | bytes 786440 | tf_op jit(solution)/shard_map/ppermute | solution.py:392
  52.8 4.1 %collective-permute-start.11 = (bf16[256,256]{1,0:T(8,128)(2,1)S(1)}, bf16[256,256]{1,0:T(8,128)(2,1)S(1)}, u32[]{:S(2)}, u32[]{:S(2)}) collective-permute-start(bf16[256,256]{1,0:T(8,128)(2,1)S(1)} %shard_map.82.refs_3_), channel_id=1, source_target_pairs={{0,64},{1,17},{16,80},{17,1},{32,96},{33,49},{48,112},{49,33},{64,... | collective-permute-start | bytes 393224 | tf_op jit(solution)/shard_map/ppermute | solution.py:342
  59.1 10.0 %collective-permute-start.15 = (bf16[512,256]{1,0:T(8,128)(2,1)S(1)}, bf16[512,256]{1,0:T(8,128)(2,1)S(1)}, u32[]{:S(2)}, u32[]{:S(2)}) collective-permute-start(bf16[512,256]{1,0:T(8,128)(2,1)S(1)} %shard_map.85), channel_id=1, source_target_pairs={{0,32},{1,129},{16,48},{17,145},{32,0},{33,161},{48,16},{49,177},{... | collective-permute-start | bytes 786440 | tf_op jit(solution)/shard_map/ppermute | solution.py:342
  61.3 7.7 %collective-permute-start.16 = (bf16[512,256]{1,0:T(8,128)(2,1)S(1)}, bf16[512,256]{1,0:T(8,128)(2,1)S(1)}, u32[]{:S(2)}, u32[]{:S(2)}) collective-permute-start(bf16[512,256]{1,0:T(8,128)(2,1)S(1)} %shard_map.86), channel_id=1, source_target_pairs={{0,16},{1,65},{16,0},{17,81},{32,48},{33,97},{48,32},{49,113},{64,... | collective-permute-start | bytes 786440 | tf_op jit(solution)/shard_map/ppermute | solution.py:342
  64.0 6.6 %collective-permute-start.17 = (bf16[512,256]{1,0:T(8,128)(2,1)S(1)}, bf16[512,256]{1,0:T(8,128)(2,1)S(1)}, u32[]{:S(2)}, u32[]{:S(2)}) collective-permute-start(bf16[512,256]{1,0:T(8,128)(2,1)S(1)} %shard_map.87), channel_id=1, source_target_pairs={{0,48},{1,193},{16,32},{17,209},{32,16},{33,225},{48,0},{49,241},{... | collective-permute-start | bytes 786440 | tf_op jit(solution)/shard_map/ppermute | solution.py:342

commit v12 on v11

--- a/solution.py
+++ b/solution.py
@@ -57,25 +57,25 @@
     return jnp.where(core == 0, (y ^ k) * n + i, i * n + (x ^ k))
 
 
-def chunk_kernel(places_ref, mine, other, *outs):
-    n = len(outs) + 1
+def chunk_kernel(places_ref, mine, other, *outs, places):
+    n = mine.shape[1] // outs[0].shape[1]
     rows, step = mine.shape[0], outs[0].shape[1] // n
-    for k, out in enumerate(outs, 1):
+    for k, out in zip(places, outs):
         for i in range(n):
             held = pl.ds(pl.multiple_of(block_of(places_ref, k, i, n) * step, step), step)
             out[:rows, i * step : (i + 1) * step] = mine[:, held]
             out[rows:, i * step : (i + 1) * step] = other[:, held]
 
 
-def split_columns(places, mine, other, chunks):
+def split_columns(places_ref, mine, other, chunks, places):
     rows, width = mine.shape
     return pl.pallas_call(
-        chunk_kernel,
-        out_shape=(whole((2 * rows, width // chunks)),) * (chunks - 1),
+        functools.partial(chunk_kernel, places=places),
+        out_shape=(whole((2 * rows, width // chunks)),) * len(places),
         in_specs=[SCALAR, pl.BlockSpec(), pl.BlockSpec()],
         compiler_params=pltpu.CompilerParams(vmem_limit_bytes=16 * MIB),
         cost_estimate=pl.CostEstimate(flops=0, bytes_accessed=6 * MIB, transcendentals=0),
-    )(places, mine, other)
+    )(places_ref, mine, other)
 
 
 def bias_kernel(here_ref, docs, out):
@@ -178,7 +178,7 @@
         ],
         compiler_params=pltpu.CompilerParams(vmem_limit_bytes=24 * MIB),
         cost_estimate=pl.CostEstimate(
-            flops=40 * keys * chip * DH * GROUP,
+            flops=150 * keys * chip * DH * GROUP,
             bytes_accessed=4 * MIB,
             transcendentals=keys * chip * GROUP,
         ),
@@ -256,35 +256,32 @@
     )(here, mine, other)
 
 
-def project_kernel(places_ref, mine, other, *refs, offset):
+def project_kernel(places_ref, *refs, offset):
     n = len(refs) // 2
-    pieces, grads, out = refs[: n - 1], refs[n - 1 : -1], refs[-1]
+    pieces, grads, out = refs[:n], refs[n:-1], refs[-1]
     step = out.shape[0]
     place = jnp.where(places_ref[2] == 0, places_ref[1], places_ref[0]) ^ offset
     columns = pl.ds(pl.multiple_of(place * step, step), step)
-    held = pl.ds(pl.multiple_of(block_of(places_ref, 0, place, n) * step, step), step)
     left = jnp.concatenate([ref[...] for ref in grads], axis=1)
-    right = jnp.concatenate(
-        [mine[:, held], other[:, held]] + [ref[:, columns] for ref in pieces], axis=0
-    )
+    right = jnp.concatenate([ref[:, columns] for ref in pieces], axis=0)
     out[...] = dot_nn(left, right).T.astype(out.dtype)
 
 
-def project(places, own, pieces, grads, offset, dtype):
+def project(places, pieces, grads, offset, dtype):
     rows, columns = pieces[0].shape
     width = grads[0].shape[0]
-    step = columns // len(grads)
+    step = columns // len(pieces)
     return pl.pallas_call(
         functools.partial(project_kernel, offset=offset),
         out_shape=whole((step, width), dtype),
-        in_specs=[SCALAR] + [pl.BlockSpec()] * (1 + 2 * len(grads)),
+        in_specs=[SCALAR] + [pl.BlockSpec()] * (2 * len(pieces)),
         compiler_params=pltpu.CompilerParams(vmem_limit_bytes=16 * MIB),
         cost_estimate=pl.CostEstimate(
-            flops=2 * len(grads) * rows * step * width,
+            flops=2 * len(pieces) * rows * step * width,
             bytes_accessed=2 * MIB,
             transcendentals=0,
         ),
-    )(places, *own, *pieces, *grads)
+    )(places, *pieces, *grads)
 
 
 def add_kernel(*refs):
@@ -371,7 +368,7 @@
     ][::-1]
 
     own = (layer_input[0], lax.ppermute(layer_input[0], "core", swap))
-    chunks = split_columns(places_ref, *own, n_side)
+    chunks = split_columns(places_ref, *own, n_side, range(1, n_side))
     chunks, _ = lax.optimization_barrier((chunks, (q_other, do_other)))
     pieces = [cross(chunk, k, True) for k, chunk in enumerate(chunks, 1)]
     docs, _ = lax.optimization_barrier((segment_ids, chunks[0]))
@@ -386,15 +383,18 @@
         for distance, part in ((2, far_grad), (1, near_grad))
     )
 
+    (own_piece,) = split_columns(places_ref, *own, n_side, (0,))
+    far_back, own_piece = lax.optimization_barrier((far_back, own_piece))
     grad = combine(own_grad, near_back, far_back)
-    grads = [grad] + [cross(grad, k, True) for k in range(1, n_side)]
-    dq_other, grads[2:] = lax.optimization_barrier((dq_other, grads[2:]))
+    late, pieces[0], dq_other = lax.optimization_barrier((grad, pieces[0], dq_other))
+    grads = [grad] + [cross(late if k == 1 else grad, k, True) for k in range(1, n_side)]
     dq_back = lax.ppermute(dq_other, "core", swap)
     query_grad = assemble(here_ref, dq_mine, dq_back)[None]
     pieces, grads, query_grad = lax.optimization_barrier((pieces, grads, query_grad))
-    terms = [project(places_ref, own, pieces, grads, k, jnp.bfloat16) for k in (2, 1, 3)]
+    pieces = [own_piece] + list(pieces)
+    terms = [project(places_ref, pieces, grads, k, jnp.bfloat16) for k in (2, 1, 3)]
     parts = [cross(term, k, False) for term, k in zip(terms, (2, 1, 3))]
-    own_term = project(places_ref, own, pieces, grads, 0, jnp.float32)
+    own_term = project(places_ref, pieces, grads, 0, jnp.float32)
     term = add_parts(own_term, parts)
     rest = ("z_hi", "z_lo", "core")
     n_rest = lax.axis_size(rest)

time: 94.2 us -> 85.7 us (0.910)
  waiting for transfers between devices: 20.3 us -> 16.8 us
  Pallas kernels: 19.9 us -> 17.3 us
  blocking collectives: 22.4 us -> 21.2 us
  starting transfers between devices: 27.3 us -> 26.2 us
    pallas_call x4, Pallas kernels: 8.56 us -> 4.33 us  [project(): pl.pallas_call(functools.partial(project_kernel, offset=offset), out_shap...]
    ppermute x2, waiting for transfers between devices: 6.94 us -> 4.69 us  [per_device(): lax.ppermute(part, ('z_lo', 'core'), [(b, a) for a, b in behind(distance)])]
    pallas_call x1 -> x2, Pallas kernels: 1.84 us -> 3.52 us  [split_columns(): pl.pallas_call(functools.partial(chunk_kernel, places=places), out_shape=...]
    ppermute x9, waiting for transfers between devices: 12.6 us -> 11.4 us  [cross(): return lax.ppermute(part, ('y', 'x', 'core'), pairs)]
    all_to_all x1, blocking collectives: 22.4 us -> 21.2 us  [per_device(): lax.all_to_all(term.reshape(n_rest, term.shape[0] // n_rest, term.shape[1...]
  transfers between devices with their start and end apart: 18 -> 18, of which waited for: 6 -> 5; matrix products, arithmetic and copies ran while one was open for 3% -> 4% of each run, Pallas kernels for 18% -> 16%
where the time goes in v12:
time: 85.7 us; the launch traced here: 85.4 us
  starting transfers between devices  26.2 us (31%)
  blocking collectives  21.2 us (25%)
  Pallas kernels  17.3 us (20%)
  waiting for transfers between devices  16.8 us (20%)
  local copies, waits for them, and re-layouts  2.9 us (3%)
    all_to_all x1, blocking collectives, per_device(): lax.all_to_all(term.reshape(n_rest, term.shape[0] // n_rest, term.shape[1...  21.2 us
    ppermute x9, waiting for transfers between devices, cross(): return lax.ppermute(part, ('y', 'x', 'core'), pairs)  11.4 us
    ppermute x9, starting transfers between devices, cross(): return lax.ppermute(part, ('y', 'x', 'core'), pairs)  10.7 us
    ppermute x2, starting transfers between devices, per_device(): lax.ppermute(chip_pair, ('z_lo', 'core'), behind(distance))  6.7 us
    pallas_call x1, Pallas kernels, attention(): pl.pallas_call(attention_kernel, out_shape=(whole((chip, 2 * DH)), whole(...  5.34 us
    ppermute x2, waiting for transfers between devices, per_device(): lax.ppermute(part, ('z_lo', 'core'), [(b, a) for a, b in behind(distance)])  4.69 us
    pallas_call x4, Pallas kernels, project(): pl.pallas_call(functools.partial(project_kernel, offset=offset), out_shap...  4.33 us
    pallas_call x2, Pallas kernels, split_columns(): pl.pallas_call(functools.partial(chunk_kernel, places=places), out_shape=...  3.52 us
  transfers between devices with their start and end apart: 18, of which 5 were waited for; matrix products, arithmetic and copies ran while one was open for 4% of the time, Pallas kernels for 16%

profile of v12, /device:TPU:1, one launch (start us, length us, event | category | flops | bytes accessed | tf_op | source)
XLA Modules:
  0.0 85.4 jit_solution(13745632746824221874)
XLA Ops:
  0.6 3.3 %collective-permute-start.5 = (bf16[128,8192]{1,0:T(8,128)(2,1)}, bf16[128,8192]{1,0:T(8,128)(2,1)}, u32[]{:S(2)}, u32[]{:S(2)}) collective-permute-start(bf16[128,8192]{1,0:T(8,128)(2,1)} %bitcast.23), channel_id=1, source_target_pairs={{0,1},{1,0},{2,3},{3,2},{4,5},{5,4},{6,7},{7,6},{8,9},{9,8},{10,11... | collective-permute-start | bytes 6291464 | tf_op jit(solution)/shard_map/ppermute | solution.py:370
  4.0 0.8 dynamic-slice_bitcast_fusion.4
  4.8 0.2 collective-permute-start
  5.0 2.1 %dynamic-slice_bitcast_fusion = (bf16[128,1024]{1,0:T(8,128)(2,1)}, bf16[128,1024]{1,0:T(8,128)(2,1)S(1)}, bf16[128,1024]{1,0:T(8,128)(2,1)S(1)}, bf16[128,1024]{1,0:T(8,128)(2,1)}) fusion(bf16[1,128,2048]{2,1,0:T(8,128)(2,1)} %param.9, s32[]{:T(128)S(6)} %select_n.17, s32[]{:T(128)S(6)} %select_n.16, bf16[1,128,2048]{2,1,0:T(8,128)(2,1)} %param.6), kind=kLoop, calls=%fused_computation | loop fusion | bytes 2097160 | tf_op jit(solution)/shard_map/dynamic_slice | solution.py:344
  7.1 0.7 collective-permute-done.swapped
  7.9 0.5 collective-permute-start.1
  8.3 0.1 collective-permute-start.2
  8.5 3.2 %collective-permute-start.4 = (bf16[256,256]{1,0:T(8,128)(2,1)S(1)}, bf16[256,256]{1,0:T(8,128)(2,1)S(1)}, u32[]{:S(2)}, u32[]{:S(2)}) collective-permute-start(bf16[256,256]{1,0:T(8,128)(2,1)S(1)} %shard_map.77.chip_pair), channel_id=1, source_target_pairs={{0,4},{1,5},{2,6},{3,7},{8,12},{9,13},{10,14},{11,15},{16,20},{17,... | collective-permute-start | bytes 393224 | tf_op jit(solution)/shard_map/ppermute | solution.py:367
  11.6 3.5 %collective-permute-start.3 = (bf16[256,256]{1,0:T(8,128)(2,1)S(1)}, bf16[256,256]{1,0:T(8,128)(2,1)S(1)}, u32[]{:S(2)}, u32[]{:S(2)}) collective-permute-start(bf16[256,256]{1,0:T(8,128)(2,1)S(1)} %shard_map.77.chip_pair), channel_id=1, source_target_pairs={{0,2},{1,3},{2,4},{3,5},{4,6},{5,7},{8,10},{9,11},{10,12},{11,13},... | collective-permute-start | bytes 393224 | tf_op jit(solution)/shard_map/ppermute | solution.py:367
  15.2 0.1 pad_add_fusion.here_ref
  15.3 0.1 pad_add_fusion.1.places_ref
  15.3 0.0 collective-permute-done.5.other
  15.3 1.8 %shard_map.78 = (bf16[256,2048]{1,0:T(8,128)(2,1)S(1)}, bf16[256,2048]{1,0:T(8,128)(2,1)S(1)}, bf16[256,2048]{1,0:T(8,128)(2,1)S(1)}) custom-call(s32[3]{0:T(128)S(1)} %pad_add_fusion.1.places_ref, bf16[128,8192]{1,0:T(8,128)(2,1)S(1)} %bitcast.24, bf16[128,8192]{1,0:T(8,128)(2,1)} %collective-permute-done.5.other), custom_call_target="tpu_custom_call" | custom-call | bytes 6291456 | tf_op jit(solution)/shard_map/pallas_call | solution.py:72
  17.2 0.0 collective-permute-done.1.q_other
  17.2 1.3 %collective-permute-start.8 = (bf16[256,2048]{1,0:T(8,128)(2,1)S(1)}, bf16[256,2048]{1,0:T(8,128)(2,1)S(1)}, u32[]{:S(2)}, u32[]{:S(2)}) collective-permute-start(bf16[256,2048]{1,0:T(8,128)(2,1)S(1)} %get-tuple-element.36), channel_id=1, source_target_pairs={{0,64},{1,17},{16,80},{17,1},{32,96},{33,49},{48,112},{49,33},{64,... | collective-permute-start | bytes 3145736 | tf_op jit(solution)/shard_map/ppermute | solution.py:339
  18.5 2.4 %collective-permute-start.9 = (bf16[256,2048]{1,0:T(8,128)(2,1)S(1)}, bf16[256,2048]{1,0:T(8,128)(2,1)S(1)}, u32[]{:S(2)}, u32[]{:S(2)}) collective-permute-start(bf16[256,2048]{1,0:T(8,128)(2,1)S(1)} %get-tuple-element.46), channel_id=1, source_target_pairs={{0,128},{1,33},{16,144},{17,49},{32,160},{33,1},{48,176},{49,17},{... | collective-permute-start | bytes 3145736 | tf_op jit(solution)/shard_map/ppermute | solution.py:339
  21.0 0.2 collective-permute-start.10
  21.2 0.7 shard_map.79.bias
  21.9 0.0 collective-permute-done.3.near_pair
  21.9 5.3 %shard_map.80 = (bf16[256,256]{1,0:T(8,128)(2,1)S(1)}, bf16[256,256]{1,0:T(8,128)(2,1)S(1)}, bf16[8,768,256]{2,1,0:T(8,128)(2,1)S(1)}, bf16[8,256,256]{2,1,0:T(8,128)(2,1)S(1)}) custom-call(bf16[128,1024]{1,0:T(8,128)(2,1)S(1)} %get-tuple-element.68.q_mine, bf16[128,1024]{1,0:T(8,128)(2,1)S(1)} %get-tuple-element.61.do_mine, ...), custom_call_target="tpu_custom_call" | custom-call | flops 30198988800 | bytes 4194304 | tf_op jit(solution)/shard_map/pallas_call | solution.py:167
  27.3 1.3 %collective-permute-start.7 = (bf16[256,256]{1,0:T(8,128)(2,1)S(1)}, bf16[256,256]{1,0:T(8,128)(2,1)S(1)}, u32[]{:S(2)}, u32[]{:S(2)}) collective-permute-start(bf16[256,256]{1,0:T(8,128)(2,1)S(1)} %get-tuple-element.42), channel_id=1, source_target_pairs={{4,0},{5,1},{6,2},{7,3},{12,8},{13,9},{14,10},{15,11},{20,16},{21,... | collective-permute-start | bytes 393224 | tf_op jit(solution)/shard_map/ppermute | solution.py:382
  28.6 1.3 %collective-permute-start.6 = (bf16[256,256]{1,0:T(8,128)(2,1)S(1)}, bf16[256,256]{1,0:T(8,128)(2,1)S(1)}, u32[]{:S(2)}, u32[]{:S(2)}) collective-permute-start(bf16[256,256]{1,0:T(8,128)(2,1)S(1)} %get-tuple-element.41), channel_id=1, source_target_pairs={{2,0},{3,1},{4,2},{5,3},{6,4},{7,5},{10,8},{11,9},{12,10},{13,11},... | collective-permute-start | bytes 393224 | tf_op jit(solution)/shard_map/ppermute | solution.py:382
  29.9 1.7 %shard_map.82.refs_0_ = bf16[256,2048]{1,0:T(8,128)(2,1)S(1)} custom-call(s32[3]{0:T(128)S(1)} %pad_add_fusion.1.places_ref, bf16[128,8192]{1,0:T(8,128)(2,1)S(1)} %bitcast.25, bf16[128,8192]{1,0:T(8,128)(2,1)} %collective-permute-done.5.other), custom_call_target="tpu_custom_call" | custom-call | bytes 6291456 | tf_op jit(solution)/shard_map/pallas_call | solution.py:72
  31.6 1.1 %shard_map.81 = (bf16[128,1024]{1,0:T(8,128)(2,1)S(1)}, bf16[128,1024]{1,0:T(8,128)(2,1)S(1)}, f32[256,256]{1,0:T(8,128)S(1)}) custom-call(bf16[128,1024]{1,0:T(8,128)(2,1)S(1)} %get-tuple-element.68.q_mine, bf16[128,1024]{1,0:T(8,128)(2,1)S(1)} %get-tuple-element.61.do_mine, bf16[128,1024]{1,0:T(8,128)(2,1)S(1)} %collective-permute-done.1.q_other, ...), custom_call_target="tpu_custom_call" | custom-call | flops 1207959552 | bytes 6291456 | tf_op jit(solution)/shard_map/pallas_call | solution.py:214
  32.7 4.7 %collective-permute-done.7.far = bf16[256,256]{1,0:T(8,128)(2,1)S(1)} collective-permute-done((bf16[256,256]{1,0:T(8,128)(2,1)S(1)}, bf16[256,256]{1,0:T(8,128)(2,1)S(1)}, u32[]{:S(2)}, u32[]{:S(2)}) %collective-permute-start.7) | collective-permute-done | bytes 131104 | tf_op jit(solution)/shard_map/ppermute | solution.py:382
  37.4 0.1 shard_map.83.refs_4_
  37.5 2.0 %collective-permute-start.14 = (bf16[128,1024]{1,0:T(8,128)(2,1)S(1)}, bf16[128,1024]{1,0:T(8,128)(2,1)S(1)}, u32[]{:S(2)}, u32[]{:S(2)}) collective-permute-start(bf16[128,1024]{1,0:T(8,128)(2,1)S(1)} %get-tuple-element.50), channel_id=1, source_target_pairs={{0,1},{1,0},{2,3},{3,2},{4,5},{5,4},{6,7},{7,6},{8,9},{9,8},{10,11... | collective-permute-start | bytes 786440 | tf_op jit(solution)/shard_map/ppermute | solution.py:391
  39.6 2.5 %collective-permute-start.13 = (bf16[256,256]{1,0:T(8,128)(2,1)S(1)}, bf16[256,256]{1,0:T(8,128)(2,1)S(1)}, u32[]{:S(2)}, u32[]{:S(2)}) collective-permute-start(bf16[256,256]{1,0:T(8,128)(2,1)S(1)} %shard_map.83.refs_4_), channel_id=1, source_target_pairs={{0,192},{1,49},{16,208},{17,33},{32,224},{33,17},{48,240},{49,1},{... | collective-permute-start | bytes 393224 | tf_op jit(solution)/shard_map/ppermute | solution.py:339
  42.0 0.1 collective-permute-start.12
  42.2 0.6 collective-permute-start.11
  42.8 1.4 %shard_map.84 = bf16[128,2048]{1,0:T(8,128)(2,1)} custom-call(s32[2]{0:T(128)S(1)} %pad_add_fusion.here_ref, bf16[128,1024]{1,0:T(8,128)(2,1)S(1)} %get-tuple-element.49.mine, bf16[128,1024]{1,0:T(8,128)(2,1)S(1)} %collective-permute-done.14.other), custom_call_target="tpu_custom_call" | custom-call | bytes 1048576 | tf_op jit(solution)/shard_map/pallas_call | solution.py:250
  44.2 6.0 %collective-permute-done.13.refs_7_ = bf16[256,256]{1,0:T(8,128)(2,1)S(1)} collective-permute-done((bf16[256,256]{1,0:T(8,128)(2,1)S(1)}, bf16[256,256]{1,0:T(8,128)(2,1)S(1)}, u32[]{:S(2)}, u32[]{:S(2)}) %collective-permute-start.13) | collective-permute-done | bytes 131104 | tf_op jit(solution)/shard_map/ppermute | solution.py:339
  50.2 0.0 collective-permute-done.12.refs_6_
  50.2 0.0 collective-permute-done.9.refs_2_
  50.2 0.0 collective-permute-done.10.refs_3_
  50.2 1.1 %shard_map.88 = bf16[512,256]{1,0:T(8,128)(2,1)S(1)} custom-call(s32[3]{0:T(128)S(1)} %pad_add_fusion.1.places_ref, bf16[256,2048]{1,0:T(8,128)(2,1)S(1)} %shard_map.82.refs_0_, bf16[256,2048]{1,0:T(8,128)(2,1)S(1)} %collective-permute-done.8.refs_1_, bf16[256,2048]{1,0:T(8,128)(2,1)S(1)} %collective-permute-done.9.refs_2_, ...), custom_call_target="tpu_custom_call" | custom-call | flops 268435456 | bytes 2097152 | tf_op jit(solution)/shard_map/pallas_call | solution.py:274
  51.3 1.1 %shard_map.87 = bf16[512,256]{1,0:T(8,128)(2,1)S(1)} custom-call(s32[3]{0:T(128)S(1)} %pad_add_fusion.1.places_ref, bf16[256,2048]{1,0:T(8,128)(2,1)S(1)} %shard_map.82.refs_0_, bf16[256,2048]{1,0:T(8,128)(2,1)S(1)} %collective-permute-done.8.refs_1_, bf16[256,2048]{1,0:T(8,128)(2,1)S(1)} %collective-permute-done.9.refs_2_, ...), custom_call_target="tpu_custom_call" | custom-call | flops 268435456 | bytes 2097152 | tf_op jit(solution)/shard_map/pallas_call | solution.py:274
  52.3 1.1 %shard_map.86 = bf16[512,256]{1,0:T(8,128)(2,1)S(1)} custom-call(s32[3]{0:T(128)S(1)} %pad_add_fusion.1.places_ref, bf16[256,2048]{1,0:T(8,128)(2,1)S(1)} %shard_map.82.refs_0_, bf16[256,2048]{1,0:T(8,128)(2,1)S(1)} %collective-permute-done.8.refs_1_, bf16[256,2048]{1,0:T(8,128)(2,1)S(1)} %collective-permute-done.9.refs_2_, ...), custom_call_target="tpu_custom_call" | custom-call | flops 268435456 | bytes 2097152 | tf_op jit(solution)/shard_map/pallas_call | solution.py:274
  53.4 2.7 %collective-permute-start.15 = (bf16[512,256]{1,0:T(8,128)(2,1)S(1)}, bf16[512,256]{1,0:T(8,128)(2,1)S(1)}, u32[]{:S(2)}, u32[]{:S(2)}) collective-permute-start(bf16[512,256]{1,0:T(8,128)(2,1)S(1)} %shard_map.86), channel_id=1, source_target_pairs={{0,32},{1,129},{16,48},{17,145},{32,0},{33,161},{48,16},{49,177},{... | collective-permute-start | bytes 786440 | tf_op jit(solution)/shard_map/ppermute | solution.py:339
  56.1 0.4 collective-permute-start.16
  56.5 0.4 collective-permute-start.17
  56.9 1.1 %shard_map.85.refs_0_ = f32[512,256]{1,0:T(8,128)S(1)} custom-call(s32[3]{0:T(128)S(1)} %pad_add_fusion.1.places_ref, bf16[256,2048]{1,0:T(8,128)(2,1)S(1)} %shard_map.82.refs_0_, bf16[256,2048]{1,0:T(8,128)(2,1)S(1)} %collective-permute-done.8.refs_1_, bf16[256,2048]{1,0:T(8,128)(2,1)S(1)} %collective-permute-done.9.refs_2_, ...), custom_call_target="tpu_custom_call" | custom-call | flops 268435456 | bytes 2097152 | tf_op jit(solution)/shard_map/pallas_call | solution.py:274
  58.0 2.2 %collective-permute-done.15.refs_1_ = bf16[512,256]{1,0:T(8,128)(2,1)S(1)} collective-permute-done((bf16[512,256]{1,0:T(8,128)(2,1)S(1)}, bf16[512,256]{1,0:T(8,128)(2,1)S(1)}, u32[]{:S(2)}, u32[]{:S(2)}) %collective-permute-start.15) | collective-permute-done | bytes 262176 | tf_op jit(solution)/shard_map/ppermute | solution.py:339
  60.2 3.2 %collective-permute-done.16.refs_2_ = bf16[512,256]{1,0:T(8,128)(2,1)S(1)} collective-permute-done((bf16[512,256]{1,0:T(8,128)(2,1)S(1)}, bf16[512,256]{1,0:T(8,128)(2,1)S(1)}, u32[]{:S(2)}, u32[]{:S(2)}) %collective-permute-start.16) | collective-permute-done | bytes 262176 | tf_op jit(solution)/shard_map/ppermute | solution.py:339
  63.4 0.0 collective-permute-done.17.refs_3_
  63.4 0.1 shard_map.89
  63.5 21.2 %all_to_all.5.parts = bf16[16,32,256]{2,1,0:T(8,128)(2,1)S(1)} all-to-all(bf16[16,32,256]{2,1,0:T(8,128)(2,1)S(1)} %bitcast.26), channel_id=1, replica_groups=mesh['y'=4,'x'=4,'z_hi'=2,'z_lo'=4,'core'=2] {'z_hi','z_lo','core'}, dimensions={0} | all-to-all | bytes 524288 | tf_op jit(solution)/shard_map/all_to_all | solution.py:401
  84.7 0.7 shard_map.90
  (12 shorter events, 0.1 us)
Async XLA Ops:
  0.6 14.7 %copy-start = (bf16[1,128,8192]{2,1,0:T(8,128)(2,1)S(1)}, bf16[1,128,8192]{2,1,0:T(8,128)(2,1)}, u32[]{:S(2)}) copy-start(bf16[1,128,8192]{2,1,0:T(8,128)(2,1)} %param.10) | copy-start | bytes 6291460
  0.6 14.7 %collective-permute-start.5 = (bf16[128,8192]{1,0:T(8,128)(2,1)}, bf16[128,8192]{1,0:T(8,128)(2,1)}, u32[]{:S(2)}, u32[]{:S(2)}) collective-permute-start(bf16[128,8192]{1,0:T(8,128)(2,1)} %bitcast.23), channel_id=1, source_target_pairs={{0,1},{1,0},{2,3},{3,2},{4,5},{5,4},{6,7},{7,6},{8,9},{9,8},{10,11... | collective-permute-start | bytes 6291464 | tf_op jit(solution)/shard_map/ppermute | solution.py:370
  4.8 3.0 %collective-permute-start = (bf16[128,256]{1,0:T(8,128)(2,1)S(1)}, bf16[128,256]{1,0:T(8,128)(2,1)S(1)}, u32[]{:S(2)}, u32[]{:S(2)}) collective-permute-start(bf16[128,256]{1,0:T(8,128)(2,1)S(1)} %pad_maximum_fusion), channel_id=1, source_target_pairs={{0,1},{1,0},{2,3},{3,2},{4,5},{5,4},{6,7},{7,6},{8,9},{9,8},{10,11... | collective-permute-start | bytes 196616 | tf_op jit(solution)/shard_map/ppermute | solution.py:350
  7.9 9.3 %collective-permute-start.1 = (bf16[128,1024]{1,0:T(8,128)(2,1)}, bf16[128,1024]{1,0:T(8,128)(2,1)S(1)}, u32[]{:S(2)}, u32[]{:S(2)}) collective-permute-start(bf16[128,1024]{1,0:T(8,128)(2,1)} %get-tuple-element.31), channel_id=1, source_target_pairs={{0,1},{1,0},{2,3},{3,2},{4,5},{5,4},{6,7},{7,6},{8,9},{9,8},{10,11... | collective-permute-start | bytes 786440 | tf_op jit(solution)/shard_map/ppermute | solution.py:357
  8.3 8.9 %collective-permute-start.2 = (bf16[128,1024]{1,0:T(8,128)(2,1)}, bf16[128,1024]{1,0:T(8,128)(2,1)S(1)}, u32[]{:S(2)}, u32[]{:S(2)}) collective-permute-start(bf16[128,1024]{1,0:T(8,128)(2,1)} %get-tuple-element.32), channel_id=1, source_target_pairs={{0,1},{1,0},{2,3},{3,2},{4,5},{5,4},{6,7},{7,6},{8,9},{9,8},{10,11... | collective-permute-start | bytes 786440 | tf_op jit(solution)/shard_map/ppermute | solution.py:357
  8.5 13.4 %collective-permute-start.4 = (bf16[256,256]{1,0:T(8,128)(2,1)S(1)}, bf16[256,256]{1,0:T(8,128)(2,1)S(1)}, u32[]{:S(2)}, u32[]{:S(2)}) collective-permute-start(bf16[256,256]{1,0:T(8,128)(2,1)S(1)} %shard_map.77.chip_pair), channel_id=1, source_target_pairs={{0,4},{1,5},{2,6},{3,7},{8,12},{9,13},{10,14},{11,15},{16,20},{17,... | collective-permute-start | bytes 393224 | tf_op jit(solution)/shard_map/ppermute | solution.py:367
  11.6 10.3 %collective-permute-start.3 = (bf16[256,256]{1,0:T(8,128)(2,1)S(1)}, bf16[256,256]{1,0:T(8,128)(2,1)S(1)}, u32[]{:S(2)}, u32[]{:S(2)}) collective-permute-start(bf16[256,256]{1,0:T(8,128)(2,1)S(1)} %shard_map.77.chip_pair), channel_id=1, source_target_pairs={{0,2},{1,3},{2,4},{3,5},{4,6},{5,7},{8,10},{9,11},{10,12},{11,13},... | collective-permute-start | bytes 393224 | tf_op jit(solution)/shard_map/ppermute | solution.py:367
  15.3 5.8 %copy-start.1 = (s32[1,1024]{1,0:T(1,128)S(1)}, s32[1,1024]{1,0:T(1,128)}, u32[]{:S(2)}) copy-start(s32[1,1024]{1,0:T(1,128)} %docs) | copy-start | bytes 12292
  17.2 20.3 %collective-permute-start.8 = (bf16[256,2048]{1,0:T(8,128)(2,1)S(1)}, bf16[256,2048]{1,0:T(8,128)(2,1)S(1)}, u32[]{:S(2)}, u32[]{:S(2)}) collective-permute-start(bf16[256,2048]{1,0:T(8,128)(2,1)S(1)} %get-tuple-element.36), channel_id=1, source_target_pairs={{0,64},{1,17},{16,80},{17,1},{32,96},{33,49},{48,112},{49,33},{64,... | collective-permute-start | bytes 3145736 | tf_op jit(solution)/shard_map/ppermute | solution.py:339
  18.5 31.7 %collective-permute-start.9 = (bf16[256,2048]{1,0:T(8,128)(2,1)S(1)}, bf16[256,2048]{1,0:T(8,128)(2,1)S(1)}, u32[]{:S(2)}, u32[]{:S(2)}) collective-permute-start(bf16[256,2048]{1,0:T(8,128)(2,1)S(1)} %get-tuple-element.46), channel_id=1, source_target_pairs={{0,128},{1,33},{16,144},{17,49},{32,160},{33,1},{48,176},{49,17},{... | collective-permute-start | bytes 3145736 | tf_op jit(solution)/shard_map/ppermute | solution.py:339
  21.0 29.2 %collective-permute-start.10 = (bf16[256,2048]{1,0:T(8,128)(2,1)S(1)}, bf16[256,2048]{1,0:T(8,128)(2,1)S(1)}, u32[]{:S(2)}, u32[]{:S(2)}) collective-permute-start(bf16[256,2048]{1,0:T(8,128)(2,1)S(1)} %get-tuple-element.47), channel_id=1, source_target_pairs={{0,192},{1,49},{16,208},{17,33},{32,224},{33,17},{48,240},{49,1},{... | collective-permute-start | bytes 3145736 | tf_op jit(solution)/shard_map/ppermute | solution.py:339
  27.3 10.1 %collective-permute-start.7 = (bf16[256,256]{1,0:T(8,128)(2,1)S(1)}, bf16[256,256]{1,0:T(8,128)(2,1)S(1)}, u32[]{:S(2)}, u32[]{:S(2)}) collective-permute-start(bf16[256,256]{1,0:T(8,128)(2,1)S(1)} %get-tuple-element.42), channel_id=1, source_target_pairs={{4,0},{5,1},{6,2},{7,3},{12,8},{13,9},{14,10},{15,11},{20,16},{21,... | collective-permute-start | bytes 393224 | tf_op jit(solution)/shard_map/ppermute | solution.py:382
  28.6 8.8 %collective-permute-start.6 = (bf16[256,256]{1,0:T(8,128)(2,1)S(1)}, bf16[256,256]{1,0:T(8,128)(2,1)S(1)}, u32[]{:S(2)}, u32[]{:S(2)}) collective-permute-start(bf16[256,256]{1,0:T(8,128)(2,1)S(1)} %get-tuple-element.41), channel_id=1, source_target_pairs={{2,0},{3,1},{4,2},{5,3},{6,4},{7,5},{10,8},{11,9},{12,10},{13,11},... | collective-permute-start | bytes 393224 | tf_op jit(solution)/shard_map/ppermute | solution.py:382
  37.5 4.7 %collective-permute-start.14 = (bf16[128,1024]{1,0:T(8,128)(2,1)S(1)}, bf16[128,1024]{1,0:T(8,128)(2,1)S(1)}, u32[]{:S(2)}, u32[]{:S(2)}) collective-permute-start(bf16[128,1024]{1,0:T(8,128)(2,1)S(1)} %get-tuple-element.50), channel_id=1, source_target_pairs={{0,1},{1,0},{2,3},{3,2},{4,5},{5,4},{6,7},{7,6},{8,9},{9,8},{10,11... | collective-permute-start | bytes 786440 | tf_op jit(solution)/shard_map/ppermute | solution.py:391
  39.6 10.6 %collective-permute-start.13 = (bf16[256,256]{1,0:T(8,128)(2,1)S(1)}, bf16[256,256]{1,0:T(8,128)(2,1)S(1)}, u32[]{:S(2)}, u32[]{:S(2)}) collective-permute-start(bf16[256,256]{1,0:T(8,128)(2,1)S(1)} %shard_map.83.refs_4_), channel_id=1, source_target_pairs={{0,192},{1,49},{16,208},{17,33},{32,224},{33,17},{48,240},{49,1},{... | collective-permute-start | bytes 393224 | tf_op jit(solution)/shard_map/ppermute | solution.py:339
  42.0 8.1 %collective-permute-start.12 = (bf16[256,256]{1,0:T(8,128)(2,1)S(1)}, bf16[256,256]{1,0:T(8,128)(2,1)S(1)}, u32[]{:S(2)}, u32[]{:S(2)}) collective-permute-start(bf16[256,256]{1,0:T(8,128)(2,1)S(1)} %shard_map.83.refs_4_), channel_id=1, source_target_pairs={{0,128},{1,33},{16,144},{17,49},{32,160},{33,1},{48,176},{49,17},{... | collective-permute-start | bytes 393224 | tf_op jit(solution)/shard_map/ppermute | solution.py:339
  42.2 8.0 %collective-permute-start.11 = (bf16[256,256]{1,0:T(8,128)(2,1)S(1)}, bf16[256,256]{1,0:T(8,128)(2,1)S(1)}, u32[]{:S(2)}, u32[]{:S(2)}) collective-permute-start(bf16[256,256]{1,0:T(8,128)(2,1)S(1)} %shard_map.83.refs_4_), channel_id=1, source_target_pairs={{0,64},{1,17},{16,80},{17,1},{32,96},{33,49},{48,112},{49,33},{64,... | collective-permute-start | bytes 393224 | tf_op jit(solution)/shard_map/ppermute | solution.py:339
  53.4 6.8 %collective-permute-start.15 = (bf16[512,256]{1,0:T(8,128)(2,1)S(1)}, bf16[512,256]{1,0:T(8,128)(2,1)S(1)}, u32[]{:S(2)}, u32[]{:S(2)}) collective-permute-start(bf16[512,256]{1,0:T(8,128)(2,1)S(1)} %shard_map.86), channel_id=1, source_target_pairs={{0,32},{1,129},{16,48},{17,145},{32,0},{33,161},{48,16},{49,177},{... | collective-permute-start | bytes 786440 | tf_op jit(solution)/shard_map/ppermute | solution.py:339
  56.1 7.3 %collective-permute-start.16 = (bf16[512,256]{1,0:T(8,128)(2,1)S(1)}, bf16[512,256]{1,0:T(8,128)(2,1)S(1)}, u32[]{:S(2)}, u32[]{:S(2)}) collective-permute-start(bf16[512,256]{1,0:T(8,128)(2,1)S(1)} %shard_map.87), channel_id=1, source_target_pairs={{0,16},{1,65},{16,0},{17,81},{32,48},{33,97},{48,32},{49,113},{64,... | collective-permute-start | bytes 786440 | tf_op jit(solution)/shard_map/ppermute | solution.py:339
  56.5 6.9 %collective-permute-start.17 = (bf16[512,256]{1,0:T(8,128)(2,1)S(1)}, bf16[512,256]{1,0:T(8,128)(2,1)S(1)}, u32[]{:S(2)}, u32[]{:S(2)}) collective-permute-start(bf16[512,256]{1,0:T(8,128)(2,1)S(1)} %shard_map.88), channel_id=1, source_target_pairs={{0,48},{1,193},{16,32},{17,209},{32,16},{33,225},{48,0},{49,241},{... | collective-permute-start | bytes 786440 | tf_op jit(solution)/shard_map/ppermute | solution.py:339

commit v13 on v12

--- a/solution.py
+++ b/solution.py
@@ -57,14 +57,27 @@
     return jnp.where(core == 0, (y ^ k) * n + i, i * n + (x ^ k))
 
 
-def chunk_kernel(places_ref, mine, other, *outs, places):
+def chunk_kernel(places_ref, mine, other, *refs, places):
+    outs, sems = refs[:-1], refs[-1]
     n = mine.shape[1] // outs[0].shape[1]
     rows, step = mine.shape[0], outs[0].shape[1] // n
-    for k, out in zip(places, outs):
-        for i in range(n):
-            held = pl.ds(pl.multiple_of(block_of(places_ref, k, i, n) * step, step), step)
-            out[:rows, i * step : (i + 1) * step] = mine[:, held]
-            out[rows:, i * step : (i + 1) * step] = other[:, held]
+    parts = [
+        (out, i, pl.ds(pl.multiple_of(block_of(places_ref, k, i, n) * step, step), step))
+        for k, out in zip(places, outs)
+        for i in range(n)
+    ]
+    copies = [
+        pltpu.make_async_copy(
+            other.at[:, held], out.at[rows:, i * step : (i + 1) * step], sems.at[index]
+        )
+        for index, (out, i, held) in enumerate(parts)
+    ]
+    for copy in copies:
+        copy.start()
+    for out, i, held in parts:
+        out[:rows, i * step : (i + 1) * step] = mine[:, held]
+    for copy in copies:
+        copy.wait()
 
 
 def split_columns(places_ref, mine, other, chunks, places):
@@ -72,7 +85,8 @@
     return pl.pallas_call(
         functools.partial(chunk_kernel, places=places),
         out_shape=(whole((2 * rows, width // chunks)),) * len(places),
-        in_specs=[SCALAR, pl.BlockSpec(), pl.BlockSpec()],
+        in_specs=[SCALAR, pl.BlockSpec(), pl.BlockSpec(memory_space=pl.ANY)],
+        scratch_shapes=[pltpu.SemaphoreType.DMA((chunks * len(places),))],
         compiler_params=pltpu.CompilerParams(vmem_limit_bytes=16 * MIB),
         cost_estimate=pl.CostEstimate(flops=0, bytes_accessed=6 * MIB, transcendentals=0),
     )(places_ref, mine, other)

time: 85.7 us -> 86 us (level)
  no operation moved by 1% of the time
where the time goes in v13:
time: 86 us; the launch traced here: 85.6 us
  starting transfers between devices  26.1 us (30%)
  blocking collectives  21.2 us (25%)
  Pallas kernels  17.6 us (20%)
  waiting for transfers between devices  16.8 us (20%)
  local copies, waits for them, and re-layouts  2.9 us (3%)
    all_to_all x1, blocking collectives, per_device(): lax.all_to_all(term.reshape(n_rest, term.shape[0] // n_rest, term.shape[1...  21.2 us
    ppermute x9, waiting for transfers between devices, cross(): return lax.ppermute(part, ('y', 'x', 'core'), pairs)  11.4 us
    ppermute x9, starting transfers between devices, cross(): return lax.ppermute(part, ('y', 'x', 'core'), pairs)  10.7 us
    ppermute x2, starting transfers between devices, per_device(): lax.ppermute(chip_pair, ('z_lo', 'core'), behind(distance))  6.7 us
    pallas_call x1, Pallas kernels, attention(): pl.pallas_call(attention_kernel, out_shape=(whole((chip, 2 * DH)), whole(...  5.34 us
    ppermute x2, waiting for transfers between devices, per_device(): lax.ppermute(part, ('z_lo', 'core'), [(b, a) for a, b in behind(distance)])  4.73 us
    pallas_call x4, Pallas kernels, project(): pl.pallas_call(functools.partial(project_kernel, offset=offset), out_shap...  4.33 us
    pallas_call x2, Pallas kernels, split_columns(): pl.pallas_call(functools.partial(chunk_kernel, places=places), out_shape=...  3.8 us
  transfers between devices with their start and end apart: 18, of which 5 were waited for; matrix products, arithmetic and copies ran while one was open for 4% of the time, Pallas kernels for 16%

profile of v13, /device:TPU:1, one launch (start us, length us, event | category | flops | bytes accessed | tf_op | source)
XLA Modules:
  0.0 85.6 jit_solution(9051388451152410528)
XLA Ops:
  0.6 3.3 %collective-permute-start.5 = (bf16[128,8192]{1,0:T(8,128)(2,1)}, bf16[128,8192]{1,0:T(8,128)(2,1)}, u32[]{:S(2)}, u32[]{:S(2)}) collective-permute-start(bf16[128,8192]{1,0:T(8,128)(2,1)} %bitcast.23), channel_id=1, source_target_pairs={{0,1},{1,0},{2,3},{3,2},{4,5},{5,4},{6,7},{7,6},{8,9},{9,8},{10,11... | collective-permute-start | bytes 6291464 | tf_op jit(solution)/shard_map/ppermute | solution.py:384
  4.0 0.8 dynamic-slice_bitcast_fusion.4
  4.8 0.2 collective-permute-start
  5.0 2.1 %dynamic-slice_bitcast_fusion = (bf16[128,1024]{1,0:T(8,128)(2,1)}, bf16[128,1024]{1,0:T(8,128)(2,1)S(1)}, bf16[128,1024]{1,0:T(8,128)(2,1)S(1)}, bf16[128,1024]{1,0:T(8,128)(2,1)}) fusion(bf16[1,128,2048]{2,1,0:T(8,128)(2,1)} %param.9, s32[]{:T(128)S(6)} %select_n.17, s32[]{:T(128)S(6)} %select_n.16, bf16[1,128,2048]{2,1,0:T(8,128)(2,1)} %param.6), kind=kLoop, calls=%fused_computation | loop fusion | bytes 2097160 | tf_op jit(solution)/shard_map/dynamic_slice | solution.py:358
  7.1 0.7 collective-permute-done.swapped
  7.9 0.5 collective-permute-start.1
  8.3 0.1 collective-permute-start.2
  8.5 3.2 %collective-permute-start.4 = (bf16[256,256]{1,0:T(8,128)(2,1)S(1)}, bf16[256,256]{1,0:T(8,128)(2,1)S(1)}, u32[]{:S(2)}, u32[]{:S(2)}) collective-permute-start(bf16[256,256]{1,0:T(8,128)(2,1)S(1)} %shard_map.77.chip_pair), channel_id=1, source_target_pairs={{0,4},{1,5},{2,6},{3,7},{8,12},{9,13},{10,14},{11,15},{16,20},{17,... | collective-permute-start | bytes 393224 | tf_op jit(solution)/shard_map/ppermute | solution.py:381
  11.6 3.5 %collective-permute-start.3 = (bf16[256,256]{1,0:T(8,128)(2,1)S(1)}, bf16[256,256]{1,0:T(8,128)(2,1)S(1)}, u32[]{:S(2)}, u32[]{:S(2)}) collective-permute-start(bf16[256,256]{1,0:T(8,128)(2,1)S(1)} %shard_map.77.chip_pair), channel_id=1, source_target_pairs={{0,2},{1,3},{2,4},{3,5},{4,6},{5,7},{8,10},{9,11},{10,12},{11,13},... | collective-permute-start | bytes 393224 | tf_op jit(solution)/shard_map/ppermute | solution.py:381
  15.2 0.1 pad_add_fusion.here_ref
  15.3 0.1 pad_add_fusion.1.places_ref
  15.3 2.1 %shard_map.78 = (bf16[256,2048]{1,0:T(8,128)(2,1)S(1)}, bf16[256,2048]{1,0:T(8,128)(2,1)S(1)}, bf16[256,2048]{1,0:T(8,128)(2,1)S(1)}) custom-call(s32[3]{0:T(128)S(1)} %pad_add_fusion.1.places_ref, bf16[128,8192]{1,0:T(8,128)(2,1)S(1)} %bitcast.24, bf16[128,8192]{1,0:T(8,128)(2,1)} %collective-permute-done.5.other), custom_call_target="tpu_custom_call" | custom-call | bytes 6291456 | tf_op jit(solution)/shard_map/pallas_call | solution.py:85
  17.5 0.0 collective-permute-done.1.q_other
  17.5 0.0 collective-permute-done.2.do_other
  17.5 1.3 %collective-permute-start.8 = (bf16[256,2048]{1,0:T(8,128)(2,1)S(1)}, bf16[256,2048]{1,0:T(8,128)(2,1)S(1)}, u32[]{:S(2)}, u32[]{:S(2)}) collective-permute-start(bf16[256,2048]{1,0:T(8,128)(2,1)S(1)} %get-tuple-element.36), channel_id=1, source_target_pairs={{0,64},{1,17},{16,80},{17,1},{32,96},{33,49},{48,112},{49,33},{64,... | collective-permute-start | bytes 3145736 | tf_op jit(solution)/shard_map/ppermute | solution.py:353
  18.8 2.5 %collective-permute-start.9 = (bf16[256,2048]{1,0:T(8,128)(2,1)S(1)}, bf16[256,2048]{1,0:T(8,128)(2,1)S(1)}, u32[]{:S(2)}, u32[]{:S(2)}) collective-permute-start(bf16[256,2048]{1,0:T(8,128)(2,1)S(1)} %get-tuple-element.46), channel_id=1, source_target_pairs={{0,128},{1,33},{16,144},{17,49},{32,160},{33,1},{48,176},{49,17},{... | collective-permute-start | bytes 3145736 | tf_op jit(solution)/shard_map/ppermute | solution.py:353
  21.2 0.2 collective-permute-start.10
  21.4 0.7 shard_map.79.bias
  22.2 0.0 collective-permute-done.4.far_pair
  22.2 5.3 %shard_map.80 = (bf16[256,256]{1,0:T(8,128)(2,1)S(1)}, bf16[256,256]{1,0:T(8,128)(2,1)S(1)}, bf16[8,768,256]{2,1,0:T(8,128)(2,1)S(1)}, bf16[8,256,256]{2,1,0:T(8,128)(2,1)S(1)}) custom-call(bf16[128,1024]{1,0:T(8,128)(2,1)S(1)} %get-tuple-element.68.q_mine, bf16[128,1024]{1,0:T(8,128)(2,1)S(1)} %get-tuple-element.61.do_mine, ...), custom_call_target="tpu_custom_call" | custom-call | flops 30198988800 | bytes 4194304 | tf_op jit(solution)/shard_map/pallas_call | solution.py:181
  27.5 1.3 %collective-permute-start.7 = (bf16[256,256]{1,0:T(8,128)(2,1)S(1)}, bf16[256,256]{1,0:T(8,128)(2,1)S(1)}, u32[]{:S(2)}, u32[]{:S(2)}) collective-permute-start(bf16[256,256]{1,0:T(8,128)(2,1)S(1)} %get-tuple-element.42), channel_id=1, source_target_pairs={{4,0},{5,1},{6,2},{7,3},{12,8},{13,9},{14,10},{15,11},{20,16},{21,... | collective-permute-start | bytes 393224 | tf_op jit(solution)/shard_map/ppermute | solution.py:396
  28.8 1.3 %collective-permute-start.6 = (bf16[256,256]{1,0:T(8,128)(2,1)S(1)}, bf16[256,256]{1,0:T(8,128)(2,1)S(1)}, u32[]{:S(2)}, u32[]{:S(2)}) collective-permute-start(bf16[256,256]{1,0:T(8,128)(2,1)S(1)} %get-tuple-element.41), channel_id=1, source_target_pairs={{2,0},{3,1},{4,2},{5,3},{6,4},{7,5},{10,8},{11,9},{12,10},{13,11},... | collective-permute-start | bytes 393224 | tf_op jit(solution)/shard_map/ppermute | solution.py:396
  30.1 1.7 %shard_map.82.refs_0_ = bf16[256,2048]{1,0:T(8,128)(2,1)S(1)} custom-call(s32[3]{0:T(128)S(1)} %pad_add_fusion.1.places_ref, bf16[128,8192]{1,0:T(8,128)(2,1)S(1)} %bitcast.25, bf16[128,8192]{1,0:T(8,128)(2,1)} %collective-permute-done.5.other), custom_call_target="tpu_custom_call" | custom-call | bytes 6291456 | tf_op jit(solution)/shard_map/pallas_call | solution.py:85
  31.8 1.1 %shard_map.81 = (bf16[128,1024]{1,0:T(8,128)(2,1)S(1)}, bf16[128,1024]{1,0:T(8,128)(2,1)S(1)}, f32[256,256]{1,0:T(8,128)S(1)}) custom-call(bf16[128,1024]{1,0:T(8,128)(2,1)S(1)} %get-tuple-element.68.q_mine, bf16[128,1024]{1,0:T(8,128)(2,1)S(1)} %get-tuple-element.61.do_mine, bf16[128,1024]{1,0:T(8,128)(2,1)S(1)} %collective-permute-done.1.q_other, ...), custom_call_target="tpu_custom_call" | custom-call | flops 1207959552 | bytes 6291456 | tf_op jit(solution)/shard_map/pallas_call | solution.py:228
  33.0 4.7 %collective-permute-done.7.far = bf16[256,256]{1,0:T(8,128)(2,1)S(1)} collective-permute-done((bf16[256,256]{1,0:T(8,128)(2,1)S(1)}, bf16[256,256]{1,0:T(8,128)(2,1)S(1)}, u32[]{:S(2)}, u32[]{:S(2)}) %collective-permute-start.7) | collective-permute-done | bytes 131104 | tf_op jit(solution)/shard_map/ppermute | solution.py:396
  37.7 0.0 collective-permute-done.6.near
  37.7 0.1 shard_map.83.refs_4_
  37.8 0.0 collective-permute-done.8.refs_1_
  37.8 2.0 %collective-permute-start.14 = (bf16[128,1024]{1,0:T(8,128)(2,1)S(1)}, bf16[128,1024]{1,0:T(8,128)(2,1)S(1)}, u32[]{:S(2)}, u32[]{:S(2)}) collective-permute-start(bf16[128,1024]{1,0:T(8,128)(2,1)S(1)} %get-tuple-element.50), channel_id=1, source_target_pairs={{0,1},{1,0},{2,3},{3,2},{4,5},{5,4},{6,7},{7,6},{8,9},{9,8},{10,11... | collective-permute-start | bytes 786440 | tf_op jit(solution)/shard_map/ppermute | solution.py:405
  39.8 2.5 %collective-permute-start.13 = (bf16[256,256]{1,0:T(8,128)(2,1)S(1)}, bf16[256,256]{1,0:T(8,128)(2,1)S(1)}, u32[]{:S(2)}, u32[]{:S(2)}) collective-permute-start(bf16[256,256]{1,0:T(8,128)(2,1)S(1)} %shard_map.83.refs_4_), channel_id=1, source_target_pairs={{0,192},{1,49},{16,208},{17,33},{32,224},{33,17},{48,240},{49,1},{... | collective-permute-start | bytes 393224 | tf_op jit(solution)/shard_map/ppermute | solution.py:353
  42.3 0.1 collective-permute-start.12
  42.5 0.0 collective-permute-done.14.other
  42.5 0.6 collective-permute-start.11
  43.1 1.4 %shard_map.84 = bf16[128,2048]{1,0:T(8,128)(2,1)} custom-call(s32[2]{0:T(128)S(1)} %pad_add_fusion.here_ref, bf16[128,1024]{1,0:T(8,128)(2,1)S(1)} %get-tuple-element.49.mine, bf16[128,1024]{1,0:T(8,128)(2,1)S(1)} %collective-permute-done.14.other), custom_call_target="tpu_custom_call" | custom-call | bytes 1048576 | tf_op jit(solution)/shard_map/pallas_call | solution.py:264
  44.5 6.0 %collective-permute-done.13.refs_7_ = bf16[256,256]{1,0:T(8,128)(2,1)S(1)} collective-permute-done((bf16[256,256]{1,0:T(8,128)(2,1)S(1)}, bf16[256,256]{1,0:T(8,128)(2,1)S(1)}, u32[]{:S(2)}, u32[]{:S(2)}) %collective-permute-start.13) | collective-permute-done | bytes 131104 | tf_op jit(solution)/shard_map/ppermute | solution.py:353
  50.4 0.0 collective-permute-done.12.refs_6_
  50.5 1.1 %shard_map.88 = bf16[512,256]{1,0:T(8,128)(2,1)S(1)} custom-call(s32[3]{0:T(128)S(1)} %pad_add_fusion.1.places_ref, bf16[256,2048]{1,0:T(8,128)(2,1)S(1)} %shard_map.82.refs_0_, bf16[256,2048]{1,0:T(8,128)(2,1)S(1)} %collective-permute-done.8.refs_1_, bf16[256,2048]{1,0:T(8,128)(2,1)S(1)} %collective-permute-done.9.refs_2_, ...), custom_call_target="tpu_custom_call" | custom-call | flops 268435456 | bytes 2097152 | tf_op jit(solution)/shard_map/pallas_call | solution.py:288
  51.5 1.1 %shard_map.87 = bf16[512,256]{1,0:T(8,128)(2,1)S(1)} custom-call(s32[3]{0:T(128)S(1)} %pad_add_fusion.1.places_ref, bf16[256,2048]{1,0:T(8,128)(2,1)S(1)} %shard_map.82.refs_0_, bf16[256,2048]{1,0:T(8,128)(2,1)S(1)} %collective-permute-done.8.refs_1_, bf16[256,2048]{1,0:T(8,128)(2,1)S(1)} %collective-permute-done.9.refs_2_, ...), custom_call_target="tpu_custom_call" | custom-call | flops 268435456 | bytes 2097152 | tf_op jit(solution)/shard_map/pallas_call | solution.py:288
  52.6 1.1 %shard_map.86 = bf16[512,256]{1,0:T(8,128)(2,1)S(1)} custom-call(s32[3]{0:T(128)S(1)} %pad_add_fusion.1.places_ref, bf16[256,2048]{1,0:T(8,128)(2,1)S(1)} %shard_map.82.refs_0_, bf16[256,2048]{1,0:T(8,128)(2,1)S(1)} %collective-permute-done.8.refs_1_, bf16[256,2048]{1,0:T(8,128)(2,1)S(1)} %collective-permute-done.9.refs_2_, ...), custom_call_target="tpu_custom_call" | custom-call | flops 268435456 | bytes 2097152 | tf_op jit(solution)/shard_map/pallas_call | solution.py:288
  53.7 2.7 %collective-permute-start.15 = (bf16[512,256]{1,0:T(8,128)(2,1)S(1)}, bf16[512,256]{1,0:T(8,128)(2,1)S(1)}, u32[]{:S(2)}, u32[]{:S(2)}) collective-permute-start(bf16[512,256]{1,0:T(8,128)(2,1)S(1)} %shard_map.86), channel_id=1, source_target_pairs={{0,32},{1,129},{16,48},{17,145},{32,0},{33,161},{48,16},{49,177},{... | collective-permute-start | bytes 786440 | tf_op jit(solution)/shard_map/ppermute | solution.py:353
  56.4 0.4 collective-permute-start.16
  56.8 0.4 collective-permute-start.17
  57.2 1.1 %shard_map.85.refs_0_ = f32[512,256]{1,0:T(8,128)S(1)} custom-call(s32[3]{0:T(128)S(1)} %pad_add_fusion.1.places_ref, bf16[256,2048]{1,0:T(8,128)(2,1)S(1)} %shard_map.82.refs_0_, bf16[256,2048]{1,0:T(8,128)(2,1)S(1)} %collective-permute-done.8.refs_1_, bf16[256,2048]{1,0:T(8,128)(2,1)S(1)} %collective-permute-done.9.refs_2_, ...), custom_call_target="tpu_custom_call" | custom-call | flops 268435456 | bytes 2097152 | tf_op jit(solution)/shard_map/pallas_call | solution.py:288
  58.3 2.2 %collective-permute-done.15.refs_1_ = bf16[512,256]{1,0:T(8,128)(2,1)S(1)} collective-permute-done((bf16[512,256]{1,0:T(8,128)(2,1)S(1)}, bf16[512,256]{1,0:T(8,128)(2,1)S(1)}, u32[]{:S(2)}, u32[]{:S(2)}) %collective-permute-start.15) | collective-permute-done | bytes 262176 | tf_op jit(solution)/shard_map/ppermute | solution.py:353
  60.5 3.2 %collective-permute-done.16.refs_2_ = bf16[512,256]{1,0:T(8,128)(2,1)S(1)} collective-permute-done((bf16[512,256]{1,0:T(8,128)(2,1)S(1)}, bf16[512,256]{1,0:T(8,128)(2,1)S(1)}, u32[]{:S(2)}, u32[]{:S(2)}) %collective-permute-start.16) | collective-permute-done | bytes 262176 | tf_op jit(solution)/shard_map/ppermute | solution.py:353
  63.7 0.1 shard_map.89
  63.8 21.2 %all_to_all.5.parts = bf16[16,32,256]{2,1,0:T(8,128)(2,1)S(1)} all-to-all(bf16[16,32,256]{2,1,0:T(8,128)(2,1)S(1)} %bitcast.26), channel_id=1, replica_groups=mesh['y'=4,'x'=4,'z_hi'=2,'z_lo'=4,'core'=2] {'z_hi','z_lo','core'}, dimensions={0} | all-to-all | bytes 524288 | tf_op jit(solution)/shard_map/all_to_all | solution.py:415
  85.0 0.7 shard_map.90
  (12 shorter events, 0.1 us)
Async XLA Ops:
  0.6 14.7 %copy-start = (bf16[1,128,8192]{2,1,0:T(8,128)(2,1)S(1)}, bf16[1,128,8192]{2,1,0:T(8,128)(2,1)}, u32[]{:S(2)}) copy-start(bf16[1,128,8192]{2,1,0:T(8,128)(2,1)} %param.10) | copy-start | bytes 6291460
  0.6 14.7 %collective-permute-start.5 = (bf16[128,8192]{1,0:T(8,128)(2,1)}, bf16[128,8192]{1,0:T(8,128)(2,1)}, u32[]{:S(2)}, u32[]{:S(2)}) collective-permute-start(bf16[128,8192]{1,0:T(8,128)(2,1)} %bitcast.23), channel_id=1, source_target_pairs={{0,1},{1,0},{2,3},{3,2},{4,5},{5,4},{6,7},{7,6},{8,9},{9,8},{10,11... | collective-permute-start | bytes 6291464 | tf_op jit(solution)/shard_map/ppermute | solution.py:384
  4.8 3.0 %collective-permute-start = (bf16[128,256]{1,0:T(8,128)(2,1)S(1)}, bf16[128,256]{1,0:T(8,128)(2,1)S(1)}, u32[]{:S(2)}, u32[]{:S(2)}) collective-permute-start(bf16[128,256]{1,0:T(8,128)(2,1)S(1)} %pad_maximum_fusion), channel_id=1, source_target_pairs={{0,1},{1,0},{2,3},{3,2},{4,5},{5,4},{6,7},{7,6},{8,9},{9,8},{10,11... | collective-permute-start | bytes 196616 | tf_op jit(solution)/shard_map/ppermute | solution.py:364
  7.9 9.6 %collective-permute-start.1 = (bf16[128,1024]{1,0:T(8,128)(2,1)}, bf16[128,1024]{1,0:T(8,128)(2,1)S(1)}, u32[]{:S(2)}, u32[]{:S(2)}) collective-permute-start(bf16[128,1024]{1,0:T(8,128)(2,1)} %get-tuple-element.31), channel_id=1, source_target_pairs={{0,1},{1,0},{2,3},{3,2},{4,5},{5,4},{6,7},{7,6},{8,9},{9,8},{10,11... | collective-permute-start | bytes 786440 | tf_op jit(solution)/shard_map/ppermute | solution.py:371
  8.3 9.2 %collective-permute-start.2 = (bf16[128,1024]{1,0:T(8,128)(2,1)}, bf16[128,1024]{1,0:T(8,128)(2,1)S(1)}, u32[]{:S(2)}, u32[]{:S(2)}) collective-permute-start(bf16[128,1024]{1,0:T(8,128)(2,1)} %get-tuple-element.32), channel_id=1, source_target_pairs={{0,1},{1,0},{2,3},{3,2},{4,5},{5,4},{6,7},{7,6},{8,9},{9,8},{10,11... | collective-permute-start | bytes 786440 | tf_op jit(solution)/shard_map/ppermute | solution.py:371
  8.5 13.7 %collective-permute-start.4 = (bf16[256,256]{1,0:T(8,128)(2,1)S(1)}, bf16[256,256]{1,0:T(8,128)(2,1)S(1)}, u32[]{:S(2)}, u32[]{:S(2)}) collective-permute-start(bf16[256,256]{1,0:T(8,128)(2,1)S(1)} %shard_map.77.chip_pair), channel_id=1, source_target_pairs={{0,4},{1,5},{2,6},{3,7},{8,12},{9,13},{10,14},{11,15},{16,20},{17,... | collective-permute-start | bytes 393224 | tf_op jit(solution)/shard_map/ppermute | solution.py:381
  11.6 10.6 %collective-permute-start.3 = (bf16[256,256]{1,0:T(8,128)(2,1)S(1)}, bf16[256,256]{1,0:T(8,128)(2,1)S(1)}, u32[]{:S(2)}, u32[]{:S(2)}) collective-permute-start(bf16[256,256]{1,0:T(8,128)(2,1)S(1)} %shard_map.77.chip_pair), channel_id=1, source_target_pairs={{0,2},{1,3},{2,4},{3,5},{4,6},{5,7},{8,10},{9,11},{10,12},{11,13},... | collective-permute-start | bytes 393224 | tf_op jit(solution)/shard_map/ppermute | solution.py:381
  15.3 6.1 %copy-start.1 = (s32[1,1024]{1,0:T(1,128)S(1)}, s32[1,1024]{1,0:T(1,128)}, u32[]{:S(2)}) copy-start(s32[1,1024]{1,0:T(1,128)} %docs) | copy-start | bytes 12292
  17.5 20.3 %collective-permute-start.8 = (bf16[256,2048]{1,0:T(8,128)(2,1)S(1)}, bf16[256,2048]{1,0:T(8,128)(2,1)S(1)}, u32[]{:S(2)}, u32[]{:S(2)}) collective-permute-start(bf16[256,2048]{1,0:T(8,128)(2,1)S(1)} %get-tuple-element.36), channel_id=1, source_target_pairs={{0,64},{1,17},{16,80},{17,1},{32,96},{33,49},{48,112},{49,33},{64,... | collective-permute-start | bytes 3145736 | tf_op jit(solution)/shard_map/ppermute | solution.py:353
  18.8 31.7 %collective-permute-start.9 = (bf16[256,2048]{1,0:T(8,128)(2,1)S(1)}, bf16[256,2048]{1,0:T(8,128)(2,1)S(1)}, u32[]{:S(2)}, u32[]{:S(2)}) collective-permute-start(bf16[256,2048]{1,0:T(8,128)(2,1)S(1)} %get-tuple-element.46), channel_id=1, source_target_pairs={{0,128},{1,33},{16,144},{17,49},{32,160},{33,1},{48,176},{49,17},{... | collective-permute-start | bytes 3145736 | tf_op jit(solution)/shard_map/ppermute | solution.py:353
  21.2 29.2 %collective-permute-start.10 = (bf16[256,2048]{1,0:T(8,128)(2,1)S(1)}, bf16[256,2048]{1,0:T(8,128)(2,1)S(1)}, u32[]{:S(2)}, u32[]{:S(2)}) collective-permute-start(bf16[256,2048]{1,0:T(8,128)(2,1)S(1)} %get-tuple-element.47), channel_id=1, source_target_pairs={{0,192},{1,49},{16,208},{17,33},{32,224},{33,17},{48,240},{49,1},{... | collective-permute-start | bytes 3145736 | tf_op jit(solution)/shard_map/ppermute | solution.py:353
  27.5 10.2 %collective-permute-start.7 = (bf16[256,256]{1,0:T(8,128)(2,1)S(1)}, bf16[256,256]{1,0:T(8,128)(2,1)S(1)}, u32[]{:S(2)}, u32[]{:S(2)}) collective-permute-start(bf16[256,256]{1,0:T(8,128)(2,1)S(1)} %get-tuple-element.42), channel_id=1, source_target_pairs={{4,0},{5,1},{6,2},{7,3},{12,8},{13,9},{14,10},{15,11},{20,16},{21,... | collective-permute-start | bytes 393224 | tf_op jit(solution)/shard_map/ppermute | solution.py:396
  28.8 8.9 %collective-permute-start.6 = (bf16[256,256]{1,0:T(8,128)(2,1)S(1)}, bf16[256,256]{1,0:T(8,128)(2,1)S(1)}, u32[]{:S(2)}, u32[]{:S(2)}) collective-permute-start(bf16[256,256]{1,0:T(8,128)(2,1)S(1)} %get-tuple-element.41), channel_id=1, source_target_pairs={{2,0},{3,1},{4,2},{5,3},{6,4},{7,5},{10,8},{11,9},{12,10},{13,11},... | collective-permute-start | bytes 393224 | tf_op jit(solution)/shard_map/ppermute | solution.py:396
  37.8 4.6 %collective-permute-start.14 = (bf16[128,1024]{1,0:T(8,128)(2,1)S(1)}, bf16[128,1024]{1,0:T(8,128)(2,1)S(1)}, u32[]{:S(2)}, u32[]{:S(2)}) collective-permute-start(bf16[128,1024]{1,0:T(8,128)(2,1)S(1)} %get-tuple-element.50), channel_id=1, source_target_pairs={{0,1},{1,0},{2,3},{3,2},{4,5},{5,4},{6,7},{7,6},{8,9},{9,8},{10,11... | collective-permute-start | bytes 786440 | tf_op jit(solution)/shard_map/ppermute | solution.py:405
  39.8 10.6 %collective-permute-start.13 = (bf16[256,256]{1,0:T(8,128)(2,1)S(1)}, bf16[256,256]{1,0:T(8,128)(2,1)S(1)}, u32[]{:S(2)}, u32[]{:S(2)}) collective-permute-start(bf16[256,256]{1,0:T(8,128)(2,1)S(1)} %shard_map.83.refs_4_), channel_id=1, source_target_pairs={{0,192},{1,49},{16,208},{17,33},{32,224},{33,17},{48,240},{49,1},{... | collective-permute-start | bytes 393224 | tf_op jit(solution)/shard_map/ppermute | solution.py:353
  42.3 8.1 %collective-permute-start.12 = (bf16[256,256]{1,0:T(8,128)(2,1)S(1)}, bf16[256,256]{1,0:T(8,128)(2,1)S(1)}, u32[]{:S(2)}, u32[]{:S(2)}) collective-permute-start(bf16[256,256]{1,0:T(8,128)(2,1)S(1)} %shard_map.83.refs_4_), channel_id=1, source_target_pairs={{0,128},{1,33},{16,144},{17,49},{32,160},{33,1},{48,176},{49,17},{... | collective-permute-start | bytes 393224 | tf_op jit(solution)/shard_map/ppermute | solution.py:353
  42.5 8.0 %collective-permute-start.11 = (bf16[256,256]{1,0:T(8,128)(2,1)S(1)}, bf16[256,256]{1,0:T(8,128)(2,1)S(1)}, u32[]{:S(2)}, u32[]{:S(2)}) collective-permute-start(bf16[256,256]{1,0:T(8,128)(2,1)S(1)} %shard_map.83.refs_4_), channel_id=1, source_target_pairs={{0,64},{1,17},{16,80},{17,1},{32,96},{33,49},{48,112},{49,33},{64,... | collective-permute-start | bytes 393224 | tf_op jit(solution)/shard_map/ppermute | solution.py:353
  53.7 6.8 %collective-permute-start.15 = (bf16[512,256]{1,0:T(8,128)(2,1)S(1)}, bf16[512,256]{1,0:T(8,128)(2,1)S(1)}, u32[]{:S(2)}, u32[]{:S(2)}) collective-permute-start(bf16[512,256]{1,0:T(8,128)(2,1)S(1)} %shard_map.86), channel_id=1, source_target_pairs={{0,32},{1,129},{16,48},{17,145},{32,0},{33,161},{48,16},{49,177},{... | collective-permute-start | bytes 786440 | tf_op jit(solution)/shard_map/ppermute | solution.py:353
  56.4 7.3 %collective-permute-start.16 = (bf16[512,256]{1,0:T(8,128)(2,1)S(1)}, bf16[512,256]{1,0:T(8,128)(2,1)S(1)}, u32[]{:S(2)}, u32[]{:S(2)}) collective-permute-start(bf16[512,256]{1,0:T(8,128)(2,1)S(1)} %shard_map.87), channel_id=1, source_target_pairs={{0,16},{1,65},{16,0},{17,81},{32,48},{33,97},{48,32},{49,113},{64,... | collective-permute-start | bytes 786440 | tf_op jit(solution)/shard_map/ppermute | solution.py:353
  56.8 6.9 %collective-permute-start.17 = (bf16[512,256]{1,0:T(8,128)(2,1)S(1)}, bf16[512,256]{1,0:T(8,128)(2,1)S(1)}, u32[]{:S(2)}, u32[]{:S(2)}) collective-permute-start(bf16[512,256]{1,0:T(8,128)(2,1)S(1)} %shard_map.88), channel_id=1, source_target_pairs={{0,48},{1,193},{16,32},{17,209},{32,16},{33,225},{48,0},{49,241},{... | collective-permute-start | bytes 786440 | tf_op jit(solution)/shard_map/ppermute | solution.py:353

commit v14 on v12

--- a/solution.py
+++ b/solution.py
@@ -344,16 +344,14 @@
         return lax.dynamic_slice_in_dim(array[0], which * width, width, 1)
 
     k_mine, v_mine = half_of(keys, core), half_of(values, core)
-    chip_pair = chip_pairs(
-        k_mine,
-        v_mine,
-        lax.ppermute(
-            jnp.concatenate([half_of(keys, 1 - core), half_of(values, 1 - core)], axis=1), "core", swap
-        ),
+    swapped = lax.ppermute(
+        jnp.concatenate([half_of(keys, 1 - core), half_of(values, 1 - core)], axis=1), "core", swap
     )
     q_mine, do_mine = half_of(queries, core), half_of(out_grad, core)
     q_out, do_out = half_of(queries, 1 - core), half_of(out_grad, 1 - core)
-    q_out, do_out, _ = lax.optimization_barrier((q_out, do_out, chip_pair))
+    swapped, q_out, do_out = lax.optimization_barrier((swapped, q_out, do_out))
+    chip_pair = chip_pairs(k_mine, v_mine, swapped)
+    columns, q_out, do_out, _ = lax.optimization_barrier((layer_input[0], q_out, do_out, chip_pair))
     q_other, do_other = (lax.ppermute(part, "core", swap) for part in (q_out, do_out))
 
     def behind(distance):
@@ -367,7 +365,7 @@
         lax.ppermute(chip_pair, ("z_lo", "core"), behind(distance)) for distance in (2, 1)
     ][::-1]
 
-    own = (layer_input[0], lax.ppermute(layer_input[0], "core", swap))
+    own = (columns, lax.ppermute(columns, "core", swap))
     chunks = split_columns(places_ref, *own, n_side, range(1, n_side))
     chunks, _ = lax.optimization_barrier((chunks, (q_other, do_other)))
     pieces = [cross(chunk, k, True) for k, chunk in enumerate(chunks, 1)]

time: 85.7 us -> 85.1 us (level)
    ppermute x1, starting transfers between devices: 3.33 us -> 0.11 us  [per_device(): own = (columns, lax.ppermute(columns, 'core', swap))]
    ppermute x1, starting transfers between devices: 0.24 us -> 3.33 us  [per_device(): lax.ppermute(jnp.concatenate([half_of(keys, 1 - core), half_of(values, 1...]
  transfers between devices with their start and end apart: 18 -> 18, of which waited for: 5 -> 4; matrix products, arithmetic and copies ran while one was open for 4% -> 3% of each run, Pallas kernels for 16% -> 16%
where the time goes in v14:
time: 85.1 us; the launch traced here: 84.7 us
  starting transfers between devices  26.1 us (31%)
  blocking collectives  21.2 us (25%)
  Pallas kernels  17.3 us (20%)
  waiting for transfers between devices  16.1 us (19%)
  local copies, waits for them, and re-layouts  3.05 us (4%)
    all_to_all x1, blocking collectives, per_device(): lax.all_to_all(term.reshape(n_rest, term.shape[0] // n_rest, term.shape[1...  21.2 us
    ppermute x9, waiting for transfers between devices, cross(): return lax.ppermute(part, ('y', 'x', 'core'), pairs)  11.4 us
    ppermute x9, starting transfers between devices, cross(): return lax.ppermute(part, ('y', 'x', 'core'), pairs)  10.7 us
    ppermute x2, starting transfers between devices, per_device(): lax.ppermute(chip_pair, ('z_lo', 'core'), behind(distance))  6.7 us
    pallas_call x1, Pallas kernels, attention(): pl.pallas_call(attention_kernel, out_shape=(whole((chip, 2 * DH)), whole(...  5.34 us
    ppermute x2, waiting for transfers between devices, per_device(): lax.ppermute(part, ('z_lo', 'core'), [(b, a) for a, b in behind(distance)])  4.66 us
    pallas_call x4, Pallas kernels, project(): pl.pallas_call(functools.partial(project_kernel, offset=offset), out_shap...  4.32 us
    pallas_call x2, Pallas kernels, split_columns(): pl.pallas_call(functools.partial(chunk_kernel, places=places), out_shape=...  3.53 us
  transfers between devices with their start and end apart: 18, of which 4 were waited for; matrix products, arithmetic and copies ran while one was open for 3% of the time, Pallas kernels for 16%

profile of v14, /device:TPU:1, one launch (start us, length us, event | category | flops | bytes accessed | tf_op | source)
XLA Modules:
  0.0 84.7 jit_solution(17094720297256525920)
XLA Ops:
  0.6 1.0 %dynamic-slice_bitcast_fusion.4 = (bf16[128,128]{1,0:T(8,128)(2,1)S(1)}, bf16[128,128]{1,0:T(8,128)(2,1)S(1)}, bf16[128,128]{1,0:T(8,128)(2,1)S(1)}, bf16[128,128]{1,0:T(8,128)(2,1)S(1)}) fusion(bf16[1,128,256]{2,1,0:T(8,128)(2,1)} %param.8, s32[]{:T(128)S(6)} %select_n.19, s32[]{:T(128)S(6)} %select_n.17, bf16[1,128,256]{2,1,0:T(8,128)(2,1)} %param.7), kind=kLoop, calls=%fused_computation.5 | loop fusion | bytes 262152 | tf_op jit(solution)/shard_map/dynamic_slice | solution.py:344
  1.6 3.3 %collective-permute-start = (bf16[128,256]{1,0:T(8,128)(2,1)S(1)}, bf16[128,256]{1,0:T(8,128)(2,1)S(1)}, u32[]{:S(2)}, u32[]{:S(2)}) collective-permute-start(bf16[128,256]{1,0:T(8,128)(2,1)S(1)} %pad_maximum_fusion), channel_id=1, source_target_pairs={{0,1},{1,0},{2,3},{3,2},{4,5},{5,4},{6,7},{7,6},{8,9},{9,8},{10,11... | collective-permute-start | bytes 196616 | tf_op jit(solution)/shard_map/ppermute | solution.py:347
  5.0 2.1 %dynamic-slice_bitcast_fusion = (bf16[128,1024]{1,0:T(8,128)(2,1)}, bf16[128,1024]{1,0:T(8,128)(2,1)S(1)}, bf16[128,1024]{1,0:T(8,128)(2,1)S(1)}, bf16[128,1024]{1,0:T(8,128)(2,1)}) fusion(bf16[1,128,2048]{2,1,0:T(8,128)(2,1)} %param.9, s32[]{:T(128)S(6)} %select_n.18, s32[]{:T(128)S(6)} %select_n.16, bf16[1,128,2048]{2,1,0:T(8,128)(2,1)} %param.6), kind=kLoop, calls=%fused_computation | loop fusion | bytes 2097160 | tf_op jit(solution)/shard_map/dynamic_slice | solution.py:344
  7.1 0.1 collective-permute-start.5
  7.2 0.5 collective-permute-start.1
  7.7 0.1 collective-permute-start.2
  7.8 3.2 %collective-permute-start.4 = (bf16[256,256]{1,0:T(8,128)(2,1)S(1)}, bf16[256,256]{1,0:T(8,128)(2,1)S(1)}, u32[]{:S(2)}, u32[]{:S(2)}) collective-permute-start(bf16[256,256]{1,0:T(8,128)(2,1)S(1)} %shard_map.77.chip_pair), channel_id=1, source_target_pairs={{0,4},{1,5},{2,6},{3,7},{8,12},{9,13},{10,14},{11,15},{16,20},{17,... | collective-permute-start | bytes 393224 | tf_op jit(solution)/shard_map/ppermute | solution.py:365
  10.9 3.5 %collective-permute-start.3 = (bf16[256,256]{1,0:T(8,128)(2,1)S(1)}, bf16[256,256]{1,0:T(8,128)(2,1)S(1)}, u32[]{:S(2)}, u32[]{:S(2)}) collective-permute-start(bf16[256,256]{1,0:T(8,128)(2,1)S(1)} %shard_map.77.chip_pair), channel_id=1, source_target_pairs={{0,2},{1,3},{2,4},{3,5},{4,6},{5,7},{8,10},{9,11},{10,12},{11,13},... | collective-permute-start | bytes 393224 | tf_op jit(solution)/shard_map/ppermute | solution.py:365
  14.5 0.1 pad_add_fusion.here_ref
  14.6 0.1 pad_add_fusion.1.places_ref
  14.7 1.8 %shard_map.78 = (bf16[256,2048]{1,0:T(8,128)(2,1)S(1)}, bf16[256,2048]{1,0:T(8,128)(2,1)S(1)}, bf16[256,2048]{1,0:T(8,128)(2,1)S(1)}) custom-call(s32[3]{0:T(128)S(1)} %pad_add_fusion.1.places_ref, bf16[128,8192]{1,0:T(8,128)(2,1)S(1)} %bitcast.24, bf16[128,8192]{1,0:T(8,128)(2,1)} %collective-permute-done.5.other), custom_call_target="tpu_custom_call" | custom-call | bytes 6291456 | tf_op jit(solution)/shard_map/pallas_call | solution.py:72
  16.5 0.0 collective-permute-done.1.q_other
  16.5 1.3 %collective-permute-start.8 = (bf16[256,2048]{1,0:T(8,128)(2,1)S(1)}, bf16[256,2048]{1,0:T(8,128)(2,1)S(1)}, u32[]{:S(2)}, u32[]{:S(2)}) collective-permute-start(bf16[256,2048]{1,0:T(8,128)(2,1)S(1)} %get-tuple-element.44), channel_id=1, source_target_pairs={{0,64},{1,17},{16,80},{17,1},{32,96},{33,49},{48,112},{49,33},{64,... | collective-permute-start | bytes 3145736 | tf_op jit(solution)/shard_map/ppermute | solution.py:339
  17.8 2.4 %collective-permute-start.9 = (bf16[256,2048]{1,0:T(8,128)(2,1)S(1)}, bf16[256,2048]{1,0:T(8,128)(2,1)S(1)}, u32[]{:S(2)}, u32[]{:S(2)}) collective-permute-start(bf16[256,2048]{1,0:T(8,128)(2,1)S(1)} %get-tuple-element.54), channel_id=1, source_target_pairs={{0,128},{1,33},{16,144},{17,49},{32,160},{33,1},{48,176},{49,17},{... | collective-permute-start | bytes 3145736 | tf_op jit(solution)/shard_map/ppermute | solution.py:339
  20.3 0.2 collective-permute-start.10
  20.5 0.7 shard_map.79.bias
  21.2 0.0 collective-permute-done.3.near_pair
  21.2 5.3 %shard_map.80 = (bf16[256,256]{1,0:T(8,128)(2,1)S(1)}, bf16[256,256]{1,0:T(8,128)(2,1)S(1)}, bf16[8,768,256]{2,1,0:T(8,128)(2,1)S(1)}, bf16[8,256,256]{2,1,0:T(8,128)(2,1)S(1)}) custom-call(bf16[128,1024]{1,0:T(8,128)(2,1)S(1)} %get-tuple-element.76.q_mine, bf16[128,1024]{1,0:T(8,128)(2,1)S(1)} %get-tuple-element.69.do_mine, ...), custom_call_target="tpu_custom_call" | custom-call | flops 30198988800 | bytes 4194304 | tf_op jit(solution)/shard_map/pallas_call | solution.py:167
  26.6 1.3 %collective-permute-start.7 = (bf16[256,256]{1,0:T(8,128)(2,1)S(1)}, bf16[256,256]{1,0:T(8,128)(2,1)S(1)}, u32[]{:S(2)}, u32[]{:S(2)}) collective-permute-start(bf16[256,256]{1,0:T(8,128)(2,1)S(1)} %get-tuple-element.50), channel_id=1, source_target_pairs={{4,0},{5,1},{6,2},{7,3},{12,8},{13,9},{14,10},{15,11},{20,16},{21,... | collective-permute-start | bytes 393224 | tf_op jit(solution)/shard_map/ppermute | solution.py:380
  27.9 1.3 %collective-permute-start.6 = (bf16[256,256]{1,0:T(8,128)(2,1)S(1)}, bf16[256,256]{1,0:T(8,128)(2,1)S(1)}, u32[]{:S(2)}, u32[]{:S(2)}) collective-permute-start(bf16[256,256]{1,0:T(8,128)(2,1)S(1)} %get-tuple-element.49), channel_id=1, source_target_pairs={{2,0},{3,1},{4,2},{5,3},{6,4},{7,5},{10,8},{11,9},{12,10},{13,11},... | collective-permute-start | bytes 393224 | tf_op jit(solution)/shard_map/ppermute | solution.py:380
  29.2 1.7 %shard_map.82.refs_0_ = bf16[256,2048]{1,0:T(8,128)(2,1)S(1)} custom-call(s32[3]{0:T(128)S(1)} %pad_add_fusion.1.places_ref, bf16[128,8192]{1,0:T(8,128)(2,1)S(1)} %bitcast.25, bf16[128,8192]{1,0:T(8,128)(2,1)} %collective-permute-done.5.other), custom_call_target="tpu_custom_call" | custom-call | bytes 6291456 | tf_op jit(solution)/shard_map/pallas_call | solution.py:72
  30.9 1.1 %shard_map.81 = (bf16[128,1024]{1,0:T(8,128)(2,1)S(1)}, bf16[128,1024]{1,0:T(8,128)(2,1)S(1)}, f32[256,256]{1,0:T(8,128)S(1)}) custom-call(bf16[128,1024]{1,0:T(8,128)(2,1)S(1)} %get-tuple-element.76.q_mine, bf16[128,1024]{1,0:T(8,128)(2,1)S(1)} %get-tuple-element.69.do_mine, bf16[128,1024]{1,0:T(8,128)(2,1)S(1)} %collective-permute-done.1.q_other, ...), custom_call_target="tpu_custom_call" | custom-call | flops 1207959552 | bytes 6291456 | tf_op jit(solution)/shard_map/pallas_call | solution.py:214
  32.0 4.7 %collective-permute-done.7.far = bf16[256,256]{1,0:T(8,128)(2,1)S(1)} collective-permute-done((bf16[256,256]{1,0:T(8,128)(2,1)S(1)}, bf16[256,256]{1,0:T(8,128)(2,1)S(1)}, u32[]{:S(2)}, u32[]{:S(2)}) %collective-permute-start.7) | collective-permute-done | bytes 131104 | tf_op jit(solution)/shard_map/ppermute | solution.py:380
  36.7 0.0 collective-permute-done.6.near
  36.7 0.1 shard_map.83.refs_4_
  36.8 2.1 %collective-permute-start.14 = (bf16[128,1024]{1,0:T(8,128)(2,1)S(1)}, bf16[128,1024]{1,0:T(8,128)(2,1)S(1)}, u32[]{:S(2)}, u32[]{:S(2)}) collective-permute-start(bf16[128,1024]{1,0:T(8,128)(2,1)S(1)} %get-tuple-element.58), channel_id=1, source_target_pairs={{0,1},{1,0},{2,3},{3,2},{4,5},{5,4},{6,7},{7,6},{8,9},{9,8},{10,11... | collective-permute-start | bytes 786440 | tf_op jit(solution)/shard_map/ppermute | solution.py:389
  38.9 2.5 %collective-permute-start.13 = (bf16[256,256]{1,0:T(8,128)(2,1)S(1)}, bf16[256,256]{1,0:T(8,128)(2,1)S(1)}, u32[]{:S(2)}, u32[]{:S(2)}) collective-permute-start(bf16[256,256]{1,0:T(8,128)(2,1)S(1)} %shard_map.83.refs_4_), channel_id=1, source_target_pairs={{0,192},{1,49},{16,208},{17,33},{32,224},{33,17},{48,240},{49,1},{... | collective-permute-start | bytes 393224 | tf_op jit(solution)/shard_map/ppermute | solution.py:339
  41.4 0.1 collective-permute-start.12
  41.5 0.0 collective-permute-done.14.other
  41.5 0.6 collective-permute-start.11
  42.1 1.4 %shard_map.84 = bf16[128,2048]{1,0:T(8,128)(2,1)} custom-call(s32[2]{0:T(128)S(1)} %pad_add_fusion.here_ref, bf16[128,1024]{1,0:T(8,128)(2,1)S(1)} %get-tuple-element.57.mine, bf16[128,1024]{1,0:T(8,128)(2,1)S(1)} %collective-permute-done.14.other), custom_call_target="tpu_custom_call" | custom-call | bytes 1048576 | tf_op jit(solution)/shard_map/pallas_call | solution.py:250
  43.5 6.0 %collective-permute-done.13.refs_7_ = bf16[256,256]{1,0:T(8,128)(2,1)S(1)} collective-permute-done((bf16[256,256]{1,0:T(8,128)(2,1)S(1)}, bf16[256,256]{1,0:T(8,128)(2,1)S(1)}, u32[]{:S(2)}, u32[]{:S(2)}) %collective-permute-start.13) | collective-permute-done | bytes 131104 | tf_op jit(solution)/shard_map/ppermute | solution.py:339
  49.5 0.0 collective-permute-done.12.refs_6_
  49.5 0.0 collective-permute-done.9.refs_2_
  49.5 0.0 collective-permute-done.10.refs_3_
  49.5 1.1 %shard_map.88 = bf16[512,256]{1,0:T(8,128)(2,1)S(1)} custom-call(s32[3]{0:T(128)S(1)} %pad_add_fusion.1.places_ref, bf16[256,2048]{1,0:T(8,128)(2,1)S(1)} %shard_map.82.refs_0_, bf16[256,2048]{1,0:T(8,128)(2,1)S(1)} %collective-permute-done.8.refs_1_, bf16[256,2048]{1,0:T(8,128)(2,1)S(1)} %collective-permute-done.9.refs_2_, ...), custom_call_target="tpu_custom_call" | custom-call | flops 268435456 | bytes 2097152 | tf_op jit(solution)/shard_map/pallas_call | solution.py:274
  50.6 1.1 %shard_map.87 = bf16[512,256]{1,0:T(8,128)(2,1)S(1)} custom-call(s32[3]{0:T(128)S(1)} %pad_add_fusion.1.places_ref, bf16[256,2048]{1,0:T(8,128)(2,1)S(1)} %shard_map.82.refs_0_, bf16[256,2048]{1,0:T(8,128)(2,1)S(1)} %collective-permute-done.8.refs_1_, bf16[256,2048]{1,0:T(8,128)(2,1)S(1)} %collective-permute-done.9.refs_2_, ...), custom_call_target="tpu_custom_call" | custom-call | flops 268435456 | bytes 2097152 | tf_op jit(solution)/shard_map/pallas_call | solution.py:274
  51.7 1.1 %shard_map.86 = bf16[512,256]{1,0:T(8,128)(2,1)S(1)} custom-call(s32[3]{0:T(128)S(1)} %pad_add_fusion.1.places_ref, bf16[256,2048]{1,0:T(8,128)(2,1)S(1)} %shard_map.82.refs_0_, bf16[256,2048]{1,0:T(8,128)(2,1)S(1)} %collective-permute-done.8.refs_1_, bf16[256,2048]{1,0:T(8,128)(2,1)S(1)} %collective-permute-done.9.refs_2_, ...), custom_call_target="tpu_custom_call" | custom-call | flops 268435456 | bytes 2097152 | tf_op jit(solution)/shard_map/pallas_call | solution.py:274
  52.7 2.7 %collective-permute-start.15 = (bf16[512,256]{1,0:T(8,128)(2,1)S(1)}, bf16[512,256]{1,0:T(8,128)(2,1)S(1)}, u32[]{:S(2)}, u32[]{:S(2)}) collective-permute-start(bf16[512,256]{1,0:T(8,128)(2,1)S(1)} %shard_map.86), channel_id=1, source_target_pairs={{0,32},{1,129},{16,48},{17,145},{32,0},{33,161},{48,16},{49,177},{... | collective-permute-start | bytes 786440 | tf_op jit(solution)/shard_map/ppermute | solution.py:339
  55.4 0.4 collective-permute-start.16
  55.8 0.4 collective-permute-start.17
  56.2 1.1 %shard_map.85.refs_0_ = f32[512,256]{1,0:T(8,128)S(1)} custom-call(s32[3]{0:T(128)S(1)} %pad_add_fusion.1.places_ref, bf16[256,2048]{1,0:T(8,128)(2,1)S(1)} %shard_map.82.refs_0_, bf16[256,2048]{1,0:T(8,128)(2,1)S(1)} %collective-permute-done.8.refs_1_, bf16[256,2048]{1,0:T(8,128)(2,1)S(1)} %collective-permute-done.9.refs_2_, ...), custom_call_target="tpu_custom_call" | custom-call | flops 268435456 | bytes 2097152 | tf_op jit(solution)/shard_map/pallas_call | solution.py:274
  57.3 2.2 %collective-permute-done.15.refs_1_ = bf16[512,256]{1,0:T(8,128)(2,1)S(1)} collective-permute-done((bf16[512,256]{1,0:T(8,128)(2,1)S(1)}, bf16[512,256]{1,0:T(8,128)(2,1)S(1)}, u32[]{:S(2)}, u32[]{:S(2)}) %collective-permute-start.15) | collective-permute-done | bytes 262176 | tf_op jit(solution)/shard_map/ppermute | solution.py:339
  59.5 3.2 %collective-permute-done.16.refs_2_ = bf16[512,256]{1,0:T(8,128)(2,1)S(1)} collective-permute-done((bf16[512,256]{1,0:T(8,128)(2,1)S(1)}, bf16[512,256]{1,0:T(8,128)(2,1)S(1)}, u32[]{:S(2)}, u32[]{:S(2)}) %collective-permute-start.16) | collective-permute-done | bytes 262176 | tf_op jit(solution)/shard_map/ppermute | solution.py:339
  62.7 0.0 collective-permute-done.17.refs_3_
  62.7 0.1 shard_map.89
  62.8 21.2 %all_to_all.5.parts = bf16[16,32,256]{2,1,0:T(8,128)(2,1)S(1)} all-to-all(bf16[16,32,256]{2,1,0:T(8,128)(2,1)S(1)} %bitcast.26), channel_id=1, replica_groups=mesh['y'=4,'x'=4,'z_hi'=2,'z_lo'=4,'core'=2] {'z_hi','z_lo','core'}, dimensions={0} | all-to-all | bytes 524288 | tf_op jit(solution)/shard_map/all_to_all | solution.py:399
  84.1 0.7 shard_map.90
  (12 shorter events, 0.1 us)
Async XLA Ops:
  0.6 6.4 %copy-start = (bf16[1,128,8192]{2,1,0:T(8,128)(2,1)S(1)}, bf16[1,128,8192]{2,1,0:T(8,128)(2,1)}, u32[]{:S(2)}) copy-start(bf16[1,128,8192]{2,1,0:T(8,128)(2,1)} %param.10) | copy-start | bytes 6291460
  1.6 5.4 %collective-permute-start = (bf16[128,256]{1,0:T(8,128)(2,1)S(1)}, bf16[128,256]{1,0:T(8,128)(2,1)S(1)}, u32[]{:S(2)}, u32[]{:S(2)}) collective-permute-start(bf16[128,256]{1,0:T(8,128)(2,1)S(1)} %pad_maximum_fusion), channel_id=1, source_target_pairs={{0,1},{1,0},{2,3},{3,2},{4,5},{5,4},{6,7},{7,6},{8,9},{9,8},{10,11... | collective-permute-start | bytes 196616 | tf_op jit(solution)/shard_map/ppermute | solution.py:347
  7.1 7.6 %collective-permute-start.5 = (bf16[128,8192]{1,0:T(8,128)(2,1)S(1)}, bf16[128,8192]{1,0:T(8,128)(2,1)}, u32[]{:S(2)}, u32[]{:S(2)}) collective-permute-start(bf16[128,8192]{1,0:T(8,128)(2,1)S(1)} %bitcast.23), channel_id=1, source_target_pairs={{0,1},{1,0},{2,3},{3,2},{4,5},{5,4},{6,7},{7,6},{8,9},{9,8},{10,11... | collective-permute-start | bytes 6291464 | tf_op jit(solution)/shard_map/ppermute | solution.py:368
  7.2 9.3 %collective-permute-start.1 = (bf16[128,1024]{1,0:T(8,128)(2,1)}, bf16[128,1024]{1,0:T(8,128)(2,1)S(1)}, u32[]{:S(2)}, u32[]{:S(2)}) collective-permute-start(bf16[128,1024]{1,0:T(8,128)(2,1)} %get-tuple-element.38), channel_id=1, source_target_pairs={{0,1},{1,0},{2,3},{3,2},{4,5},{5,4},{6,7},{7,6},{8,9},{9,8},{10,11... | collective-permute-start | bytes 786440 | tf_op jit(solution)/shard_map/ppermute | solution.py:355
  7.7 8.8 %collective-permute-start.2 = (bf16[128,1024]{1,0:T(8,128)(2,1)}, bf16[128,1024]{1,0:T(8,128)(2,1)S(1)}, u32[]{:S(2)}, u32[]{:S(2)}) collective-permute-start(bf16[128,1024]{1,0:T(8,128)(2,1)} %get-tuple-element.39), channel_id=1, source_target_pairs={{0,1},{1,0},{2,3},{3,2},{4,5},{5,4},{6,7},{7,6},{8,9},{9,8},{10,11... | collective-permute-start | bytes 786440 | tf_op jit(solution)/shard_map/ppermute | solution.py:355
  7.8 13.4 %collective-permute-start.4 = (bf16[256,256]{1,0:T(8,128)(2,1)S(1)}, bf16[256,256]{1,0:T(8,128)(2,1)S(1)}, u32[]{:S(2)}, u32[]{:S(2)}) collective-permute-start(bf16[256,256]{1,0:T(8,128)(2,1)S(1)} %shard_map.77.chip_pair), channel_id=1, source_target_pairs={{0,4},{1,5},{2,6},{3,7},{8,12},{9,13},{10,14},{11,15},{16,20},{17,... | collective-permute-start | bytes 393224 | tf_op jit(solution)/shard_map/ppermute | solution.py:365
  10.9 10.3 %collective-permute-start.3 = (bf16[256,256]{1,0:T(8,128)(2,1)S(1)}, bf16[256,256]{1,0:T(8,128)(2,1)S(1)}, u32[]{:S(2)}, u32[]{:S(2)}) collective-permute-start(bf16[256,256]{1,0:T(8,128)(2,1)S(1)} %shard_map.77.chip_pair), channel_id=1, source_target_pairs={{0,2},{1,3},{2,4},{3,5},{4,6},{5,7},{8,10},{9,11},{10,12},{11,13},... | collective-permute-start | bytes 393224 | tf_op jit(solution)/shard_map/ppermute | solution.py:365
  14.6 5.8 %copy-start.1 = (s32[1,1024]{1,0:T(1,128)S(1)}, s32[1,1024]{1,0:T(1,128)}, u32[]{:S(2)}) copy-start(s32[1,1024]{1,0:T(1,128)} %docs) | copy-start | bytes 12292
  16.5 20.3 %collective-permute-start.8 = (bf16[256,2048]{1,0:T(8,128)(2,1)S(1)}, bf16[256,2048]{1,0:T(8,128)(2,1)S(1)}, u32[]{:S(2)}, u32[]{:S(2)}) collective-permute-start(bf16[256,2048]{1,0:T(8,128)(2,1)S(1)} %get-tuple-element.44), channel_id=1, source_target_pairs={{0,64},{1,17},{16,80},{17,1},{32,96},{33,49},{48,112},{49,33},{64,... | collective-permute-start | bytes 3145736 | tf_op jit(solution)/shard_map/ppermute | solution.py:339
  17.8 31.7 %collective-permute-start.9 = (bf16[256,2048]{1,0:T(8,128)(2,1)S(1)}, bf16[256,2048]{1,0:T(8,128)(2,1)S(1)}, u32[]{:S(2)}, u32[]{:S(2)}) collective-permute-start(bf16[256,2048]{1,0:T(8,128)(2,1)S(1)} %get-tuple-element.54), channel_id=1, source_target_pairs={{0,128},{1,33},{16,144},{17,49},{32,160},{33,1},{48,176},{49,17},{... | collective-permute-start | bytes 3145736 | tf_op jit(solution)/shard_map/ppermute | solution.py:339
  20.3 29.2 %collective-permute-start.10 = (bf16[256,2048]{1,0:T(8,128)(2,1)S(1)}, bf16[256,2048]{1,0:T(8,128)(2,1)S(1)}, u32[]{:S(2)}, u32[]{:S(2)}) collective-permute-start(bf16[256,2048]{1,0:T(8,128)(2,1)S(1)} %get-tuple-element.55), channel_id=1, source_target_pairs={{0,192},{1,49},{16,208},{17,33},{32,224},{33,17},{48,240},{49,1},{... | collective-permute-start | bytes 3145736 | tf_op jit(solution)/shard_map/ppermute | solution.py:339
  26.6 10.1 %collective-permute-start.7 = (bf16[256,256]{1,0:T(8,128)(2,1)S(1)}, bf16[256,256]{1,0:T(8,128)(2,1)S(1)}, u32[]{:S(2)}, u32[]{:S(2)}) collective-permute-start(bf16[256,256]{1,0:T(8,128)(2,1)S(1)} %get-tuple-element.50), channel_id=1, source_target_pairs={{4,0},{5,1},{6,2},{7,3},{12,8},{13,9},{14,10},{15,11},{20,16},{21,... | collective-permute-start | bytes 393224 | tf_op jit(solution)/shard_map/ppermute | solution.py:380
  27.9 8.8 %collective-permute-start.6 = (bf16[256,256]{1,0:T(8,128)(2,1)S(1)}, bf16[256,256]{1,0:T(8,128)(2,1)S(1)}, u32[]{:S(2)}, u32[]{:S(2)}) collective-permute-start(bf16[256,256]{1,0:T(8,128)(2,1)S(1)} %get-tuple-element.49), channel_id=1, source_target_pairs={{2,0},{3,1},{4,2},{5,3},{6,4},{7,5},{10,8},{11,9},{12,10},{13,11},... | collective-permute-start | bytes 393224 | tf_op jit(solution)/shard_map/ppermute | solution.py:380
  36.8 4.7 %collective-permute-start.14 = (bf16[128,1024]{1,0:T(8,128)(2,1)S(1)}, bf16[128,1024]{1,0:T(8,128)(2,1)S(1)}, u32[]{:S(2)}, u32[]{:S(2)}) collective-permute-start(bf16[128,1024]{1,0:T(8,128)(2,1)S(1)} %get-tuple-element.58), channel_id=1, source_target_pairs={{0,1},{1,0},{2,3},{3,2},{4,5},{5,4},{6,7},{7,6},{8,9},{9,8},{10,11... | collective-permute-start | bytes 786440 | tf_op jit(solution)/shard_map/ppermute | solution.py:389
  38.9 10.6 %collective-permute-start.13 = (bf16[256,256]{1,0:T(8,128)(2,1)S(1)}, bf16[256,256]{1,0:T(8,128)(2,1)S(1)}, u32[]{:S(2)}, u32[]{:S(2)}) collective-permute-start(bf16[256,256]{1,0:T(8,128)(2,1)S(1)} %shard_map.83.refs_4_), channel_id=1, source_target_pairs={{0,192},{1,49},{16,208},{17,33},{32,224},{33,17},{48,240},{49,1},{... | collective-permute-start | bytes 393224 | tf_op jit(solution)/shard_map/ppermute | solution.py:339
  41.4 8.1 %collective-permute-start.12 = (bf16[256,256]{1,0:T(8,128)(2,1)S(1)}, bf16[256,256]{1,0:T(8,128)(2,1)S(1)}, u32[]{:S(2)}, u32[]{:S(2)}) collective-permute-start(bf16[256,256]{1,0:T(8,128)(2,1)S(1)} %shard_map.83.refs_4_), channel_id=1, source_target_pairs={{0,128},{1,33},{16,144},{17,49},{32,160},{33,1},{48,176},{49,17},{... | collective-permute-start | bytes 393224 | tf_op jit(solution)/shard_map/ppermute | solution.py:339
  41.5 8.0 %collective-permute-start.11 = (bf16[256,256]{1,0:T(8,128)(2,1)S(1)}, bf16[256,256]{1,0:T(8,128)(2,1)S(1)}, u32[]{:S(2)}, u32[]{:S(2)}) collective-permute-start(bf16[256,256]{1,0:T(8,128)(2,1)S(1)} %shard_map.83.refs_4_), channel_id=1, source_target_pairs={{0,64},{1,17},{16,80},{17,1},{32,96},{33,49},{48,112},{49,33},{64,... | collective-permute-start | bytes 393224 | tf_op jit(solution)/shard_map/ppermute | solution.py:339
  52.7 6.8 %collective-permute-start.15 = (bf16[512,256]{1,0:T(8,128)(2,1)S(1)}, bf16[512,256]{1,0:T(8,128)(2,1)S(1)}, u32[]{:S(2)}, u32[]{:S(2)}) collective-permute-start(bf16[512,256]{1,0:T(8,128)(2,1)S(1)} %shard_map.86), channel_id=1, source_target_pairs={{0,32},{1,129},{16,48},{17,145},{32,0},{33,161},{48,16},{49,177},{... | collective-permute-start | bytes 786440 | tf_op jit(solution)/shard_map/ppermute | solution.py:339
  55.4 7.3 %collective-permute-start.16 = (bf16[512,256]{1,0:T(8,128)(2,1)S(1)}, bf16[512,256]{1,0:T(8,128)(2,1)S(1)}, u32[]{:S(2)}, u32[]{:S(2)}) collective-permute-start(bf16[512,256]{1,0:T(8,128)(2,1)S(1)} %shard_map.87), channel_id=1, source_target_pairs={{0,16},{1,65},{16,0},{17,81},{32,48},{33,97},{48,32},{49,113},{64,... | collective-permute-start | bytes 786440 | tf_op jit(solution)/shard_map/ppermute | solution.py:339
  55.8 6.9 %collective-permute-start.17 = (bf16[512,256]{1,0:T(8,128)(2,1)S(1)}, bf16[512,256]{1,0:T(8,128)(2,1)S(1)}, u32[]{:S(2)}, u32[]{:S(2)}) collective-permute-start(bf16[512,256]{1,0:T(8,128)(2,1)S(1)} %shard_map.88), channel_id=1, source_target_pairs={{0,48},{1,193},{16,32},{17,209},{32,16},{33,225},{48,0},{49,241},{... | collective-permute-start | bytes 786440 | tf_op jit(solution)/shard_map/ppermute | solution.py:339

commit v15 on v14

--- a/solution.py
+++ b/solution.py
@@ -256,29 +256,30 @@
     )(here, mine, other)
 
 
-def project_kernel(places_ref, *refs, offset):
-    n = len(refs) // 2
-    pieces, grads, out = refs[:n], refs[n:-1], refs[-1]
-    step = out.shape[0]
-    place = jnp.where(places_ref[2] == 0, places_ref[1], places_ref[0]) ^ offset
-    columns = pl.ds(pl.multiple_of(place * step, step), step)
+def project_kernel(places_ref, *refs, offsets):
+    n = (len(refs) - len(offsets)) // 2
+    pieces, grads, outs = refs[:n], refs[n : 2 * n], refs[2 * n :]
+    step = outs[0].shape[0]
+    place = jnp.where(places_ref[2] == 0, places_ref[1], places_ref[0])
     left = jnp.concatenate([ref[...] for ref in grads], axis=1)
-    right = jnp.concatenate([ref[:, columns] for ref in pieces], axis=0)
-    out[...] = dot_nn(left, right).T.astype(out.dtype)
-
-
-def project(places, pieces, grads, offset, dtype):
+    for offset, out in zip(offsets, outs):
+        columns = pl.ds(pl.multiple_of((place ^ offset) * step, step), step)
+        right = jnp.concatenate([ref[:, columns] for ref in pieces], axis=0)
+        out[...] = dot_nn(left, right).T.astype(out.dtype)
+
+
+def project(places, pieces, grads, offsets, dtype):
     rows, columns = pieces[0].shape
     width = grads[0].shape[0]
     step = columns // len(pieces)
     return pl.pallas_call(
-        functools.partial(project_kernel, offset=offset),
-        out_shape=whole((step, width), dtype),
+        functools.partial(project_kernel, offsets=offsets),
+        out_shape=(whole((step, width), dtype),) * len(offsets),
         in_specs=[SCALAR] + [pl.BlockSpec()] * (2 * len(pieces)),
         compiler_params=pltpu.CompilerParams(vmem_limit_bytes=16 * MIB),
         cost_estimate=pl.CostEstimate(
-            flops=2 * len(pieces) * rows * step * width,
-            bytes_accessed=2 * MIB,
+            flops=2 * len(offsets) * len(pieces) * rows * step * width,
+            bytes_accessed=2 * MIB * len(offsets),
             transcendentals=0,
         ),
     )(places, *pieces, *grads)
@@ -390,9 +391,9 @@
     query_grad = assemble(here_ref, dq_mine, dq_back)[None]
     pieces, grads, query_grad = lax.optimization_barrier((pieces, grads, query_grad))
     pieces = [own_piece] + list(pieces)
-    terms = [project(places_ref, pieces, grads, k, jnp.bfloat16) for k in (2, 1, 3)]
+    terms = project(places_ref, pieces, grads, (2, 1, 3), jnp.bfloat16)
     parts = [cross(term, k, False) for term, k in zip(terms, (2, 1, 3))]
-    own_term = project(places_ref, pieces, grads, 0, jnp.float32)
+    (own_term,) = project(places_ref, pieces, grads, (0,), jnp.float32)
     term = add_parts(own_term, parts)
     rest = ("z_hi", "z_lo", "core")
     n_rest = lax.axis_size(rest)

time: 85.1 us -> 83.5 us (0.981)
  Pallas kernels: 17.3 us -> 15.8 us
    pallas_call x4 -> x2, Pallas kernels: 4.32 us -> 2.75 us  [project(): pl.pallas_call(functools.partial(project_kernel, offsets=offsets), out_sh...]
where the time goes in v15:
time: 83.5 us; the launch traced here: 83.2 us
  starting transfers between devices  26.1 us (31%)
  blocking collectives  21.2 us (25%)
  waiting for transfers between devices  16.1 us (19%)
  Pallas kernels  15.8 us (19%)
  local copies, waits for them, and re-layouts  3.05 us (4%)
    all_to_all x1, blocking collectives, per_device(): lax.all_to_all(term.reshape(n_rest, term.shape[0] // n_rest, term.shape[1...  21.2 us
    ppermute x9, waiting for transfers between devices, cross(): return lax.ppermute(part, ('y', 'x', 'core'), pairs)  11.4 us
    ppermute x9, starting transfers between devices, cross(): return lax.ppermute(part, ('y', 'x', 'core'), pairs)  10.7 us
    ppermute x2, starting transfers between devices, per_device(): lax.ppermute(chip_pair, ('z_lo', 'core'), behind(distance))  6.7 us
    pallas_call x1, Pallas kernels, attention(): pl.pallas_call(attention_kernel, out_shape=(whole((chip, 2 * DH)), whole(...  5.34 us
    ppermute x2, waiting for transfers between devices, per_device(): lax.ppermute(part, ('z_lo', 'core'), [(b, a) for a, b in behind(distance)])  4.65 us
    pallas_call x2, Pallas kernels, split_columns(): pl.pallas_call(functools.partial(chunk_kernel, places=places), out_shape=...  3.53 us
    ppermute x1, starting transfers between devices, per_device(): lax.ppermute(jnp.concatenate([half_of(keys, 1 - core), half_of(values, 1...  3.33 us
  transfers between devices with their start and end apart: 18, of which 4 were waited for; matrix products, arithmetic and copies ran while one was open for 3% of the time, Pallas kernels for 16%

profile of v15, /device:TPU:1, one launch (start us, length us, event | category | flops | bytes accessed | tf_op | source)
XLA Modules:
  0.0 83.2 jit_solution(17192186383350157352)
XLA Ops:
  0.6 1.0 %dynamic-slice_bitcast_fusion.4 = (bf16[128,128]{1,0:T(8,128)(2,1)S(1)}, bf16[128,128]{1,0:T(8,128)(2,1)S(1)}, bf16[128,128]{1,0:T(8,128)(2,1)S(1)}, bf16[128,128]{1,0:T(8,128)(2,1)S(1)}) fusion(bf16[1,128,256]{2,1,0:T(8,128)(2,1)} %param.8, s32[]{:T(128)S(6)} %select_n.19, s32[]{:T(128)S(6)} %select_n.17, bf16[1,128,256]{2,1,0:T(8,128)(2,1)} %param.7), kind=kLoop, calls=%fused_computation.5 | loop fusion | bytes 262152 | tf_op jit(solution)/shard_map/dynamic_slice | solution.py:345
  1.6 3.3 %collective-permute-start = (bf16[128,256]{1,0:T(8,128)(2,1)S(1)}, bf16[128,256]{1,0:T(8,128)(2,1)S(1)}, u32[]{:S(2)}, u32[]{:S(2)}) collective-permute-start(bf16[128,256]{1,0:T(8,128)(2,1)S(1)} %pad_maximum_fusion), channel_id=1, source_target_pairs={{0,1},{1,0},{2,3},{3,2},{4,5},{5,4},{6,7},{7,6},{8,9},{9,8},{10,11... | collective-permute-start | bytes 196616 | tf_op jit(solution)/shard_map/ppermute | solution.py:348
  5.0 2.1 %dynamic-slice_bitcast_fusion = (bf16[128,1024]{1,0:T(8,128)(2,1)}, bf16[128,1024]{1,0:T(8,128)(2,1)S(1)}, bf16[128,1024]{1,0:T(8,128)(2,1)S(1)}, bf16[128,1024]{1,0:T(8,128)(2,1)}) fusion(bf16[1,128,2048]{2,1,0:T(8,128)(2,1)} %param.9, s32[]{:T(128)S(6)} %select_n.18, s32[]{:T(128)S(6)} %select_n.16, bf16[1,128,2048]{2,1,0:T(8,128)(2,1)} %param.6), kind=kLoop, calls=%fused_computation | loop fusion | bytes 2097160 | tf_op jit(solution)/shard_map/dynamic_slice | solution.py:345
  7.0 0.0 collective-permute-done.swapped
  7.1 0.1 collective-permute-start.5
  7.2 0.5 collective-permute-start.1
  7.7 0.1 collective-permute-start.2
  7.8 3.2 %collective-permute-start.4 = (bf16[256,256]{1,0:T(8,128)(2,1)S(1)}, bf16[256,256]{1,0:T(8,128)(2,1)S(1)}, u32[]{:S(2)}, u32[]{:S(2)}) collective-permute-start(bf16[256,256]{1,0:T(8,128)(2,1)S(1)} %shard_map.77.chip_pair), channel_id=1, source_target_pairs={{0,4},{1,5},{2,6},{3,7},{8,12},{9,13},{10,14},{11,15},{16,20},{17,... | collective-permute-start | bytes 393224 | tf_op jit(solution)/shard_map/ppermute | solution.py:366
  10.9 3.5 %collective-permute-start.3 = (bf16[256,256]{1,0:T(8,128)(2,1)S(1)}, bf16[256,256]{1,0:T(8,128)(2,1)S(1)}, u32[]{:S(2)}, u32[]{:S(2)}) collective-permute-start(bf16[256,256]{1,0:T(8,128)(2,1)S(1)} %shard_map.77.chip_pair), channel_id=1, source_target_pairs={{0,2},{1,3},{2,4},{3,5},{4,6},{5,7},{8,10},{9,11},{10,12},{11,13},... | collective-permute-start | bytes 393224 | tf_op jit(solution)/shard_map/ppermute | solution.py:366
  14.5 0.1 pad_add_fusion.here_ref
  14.6 0.1 pad_add_fusion.1.places_ref
  14.6 0.0 collective-permute-done.5.other
  14.7 1.8 %shard_map.78 = (bf16[256,2048]{1,0:T(8,128)(2,1)S(1)}, bf16[256,2048]{1,0:T(8,128)(2,1)S(1)}, bf16[256,2048]{1,0:T(8,128)(2,1)S(1)}) custom-call(s32[3]{0:T(128)S(1)} %pad_add_fusion.1.places_ref, bf16[128,8192]{1,0:T(8,128)(2,1)S(1)} %bitcast.24, bf16[128,8192]{1,0:T(8,128)(2,1)} %collective-permute-done.5.other), custom_call_target="tpu_custom_call" | custom-call | bytes 6291456 | tf_op jit(solution)/shard_map/pallas_call | solution.py:72
  16.5 0.0 collective-permute-done.1.q_other
  16.5 0.0 collective-permute-done.2.do_other
  16.5 1.3 %collective-permute-start.8 = (bf16[256,2048]{1,0:T(8,128)(2,1)S(1)}, bf16[256,2048]{1,0:T(8,128)(2,1)S(1)}, u32[]{:S(2)}, u32[]{:S(2)}) collective-permute-start(bf16[256,2048]{1,0:T(8,128)(2,1)S(1)} %get-tuple-element.47), channel_id=1, source_target_pairs={{0,64},{1,17},{16,80},{17,1},{32,96},{33,49},{48,112},{49,33},{64,... | collective-permute-start | bytes 3145736 | tf_op jit(solution)/shard_map/ppermute | solution.py:340
  17.8 2.4 %collective-permute-start.9 = (bf16[256,2048]{1,0:T(8,128)(2,1)S(1)}, bf16[256,2048]{1,0:T(8,128)(2,1)S(1)}, u32[]{:S(2)}, u32[]{:S(2)}) collective-permute-start(bf16[256,2048]{1,0:T(8,128)(2,1)S(1)} %get-tuple-element.57), channel_id=1, source_target_pairs={{0,128},{1,33},{16,144},{17,49},{32,160},{33,1},{48,176},{49,17},{... | collective-permute-start | bytes 3145736 | tf_op jit(solution)/shard_map/ppermute | solution.py:340
  20.3 0.2 collective-permute-start.10
  20.5 0.7 shard_map.79.bias
  21.2 0.0 collective-permute-done.4.far_pair
  21.2 0.0 collective-permute-done.3.near_pair
  21.2 5.3 %shard_map.80 = (bf16[256,256]{1,0:T(8,128)(2,1)S(1)}, bf16[256,256]{1,0:T(8,128)(2,1)S(1)}, bf16[8,768,256]{2,1,0:T(8,128)(2,1)S(1)}, bf16[8,256,256]{2,1,0:T(8,128)(2,1)S(1)}) custom-call(bf16[128,1024]{1,0:T(8,128)(2,1)S(1)} %get-tuple-element.82.q_mine, bf16[128,1024]{1,0:T(8,128)(2,1)S(1)} %get-tuple-element.75.do_mine, ...), custom_call_target="tpu_custom_call" | custom-call | flops 30198988800 | bytes 4194304 | tf_op jit(solution)/shard_map/pallas_call | solution.py:167
  26.6 1.3 %collective-permute-start.7 = (bf16[256,256]{1,0:T(8,128)(2,1)S(1)}, bf16[256,256]{1,0:T(8,128)(2,1)S(1)}, u32[]{:S(2)}, u32[]{:S(2)}) collective-permute-start(bf16[256,256]{1,0:T(8,128)(2,1)S(1)} %get-tuple-element.53), channel_id=1, source_target_pairs={{4,0},{5,1},{6,2},{7,3},{12,8},{13,9},{14,10},{15,11},{20,16},{21,... | collective-permute-start | bytes 393224 | tf_op jit(solution)/shard_map/ppermute | solution.py:381
  27.9 1.3 %collective-permute-start.6 = (bf16[256,256]{1,0:T(8,128)(2,1)S(1)}, bf16[256,256]{1,0:T(8,128)(2,1)S(1)}, u32[]{:S(2)}, u32[]{:S(2)}) collective-permute-start(bf16[256,256]{1,0:T(8,128)(2,1)S(1)} %get-tuple-element.52), channel_id=1, source_target_pairs={{2,0},{3,1},{4,2},{5,3},{6,4},{7,5},{10,8},{11,9},{12,10},{13,11},... | collective-permute-start | bytes 393224 | tf_op jit(solution)/shard_map/ppermute | solution.py:381
  29.2 1.7 %shard_map.82.refs_0_ = bf16[256,2048]{1,0:T(8,128)(2,1)S(1)} custom-call(s32[3]{0:T(128)S(1)} %pad_add_fusion.1.places_ref, bf16[128,8192]{1,0:T(8,128)(2,1)S(1)} %bitcast.25, bf16[128,8192]{1,0:T(8,128)(2,1)} %collective-permute-done.5.other), custom_call_target="tpu_custom_call" | custom-call | bytes 6291456 | tf_op jit(solution)/shard_map/pallas_call | solution.py:72
  30.9 1.1 %shard_map.81 = (bf16[128,1024]{1,0:T(8,128)(2,1)S(1)}, bf16[128,1024]{1,0:T(8,128)(2,1)S(1)}, f32[256,256]{1,0:T(8,128)S(1)}) custom-call(bf16[128,1024]{1,0:T(8,128)(2,1)S(1)} %get-tuple-element.82.q_mine, bf16[128,1024]{1,0:T(8,128)(2,1)S(1)} %get-tuple-element.75.do_mine, bf16[128,1024]{1,0:T(8,128)(2,1)S(1)} %collective-permute-done.1.q_other, ...), custom_call_target="tpu_custom_call" | custom-call | flops 1207959552 | bytes 6291456 | tf_op jit(solution)/shard_map/pallas_call | solution.py:214
  32.0 4.6 %collective-permute-done.7.far = bf16[256,256]{1,0:T(8,128)(2,1)S(1)} collective-permute-done((bf16[256,256]{1,0:T(8,128)(2,1)S(1)}, bf16[256,256]{1,0:T(8,128)(2,1)S(1)}, u32[]{:S(2)}, u32[]{:S(2)}) %collective-permute-start.7) | collective-permute-done | bytes 131104 | tf_op jit(solution)/shard_map/ppermute | solution.py:381
  36.7 0.1 shard_map.83.refs_4_
  36.8 0.0 collective-permute-done.8.refs_1_
  36.8 2.1 %collective-permute-start.14 = (bf16[128,1024]{1,0:T(8,128)(2,1)S(1)}, bf16[128,1024]{1,0:T(8,128)(2,1)S(1)}, u32[]{:S(2)}, u32[]{:S(2)}) collective-permute-start(bf16[128,1024]{1,0:T(8,128)(2,1)S(1)} %get-tuple-element.61), channel_id=1, source_target_pairs={{0,1},{1,0},{2,3},{3,2},{4,5},{5,4},{6,7},{7,6},{8,9},{9,8},{10,11... | collective-permute-start | bytes 786440 | tf_op jit(solution)/shard_map/ppermute | solution.py:390
  38.9 2.5 %collective-permute-start.13 = (bf16[256,256]{1,0:T(8,128)(2,1)S(1)}, bf16[256,256]{1,0:T(8,128)(2,1)S(1)}, u32[]{:S(2)}, u32[]{:S(2)}) collective-permute-start(bf16[256,256]{1,0:T(8,128)(2,1)S(1)} %shard_map.83.refs_4_), channel_id=1, source_target_pairs={{0,192},{1,49},{16,208},{17,33},{32,224},{33,17},{48,240},{49,1},{... | collective-permute-start | bytes 393224 | tf_op jit(solution)/shard_map/ppermute | solution.py:340
  41.4 0.1 collective-permute-start.12
  41.5 0.0 collective-permute-done.14.other
  41.5 0.6 collective-permute-start.11
  42.1 1.4 %shard_map.84 = bf16[128,2048]{1,0:T(8,128)(2,1)} custom-call(s32[2]{0:T(128)S(1)} %pad_add_fusion.here_ref, bf16[128,1024]{1,0:T(8,128)(2,1)S(1)} %get-tuple-element.60.mine, bf16[128,1024]{1,0:T(8,128)(2,1)S(1)} %collective-permute-done.14.other), custom_call_target="tpu_custom_call" | custom-call | bytes 1048576 | tf_op jit(solution)/shard_map/pallas_call | solution.py:250
  43.5 6.0 %collective-permute-done.13.refs_7_ = bf16[256,256]{1,0:T(8,128)(2,1)S(1)} collective-permute-done((bf16[256,256]{1,0:T(8,128)(2,1)S(1)}, bf16[256,256]{1,0:T(8,128)(2,1)S(1)}, u32[]{:S(2)}, u32[]{:S(2)}) %collective-permute-start.13) | collective-permute-done | bytes 131104 | tf_op jit(solution)/shard_map/ppermute | solution.py:340
  49.5 0.0 collective-permute-done.12.refs_6_
  49.5 1.6 %shard_map.86 = (bf16[512,256]{1,0:T(8,128)(2,1)S(1)}, bf16[512,256]{1,0:T(8,128)(2,1)S(1)}, bf16[512,256]{1,0:T(8,128)(2,1)S(1)}) custom-call(s32[3]{0:T(128)S(1)} %pad_add_fusion.1.places_ref, bf16[256,2048]{1,0:T(8,128)(2,1)S(1)} %shard_map.82.refs_0_, bf16[256,2048]{1,0:T(8,128)(2,1)S(1)} %collective-permute-done.8.refs_1_, ...), custom_call_target="tpu_custom_call" | custom-call | flops 805306368 | bytes 6291456 | tf_op jit(solution)/shard_map/pallas_call | solution.py:275
  51.1 2.7 %collective-permute-start.15 = (bf16[512,256]{1,0:T(8,128)(2,1)S(1)}, bf16[512,256]{1,0:T(8,128)(2,1)S(1)}, u32[]{:S(2)}, u32[]{:S(2)}) collective-permute-start(bf16[512,256]{1,0:T(8,128)(2,1)S(1)} %get-tuple-element.71), channel_id=1, source_target_pairs={{0,32},{1,129},{16,48},{17,145},{32,0},{33,161},{48,16},{49,177},{... | collective-permute-start | bytes 786440 | tf_op jit(solution)/shard_map/ppermute | solution.py:340
  53.8 0.4 collective-permute-start.16
  54.2 0.4 collective-permute-start.17
  54.6 1.1 %shard_map.85.refs_0_ = f32[512,256]{1,0:T(8,128)S(1)} custom-call(s32[3]{0:T(128)S(1)} %pad_add_fusion.1.places_ref, bf16[256,2048]{1,0:T(8,128)(2,1)S(1)} %shard_map.82.refs_0_, bf16[256,2048]{1,0:T(8,128)(2,1)S(1)} %collective-permute-done.8.refs_1_, bf16[256,2048]{1,0:T(8,128)(2,1)S(1)} %collective-permute-done.9.refs_2_, ...), custom_call_target="tpu_custom_call" | custom-call | flops 268435456 | bytes 2097152 | tf_op jit(solution)/shard_map/pallas_call | solution.py:275
  55.8 2.2 %collective-permute-done.15.refs_1_ = bf16[512,256]{1,0:T(8,128)(2,1)S(1)} collective-permute-done((bf16[512,256]{1,0:T(8,128)(2,1)S(1)}, bf16[512,256]{1,0:T(8,128)(2,1)S(1)}, u32[]{:S(2)}, u32[]{:S(2)}) %collective-permute-start.15) | collective-permute-done | bytes 262176 | tf_op jit(solution)/shard_map/ppermute | solution.py:340
  57.9 3.2 %collective-permute-done.16.refs_2_ = bf16[512,256]{1,0:T(8,128)(2,1)S(1)} collective-permute-done((bf16[512,256]{1,0:T(8,128)(2,1)S(1)}, bf16[512,256]{1,0:T(8,128)(2,1)S(1)}, u32[]{:S(2)}, u32[]{:S(2)}) %collective-permute-start.16) | collective-permute-done | bytes 262176 | tf_op jit(solution)/shard_map/ppermute | solution.py:340
  61.1 0.0 collective-permute-done.17.refs_3_
  61.1 0.1 shard_map.87
  61.3 21.2 %all_to_all.5.parts = bf16[16,32,256]{2,1,0:T(8,128)(2,1)S(1)} all-to-all(bf16[16,32,256]{2,1,0:T(8,128)(2,1)S(1)} %bitcast.26), channel_id=1, replica_groups=mesh['y'=4,'x'=4,'z_hi'=2,'z_lo'=4,'core'=2] {'z_hi','z_lo','core'}, dimensions={0} | all-to-all | bytes 524288 | tf_op jit(solution)/shard_map/all_to_all | solution.py:400
  82.5 0.7 shard_map.88
  (10 shorter events, 0.0 us)
Async XLA Ops:
  0.6 6.4 %copy-start = (bf16[1,128,8192]{2,1,0:T(8,128)(2,1)S(1)}, bf16[1,128,8192]{2,1,0:T(8,128)(2,1)}, u32[]{:S(2)}) copy-start(bf16[1,128,8192]{2,1,0:T(8,128)(2,1)} %param.10) | copy-start | bytes 6291460
  1.6 5.4 %collective-permute-start = (bf16[128,256]{1,0:T(8,128)(2,1)S(1)}, bf16[128,256]{1,0:T(8,128)(2,1)S(1)}, u32[]{:S(2)}, u32[]{:S(2)}) collective-permute-start(bf16[128,256]{1,0:T(8,128)(2,1)S(1)} %pad_maximum_fusion), channel_id=1, source_target_pairs={{0,1},{1,0},{2,3},{3,2},{4,5},{5,4},{6,7},{7,6},{8,9},{9,8},{10,11... | collective-permute-start | bytes 196616 | tf_op jit(solution)/shard_map/ppermute | solution.py:348
  7.1 7.6 %collective-permute-start.5 = (bf16[128,8192]{1,0:T(8,128)(2,1)S(1)}, bf16[128,8192]{1,0:T(8,128)(2,1)}, u32[]{:S(2)}, u32[]{:S(2)}) collective-permute-start(bf16[128,8192]{1,0:T(8,128)(2,1)S(1)} %bitcast.23), channel_id=1, source_target_pairs={{0,1},{1,0},{2,3},{3,2},{4,5},{5,4},{6,7},{7,6},{8,9},{9,8},{10,11... | collective-permute-start | bytes 6291464 | tf_op jit(solution)/shard_map/ppermute | solution.py:369
  7.2 9.3 %collective-permute-start.1 = (bf16[128,1024]{1,0:T(8,128)(2,1)}, bf16[128,1024]{1,0:T(8,128)(2,1)S(1)}, u32[]{:S(2)}, u32[]{:S(2)}) collective-permute-start(bf16[128,1024]{1,0:T(8,128)(2,1)} %get-tuple-element.41), channel_id=1, source_target_pairs={{0,1},{1,0},{2,3},{3,2},{4,5},{5,4},{6,7},{7,6},{8,9},{9,8},{10,11... | collective-permute-start | bytes 786440 | tf_op jit(solution)/shard_map/ppermute | solution.py:356
  7.7 8.8 %collective-permute-start.2 = (bf16[128,1024]{1,0:T(8,128)(2,1)}, bf16[128,1024]{1,0:T(8,128)(2,1)S(1)}, u32[]{:S(2)}, u32[]{:S(2)}) collective-permute-start(bf16[128,1024]{1,0:T(8,128)(2,1)} %get-tuple-element.42), channel_id=1, source_target_pairs={{0,1},{1,0},{2,3},{3,2},{4,5},{5,4},{6,7},{7,6},{8,9},{9,8},{10,11... | collective-permute-start | bytes 786440 | tf_op jit(solution)/shard_map/ppermute | solution.py:356
  7.8 13.4 %collective-permute-start.4 = (bf16[256,256]{1,0:T(8,128)(2,1)S(1)}, bf16[256,256]{1,0:T(8,128)(2,1)S(1)}, u32[]{:S(2)}, u32[]{:S(2)}) collective-permute-start(bf16[256,256]{1,0:T(8,128)(2,1)S(1)} %shard_map.77.chip_pair), channel_id=1, source_target_pairs={{0,4},{1,5},{2,6},{3,7},{8,12},{9,13},{10,14},{11,15},{16,20},{17,... | collective-permute-start | bytes 393224 | tf_op jit(solution)/shard_map/ppermute | solution.py:366
  10.9 10.3 %collective-permute-start.3 = (bf16[256,256]{1,0:T(8,128)(2,1)S(1)}, bf16[256,256]{1,0:T(8,128)(2,1)S(1)}, u32[]{:S(2)}, u32[]{:S(2)}) collective-permute-start(bf16[256,256]{1,0:T(8,128)(2,1)S(1)} %shard_map.77.chip_pair), channel_id=1, source_target_pairs={{0,2},{1,3},{2,4},{3,5},{4,6},{5,7},{8,10},{9,11},{10,12},{11,13},... | collective-permute-start | bytes 393224 | tf_op jit(solution)/shard_map/ppermute | solution.py:366
  14.6 5.8 %copy-start.1 = (s32[1,1024]{1,0:T(1,128)S(1)}, s32[1,1024]{1,0:T(1,128)}, u32[]{:S(2)}) copy-start(s32[1,1024]{1,0:T(1,128)} %docs) | copy-start | bytes 12292
  16.5 20.2 %collective-permute-start.8 = (bf16[256,2048]{1,0:T(8,128)(2,1)S(1)}, bf16[256,2048]{1,0:T(8,128)(2,1)S(1)}, u32[]{:S(2)}, u32[]{:S(2)}) collective-permute-start(bf16[256,2048]{1,0:T(8,128)(2,1)S(1)} %get-tuple-element.47), channel_id=1, source_target_pairs={{0,64},{1,17},{16,80},{17,1},{32,96},{33,49},{48,112},{49,33},{64,... | collective-permute-start | bytes 3145736 | tf_op jit(solution)/shard_map/ppermute | solution.py:340
  17.8 31.7 %collective-permute-start.9 = (bf16[256,2048]{1,0:T(8,128)(2,1)S(1)}, bf16[256,2048]{1,0:T(8,128)(2,1)S(1)}, u32[]{:S(2)}, u32[]{:S(2)}) collective-permute-start(bf16[256,2048]{1,0:T(8,128)(2,1)S(1)} %get-tuple-element.57), channel_id=1, source_target_pairs={{0,128},{1,33},{16,144},{17,49},{32,160},{33,1},{48,176},{49,17},{... | collective-permute-start | bytes 3145736 | tf_op jit(solution)/shard_map/ppermute | solution.py:340
  20.3 29.2 %collective-permute-start.10 = (bf16[256,2048]{1,0:T(8,128)(2,1)S(1)}, bf16[256,2048]{1,0:T(8,128)(2,1)S(1)}, u32[]{:S(2)}, u32[]{:S(2)}) collective-permute-start(bf16[256,2048]{1,0:T(8,128)(2,1)S(1)} %get-tuple-element.58), channel_id=1, source_target_pairs={{0,192},{1,49},{16,208},{17,33},{32,224},{33,17},{48,240},{49,1},{... | collective-permute-start | bytes 3145736 | tf_op jit(solution)/shard_map/ppermute | solution.py:340
  26.6 10.1 %collective-permute-start.7 = (bf16[256,256]{1,0:T(8,128)(2,1)S(1)}, bf16[256,256]{1,0:T(8,128)(2,1)S(1)}, u32[]{:S(2)}, u32[]{:S(2)}) collective-permute-start(bf16[256,256]{1,0:T(8,128)(2,1)S(1)} %get-tuple-element.53), channel_id=1, source_target_pairs={{4,0},{5,1},{6,2},{7,3},{12,8},{13,9},{14,10},{15,11},{20,16},{21,... | collective-permute-start | bytes 393224 | tf_op jit(solution)/shard_map/ppermute | solution.py:381
  27.9 8.8 %collective-permute-start.6 = (bf16[256,256]{1,0:T(8,128)(2,1)S(1)}, bf16[256,256]{1,0:T(8,128)(2,1)S(1)}, u32[]{:S(2)}, u32[]{:S(2)}) collective-permute-start(bf16[256,256]{1,0:T(8,128)(2,1)S(1)} %get-tuple-element.52), channel_id=1, source_target_pairs={{2,0},{3,1},{4,2},{5,3},{6,4},{7,5},{10,8},{11,9},{12,10},{13,11},... | collective-permute-start | bytes 393224 | tf_op jit(solution)/shard_map/ppermute | solution.py:381
  36.8 4.7 %collective-permute-start.14 = (bf16[128,1024]{1,0:T(8,128)(2,1)S(1)}, bf16[128,1024]{1,0:T(8,128)(2,1)S(1)}, u32[]{:S(2)}, u32[]{:S(2)}) collective-permute-start(bf16[128,1024]{1,0:T(8,128)(2,1)S(1)} %get-tuple-element.61), channel_id=1, source_target_pairs={{0,1},{1,0},{2,3},{3,2},{4,5},{5,4},{6,7},{7,6},{8,9},{9,8},{10,11... | collective-permute-start | bytes 786440 | tf_op jit(solution)/shard_map/ppermute | solution.py:390
  38.9 10.6 %collective-permute-start.13 = (bf16[256,256]{1,0:T(8,128)(2,1)S(1)}, bf16[256,256]{1,0:T(8,128)(2,1)S(1)}, u32[]{:S(2)}, u32[]{:S(2)}) collective-permute-start(bf16[256,256]{1,0:T(8,128)(2,1)S(1)} %shard_map.83.refs_4_), channel_id=1, source_target_pairs={{0,192},{1,49},{16,208},{17,33},{32,224},{33,17},{48,240},{49,1},{... | collective-permute-start | bytes 393224 | tf_op jit(solution)/shard_map/ppermute | solution.py:340
  41.4 8.1 %collective-permute-start.12 = (bf16[256,256]{1,0:T(8,128)(2,1)S(1)}, bf16[256,256]{1,0:T(8,128)(2,1)S(1)}, u32[]{:S(2)}, u32[]{:S(2)}) collective-permute-start(bf16[256,256]{1,0:T(8,128)(2,1)S(1)} %shard_map.83.refs_4_), channel_id=1, source_target_pairs={{0,128},{1,33},{16,144},{17,49},{32,160},{33,1},{48,176},{49,17},{... | collective-permute-start | bytes 393224 | tf_op jit(solution)/shard_map/ppermute | solution.py:340
  41.5 8.0 %collective-permute-start.11 = (bf16[256,256]{1,0:T(8,128)(2,1)S(1)}, bf16[256,256]{1,0:T(8,128)(2,1)S(1)}, u32[]{:S(2)}, u32[]{:S(2)}) collective-permute-start(bf16[256,256]{1,0:T(8,128)(2,1)S(1)} %shard_map.83.refs_4_), channel_id=1, source_target_pairs={{0,64},{1,17},{16,80},{17,1},{32,96},{33,49},{48,112},{49,33},{64,... | collective-permute-start | bytes 393224 | tf_op jit(solution)/shard_map/ppermute | solution.py:340
  51.1 6.8 %collective-permute-start.15 = (bf16[512,256]{1,0:T(8,128)(2,1)S(1)}, bf16[512,256]{1,0:T(8,128)(2,1)S(1)}, u32[]{:S(2)}, u32[]{:S(2)}) collective-permute-start(bf16[512,256]{1,0:T(8,128)(2,1)S(1)} %get-tuple-element.71), channel_id=1, source_target_pairs={{0,32},{1,129},{16,48},{17,145},{32,0},{33,161},{48,16},{49,177},{... | collective-permute-start | bytes 786440 | tf_op jit(solution)/shard_map/ppermute | solution.py:340
  53.8 7.3 %collective-permute-start.16 = (bf16[512,256]{1,0:T(8,128)(2,1)S(1)}, bf16[512,256]{1,0:T(8,128)(2,1)S(1)}, u32[]{:S(2)}, u32[]{:S(2)}) collective-permute-start(bf16[512,256]{1,0:T(8,128)(2,1)S(1)} %get-tuple-element.72), channel_id=1, source_target_pairs={{0,16},{1,65},{16,0},{17,81},{32,48},{33,97},{48,32},{49,113},{64,... | collective-permute-start | bytes 786440 | tf_op jit(solution)/shard_map/ppermute | solution.py:340
  54.2 6.9 %collective-permute-start.17 = (bf16[512,256]{1,0:T(8,128)(2,1)S(1)}, bf16[512,256]{1,0:T(8,128)(2,1)S(1)}, u32[]{:S(2)}, u32[]{:S(2)}) collective-permute-start(bf16[512,256]{1,0:T(8,128)(2,1)S(1)} %get-tuple-element.73), channel_id=1, source_target_pairs={{0,48},{1,193},{16,32},{17,209},{32,16},{33,225},{48,0},{49,241},{... | collective-permute-start | bytes 786440 | tf_op jit(solution)/shard_map/ppermute | solution.py:340

commit v16 on v15

--- a/solution.py
+++ b/solution.py
@@ -383,13 +383,14 @@
     )
 
     (own_piece,) = split_columns(places_ref, *own, n_side, (0,))
-    far_back, own_piece = lax.optimization_barrier((far_back, own_piece))
     grad = combine(own_grad, near_back, far_back)
     late, pieces[0], dq_other = lax.optimization_barrier((grad, pieces[0], dq_other))
     grads = [grad] + [cross(late if k == 1 else grad, k, True) for k in range(1, n_side)]
     dq_back = lax.ppermute(dq_other, "core", swap)
     query_grad = assemble(here_ref, dq_mine, dq_back)[None]
-    pieces, grads, query_grad = lax.optimization_barrier((pieces, grads, query_grad))
+    pieces, grads, query_grad, own_piece = lax.optimization_barrier(
+        (pieces, grads, query_grad, own_piece)
+    )
     pieces = [own_piece] + list(pieces)
     terms = project(places_ref, pieces, grads, (2, 1, 3), jnp.bfloat16)
     parts = [cross(term, k, False) for term, k in zip(terms, (2, 1, 3))]

time: 83.5 us -> 83.5 us (level)
  waiting for transfers between devices: 16.1 us -> 15 us
  starting transfers between devices: 26.1 us -> 27.1 us
    ppermute x9, waiting for transfers between devices: 11.4 us -> 8.01 us  [cross(): return lax.ppermute(part, ('y', 'x', 'core'), pairs)]
    ppermute x2, waiting for transfers between devices: 4.65 us -> 7.02 us  [per_device(): lax.ppermute(part, ('z_lo', 'core'), [(b, a) for a, b in behind(distance)])]
    ppermute x1, starting transfers between devices: 2.09 us -> 3.1 us  [per_device(): dq_back = lax.ppermute(dq_other, 'core', swap)]
  transfers between devices with their start and end apart: 18 -> 18, of which waited for: 4 -> 5; matrix products, arithmetic and copies ran while one was open for 3% -> 3% of each run, Pallas kernels for 16% -> 16%
where the time goes in v16:
time: 83.5 us; the launch traced here: 83.2 us
  starting transfers between devices  27.1 us (32%)
  blocking collectives  21.2 us (25%)
  Pallas kernels  15.8 us (19%)
  waiting for transfers between devices  15 us (18%)
  local copies, waits for them, and re-layouts  3.05 us (4%)
    all_to_all x1, blocking collectives, per_device(): lax.all_to_all(term.reshape(n_rest, term.shape[0] // n_rest, term.shape[1...  21.2 us
    ppermute x9, starting transfers between devices, cross(): return lax.ppermute(part, ('y', 'x', 'core'), pairs)  10.7 us
    ppermute x9, waiting for transfers between devices, cross(): return lax.ppermute(part, ('y', 'x', 'core'), pairs)  8.01 us
    ppermute x2, waiting for transfers between devices, per_device(): lax.ppermute(part, ('z_lo', 'core'), [(b, a) for a, b in behind(distance)])  7.02 us
    ppermute x2, starting transfers between devices, per_device(): lax.ppermute(chip_pair, ('z_lo', 'core'), behind(distance))  6.7 us
    pallas_call x1, Pallas kernels, attention(): pl.pallas_call(attention_kernel, out_shape=(whole((chip, 2 * DH)), whole(...  5.34 us
    pallas_call x2, Pallas kernels, split_columns(): pl.pallas_call(functools.partial(chunk_kernel, places=places), out_shape=...  3.53 us
    ppermute x1, starting transfers between devices, per_device(): lax.ppermute(jnp.concatenate([half_of(keys, 1 - core), half_of(values, 1...  3.33 us
  transfers between devices with their start and end apart: 18, of which 5 were waited for; matrix products, arithmetic and copies ran while one was open for 3% of the time, Pallas kernels for 16%

profile of v16, /device:TPU:1, one launch (start us, length us, event | category | flops | bytes accessed | tf_op | source)
XLA Modules:
  0.0 83.2 jit_solution(11985346739620037557)
XLA Ops:
  0.6 1.0 %dynamic-slice_bitcast_fusion.4 = (bf16[128,128]{1,0:T(8,128)(2,1)S(1)}, bf16[128,128]{1,0:T(8,128)(2,1)S(1)}, bf16[128,128]{1,0:T(8,128)(2,1)S(1)}, bf16[128,128]{1,0:T(8,128)(2,1)S(1)}) fusion(bf16[1,128,256]{2,1,0:T(8,128)(2,1)} %param.8, s32[]{:T(128)S(6)} %select_n.19, s32[]{:T(128)S(6)} %select_n.17, bf16[1,128,256]{2,1,0:T(8,128)(2,1)} %param.7), kind=kLoop, calls=%fused_computation.5 | loop fusion | bytes 262152 | tf_op jit(solution)/shard_map/dynamic_slice | solution.py:345
  1.6 3.3 %collective-permute-start = (bf16[128,256]{1,0:T(8,128)(2,1)S(1)}, bf16[128,256]{1,0:T(8,128)(2,1)S(1)}, u32[]{:S(2)}, u32[]{:S(2)}) collective-permute-start(bf16[128,256]{1,0:T(8,128)(2,1)S(1)} %pad_maximum_fusion), channel_id=1, source_target_pairs={{0,1},{1,0},{2,3},{3,2},{4,5},{5,4},{6,7},{7,6},{8,9},{9,8},{10,11... | collective-permute-start | bytes 196616 | tf_op jit(solution)/shard_map/ppermute | solution.py:348
  5.0 2.1 %dynamic-slice_bitcast_fusion = (bf16[128,1024]{1,0:T(8,128)(2,1)}, bf16[128,1024]{1,0:T(8,128)(2,1)S(1)}, bf16[128,1024]{1,0:T(8,128)(2,1)S(1)}, bf16[128,1024]{1,0:T(8,128)(2,1)}) fusion(bf16[1,128,2048]{2,1,0:T(8,128)(2,1)} %param.9, s32[]{:T(128)S(6)} %select_n.18, s32[]{:T(128)S(6)} %select_n.16, bf16[1,128,2048]{2,1,0:T(8,128)(2,1)} %param.6), kind=kLoop, calls=%fused_computation | loop fusion | bytes 2097160 | tf_op jit(solution)/shard_map/dynamic_slice | solution.py:345
  7.0 0.0 collective-permute-done.swapped
  7.1 0.1 collective-permute-start.5
  7.2 0.5 collective-permute-start.1
  7.7 0.1 collective-permute-start.2
  7.8 3.2 %collective-permute-start.4 = (bf16[256,256]{1,0:T(8,128)(2,1)S(1)}, bf16[256,256]{1,0:T(8,128)(2,1)S(1)}, u32[]{:S(2)}, u32[]{:S(2)}) collective-permute-start(bf16[256,256]{1,0:T(8,128)(2,1)S(1)} %shard_map.77.chip_pair), channel_id=1, source_target_pairs={{0,4},{1,5},{2,6},{3,7},{8,12},{9,13},{10,14},{11,15},{16,20},{17,... | collective-permute-start | bytes 393224 | tf_op jit(solution)/shard_map/ppermute | solution.py:366
  10.9 3.5 %collective-permute-start.3 = (bf16[256,256]{1,0:T(8,128)(2,1)S(1)}, bf16[256,256]{1,0:T(8,128)(2,1)S(1)}, u32[]{:S(2)}, u32[]{:S(2)}) collective-permute-start(bf16[256,256]{1,0:T(8,128)(2,1)S(1)} %shard_map.77.chip_pair), channel_id=1, source_target_pairs={{0,2},{1,3},{2,4},{3,5},{4,6},{5,7},{8,10},{9,11},{10,12},{11,13},... | collective-permute-start | bytes 393224 | tf_op jit(solution)/shard_map/ppermute | solution.py:366
  14.5 0.1 pad_add_fusion.here_ref
  14.6 0.1 pad_add_fusion.1.places_ref
  14.6 0.0 collective-permute-done.5.other
  14.7 1.8 %shard_map.78 = (bf16[256,2048]{1,0:T(8,128)(2,1)S(1)}, bf16[256,2048]{1,0:T(8,128)(2,1)S(1)}, bf16[256,2048]{1,0:T(8,128)(2,1)S(1)}) custom-call(s32[3]{0:T(128)S(1)} %pad_add_fusion.1.places_ref, bf16[128,8192]{1,0:T(8,128)(2,1)S(1)} %bitcast.24, bf16[128,8192]{1,0:T(8,128)(2,1)} %collective-permute-done.5.other), custom_call_target="tpu_custom_call" | custom-call | bytes 6291456 | tf_op jit(solution)/shard_map/pallas_call | solution.py:72
  16.5 0.0 collective-permute-done.1.q_other
  16.5 0.0 collective-permute-done.2.do_other
  16.5 1.3 %collective-permute-start.8 = (bf16[256,2048]{1,0:T(8,128)(2,1)S(1)}, bf16[256,2048]{1,0:T(8,128)(2,1)S(1)}, u32[]{:S(2)}, u32[]{:S(2)}) collective-permute-start(bf16[256,2048]{1,0:T(8,128)(2,1)S(1)} %get-tuple-element.46), channel_id=1, source_target_pairs={{0,64},{1,17},{16,80},{17,1},{32,96},{33,49},{48,112},{49,33},{64,... | collective-permute-start | bytes 3145736 | tf_op jit(solution)/shard_map/ppermute | solution.py:340
  17.8 2.4 %collective-permute-start.9 = (bf16[256,2048]{1,0:T(8,128)(2,1)S(1)}, bf16[256,2048]{1,0:T(8,128)(2,1)S(1)}, u32[]{:S(2)}, u32[]{:S(2)}) collective-permute-start(bf16[256,2048]{1,0:T(8,128)(2,1)S(1)} %get-tuple-element.55), channel_id=1, source_target_pairs={{0,128},{1,33},{16,144},{17,49},{32,160},{33,1},{48,176},{49,17},{... | collective-permute-start | bytes 3145736 | tf_op jit(solution)/shard_map/ppermute | solution.py:340
  20.3 0.2 collective-permute-start.10
  20.5 0.7 shard_map.79.bias
  21.2 0.0 collective-permute-done.4.far_pair
  21.2 0.0 collective-permute-done.3.near_pair
  21.2 5.3 %shard_map.80 = (bf16[256,256]{1,0:T(8,128)(2,1)S(1)}, bf16[256,256]{1,0:T(8,128)(2,1)S(1)}, bf16[8,768,256]{2,1,0:T(8,128)(2,1)S(1)}, bf16[8,256,256]{2,1,0:T(8,128)(2,1)S(1)}) custom-call(bf16[128,1024]{1,0:T(8,128)(2,1)S(1)} %get-tuple-element.80.q_mine, bf16[128,1024]{1,0:T(8,128)(2,1)S(1)} %get-tuple-element.73.do_mine, ...), custom_call_target="tpu_custom_call" | custom-call | flops 30198988800 | bytes 4194304 | tf_op jit(solution)/shard_map/pallas_call | solution.py:167
  26.6 1.3 %collective-permute-start.6 = (bf16[256,256]{1,0:T(8,128)(2,1)S(1)}, bf16[256,256]{1,0:T(8,128)(2,1)S(1)}, u32[]{:S(2)}, u32[]{:S(2)}) collective-permute-start(bf16[256,256]{1,0:T(8,128)(2,1)S(1)} %get-tuple-element.51), channel_id=1, source_target_pairs={{2,0},{3,1},{4,2},{5,3},{6,4},{7,5},{10,8},{11,9},{12,10},{13,11},... | collective-permute-start | bytes 393224 | tf_op jit(solution)/shard_map/ppermute | solution.py:381
  27.9 1.3 %collective-permute-start.7 = (bf16[256,256]{1,0:T(8,128)(2,1)S(1)}, bf16[256,256]{1,0:T(8,128)(2,1)S(1)}, u32[]{:S(2)}, u32[]{:S(2)}) collective-permute-start(bf16[256,256]{1,0:T(8,128)(2,1)S(1)} %get-tuple-element.52), channel_id=1, source_target_pairs={{4,0},{5,1},{6,2},{7,3},{12,8},{13,9},{14,10},{15,11},{20,16},{21,... | collective-permute-start | bytes 393224 | tf_op jit(solution)/shard_map/ppermute | solution.py:381
  29.2 1.1 %shard_map.81 = (bf16[128,1024]{1,0:T(8,128)(2,1)S(1)}, bf16[128,1024]{1,0:T(8,128)(2,1)S(1)}, f32[256,256]{1,0:T(8,128)S(1)}) custom-call(bf16[128,1024]{1,0:T(8,128)(2,1)S(1)} %get-tuple-element.80.q_mine, bf16[128,1024]{1,0:T(8,128)(2,1)S(1)} %get-tuple-element.73.do_mine, bf16[128,1024]{1,0:T(8,128)(2,1)S(1)} %collective-permute-done.1.q_other, ...), custom_call_target="tpu_custom_call" | custom-call | flops 1207959552 | bytes 6291456 | tf_op jit(solution)/shard_map/pallas_call | solution.py:214
  30.3 2.3 %collective-permute-done.6.near = bf16[256,256]{1,0:T(8,128)(2,1)S(1)} collective-permute-done((bf16[256,256]{1,0:T(8,128)(2,1)S(1)}, bf16[256,256]{1,0:T(8,128)(2,1)S(1)}, u32[]{:S(2)}, u32[]{:S(2)}) %collective-permute-start.6) | collective-permute-done | bytes 131104 | tf_op jit(solution)/shard_map/ppermute | solution.py:381
  32.6 4.8 %collective-permute-done.7.far = bf16[256,256]{1,0:T(8,128)(2,1)S(1)} collective-permute-done((bf16[256,256]{1,0:T(8,128)(2,1)S(1)}, bf16[256,256]{1,0:T(8,128)(2,1)S(1)}, u32[]{:S(2)}, u32[]{:S(2)}) %collective-permute-start.7) | collective-permute-done | bytes 131104 | tf_op jit(solution)/shard_map/ppermute | solution.py:381
  37.3 0.1 shard_map.82.refs_4_
  37.5 3.1 %collective-permute-start.14 = (bf16[128,1024]{1,0:T(8,128)(2,1)S(1)}, bf16[128,1024]{1,0:T(8,128)(2,1)S(1)}, u32[]{:S(2)}, u32[]{:S(2)}) collective-permute-start(bf16[128,1024]{1,0:T(8,128)(2,1)S(1)} %get-tuple-element.59), channel_id=1, source_target_pairs={{0,1},{1,0},{2,3},{3,2},{4,5},{5,4},{6,7},{7,6},{8,9},{9,8},{10,11... | collective-permute-start | bytes 786440 | tf_op jit(solution)/shard_map/ppermute | solution.py:389
  40.6 2.5 %collective-permute-start.13 = (bf16[256,256]{1,0:T(8,128)(2,1)S(1)}, bf16[256,256]{1,0:T(8,128)(2,1)S(1)}, u32[]{:S(2)}, u32[]{:S(2)}) collective-permute-start(bf16[256,256]{1,0:T(8,128)(2,1)S(1)} %shard_map.82.refs_4_), channel_id=1, source_target_pairs={{0,192},{1,49},{16,208},{17,33},{32,224},{33,17},{48,240},{49,1},{... | collective-permute-start | bytes 393224 | tf_op jit(solution)/shard_map/ppermute | solution.py:340
  43.0 0.4 collective-permute-start.12
  43.4 0.0 collective-permute-done.14.other
  43.4 0.4 collective-permute-start.11
  43.8 1.7 %shard_map.84.refs_0_ = bf16[256,2048]{1,0:T(8,128)(2,1)S(1)} custom-call(s32[3]{0:T(128)S(1)} %pad_add_fusion.1.places_ref, bf16[128,8192]{1,0:T(8,128)(2,1)S(1)} %bitcast.25, bf16[128,8192]{1,0:T(8,128)(2,1)} %collective-permute-done.5.other), custom_call_target="tpu_custom_call" | custom-call | bytes 6291456 | tf_op jit(solution)/shard_map/pallas_call | solution.py:72
  45.5 1.4 %shard_map.83 = bf16[128,2048]{1,0:T(8,128)(2,1)} custom-call(s32[2]{0:T(128)S(1)} %pad_add_fusion.here_ref, bf16[128,1024]{1,0:T(8,128)(2,1)S(1)} %get-tuple-element.58.mine, bf16[128,1024]{1,0:T(8,128)(2,1)S(1)} %collective-permute-done.14.other), custom_call_target="tpu_custom_call" | custom-call | bytes 1048576 | tf_op jit(solution)/shard_map/pallas_call | solution.py:250
  46.9 2.6 %collective-permute-done.13.refs_7_ = bf16[256,256]{1,0:T(8,128)(2,1)S(1)} collective-permute-done((bf16[256,256]{1,0:T(8,128)(2,1)S(1)}, bf16[256,256]{1,0:T(8,128)(2,1)S(1)}, u32[]{:S(2)}, u32[]{:S(2)}) %collective-permute-start.13) | collective-permute-done | bytes 131104 | tf_op jit(solution)/shard_map/ppermute | solution.py:340
  49.5 0.0 collective-permute-done.12.refs_6_
  49.5 1.6 %shard_map.86 = (bf16[512,256]{1,0:T(8,128)(2,1)S(1)}, bf16[512,256]{1,0:T(8,128)(2,1)S(1)}, bf16[512,256]{1,0:T(8,128)(2,1)S(1)}) custom-call(s32[3]{0:T(128)S(1)} %pad_add_fusion.1.places_ref, bf16[256,2048]{1,0:T(8,128)(2,1)S(1)} %shard_map.84.refs_0_, bf16[256,2048]{1,0:T(8,128)(2,1)S(1)} %collective-permute-done.8.refs_1_, ...), custom_call_target="tpu_custom_call" | custom-call | flops 805306368 | bytes 6291456 | tf_op jit(solution)/shard_map/pallas_call | solution.py:275
  51.1 2.7 %collective-permute-start.15 = (bf16[512,256]{1,0:T(8,128)(2,1)S(1)}, bf16[512,256]{1,0:T(8,128)(2,1)S(1)}, u32[]{:S(2)}, u32[]{:S(2)}) collective-permute-start(bf16[512,256]{1,0:T(8,128)(2,1)S(1)} %get-tuple-element.69), channel_id=1, source_target_pairs={{0,32},{1,129},{16,48},{17,145},{32,0},{33,161},{48,16},{49,177},{... | collective-permute-start | bytes 786440 | tf_op jit(solution)/shard_map/ppermute | solution.py:340
  53.8 0.4 collective-permute-start.16
  54.2 0.4 collective-permute-start.17
  54.6 1.1 %shard_map.85.refs_0_ = f32[512,256]{1,0:T(8,128)S(1)} custom-call(s32[3]{0:T(128)S(1)} %pad_add_fusion.1.places_ref, bf16[256,2048]{1,0:T(8,128)(2,1)S(1)} %shard_map.84.refs_0_, bf16[256,2048]{1,0:T(8,128)(2,1)S(1)} %collective-permute-done.8.refs_1_, bf16[256,2048]{1,0:T(8,128)(2,1)S(1)} %collective-permute-done.9.refs_2_, ...), custom_call_target="tpu_custom_call" | custom-call | flops 268435456 | bytes 2097152 | tf_op jit(solution)/shard_map/pallas_call | solution.py:275
  55.7 2.2 %collective-permute-done.15.refs_1_ = bf16[512,256]{1,0:T(8,128)(2,1)S(1)} collective-permute-done((bf16[512,256]{1,0:T(8,128)(2,1)S(1)}, bf16[512,256]{1,0:T(8,128)(2,1)S(1)}, u32[]{:S(2)}, u32[]{:S(2)}) %collective-permute-start.15) | collective-permute-done | bytes 262176 | tf_op jit(solution)/shard_map/ppermute | solution.py:340
  58.0 3.2 %collective-permute-done.16.refs_2_ = bf16[512,256]{1,0:T(8,128)(2,1)S(1)} collective-permute-done((bf16[512,256]{1,0:T(8,128)(2,1)S(1)}, bf16[512,256]{1,0:T(8,128)(2,1)S(1)}, u32[]{:S(2)}, u32[]{:S(2)}) %collective-permute-start.16) | collective-permute-done | bytes 262176 | tf_op jit(solution)/shard_map/ppermute | solution.py:340
  61.1 0.0 collective-permute-done.17.refs_3_
  61.1 0.1 shard_map.87
  61.3 21.2 %all_to_all.5.parts = bf16[16,32,256]{2,1,0:T(8,128)(2,1)S(1)} all-to-all(bf16[16,32,256]{2,1,0:T(8,128)(2,1)S(1)} %bitcast.26), channel_id=1, replica_groups=mesh['y'=4,'x'=4,'z_hi'=2,'z_lo'=4,'core'=2] {'z_hi','z_lo','core'}, dimensions={0} | all-to-all | bytes 524288 | tf_op jit(solution)/shard_map/all_to_all | solution.py:401
  82.5 0.7 shard_map.88
  (10 shorter events, 0.0 us)
Async XLA Ops:
  0.6 6.4 %copy-start = (bf16[1,128,8192]{2,1,0:T(8,128)(2,1)S(1)}, bf16[1,128,8192]{2,1,0:T(8,128)(2,1)}, u32[]{:S(2)}) copy-start(bf16[1,128,8192]{2,1,0:T(8,128)(2,1)} %param.10) | copy-start | bytes 6291460
  1.6 5.4 %collective-permute-start = (bf16[128,256]{1,0:T(8,128)(2,1)S(1)}, bf16[128,256]{1,0:T(8,128)(2,1)S(1)}, u32[]{:S(2)}, u32[]{:S(2)}) collective-permute-start(bf16[128,256]{1,0:T(8,128)(2,1)S(1)} %pad_maximum_fusion), channel_id=1, source_target_pairs={{0,1},{1,0},{2,3},{3,2},{4,5},{5,4},{6,7},{7,6},{8,9},{9,8},{10,11... | collective-permute-start | bytes 196616 | tf_op jit(solution)/shard_map/ppermute | solution.py:348
  7.1 7.6 %collective-permute-start.5 = (bf16[128,8192]{1,0:T(8,128)(2,1)S(1)}, bf16[128,8192]{1,0:T(8,128)(2,1)}, u32[]{:S(2)}, u32[]{:S(2)}) collective-permute-start(bf16[128,8192]{1,0:T(8,128)(2,1)S(1)} %bitcast.23), channel_id=1, source_target_pairs={{0,1},{1,0},{2,3},{3,2},{4,5},{5,4},{6,7},{7,6},{8,9},{9,8},{10,11... | collective-permute-start | bytes 6291464 | tf_op jit(solution)/shard_map/ppermute | solution.py:369
  7.2 9.3 %collective-permute-start.1 = (bf16[128,1024]{1,0:T(8,128)(2,1)}, bf16[128,1024]{1,0:T(8,128)(2,1)S(1)}, u32[]{:S(2)}, u32[]{:S(2)}) collective-permute-start(bf16[128,1024]{1,0:T(8,128)(2,1)} %get-tuple-element.40), channel_id=1, source_target_pairs={{0,1},{1,0},{2,3},{3,2},{4,5},{5,4},{6,7},{7,6},{8,9},{9,8},{10,11... | collective-permute-start | bytes 786440 | tf_op jit(solution)/shard_map/ppermute | solution.py:356
  7.7 8.8 %collective-permute-start.2 = (bf16[128,1024]{1,0:T(8,128)(2,1)}, bf16[128,1024]{1,0:T(8,128)(2,1)S(1)}, u32[]{:S(2)}, u32[]{:S(2)}) collective-permute-start(bf16[128,1024]{1,0:T(8,128)(2,1)} %get-tuple-element.41), channel_id=1, source_target_pairs={{0,1},{1,0},{2,3},{3,2},{4,5},{5,4},{6,7},{7,6},{8,9},{9,8},{10,11... | collective-permute-start | bytes 786440 | tf_op jit(solution)/shard_map/ppermute | solution.py:356
  7.8 13.4 %collective-permute-start.4 = (bf16[256,256]{1,0:T(8,128)(2,1)S(1)}, bf16[256,256]{1,0:T(8,128)(2,1)S(1)}, u32[]{:S(2)}, u32[]{:S(2)}) collective-permute-start(bf16[256,256]{1,0:T(8,128)(2,1)S(1)} %shard_map.77.chip_pair), channel_id=1, source_target_pairs={{0,4},{1,5},{2,6},{3,7},{8,12},{9,13},{10,14},{11,15},{16,20},{17,... | collective-permute-start | bytes 393224 | tf_op jit(solution)/shard_map/ppermute | solution.py:366
  10.9 10.3 %collective-permute-start.3 = (bf16[256,256]{1,0:T(8,128)(2,1)S(1)}, bf16[256,256]{1,0:T(8,128)(2,1)S(1)}, u32[]{:S(2)}, u32[]{:S(2)}) collective-permute-start(bf16[256,256]{1,0:T(8,128)(2,1)S(1)} %shard_map.77.chip_pair), channel_id=1, source_target_pairs={{0,2},{1,3},{2,4},{3,5},{4,6},{5,7},{8,10},{9,11},{10,12},{11,13},... | collective-permute-start | bytes 393224 | tf_op jit(solution)/shard_map/ppermute | solution.py:366
  14.6 5.8 %copy-start.1 = (s32[1,1024]{1,0:T(1,128)S(1)}, s32[1,1024]{1,0:T(1,128)}, u32[]{:S(2)}) copy-start(s32[1,1024]{1,0:T(1,128)} %docs) | copy-start | bytes 12292
  16.5 20.9 %collective-permute-start.8 = (bf16[256,2048]{1,0:T(8,128)(2,1)S(1)}, bf16[256,2048]{1,0:T(8,128)(2,1)S(1)}, u32[]{:S(2)}, u32[]{:S(2)}) collective-permute-start(bf16[256,2048]{1,0:T(8,128)(2,1)S(1)} %get-tuple-element.46), channel_id=1, source_target_pairs={{0,64},{1,17},{16,80},{17,1},{32,96},{33,49},{48,112},{49,33},{64,... | collective-permute-start | bytes 3145736 | tf_op jit(solution)/shard_map/ppermute | solution.py:340
  17.8 31.7 %collective-permute-start.9 = (bf16[256,2048]{1,0:T(8,128)(2,1)S(1)}, bf16[256,2048]{1,0:T(8,128)(2,1)S(1)}, u32[]{:S(2)}, u32[]{:S(2)}) collective-permute-start(bf16[256,2048]{1,0:T(8,128)(2,1)S(1)} %get-tuple-element.55), channel_id=1, source_target_pairs={{0,128},{1,33},{16,144},{17,49},{32,160},{33,1},{48,176},{49,17},{... | collective-permute-start | bytes 3145736 | tf_op jit(solution)/shard_map/ppermute | solution.py:340
  20.3 29.2 %collective-permute-start.10 = (bf16[256,2048]{1,0:T(8,128)(2,1)S(1)}, bf16[256,2048]{1,0:T(8,128)(2,1)S(1)}, u32[]{:S(2)}, u32[]{:S(2)}) collective-permute-start(bf16[256,2048]{1,0:T(8,128)(2,1)S(1)} %get-tuple-element.56), channel_id=1, source_target_pairs={{0,192},{1,49},{16,208},{17,33},{32,224},{33,17},{48,240},{49,1},{... | collective-permute-start | bytes 3145736 | tf_op jit(solution)/shard_map/ppermute | solution.py:340
  26.6 6.0 %collective-permute-start.6 = (bf16[256,256]{1,0:T(8,128)(2,1)S(1)}, bf16[256,256]{1,0:T(8,128)(2,1)S(1)}, u32[]{:S(2)}, u32[]{:S(2)}) collective-permute-start(bf16[256,256]{1,0:T(8,128)(2,1)S(1)} %get-tuple-element.51), channel_id=1, source_target_pairs={{2,0},{3,1},{4,2},{5,3},{6,4},{7,5},{10,8},{11,9},{12,10},{13,11},... | collective-permute-start | bytes 393224 | tf_op jit(solution)/shard_map/ppermute | solution.py:381
  27.9 9.5 %collective-permute-start.7 = (bf16[256,256]{1,0:T(8,128)(2,1)S(1)}, bf16[256,256]{1,0:T(8,128)(2,1)S(1)}, u32[]{:S(2)}, u32[]{:S(2)}) collective-permute-start(bf16[256,256]{1,0:T(8,128)(2,1)S(1)} %get-tuple-element.52), channel_id=1, source_target_pairs={{4,0},{5,1},{6,2},{7,3},{12,8},{13,9},{14,10},{15,11},{20,16},{21,... | collective-permute-start | bytes 393224 | tf_op jit(solution)/shard_map/ppermute | solution.py:381
  37.5 6.0 %collective-permute-start.14 = (bf16[128,1024]{1,0:T(8,128)(2,1)S(1)}, bf16[128,1024]{1,0:T(8,128)(2,1)S(1)}, u32[]{:S(2)}, u32[]{:S(2)}) collective-permute-start(bf16[128,1024]{1,0:T(8,128)(2,1)S(1)} %get-tuple-element.59), channel_id=1, source_target_pairs={{0,1},{1,0},{2,3},{3,2},{4,5},{5,4},{6,7},{7,6},{8,9},{9,8},{10,11... | collective-permute-start | bytes 786440 | tf_op jit(solution)/shard_map/ppermute | solution.py:389
  40.6 8.9 %collective-permute-start.13 = (bf16[256,256]{1,0:T(8,128)(2,1)S(1)}, bf16[256,256]{1,0:T(8,128)(2,1)S(1)}, u32[]{:S(2)}, u32[]{:S(2)}) collective-permute-start(bf16[256,256]{1,0:T(8,128)(2,1)S(1)} %shard_map.82.refs_4_), channel_id=1, source_target_pairs={{0,192},{1,49},{16,208},{17,33},{32,224},{33,17},{48,240},{49,1},{... | collective-permute-start | bytes 393224 | tf_op jit(solution)/shard_map/ppermute | solution.py:340
  43.0 6.4 %collective-permute-start.12 = (bf16[256,256]{1,0:T(8,128)(2,1)S(1)}, bf16[256,256]{1,0:T(8,128)(2,1)S(1)}, u32[]{:S(2)}, u32[]{:S(2)}) collective-permute-start(bf16[256,256]{1,0:T(8,128)(2,1)S(1)} %shard_map.82.refs_4_), channel_id=1, source_target_pairs={{0,128},{1,33},{16,144},{17,49},{32,160},{33,1},{48,176},{49,17},{... | collective-permute-start | bytes 393224 | tf_op jit(solution)/shard_map/ppermute | solution.py:340
  43.4 6.0 %collective-permute-start.11 = (bf16[256,256]{1,0:T(8,128)(2,1)S(1)}, bf16[256,256]{1,0:T(8,128)(2,1)S(1)}, u32[]{:S(2)}, u32[]{:S(2)}) collective-permute-start(bf16[256,256]{1,0:T(8,128)(2,1)S(1)} %shard_map.82.refs_4_), channel_id=1, source_target_pairs={{0,64},{1,17},{16,80},{17,1},{32,96},{33,49},{48,112},{49,33},{64,... | collective-permute-start | bytes 393224 | tf_op jit(solution)/shard_map/ppermute | solution.py:340
  51.1 6.8 %collective-permute-start.15 = (bf16[512,256]{1,0:T(8,128)(2,1)S(1)}, bf16[512,256]{1,0:T(8,128)(2,1)S(1)}, u32[]{:S(2)}, u32[]{:S(2)}) collective-permute-start(bf16[512,256]{1,0:T(8,128)(2,1)S(1)} %get-tuple-element.69), channel_id=1, source_target_pairs={{0,32},{1,129},{16,48},{17,145},{32,0},{33,161},{48,16},{49,177},{... | collective-permute-start | bytes 786440 | tf_op jit(solution)/shard_map/ppermute | solution.py:340
  53.8 7.3 %collective-permute-start.16 = (bf16[512,256]{1,0:T(8,128)(2,1)S(1)}, bf16[512,256]{1,0:T(8,128)(2,1)S(1)}, u32[]{:S(2)}, u32[]{:S(2)}) collective-permute-start(bf16[512,256]{1,0:T(8,128)(2,1)S(1)} %get-tuple-element.70), channel_id=1, source_target_pairs={{0,16},{1,65},{16,0},{17,81},{32,48},{33,97},{48,32},{49,113},{64,... | collective-permute-start | bytes 786440 | tf_op jit(solution)/shard_map/ppermute | solution.py:340
  54.2 6.9 %collective-permute-start.17 = (bf16[512,256]{1,0:T(8,128)(2,1)S(1)}, bf16[512,256]{1,0:T(8,128)(2,1)S(1)}, u32[]{:S(2)}, u32[]{:S(2)}) collective-permute-start(bf16[512,256]{1,0:T(8,128)(2,1)S(1)} %get-tuple-element.71), channel_id=1, source_target_pairs={{0,48},{1,193},{16,32},{17,209},{32,16},{33,225},{48,0},{49,241},{... | collective-permute-start | bytes 786440 | tf_op jit(solution)/shard_map/ppermute | solution.py:340

commit v17 on v16

--- a/solution.py
+++ b/solution.py
@@ -225,18 +225,18 @@
     )(*operands, score_grads, probs)
 
 
-def combine_kernel(own, near, far, out):
+def combine_kernel(own, far, near, out):
     total = own[...] + near[...].astype(jnp.float32) + far[...].astype(jnp.float32)
     out[...] = total.T.astype(jnp.bfloat16)
 
 
-def combine(own, near, far):
+def combine(own, far, near):
     return pl.pallas_call(
         combine_kernel,
         out_shape=whole((own.shape[1], own.shape[0])),
         compiler_params=SMALL,
         cost_estimate=pl.CostEstimate(flops=0, bytes_accessed=MIB, transcendentals=0),
-    )(own, near, far)
+    )(own, far, near)
 
 
 def assemble_kernel(here_ref, mine, other, out):
@@ -377,13 +377,13 @@
         operands, make_bias(here_ref, docs, rows)
     )
     dq_mine, dq_other, own_grad = own_gradients(operands, score_grads, probs)
-    far_back, near_back = (
+    near_back, far_back = (
         lax.ppermute(part, ("z_lo", "core"), [(b, a) for a, b in behind(distance)])
-        for distance, part in ((2, far_grad), (1, near_grad))
+        for distance, part in ((1, near_grad), (2, far_grad))
     )
 
     (own_piece,) = split_columns(places_ref, *own, n_side, (0,))
-    grad = combine(own_grad, near_back, far_back)
+    grad = combine(own_grad, far_back, near_back)
     late, pieces[0], dq_other = lax.optimization_barrier((grad, pieces[0], dq_other))
     grads = [grad] + [cross(late if k == 1 else grad, k, True) for k in range(1, n_side)]
     dq_back = lax.ppermute(dq_other, "core", swap)

time: 83.5 us -> 83.5 us (level)
  waiting for transfers between devices: 15 us -> 16.1 us
  starting transfers between devices: 27.1 us -> 26.1 us
    ppermute x9, waiting for transfers between devices: 8.01 us -> 9.69 us  [cross(): return lax.ppermute(part, ('y', 'x', 'core'), pairs)]
    ppermute x1, starting transfers between devices: 3.1 us -> 2.09 us  [per_device(): dq_back = lax.ppermute(dq_other, 'core', swap)]
  transfers between devices with their start and end apart: 18 -> 18, of which waited for: 5 -> 4; matrix products, arithmetic and copies ran while one was open for 3% -> 3% of each run, Pallas kernels for 16% -> 16%
where the time goes in v17:
time: 83.5 us; the launch traced here: 83.2 us
  starting transfers between devices  26.1 us (31%)
  blocking collectives  21.2 us (25%)
  waiting for transfers between devices  16.1 us (19%)
  Pallas kernels  15.8 us (19%)
  local copies, waits for them, and re-layouts  3.05 us (4%)
    all_to_all x1, blocking collectives, per_device(): lax.all_to_all(term.reshape(n_rest, term.shape[0] // n_rest, term.shape[1...  21.2 us
    ppermute x9, starting transfers between devices, cross(): return lax.ppermute(part, ('y', 'x', 'core'), pairs)  10.7 us
    ppermute x9, waiting for transfers between devices, cross(): return lax.ppermute(part, ('y', 'x', 'core'), pairs)  9.69 us
    ppermute x2, starting transfers between devices, per_device(): lax.ppermute(chip_pair, ('z_lo', 'core'), behind(distance))  6.7 us
    ppermute x2, waiting for transfers between devices, per_device(): lax.ppermute(part, ('z_lo', 'core'), [(b, a) for a, b in behind(distance)])  6.34 us
    pallas_call x1, Pallas kernels, attention(): pl.pallas_call(attention_kernel, out_shape=(whole((chip, 2 * DH)), whole(...  5.34 us
    pallas_call x2, Pallas kernels, split_columns(): pl.pallas_call(functools.partial(chunk_kernel, places=places), out_shape=...  3.53 us
    ppermute x1, starting transfers between devices, per_device(): lax.ppermute(jnp.concatenate([half_of(keys, 1 - core), half_of(values, 1...  3.33 us
  transfers between devices with their start and end apart: 18, of which 4 were waited for; matrix products, arithmetic and copies ran while one was open for 3% of the time, Pallas kernels for 16%

profile of v17, /device:TPU:1, one launch (start us, length us, event | category | flops | bytes accessed | tf_op | source)
XLA Modules:
  0.0 83.2 jit_solution(11302677029674559455)
XLA Ops:
  0.6 1.0 %dynamic-slice_bitcast_fusion.4 = (bf16[128,128]{1,0:T(8,128)(2,1)S(1)}, bf16[128,128]{1,0:T(8,128)(2,1)S(1)}, bf16[128,128]{1,0:T(8,128)(2,1)S(1)}, bf16[128,128]{1,0:T(8,128)(2,1)S(1)}) fusion(bf16[1,128,256]{2,1,0:T(8,128)(2,1)} %param.8, s32[]{:T(128)S(6)} %select_n.19, s32[]{:T(128)S(6)} %select_n.17, bf16[1,128,256]{2,1,0:T(8,128)(2,1)} %param.7), kind=kLoop, calls=%fused_computation.5 | loop fusion | bytes 262152 | tf_op jit(solution)/shard_map/dynamic_slice | solution.py:345
  1.6 3.3 %collective-permute-start = (bf16[128,256]{1,0:T(8,128)(2,1)S(1)}, bf16[128,256]{1,0:T(8,128)(2,1)S(1)}, u32[]{:S(2)}, u32[]{:S(2)}) collective-permute-start(bf16[128,256]{1,0:T(8,128)(2,1)S(1)} %pad_maximum_fusion), channel_id=1, source_target_pairs={{0,1},{1,0},{2,3},{3,2},{4,5},{5,4},{6,7},{7,6},{8,9},{9,8},{10,11... | collective-permute-start | bytes 196616 | tf_op jit(solution)/shard_map/ppermute | solution.py:348
  5.0 2.1 %dynamic-slice_bitcast_fusion = (bf16[128,1024]{1,0:T(8,128)(2,1)}, bf16[128,1024]{1,0:T(8,128)(2,1)S(1)}, bf16[128,1024]{1,0:T(8,128)(2,1)S(1)}, bf16[128,1024]{1,0:T(8,128)(2,1)}) fusion(bf16[1,128,2048]{2,1,0:T(8,128)(2,1)} %param.9, s32[]{:T(128)S(6)} %select_n.18, s32[]{:T(128)S(6)} %select_n.16, bf16[1,128,2048]{2,1,0:T(8,128)(2,1)} %param.6), kind=kLoop, calls=%fused_computation | loop fusion | bytes 2097160 | tf_op jit(solution)/shard_map/dynamic_slice | solution.py:345
  7.0 0.0 collective-permute-done.swapped
  7.1 0.1 collective-permute-start.5
  7.2 0.5 collective-permute-start.1
  7.7 0.1 collective-permute-start.2
  7.8 3.2 %collective-permute-start.4 = (bf16[256,256]{1,0:T(8,128)(2,1)S(1)}, bf16[256,256]{1,0:T(8,128)(2,1)S(1)}, u32[]{:S(2)}, u32[]{:S(2)}) collective-permute-start(bf16[256,256]{1,0:T(8,128)(2,1)S(1)} %shard_map.77.chip_pair), channel_id=1, source_target_pairs={{0,4},{1,5},{2,6},{3,7},{8,12},{9,13},{10,14},{11,15},{16,20},{17,... | collective-permute-start | bytes 393224 | tf_op jit(solution)/shard_map/ppermute | solution.py:366
  10.9 3.5 %collective-permute-start.3 = (bf16[256,256]{1,0:T(8,128)(2,1)S(1)}, bf16[256,256]{1,0:T(8,128)(2,1)S(1)}, u32[]{:S(2)}, u32[]{:S(2)}) collective-permute-start(bf16[256,256]{1,0:T(8,128)(2,1)S(1)} %shard_map.77.chip_pair), channel_id=1, source_target_pairs={{0,2},{1,3},{2,4},{3,5},{4,6},{5,7},{8,10},{9,11},{10,12},{11,13},... | collective-permute-start | bytes 393224 | tf_op jit(solution)/shard_map/ppermute | solution.py:366
  14.5 0.1 pad_add_fusion.here_ref
  14.6 0.1 pad_add_fusion.1.places_ref
  14.6 0.0 collective-permute-done.5.other
  14.7 1.8 %shard_map.78 = (bf16[256,2048]{1,0:T(8,128)(2,1)S(1)}, bf16[256,2048]{1,0:T(8,128)(2,1)S(1)}, bf16[256,2048]{1,0:T(8,128)(2,1)S(1)}) custom-call(s32[3]{0:T(128)S(1)} %pad_add_fusion.1.places_ref, bf16[128,8192]{1,0:T(8,128)(2,1)S(1)} %bitcast.24, bf16[128,8192]{1,0:T(8,128)(2,1)} %collective-permute-done.5.other), custom_call_target="tpu_custom_call" | custom-call | bytes 6291456 | tf_op jit(solution)/shard_map/pallas_call | solution.py:72
  16.5 0.0 collective-permute-done.1.q_other
  16.5 0.0 collective-permute-done.2.do_other
  16.5 1.3 %collective-permute-start.8 = (bf16[256,2048]{1,0:T(8,128)(2,1)S(1)}, bf16[256,2048]{1,0:T(8,128)(2,1)S(1)}, u32[]{:S(2)}, u32[]{:S(2)}) collective-permute-start(bf16[256,2048]{1,0:T(8,128)(2,1)S(1)} %get-tuple-element.46), channel_id=1, source_target_pairs={{0,64},{1,17},{16,80},{17,1},{32,96},{33,49},{48,112},{49,33},{64,... | collective-permute-start | bytes 3145736 | tf_op jit(solution)/shard_map/ppermute | solution.py:340
  17.8 2.4 %collective-permute-start.9 = (bf16[256,2048]{1,0:T(8,128)(2,1)S(1)}, bf16[256,2048]{1,0:T(8,128)(2,1)S(1)}, u32[]{:S(2)}, u32[]{:S(2)}) collective-permute-start(bf16[256,2048]{1,0:T(8,128)(2,1)S(1)} %get-tuple-element.55), channel_id=1, source_target_pairs={{0,128},{1,33},{16,144},{17,49},{32,160},{33,1},{48,176},{49,17},{... | collective-permute-start | bytes 3145736 | tf_op jit(solution)/shard_map/ppermute | solution.py:340
  20.3 0.2 collective-permute-start.10
  20.5 0.7 shard_map.79.bias
  21.2 0.0 collective-permute-done.4.far_pair
  21.2 0.0 collective-permute-done.3.near_pair
  21.2 5.3 %shard_map.80 = (bf16[256,256]{1,0:T(8,128)(2,1)S(1)}, bf16[256,256]{1,0:T(8,128)(2,1)S(1)}, bf16[8,768,256]{2,1,0:T(8,128)(2,1)S(1)}, bf16[8,256,256]{2,1,0:T(8,128)(2,1)S(1)}) custom-call(bf16[128,1024]{1,0:T(8,128)(2,1)S(1)} %get-tuple-element.80.q_mine, bf16[128,1024]{1,0:T(8,128)(2,1)S(1)} %get-tuple-element.73.do_mine, ...), custom_call_target="tpu_custom_call" | custom-call | flops 30198988800 | bytes 4194304 | tf_op jit(solution)/shard_map/pallas_call | solution.py:167
  26.6 1.3 %collective-permute-start.6 = (bf16[256,256]{1,0:T(8,128)(2,1)S(1)}, bf16[256,256]{1,0:T(8,128)(2,1)S(1)}, u32[]{:S(2)}, u32[]{:S(2)}) collective-permute-start(bf16[256,256]{1,0:T(8,128)(2,1)S(1)} %get-tuple-element.51), channel_id=1, source_target_pairs={{4,0},{5,1},{6,2},{7,3},{12,8},{13,9},{14,10},{15,11},{20,16},{21,... | collective-permute-start | bytes 393224 | tf_op jit(solution)/shard_map/ppermute | solution.py:381
  27.9 1.3 %collective-permute-start.7 = (bf16[256,256]{1,0:T(8,128)(2,1)S(1)}, bf16[256,256]{1,0:T(8,128)(2,1)S(1)}, u32[]{:S(2)}, u32[]{:S(2)}) collective-permute-start(bf16[256,256]{1,0:T(8,128)(2,1)S(1)} %get-tuple-element.52), channel_id=1, source_target_pairs={{2,0},{3,1},{4,2},{5,3},{6,4},{7,5},{10,8},{11,9},{12,10},{13,11},... | collective-permute-start | bytes 393224 | tf_op jit(solution)/shard_map/ppermute | solution.py:381
  29.2 1.1 %shard_map.81 = (bf16[128,1024]{1,0:T(8,128)(2,1)S(1)}, bf16[128,1024]{1,0:T(8,128)(2,1)S(1)}, f32[256,256]{1,0:T(8,128)S(1)}) custom-call(bf16[128,1024]{1,0:T(8,128)(2,1)S(1)} %get-tuple-element.80.q_mine, bf16[128,1024]{1,0:T(8,128)(2,1)S(1)} %get-tuple-element.73.do_mine, bf16[128,1024]{1,0:T(8,128)(2,1)S(1)} %collective-permute-done.1.q_other, ...), custom_call_target="tpu_custom_call" | custom-call | flops 1207959552 | bytes 6291456 | tf_op jit(solution)/shard_map/pallas_call | solution.py:214
  30.3 6.3 %collective-permute-done.6.far = bf16[256,256]{1,0:T(8,128)(2,1)S(1)} collective-permute-done((bf16[256,256]{1,0:T(8,128)(2,1)S(1)}, bf16[256,256]{1,0:T(8,128)(2,1)S(1)}, u32[]{:S(2)}, u32[]{:S(2)}) %collective-permute-start.6) | collective-permute-done | bytes 131104 | tf_op jit(solution)/shard_map/ppermute | solution.py:381
  36.7 0.1 shard_map.82.refs_4_
  36.8 0.0 collective-permute-done.8.refs_1_
  36.8 2.1 %collective-permute-start.14 = (bf16[128,1024]{1,0:T(8,128)(2,1)S(1)}, bf16[128,1024]{1,0:T(8,128)(2,1)S(1)}, u32[]{:S(2)}, u32[]{:S(2)}) collective-permute-start(bf16[128,1024]{1,0:T(8,128)(2,1)S(1)} %get-tuple-element.59), channel_id=1, source_target_pairs={{0,1},{1,0},{2,3},{3,2},{4,5},{5,4},{6,7},{7,6},{8,9},{9,8},{10,11... | collective-permute-start | bytes 786440 | tf_op jit(solution)/shard_map/ppermute | solution.py:389
  38.9 2.5 %collective-permute-start.13 = (bf16[256,256]{1,0:T(8,128)(2,1)S(1)}, bf16[256,256]{1,0:T(8,128)(2,1)S(1)}, u32[]{:S(2)}, u32[]{:S(2)}) collective-permute-start(bf16[256,256]{1,0:T(8,128)(2,1)S(1)} %shard_map.82.refs_4_), channel_id=1, source_target_pairs={{0,192},{1,49},{16,208},{17,33},{32,224},{33,17},{48,240},{49,1},{... | collective-permute-start | bytes 393224 | tf_op jit(solution)/shard_map/ppermute | solution.py:340
  41.4 0.1 collective-permute-start.12
  41.5 0.0 collective-permute-done.14.other
  41.5 0.6 collective-permute-start.11
  42.1 1.7 %shard_map.84.refs_0_ = bf16[256,2048]{1,0:T(8,128)(2,1)S(1)} custom-call(s32[3]{0:T(128)S(1)} %pad_add_fusion.1.places_ref, bf16[128,8192]{1,0:T(8,128)(2,1)S(1)} %bitcast.25, bf16[128,8192]{1,0:T(8,128)(2,1)} %collective-permute-done.5.other), custom_call_target="tpu_custom_call" | custom-call | bytes 6291456 | tf_op jit(solution)/shard_map/pallas_call | solution.py:72
  43.8 1.4 %shard_map.83 = bf16[128,2048]{1,0:T(8,128)(2,1)} custom-call(s32[2]{0:T(128)S(1)} %pad_add_fusion.here_ref, bf16[128,1024]{1,0:T(8,128)(2,1)S(1)} %get-tuple-element.58.mine, bf16[128,1024]{1,0:T(8,128)(2,1)S(1)} %collective-permute-done.14.other), custom_call_target="tpu_custom_call" | custom-call | bytes 1048576 | tf_op jit(solution)/shard_map/pallas_call | solution.py:250
  45.2 4.3 %collective-permute-done.13.refs_7_ = bf16[256,256]{1,0:T(8,128)(2,1)S(1)} collective-permute-done((bf16[256,256]{1,0:T(8,128)(2,1)S(1)}, bf16[256,256]{1,0:T(8,128)(2,1)S(1)}, u32[]{:S(2)}, u32[]{:S(2)}) %collective-permute-start.13) | collective-permute-done | bytes 131104 | tf_op jit(solution)/shard_map/ppermute | solution.py:340
  49.5 0.0 collective-permute-done.12.refs_6_
  49.5 1.6 %shard_map.86 = (bf16[512,256]{1,0:T(8,128)(2,1)S(1)}, bf16[512,256]{1,0:T(8,128)(2,1)S(1)}, bf16[512,256]{1,0:T(8,128)(2,1)S(1)}) custom-call(s32[3]{0:T(128)S(1)} %pad_add_fusion.1.places_ref, bf16[256,2048]{1,0:T(8,128)(2,1)S(1)} %shard_map.84.refs_0_, bf16[256,2048]{1,0:T(8,128)(2,1)S(1)} %collective-permute-done.8.refs_1_, ...), custom_call_target="tpu_custom_call" | custom-call | flops 805306368 | bytes 6291456 | tf_op jit(solution)/shard_map/pallas_call | solution.py:275
  51.1 2.7 %collective-permute-start.15 = (bf16[512,256]{1,0:T(8,128)(2,1)S(1)}, bf16[512,256]{1,0:T(8,128)(2,1)S(1)}, u32[]{:S(2)}, u32[]{:S(2)}) collective-permute-start(bf16[512,256]{1,0:T(8,128)(2,1)S(1)} %get-tuple-element.69), channel_id=1, source_target_pairs={{0,32},{1,129},{16,48},{17,145},{32,0},{33,161},{48,16},{49,177},{... | collective-permute-start | bytes 786440 | tf_op jit(solution)/shard_map/ppermute | solution.py:340
  53.8 0.4 collective-permute-start.16
  54.2 0.4 collective-permute-start.17
  54.6 1.1 %shard_map.85.refs_0_ = f32[512,256]{1,0:T(8,128)S(1)} custom-call(s32[3]{0:T(128)S(1)} %pad_add_fusion.1.places_ref, bf16[256,2048]{1,0:T(8,128)(2,1)S(1)} %shard_map.84.refs_0_, bf16[256,2048]{1,0:T(8,128)(2,1)S(1)} %collective-permute-done.8.refs_1_, bf16[256,2048]{1,0:T(8,128)(2,1)S(1)} %collective-permute-done.9.refs_2_, ...), custom_call_target="tpu_custom_call" | custom-call | flops 268435456 | bytes 2097152 | tf_op jit(solution)/shard_map/pallas_call | solution.py:275
  55.7 2.2 %collective-permute-done.15.refs_1_ = bf16[512,256]{1,0:T(8,128)(2,1)S(1)} collective-permute-done((bf16[512,256]{1,0:T(8,128)(2,1)S(1)}, bf16[512,256]{1,0:T(8,128)(2,1)S(1)}, u32[]{:S(2)}, u32[]{:S(2)}) %collective-permute-start.15) | collective-permute-done | bytes 262176 | tf_op jit(solution)/shard_map/ppermute | solution.py:340
  58.0 3.2 %collective-permute-done.16.refs_2_ = bf16[512,256]{1,0:T(8,128)(2,1)S(1)} collective-permute-done((bf16[512,256]{1,0:T(8,128)(2,1)S(1)}, bf16[512,256]{1,0:T(8,128)(2,1)S(1)}, u32[]{:S(2)}, u32[]{:S(2)}) %collective-permute-start.16) | collective-permute-done | bytes 262176 | tf_op jit(solution)/shard_map/ppermute | solution.py:340
  61.1 0.0 collective-permute-done.17.refs_3_
  61.1 0.1 shard_map.87
  61.3 21.2 %all_to_all.5.parts = bf16[16,32,256]{2,1,0:T(8,128)(2,1)S(1)} all-to-all(bf16[16,32,256]{2,1,0:T(8,128)(2,1)S(1)} %bitcast.26), channel_id=1, replica_groups=mesh['y'=4,'x'=4,'z_hi'=2,'z_lo'=4,'core'=2] {'z_hi','z_lo','core'}, dimensions={0} | all-to-all | bytes 524288 | tf_op jit(solution)/shard_map/all_to_all | solution.py:401
  82.5 0.7 shard_map.88
  (10 shorter events, 0.0 us)
Async XLA Ops:
  0.6 6.4 %copy-start = (bf16[1,128,8192]{2,1,0:T(8,128)(2,1)S(1)}, bf16[1,128,8192]{2,1,0:T(8,128)(2,1)}, u32[]{:S(2)}) copy-start(bf16[1,128,8192]{2,1,0:T(8,128)(2,1)} %param.10) | copy-start | bytes 6291460
  1.6 5.4 %collective-permute-start = (bf16[128,256]{1,0:T(8,128)(2,1)S(1)}, bf16[128,256]{1,0:T(8,128)(2,1)S(1)}, u32[]{:S(2)}, u32[]{:S(2)}) collective-permute-start(bf16[128,256]{1,0:T(8,128)(2,1)S(1)} %pad_maximum_fusion), channel_id=1, source_target_pairs={{0,1},{1,0},{2,3},{3,2},{4,5},{5,4},{6,7},{7,6},{8,9},{9,8},{10,11... | collective-permute-start | bytes 196616 | tf_op jit(solution)/shard_map/ppermute | solution.py:348
  7.1 7.6 %collective-permute-start.5 = (bf16[128,8192]{1,0:T(8,128)(2,1)S(1)}, bf16[128,8192]{1,0:T(8,128)(2,1)}, u32[]{:S(2)}, u32[]{:S(2)}) collective-permute-start(bf16[128,8192]{1,0:T(8,128)(2,1)S(1)} %bitcast.23), channel_id=1, source_target_pairs={{0,1},{1,0},{2,3},{3,2},{4,5},{5,4},{6,7},{7,6},{8,9},{9,8},{10,11... | collective-permute-start | bytes 6291464 | tf_op jit(solution)/shard_map/ppermute | solution.py:369
  7.2 9.3 %collective-permute-start.1 = (bf16[128,1024]{1,0:T(8,128)(2,1)}, bf16[128,1024]{1,0:T(8,128)(2,1)S(1)}, u32[]{:S(2)}, u32[]{:S(2)}) collective-permute-start(bf16[128,1024]{1,0:T(8,128)(2,1)} %get-tuple-element.40), channel_id=1, source_target_pairs={{0,1},{1,0},{2,3},{3,2},{4,5},{5,4},{6,7},{7,6},{8,9},{9,8},{10,11... | collective-permute-start | bytes 786440 | tf_op jit(solution)/shard_map/ppermute | solution.py:356
  7.7 8.8 %collective-permute-start.2 = (bf16[128,1024]{1,0:T(8,128)(2,1)}, bf16[128,1024]{1,0:T(8,128)(2,1)S(1)}, u32[]{:S(2)}, u32[]{:S(2)}) collective-permute-start(bf16[128,1024]{1,0:T(8,128)(2,1)} %get-tuple-element.41), channel_id=1, source_target_pairs={{0,1},{1,0},{2,3},{3,2},{4,5},{5,4},{6,7},{7,6},{8,9},{9,8},{10,11... | collective-permute-start | bytes 786440 | tf_op jit(solution)/shard_map/ppermute | solution.py:356
  7.8 13.4 %collective-permute-start.4 = (bf16[256,256]{1,0:T(8,128)(2,1)S(1)}, bf16[256,256]{1,0:T(8,128)(2,1)S(1)}, u32[]{:S(2)}, u32[]{:S(2)}) collective-permute-start(bf16[256,256]{1,0:T(8,128)(2,1)S(1)} %shard_map.77.chip_pair), channel_id=1, source_target_pairs={{0,4},{1,5},{2,6},{3,7},{8,12},{9,13},{10,14},{11,15},{16,20},{17,... | collective-permute-start | bytes 393224 | tf_op jit(solution)/shard_map/ppermute | solution.py:366
  10.9 10.3 %collective-permute-start.3 = (bf16[256,256]{1,0:T(8,128)(2,1)S(1)}, bf16[256,256]{1,0:T(8,128)(2,1)S(1)}, u32[]{:S(2)}, u32[]{:S(2)}) collective-permute-start(bf16[256,256]{1,0:T(8,128)(2,1)S(1)} %shard_map.77.chip_pair), channel_id=1, source_target_pairs={{0,2},{1,3},{2,4},{3,5},{4,6},{5,7},{8,10},{9,11},{10,12},{11,13},... | collective-permute-start | bytes 393224 | tf_op jit(solution)/shard_map/ppermute | solution.py:366
  14.6 5.8 %copy-start.1 = (s32[1,1024]{1,0:T(1,128)S(1)}, s32[1,1024]{1,0:T(1,128)}, u32[]{:S(2)}) copy-start(s32[1,1024]{1,0:T(1,128)} %docs) | copy-start | bytes 12292
  16.5 20.2 %collective-permute-start.8 = (bf16[256,2048]{1,0:T(8,128)(2,1)S(1)}, bf16[256,2048]{1,0:T(8,128)(2,1)S(1)}, u32[]{:S(2)}, u32[]{:S(2)}) collective-permute-start(bf16[256,2048]{1,0:T(8,128)(2,1)S(1)} %get-tuple-element.46), channel_id=1, source_target_pairs={{0,64},{1,17},{16,80},{17,1},{32,96},{33,49},{48,112},{49,33},{64,... | collective-permute-start | bytes 3145736 | tf_op jit(solution)/shard_map/ppermute | solution.py:340
  17.8 31.7 %collective-permute-start.9 = (bf16[256,2048]{1,0:T(8,128)(2,1)S(1)}, bf16[256,2048]{1,0:T(8,128)(2,1)S(1)}, u32[]{:S(2)}, u32[]{:S(2)}) collective-permute-start(bf16[256,2048]{1,0:T(8,128)(2,1)S(1)} %get-tuple-element.55), channel_id=1, source_target_pairs={{0,128},{1,33},{16,144},{17,49},{32,160},{33,1},{48,176},{49,17},{... | collective-permute-start | bytes 3145736 | tf_op jit(solution)/shard_map/ppermute | solution.py:340
  20.3 29.2 %collective-permute-start.10 = (bf16[256,2048]{1,0:T(8,128)(2,1)S(1)}, bf16[256,2048]{1,0:T(8,128)(2,1)S(1)}, u32[]{:S(2)}, u32[]{:S(2)}) collective-permute-start(bf16[256,2048]{1,0:T(8,128)(2,1)S(1)} %get-tuple-element.56), channel_id=1, source_target_pairs={{0,192},{1,49},{16,208},{17,33},{32,224},{33,17},{48,240},{49,1},{... | collective-permute-start | bytes 3145736 | tf_op jit(solution)/shard_map/ppermute | solution.py:340
  26.6 10.1 %collective-permute-start.6 = (bf16[256,256]{1,0:T(8,128)(2,1)S(1)}, bf16[256,256]{1,0:T(8,128)(2,1)S(1)}, u32[]{:S(2)}, u32[]{:S(2)}) collective-permute-start(bf16[256,256]{1,0:T(8,128)(2,1)S(1)} %get-tuple-element.51), channel_id=1, source_target_pairs={{4,0},{5,1},{6,2},{7,3},{12,8},{13,9},{14,10},{15,11},{20,16},{21,... | collective-permute-start | bytes 393224 | tf_op jit(solution)/shard_map/ppermute | solution.py:381
  27.9 8.8 %collective-permute-start.7 = (bf16[256,256]{1,0:T(8,128)(2,1)S(1)}, bf16[256,256]{1,0:T(8,128)(2,1)S(1)}, u32[]{:S(2)}, u32[]{:S(2)}) collective-permute-start(bf16[256,256]{1,0:T(8,128)(2,1)S(1)} %get-tuple-element.52), channel_id=1, source_target_pairs={{2,0},{3,1},{4,2},{5,3},{6,4},{7,5},{10,8},{11,9},{12,10},{13,11},... | collective-permute-start | bytes 393224 | tf_op jit(solution)/shard_map/ppermute | solution.py:381
  36.8 4.7 %collective-permute-start.14 = (bf16[128,1024]{1,0:T(8,128)(2,1)S(1)}, bf16[128,1024]{1,0:T(8,128)(2,1)S(1)}, u32[]{:S(2)}, u32[]{:S(2)}) collective-permute-start(bf16[128,1024]{1,0:T(8,128)(2,1)S(1)} %get-tuple-element.59), channel_id=1, source_target_pairs={{0,1},{1,0},{2,3},{3,2},{4,5},{5,4},{6,7},{7,6},{8,9},{9,8},{10,11... | collective-permute-start | bytes 786440 | tf_op jit(solution)/shard_map/ppermute | solution.py:389
  38.9 10.6 %collective-permute-start.13 = (bf16[256,256]{1,0:T(8,128)(2,1)S(1)}, bf16[256,256]{1,0:T(8,128)(2,1)S(1)}, u32[]{:S(2)}, u32[]{:S(2)}) collective-permute-start(bf16[256,256]{1,0:T(8,128)(2,1)S(1)} %shard_map.82.refs_4_), channel_id=1, source_target_pairs={{0,192},{1,49},{16,208},{17,33},{32,224},{33,17},{48,240},{49,1},{... | collective-permute-start | bytes 393224 | tf_op jit(solution)/shard_map/ppermute | solution.py:340
  41.4 8.1 %collective-permute-start.12 = (bf16[256,256]{1,0:T(8,128)(2,1)S(1)}, bf16[256,256]{1,0:T(8,128)(2,1)S(1)}, u32[]{:S(2)}, u32[]{:S(2)}) collective-permute-start(bf16[256,256]{1,0:T(8,128)(2,1)S(1)} %shard_map.82.refs_4_), channel_id=1, source_target_pairs={{0,128},{1,33},{16,144},{17,49},{32,160},{33,1},{48,176},{49,17},{... | collective-permute-start | bytes 393224 | tf_op jit(solution)/shard_map/ppermute | solution.py:340
  41.5 8.0 %collective-permute-start.11 = (bf16[256,256]{1,0:T(8,128)(2,1)S(1)}, bf16[256,256]{1,0:T(8,128)(2,1)S(1)}, u32[]{:S(2)}, u32[]{:S(2)}) collective-permute-start(bf16[256,256]{1,0:T(8,128)(2,1)S(1)} %shard_map.82.refs_4_), channel_id=1, source_target_pairs={{0,64},{1,17},{16,80},{17,1},{32,96},{33,49},{48,112},{49,33},{64,... | collective-permute-start | bytes 393224 | tf_op jit(solution)/shard_map/ppermute | solution.py:340
  51.1 6.8 %collective-permute-start.15 = (bf16[512,256]{1,0:T(8,128)(2,1)S(1)}, bf16[512,256]{1,0:T(8,128)(2,1)S(1)}, u32[]{:S(2)}, u32[]{:S(2)}) collective-permute-start(bf16[512,256]{1,0:T(8,128)(2,1)S(1)} %get-tuple-element.69), channel_id=1, source_target_pairs={{0,32},{1,129},{16,48},{17,145},{32,0},{33,161},{48,16},{49,177},{... | collective-permute-start | bytes 786440 | tf_op jit(solution)/shard_map/ppermute | solution.py:340
  53.8 7.3 %collective-permute-start.16 = (bf16[512,256]{1,0:T(8,128)(2,1)S(1)}, bf16[512,256]{1,0:T(8,128)(2,1)S(1)}, u32[]{:S(2)}, u32[]{:S(2)}) collective-permute-start(bf16[512,256]{1,0:T(8,128)(2,1)S(1)} %get-tuple-element.70), channel_id=1, source_target_pairs={{0,16},{1,65},{16,0},{17,81},{32,48},{33,97},{48,32},{49,113},{64,... | collective-permute-start | bytes 786440 | tf_op jit(solution)/shard_map/ppermute | solution.py:340
  54.2 6.9 %collective-permute-start.17 = (bf16[512,256]{1,0:T(8,128)(2,1)S(1)}, bf16[512,256]{1,0:T(8,128)(2,1)S(1)}, u32[]{:S(2)}, u32[]{:S(2)}) collective-permute-start(bf16[512,256]{1,0:T(8,128)(2,1)S(1)} %get-tuple-element.71), channel_id=1, source_target_pairs={{0,48},{1,193},{16,32},{17,209},{32,16},{33,225},{48,0},{49,241},{... | collective-permute-start | bytes 786440 | tf_op jit(solution)/shard_map/ppermute | solution.py:340
